TPU v7x, 32 devices: a whole 2x2x4 slice. The times are simulated.
32 devices in a mesh: tm: 16 (over z, x, core), section: 2 (over y).
Axes of the slice: x: 2, y: 2, z: 4, core: 2. Of those that a mesh axis runs over, the one named last changes fastest.
Arguments:
- layer_inputs: bfloat16 [2, 2048, 1024], P('section', 'tm')
- top_grad: bfloat16 [2048, 1024], P('tm'), may hold values from -6 to 6
- w_query: bfloat16 [2, 1024, 512], P('section')
- w_key: bfloat16 [2, 1024, 512], P('section')
- w_value: bfloat16 [2, 1024, 512], P('section'), may hold values from -0.1875 to 0.1875
- w_out: bfloat16 [2, 512, 1024], P('section'), may hold values from -0.25 to 0.25
- conv_kernel: float32 [2, 31, 1024], P('section'), may hold values from -1 to 1
- norm_gain: float32 [2, 1024], P('section'), may hold values from 0.5 to 1.5
- group_valid: int32 [16], replicated, may hold values from 1 to 128, as said below
Outputs:
- input_grads: bfloat16 [2, 2048, 1024], P('section', 'tm')
Inputs may be any that keep to these rules, and one draw needn't show every extreme that they name: `group_valid`: entry c counts the valid frames at the start of group c; the rest of that group is padding. The first group is full and the last one is ragged.
All inputs are finite; a program needn't handle non-finite values.
Results may differ from a plain program's by a relative error of at most 0.017.
The roundings to bfloat16 on the way count: a program that leaves them out, or rounds other values in their place, can miss the bound.
Values may be sent and summed in bfloat16 or wider, within the bound.
No kernel may reach another device: no remote copies, remote signals or barrier semaphores. Data moves between devices by JAX's collectives and lax.ppermute only.
A program may use at most 64 MiB of HBM per device.

v0:
```python
import jax
import jax.numpy as jnp
from jax import lax
from jax.sharding import PartitionSpec as P

HEADS = 8
HEAD_DIM = 64
GROUP = 128
LEFT = 4


NEGATIVE = -1e30
EPSILON = 1e-05


def shifted(value, axis, steps):
    count = lax.axis_size(axis)
    initial, last = (max(0, -steps), min(count, count - steps))
    return lax.ppermute(value, axis, [(source, source + steps) for source in range(initial, last)])


def frame_mask(counts):
    within = jnp.arange(GROUP, dtype=jnp.int32)[None, :] < counts[:, None]
    return within.reshape(-1).astype(jnp.float32)


def normalize(values):
    center = values - jnp.mean(values, axis=-1, keepdims=True)
    spread = jnp.mean(center * center, axis=-1, keepdims=True)
    inverse = lax.rsqrt(spread + EPSILON)
    return (center * inverse, inverse)


def allowed_pairs(query_first, query_count, key_first, key_count, key_valid):
    query_group = (query_first + jnp.arange(query_count, dtype=jnp.int32)) // GROUP
    key_index = key_first + jnp.arange(key_count, dtype=jnp.int32)
    key_group = jnp.floor_divide(key_index, GROUP)
    allowed = (key_group[None, :] <= query_group[:, None]) & (
        key_group[None, :] >= query_group[:, None] - LEFT
    )
    return allowed & (key_valid[None, :] > 0) & (key_index[None, :] >= 0)


def head_split(matrix):
    return matrix.reshape(matrix.shape[0], HEADS, HEAD_DIM)


def score_block(queries, key_rows, allowed):
    score_scale = HEAD_DIM ** (-0.5)
    scores = (
        jnp.einsum(
            "qhe,khe->hqk",
            head_split(queries),
            head_split(key_rows),
            preferred_element_type=jnp.float32,
        )
        * score_scale
    )
    return jnp.where(allowed[None], scores, NEGATIVE)


def attend(queries, key_rows, value_rows, allowed):
    scores = score_block(queries, key_rows, allowed)
    highest = jnp.max(scores, axis=-1, keepdims=True)
    log_total = highest[..., 0] + jnp.log(jnp.sum(jnp.exp(scores - highest), axis=-1))
    shares = jnp.exp(scores - log_total[..., None])
    shares_low = shares.astype(jnp.bfloat16)
    attended = jnp.einsum(
        "hqk,khe->qhe", shares_low, head_split(value_rows), preferred_element_type=jnp.float32
    )
    return (
        attended.reshape(queries.shape[0], -1).astype(jnp.bfloat16),
        log_total,
        shares,
        shares_low,
    )


def score_grads(shares, value_rows, attended, out_grad):
    grad_heads = head_split(out_grad)
    row_dot = jnp.sum(
        grad_heads.astype(jnp.float32) * head_split(attended).astype(jnp.float32), axis=-1
    ).T
    share_grad = jnp.einsum(
        "qhe,khe->hqk", grad_heads, head_split(value_rows), preferred_element_type=jnp.float32
    )
    return (shares * (share_grad - row_dot[..., None])).astype(jnp.bfloat16)


def key_value_grads(score_grad, shares_low, queries, out_grad):
    score_scale = HEAD_DIM ** (-0.5)
    key_grad = score_scale * jnp.einsum(
        "hqk,qhe->khe", score_grad, head_split(queries), preferred_element_type=jnp.float32
    )
    value_grad = jnp.einsum(
        "hqk,qhe->khe", shares_low, head_split(out_grad), preferred_element_type=jnp.float32
    )
    count = score_grad.shape[2]
    return (key_grad.reshape(count, -1), value_grad.reshape(count, -1))


def contract(left_rows, weight):
    return lax.dot_general(
        left_rows, weight, (((1,), (1,)), ((), ())), preferred_element_type=jnp.float32
    )


def only_if(active, function, *operands):

    def skipped(*inner):
        return jax.tree.map(jnp.zeros_like, function(*inner))

    return lax.cond(active, function, skipped, *operands)


def shards(
    layer_inputs, top_grad, w_query, w_key, w_value, w_out, conv_kernel, norm_gain, group_valid
):
    inputs = layer_inputs[0]
    frames = inputs.shape[0]
    query_weight = w_query[0]
    key_weight = w_key[0]
    value_weight = w_value[0]
    out_weight = w_out[0]
    kernel = conv_kernel[0]
    norm_scale = norm_gain[0]
    tap_count = kernel.shape[0]
    sections = lax.axis_size("section")
    section_index = lax.axis_index("section")
    position = lax.axis_index("tm")
    first_frame = position * frames
    groups_here = frames // GROUP
    span_back = -(-(LEFT * GROUP) // frames)
    window_rows = (span_back + 1) * frames
    padded_counts = jnp.concatenate([jnp.zeros((span_back * groups_here,), jnp.int32), group_valid])
    own_valid = frame_mask(
        lax.dynamic_slice_in_dim(group_valid, position * groups_here, groups_here)
    )
    window_valid = frame_mask(
        lax.dynamic_slice_in_dim(
            padded_counts, position * groups_here, (span_back + 1) * groups_here
        )
    )
    widened = inputs.astype(jnp.float32)
    unit, inverse = normalize(widened)
    normed = (unit * norm_scale).astype(jnp.bfloat16)
    queries = jnp.dot(normed, query_weight, preferred_element_type=jnp.float32).astype(jnp.bfloat16)
    key_here = jnp.dot(normed, key_weight, preferred_element_type=jnp.float32).astype(jnp.bfloat16)
    value_here = jnp.dot(normed, value_weight, preferred_element_type=jnp.float32).astype(
        jnp.bfloat16
    )
    key_parts = []
    value_parts = []
    for distance in range(span_back, 0, -1):
        far_keys, far_values = shifted((key_here, value_here), "tm", distance)
        key_parts.append(far_keys)
        value_parts.append(far_values)
    key_window = jnp.concatenate(key_parts + [key_here])
    value_window = jnp.concatenate(value_parts + [value_here])
    allowed = allowed_pairs(
        first_frame, frames, first_frame - span_back * frames, window_rows, window_valid
    )
    attended, log_total, shares, shares_low = attend(queries, key_window, value_window, allowed)
    residual = widened + jnp.dot(attended, out_weight, preferred_element_type=jnp.float32)
    mixer_input = (residual * own_valid[:, None]).astype(jnp.bfloat16)
    edge_rows = shifted(mixer_input[frames - (tap_count - 1) :], "tm", 1)
    mixer_pad = jnp.concatenate([edge_rows, mixer_input]).astype(jnp.float32)
    mixer_output = jnp.zeros_like(widened)
    for offset in range(tap_count):
        mixer_output = mixer_output + kernel[offset] * mixer_pad[offset : offset + frames]
    gate_value = jax.nn.sigmoid(mixer_output)
    swish_slope = gate_value * (1.0 + mixer_output * (1.0 - gate_value))
    key_from = 0

    def first_part(upstream, mixer_grad, next_rows):
        grad_pad = jnp.concatenate([mixer_grad, next_rows]).astype(jnp.float32)
        mixer_back = jnp.zeros_like(widened)
        for offset in range(tap_count):
            mixer_back = (
                mixer_back
                + kernel[offset]
                * grad_pad[tap_count - 1 - offset : tap_count - 1 - offset + frames]
            )
        total_grad = upstream.astype(jnp.float32) + mixer_back * own_valid[:, None]
        total_low = total_grad.astype(jnp.bfloat16)
        out_grad = contract(total_low, out_weight).astype(jnp.bfloat16)
        score_grad = score_grads(shares, value_window, attended, out_grad)
        query_grad = HEAD_DIM ** (-0.5) * jnp.einsum(
            "hqk,khe->qhe", score_grad, head_split(key_window), preferred_element_type=jnp.float32
        )
        query_grad = query_grad.reshape(frames, -1).astype(jnp.bfloat16)
        key_grad, value_grad = key_value_grads(score_grad, shares_low, queries, out_grad)
        return (total_grad, out_grad, query_grad, key_grad, value_grad)

    def last_part(total_grad, query_grad, key_sum, value_sum):
        normed_grad = contract(query_grad, query_weight)
        normed_grad = normed_grad + contract(key_sum.astype(jnp.bfloat16), key_weight)
        normed_grad = normed_grad + contract(value_sum.astype(jnp.bfloat16), value_weight)
        scaled = normed_grad * norm_scale
        norm_back = inverse * (
            scaled
            - jnp.mean(scaled, axis=-1, keepdims=True)
            - unit * jnp.mean(scaled * unit, axis=-1, keepdims=True)
        )
        return (total_grad + norm_back).astype(jnp.bfloat16)

    def step(step_number, state_pair):
        upstream, result = state_pair
        active = section_index == sections - 1 - step_number
        mixer_grad = only_if(
            active,
            lambda upper_rows: (upper_rows.astype(jnp.float32) * swish_slope).astype(jnp.bfloat16),
            upstream,
        )
        next_rows = shifted(mixer_grad[: tap_count - 1], "tm", -1)
        total_grad, out_grad, query_grad, key_grad, value_grad = only_if(
            active, first_part, upstream, mixer_grad, next_rows
        )
        key_low = key_grad.astype(jnp.bfloat16)
        value_low = value_grad.astype(jnp.bfloat16)
        own_from = span_back * frames
        key_sum = key_low[own_from:].astype(jnp.float32)
        value_sum = value_low[own_from:].astype(jnp.float32)
        for distance in range(1, span_back + 1):
            lower = (span_back - distance) * frames
            back_keys, back_values = shifted(
                (key_low[lower : lower + frames], value_low[lower : lower + frames]),
                "tm",
                -distance,
            )
            key_sum = key_sum + back_keys.astype(jnp.float32)
            value_sum = value_sum + back_values.astype(jnp.float32)
        input_grad = only_if(active, last_part, total_grad, query_grad, key_sum, value_sum)
        result = jnp.where(active, input_grad, result)
        passed = shifted(input_grad, "section", -1)
        return (passed, result)

    final_pair = lax.fori_loop(0, sections, step, (top_grad, jnp.zeros_like(inputs)))
    return final_pair[1][None]


def solution(mesh):
    placed = (
        P("section", "tm", None),
        P("tm", None),
        P("section", None, None),
        P("section", None, None),
        P("section", None, None),
        P("section", None, None),
        P("section", None, None),
        P("section", None),
        P(),
    )
    return jax.shard_map(
        shards, mesh=mesh, in_specs=placed, out_specs=P("section", "tm", None), check_vma=False
    )
```

profile of v0, /device:TPU:16, one launch (start us, length us, event | category | flops | bytes accessed | tf_op | source)
XLA Modules:
  0.0 194.1 jit_solution(2878099013737259748)
XLA Ops:
  3.0 1.7 convolution_convert_fusion.1
  4.7 3.5 %collective-permute-start.14 = (bf16[128,512]{1,0:T(8,128)(2,1)S(1)}, bf16[128,512]{1,0:T(8,128)(2,1)S(1)}, u32[]{:S(2)}, u32[]{:S(2)}) collective-permute-start(bf16[128,512]{1,0:T(8,128)(2,1)S(1)} %convolution_convert_fusion.1), channel_id=1, source_target_pairs={{0,8},{2,10},{4,12},{6,14},{8,16},{10,18},{12,20},{14,22},{16,24},... | collective-permute-start | bytes 393224 | tf_op jit(solution)/shard_map/ppermute | solution.py:19
  8.2 2.6 %collective-permute-start.15 = (bf16[128,512]{1,0:T(8,128)(2,1)S(1)}, bf16[128,512]{1,0:T(8,128)(2,1)S(1)}, u32[]{:S(2)}, u32[]{:S(2)}) collective-permute-start(bf16[128,512]{1,0:T(8,128)(2,1)S(1)} %convolution_convert_fusion.1), channel_id=1, source_target_pairs={{0,6},{2,8},{4,10},{6,12},{8,14},{10,16},{12,18},{14,20},{16,22},{... | collective-permute-start | bytes 393224 | tf_op jit(solution)/shard_map/ppermute | solution.py:19
  10.8 2.8 %collective-permute-start.16 = (bf16[128,512]{1,0:T(8,128)(2,1)S(1)}, bf16[128,512]{1,0:T(8,128)(2,1)S(1)}, u32[]{:S(2)}, u32[]{:S(2)}) collective-permute-start(bf16[128,512]{1,0:T(8,128)(2,1)S(1)} %convolution_convert_fusion.1), channel_id=1, source_target_pairs={{0,4},{2,6},{4,8},{6,10},{8,12},{10,14},{12,16},{14,18},{16,20},{1... | collective-permute-start | bytes 393224 | tf_op jit(solution)/shard_map/ppermute | solution.py:19
  13.6 1.9 collective-permute-start.17
  20.2 1.9 collective-permute-start.10
  22.2 1.9 collective-permute-start.11
  24.1 2.2 %collective-permute-start.12 = (bf16[128,512]{1,0:T(8,128)(2,1)S(1)}, bf16[128,512]{1,0:T(8,128)(2,1)}, u32[]{:S(2)}, u32[]{:S(2)}) collective-permute-start(bf16[128,512]{1,0:T(8,128)(2,1)S(1)} %convolution_convert_fusion.3), channel_id=1, source_target_pairs={{0,4},{2,6},{4,8},{6,10},{8,12},{10,14},{12,16},{14,18},{16,20},{1... | collective-permute-start | bytes 393224 | tf_op jit(solution)/shard_map/ppermute | solution.py:19
  26.4 2.0 %collective-permute-start.13 = (bf16[128,512]{1,0:T(8,128)(2,1)S(1)}, bf16[128,512]{1,0:T(8,128)(2,1)}, u32[]{:S(2)}, u32[]{:S(2)}) collective-permute-start(bf16[128,512]{1,0:T(8,128)(2,1)S(1)} %convolution_convert_fusion.3), channel_id=1, source_target_pairs={{0,2},{2,4},{4,6},{6,8},{8,10},{10,12},{12,14},{14,16},{16,18},{18... | collective-permute-start | bytes 393224 | tf_op jit(solution)/shard_map/ppermute | solution.py:19
  30.2 1.6 fusion.93
  34.3 1.6 constant_dynamic-update-slice_fusion.2
  35.9 1.6 constant_dynamic-update-slice_fusion.1
  38.1 2.2 %copy.26 = bf16[640,512]{0,1:T(8,128)(2,1)} copy(bf16[640,512]{1,0:T(8,128)(2,1)} %constant_dynamic-update-slice_fusion) | data formatting | bytes 1310720 | tf_op jit(solution)/shard_map/concatenate | solution.py:159
  40.3 2.1 %convolution_convert_fusion.4 = bf16[8,64,128]{2,1,0:T(8,128)(2,1)S(1)} fusion(bf16[640,8,64]{0,2,1:T(8,128)(2,1)} %bitcast.150, bf16[8,128,640]{2,1,0:T(8,128)(2,1)} %get-tuple-element.887), kind=kOutput, calls=%fused_computation.97 | convolution fusion | flops 83951616 | bytes 2097152 | tf_op jit(solution)/shard_map/hqk,khe->qhe/dot_general | solution.py:68
  42.4 1.6 fusion.40
  44.1 2.1 %collective-permute-start.18 = (bf16[30,1024]{1,0:T(8,128)(2,1)S(1)}, bf16[30,1024]{1,0:T(8,128)(2,1)S(1)}, u32[]{:S(2)}, u32[]{:S(2)}) collective-permute-start(bf16[30,1024]{1,0:T(8,128)(2,1)S(1)} %slice.599), channel_id=1, source_target_pairs={{0,2},{2,4},{4,6},{6,8},{8,10},{10,12},{12,14},{14,16},{16,18},{18... | collective-permute-start | bytes 184328 | tf_op jit(solution)/shard_map/ppermute | solution.py:19
  46.9 3.6 %collective-permute-done.18 = bf16[30,1024]{1,0:T(8,128)(2,1)S(1)} collective-permute-done((bf16[30,1024]{1,0:T(8,128)(2,1)S(1)}, bf16[30,1024]{1,0:T(8,128)(2,1)S(1)}, u32[]{:S(2)}, u32[]{:S(2)}) %collective-permute-start.18) | collective-permute-done | bytes 61472 | tf_op jit(solution)/shard_map/ppermute | solution.py:19
  50.7 3.8 %add_multiply_fusion = f32[128,1024]{1,0:T(8,128)} fusion(f32[158,1024]{1,0:T(8,128)S(1)} %maximum_convert_fusion.1, f32[1024]{0:T(1024)S(1)} %bitcast.225, f32[1024]{0:T(1024)S(1)} %bitcast.196, f32[1024]{0:T(1024)S(1)} %bitcast.197, f32[1024]{0:T(1024)S(1)} %bitcast.198, f32[1024]{0:T(1024)} %bitcast.199, f32[1024]{0:T(1024)} %bitcast.200, ...), kind=kLoop, calls=%fused_computation.169 | loop fusion | flops 8912896 | bytes 16904192 | tf_op jit(solution)/shard_map/mul | solution.py:172
  54.5 139.6 %while.16 = (s32[]{:T(128)}, bf16[128,1024]{1,0:T(8,128)(2,1)S(1)}, bf16[128,1024]{1,0:T(8,128)(2,1)}, s32[]{:T(128)}, f32[128,1024]{1,0:T(8,128)}, /*index=5*/f...) while((s32[]{:T(128)}, bf16[128,1024]{1,0:T(8,128)(2,1)S(1)}, ...), condition=%wide.region_14.15_spmd.clone, body=%wide.region_4.14_spmd.clone.sunk | while | flops 888200448 | bytes 87462744 | solution.py:238
  54.6 1.9 collective-permute-start
  57.1 1.2 collective-permute-done
  58.4 2.5 %conditional.10 = (f32[128,1024]{1,0:T(8,128)S(1)}, bf16[128,512]{0,1:T(8,128)(2,1)}, bf16[640,512]{0,1:T(8,128)(2,1)}, bf16[640,512]{0,1:T(8,128)(2,1)}) conditional(s32[]{:T(128)} %convert_element_type.307, () %tuple.146, (bf16[128,1024]{1,0:T(8,128)(2,1)S(1)}, f32[31,1024]{1,0:T(8,128)}, bf16[128,1024]{1,0:T(8,128)(2,1)S(1)}, ...), branch_computations={%region_7.7_spmd, %region_8.9_spmd} | conditional | flops 482008064 | bytes 49988352 | solution.py:113
  60.9 2.2 %copy.38 = bf16[640,512]{1,0:T(8,128)(2,1)} copy(bf16[640,512]{0,1:T(8,128)(2,1)} %get-tuple-element.854) | data formatting | bytes 1310720 | tf_op jit(solution)/shard_map/while/body/eval_jaxpr/cond | solution.py:113
  63.0 2.1 %fusion.122 = (bf16[128,512]{1,0:T(8,128)(2,1)}, bf16[128,512]{1,0:T(8,128)(2,1)}, bf16[128,512]{1,0:T(8,128)(2,1)}, bf16[128,512]{1,0:T(8,128)(2,1)}, f32[128,512]{1,0:T(8,128)}) fusion(bf16[640,512]{1,0:T(8,128)(2,1)} %copy.38), kind=kLoop, calls=%fused_computation.217.clone.1 | loop fusion | flops 65536 | bytes 1441792 | tf_op jit(solution)/shard_map/while/body/eval_jaxpr/slice | solution.py:227
  65.1 4.6 %collective-permute-start.1 = (bf16[128,512]{1,0:T(8,128)(2,1)}, bf16[128,512]{1,0:T(8,128)(2,1)S(1)}, u32[]{:S(2)}, u32[]{:S(2)}) collective-permute-start(bf16[128,512]{1,0:T(8,128)(2,1)} %get-tuple-element.856), channel_id=1, source_target_pairs={{2,0},{4,2},{6,4},{8,6},{10,8},{12,10},{14,12},{16,14},{18,16},{20... | collective-permute-start | bytes 393224 | tf_op jit(solution)/shard_map/while/body/eval_jaxpr/ppermute | solution.py:19
  69.7 2.1 %collective-permute-start.2 = (bf16[128,512]{1,0:T(8,128)(2,1)}, bf16[128,512]{1,0:T(8,128)(2,1)S(1)}, u32[]{:S(2)}, u32[]{:S(2)}) collective-permute-start(bf16[128,512]{1,0:T(8,128)(2,1)} %get-tuple-element.857), channel_id=1, source_target_pairs={{4,0},{6,2},{8,4},{10,6},{12,8},{14,10},{16,12},{18,14},{20,16},{2... | collective-permute-start | bytes 393224 | tf_op jit(solution)/shard_map/while/body/eval_jaxpr/ppermute | solution.py:19
  71.9 3.8 %collective-permute-start.3 = (bf16[128,512]{1,0:T(8,128)(2,1)}, bf16[128,512]{1,0:T(8,128)(2,1)}, u32[]{:S(2)}, u32[]{:S(2)}) collective-permute-start(bf16[128,512]{1,0:T(8,128)(2,1)} %get-tuple-element.858), channel_id=1, source_target_pairs={{6,0},{8,2},{10,4},{12,6},{14,8},{16,10},{18,12},{20,14},{22,16},{... | collective-permute-start | bytes 393224 | tf_op jit(solution)/shard_map/while/body/eval_jaxpr/ppermute | solution.py:19
  75.6 2.6 %collective-permute-start.4 = (bf16[128,512]{1,0:T(8,128)(2,1)}, bf16[128,512]{1,0:T(8,128)(2,1)S(1)}, u32[]{:S(2)}, u32[]{:S(2)}) collective-permute-start(bf16[128,512]{1,0:T(8,128)(2,1)} %get-tuple-element.859), channel_id=1, source_target_pairs={{8,0},{10,2},{12,4},{14,6},{16,8},{18,10},{20,12},{22,14},{24,16},... | collective-permute-start | bytes 393224 | tf_op jit(solution)/shard_map/while/body/eval_jaxpr/ppermute | solution.py:19
  78.2 2.2 %copy.39 = bf16[640,512]{1,0:T(8,128)(2,1)} copy(bf16[640,512]{0,1:T(8,128)(2,1)} %get-tuple-element.860) | data formatting | bytes 1310720 | tf_op jit(solution)/shard_map/while/body/eval_jaxpr/cond | solution.py:113
  80.4 1.9 fusion.123
  82.3 3.1 %collective-permute-start.5 = (bf16[128,512]{1,0:T(8,128)(2,1)S(1)}, bf16[128,512]{1,0:T(8,128)(2,1)S(1)}, u32[]{:S(2)}, u32[]{:S(2)}) collective-permute-start(bf16[128,512]{1,0:T(8,128)(2,1)S(1)} %get-tuple-element.862), channel_id=1, source_target_pairs={{2,0},{4,2},{6,4},{8,6},{10,8},{12,10},{14,12},{16,14},{18,16},{20... | collective-permute-start | bytes 393224 | tf_op jit(solution)/shard_map/while/body/eval_jaxpr/ppermute | solution.py:19
  85.4 1.9 collective-permute-start.6
  87.3 1.9 collective-permute-start.7
  89.3 1.9 collective-permute-start.8
  92.7 1.6 convert_element_type.310
  96.6 2.7 %collective-permute-done.8 = bf16[128,512]{1,0:T(8,128)(2,1)S(1)} collective-permute-done((bf16[128,512]{1,0:T(8,128)(2,1)S(1)}, bf16[128,512]{1,0:T(8,128)(2,1)S(1)}, u32[]{:S(2)}, u32[]{:S(2)}) %collective-permute-start.8) | collective-permute-done | bytes 131104 | tf_op jit(solution)/shard_map/while/body/eval_jaxpr/ppermute | solution.py:19
  100.8 1.3 collective-permute-start.9
  102.8 22.7 %collective-permute-done.9 = bf16[128,1024]{1,0:T(8,128)(2,1)S(1)} collective-permute-done((bf16[128,1024]{1,0:T(8,128)(2,1)}, bf16[128,1024]{1,0:T(8,128)(2,1)S(1)}, u32[]{:S(2)}, u32[]{:S(2)}) %collective-permute-start.9) | collective-permute-done | bytes 262176 | tf_op jit(solution)/shard_map/while/body/eval_jaxpr/ppermute | solution.py:19
  126.7 1.9 collective-permute-start
  130.5 11.9 %conditional.10 = (f32[128,1024]{1,0:T(8,128)S(1)}, bf16[128,512]{0,1:T(8,128)(2,1)}, bf16[640,512]{0,1:T(8,128)(2,1)}, bf16[640,512]{0,1:T(8,128)(2,1)}) conditional(s32[]{:T(128)} %convert_element_type.307, () %tuple.146, (bf16[128,1024]{1,0:T(8,128)(2,1)S(1)}, f32[31,1024]{1,0:T(8,128)}, bf16[128,1024]{1,0:T(8,128)(2,1)S(1)}, ...), branch_computations={%region_7.7_spmd, %region_8.9_spmd} | conditional | flops 482008064 | bytes 49988352 | solution.py:113
  130.5 1.4 fusion.94
  133.1 3.1 %fusion.5 = f32[128,1024]{1,0:T(8,128)S(1)} fusion(f32[158,1024]{1,0:T(8,128)S(1)} %maximum_convert_fusion, bf16[128,1024]{1,0:T(8,128)(2,1)} %copy-done.7, f32[128]{0:T(128)S(1)} %get-tuple-element.394, f32[1024]{0:T(1024)S(1)} %bitcast.160, f32[1024]{0:T(1024)S(1)} %bitcast.161, f32[1024]{0:T(1024)S(1)} %bitcast.162, f32[1024]{0:T(1024)S(1)} %bitcast.163, ...), kind=kLoop, calls=%fused_computation.10 | loop fusion | flops 8388608 | bytes 17166848 | tf_op jit(solution)/shard_map/while/body/eval_jaxpr/cond/branch_1_fun/add | solution.py:184
  137.0 1.7 multiply_convert_fusion.1
  139.9 1.3 fusion.2
  142.4 2.2 %copy.38 = bf16[640,512]{1,0:T(8,128)(2,1)} copy(bf16[640,512]{0,1:T(8,128)(2,1)} %get-tuple-element.854) | data formatting | bytes 1310720 | tf_op jit(solution)/shard_map/while/body/eval_jaxpr/cond | solution.py:113
  144.6 2.1 %fusion.122 = (bf16[128,512]{1,0:T(8,128)(2,1)}, bf16[128,512]{1,0:T(8,128)(2,1)}, bf16[128,512]{1,0:T(8,128)(2,1)}, bf16[128,512]{1,0:T(8,128)(2,1)}, f32[128,512]{1,0:T(8,128)}) fusion(bf16[640,512]{1,0:T(8,128)(2,1)} %copy.38), kind=kLoop, calls=%fused_computation.217.clone.1 | loop fusion | flops 65536 | bytes 1441792 | tf_op jit(solution)/shard_map/while/body/eval_jaxpr/slice | solution.py:227
  146.6 4.6 %collective-permute-start.1 = (bf16[128,512]{1,0:T(8,128)(2,1)}, bf16[128,512]{1,0:T(8,128)(2,1)S(1)}, u32[]{:S(2)}, u32[]{:S(2)}) collective-permute-start(bf16[128,512]{1,0:T(8,128)(2,1)} %get-tuple-element.856), channel_id=1, source_target_pairs={{2,0},{4,2},{6,4},{8,6},{10,8},{12,10},{14,12},{16,14},{18,16},{20... | collective-permute-start | bytes 393224 | tf_op jit(solution)/shard_map/while/body/eval_jaxpr/ppermute | solution.py:19
  151.2 1.9 collective-permute-start.2
  153.2 1.9 collective-permute-start.3
  155.1 1.9 collective-permute-start.4
  157.0 2.2 %copy.39 = bf16[640,512]{1,0:T(8,128)(2,1)} copy(bf16[640,512]{0,1:T(8,128)(2,1)} %get-tuple-element.860) | data formatting | bytes 1310720 | tf_op jit(solution)/shard_map/while/body/eval_jaxpr/cond | solution.py:113
  159.2 1.9 fusion.123
  161.1 2.2 %collective-permute-start.5 = (bf16[128,512]{1,0:T(8,128)(2,1)S(1)}, bf16[128,512]{1,0:T(8,128)(2,1)S(1)}, u32[]{:S(2)}, u32[]{:S(2)}) collective-permute-start(bf16[128,512]{1,0:T(8,128)(2,1)S(1)} %get-tuple-element.862), channel_id=1, source_target_pairs={{2,0},{4,2},{6,4},{8,6},{10,8},{12,10},{14,12},{16,14},{18,16},{20... | collective-permute-start | bytes 393224 | tf_op jit(solution)/shard_map/while/body/eval_jaxpr/ppermute | solution.py:19
  163.4 2.2 %collective-permute-start.6 = (bf16[128,512]{1,0:T(8,128)(2,1)S(1)}, bf16[128,512]{1,0:T(8,128)(2,1)S(1)}, u32[]{:S(2)}, u32[]{:S(2)}) collective-permute-start(bf16[128,512]{1,0:T(8,128)(2,1)S(1)} %get-tuple-element.863), channel_id=1, source_target_pairs={{4,0},{6,2},{8,4},{10,6},{12,8},{14,10},{16,12},{18,14},{20,16},{2... | collective-permute-start | bytes 393224 | tf_op jit(solution)/shard_map/while/body/eval_jaxpr/ppermute | solution.py:19
  165.6 1.9 collective-permute-start.7
  167.5 1.9 collective-permute-start.8
  170.9 1.6 convert_element_type.310
  174.8 3.1 %collective-permute-done.8 = bf16[128,512]{1,0:T(8,128)(2,1)S(1)} collective-permute-done((bf16[128,512]{1,0:T(8,128)(2,1)S(1)}, bf16[128,512]{1,0:T(8,128)(2,1)S(1)}, u32[]{:S(2)}, u32[]{:S(2)}) %collective-permute-start.8) | collective-permute-done | bytes 131104 | tf_op jit(solution)/shard_map/while/body/eval_jaxpr/ppermute | solution.py:19
  178.6 5.6 %conditional.11 = (bf16[128,1024]{1,0:T(8,128)(2,1)}) conditional(s32[]{:T(128)} %convert_element_type.307, () %tuple.145, (f32[128,1]{0,1:T(1,128)S(1)}, bf16[128,512]{0,1:T(8,128)(2,1)}, bf16[1024,512]{1,0:T(8,128)(2,1)}, f32[128,512]{1,0:T(8,128)}, f32[128,512]{1,0:T(8,128)}, /*index=5*/f32[128,512]{1,0:T(8,128)}, f32[128,512]{1,0:T(8,128)}, ...), branch_computations={%region_10.10_spmd, %region_11.13_spmd} | conditional | flops 404881408 | bytes 21373616 | solution.py:113
  178.7 1.9 fusion.101
  180.6 2.1 %convolution_add_fusion.1 = f32[128,1024]{1,0:T(8,128)S(1)} fusion(f32[128,1024]{1,0:T(8,128)S(1)} %fusion.101, bf16[1024,512]{1,0:T(8,128)(2,1)} %get-tuple-element.411, f32[128,512]{1,0:T(8,128)} %get-tuple-element.410, f32[128,512]{1,0:T(8,128)} %get-tuple-element.409, f32[128,512]{1,0:T(8,128)} %get-tuple-element.408, ...), kind=kOutput, calls=%fused_computation.75 | convolution fusion | flops 134676480 | bytes 3407872 | tf_op jit(solution)/shard_map/while/body/eval_jaxpr/cond/branch_1_fun/dot_general | solution.py:103
  184.2 1.3 collective-permute-start.9
  185.5 1.8 select_select_fusion.2
  187.3 6.8 %collective-permute-done.9 = bf16[128,1024]{1,0:T(8,128)(2,1)S(1)} collective-permute-done((bf16[128,1024]{1,0:T(8,128)(2,1)}, bf16[128,1024]{1,0:T(8,128)(2,1)S(1)}, u32[]{:S(2)}, u32[]{:S(2)}) %collective-permute-start.9) | collective-permute-done | bytes 262176 | tf_op jit(solution)/shard_map/while/body/eval_jaxpr/ppermute | solution.py:19
  (150 shorter events, 37.5 us)
Async XLA Ops:
  0.0 15.5 %copy-start.20 = (bf16[1,128,1024]{2,1,0:T(8,128)(2,1)S(1)}, bf16[1,128,1024]{2,1,0:T(8,128)(2,1)}, u32[]{:S(2)}) copy-start(bf16[1,128,1024]{2,1,0:T(8,128)(2,1)} %param.17) | copy-start | bytes 786436
  0.0 16.7 %copy-start.22 = (f32[1,1024]{1,0:T(1,128)S(1)}, f32[1,1024]{1,0:T(1,128)}, u32[]{:S(2)}) copy-start(f32[1,1024]{1,0:T(1,128)} %param.24) | copy-start | bytes 12292
  0.0 16.6 %copy-start.25 = (s32[16]{0:T(128)S(1)}, s32[16]{0:T(128)}, u32[]{:S(2)}) copy-start(s32[16]{0:T(128)} %param.25) | copy-start | bytes 196
  0.0 16.7 %copy-start.15 = (bf16[1,1024,512]{2,1,0:T(8,128)(2,1)S(1)}, bf16[1,1024,512]{2,1,0:T(8,128)(2,1)}, u32[]{:S(2)}) copy-start(bf16[1,1024,512]{2,1,0:T(8,128)(2,1)} %param.19) | copy-start | bytes 3145732
  0.0 17.1 %copy-start.9 = (bf16[1,1024,512]{2,1,0:T(8,128)(2,1)S(1)}, bf16[1,1024,512]{2,1,0:T(8,128)(2,1)}, u32[]{:S(2)}) copy-start(bf16[1,1024,512]{2,1,0:T(8,128)(2,1)} %param.21) | copy-start | bytes 3145732
  3.0 14.6 %copy-start.21 = (f32[1,31,1024]{2,0,1:T(1,128)S(1)}, f32[1,31,1024]{2,0,1:T(1,128)}, u32[]{:S(2)}) copy-start(f32[1,31,1024]{2,0,1:T(1,128)} %param.23) | copy-start | bytes 380932
  4.7 17.4 %collective-permute-start.14 = (bf16[128,512]{1,0:T(8,128)(2,1)S(1)}, bf16[128,512]{1,0:T(8,128)(2,1)S(1)}, u32[]{:S(2)}, u32[]{:S(2)}) collective-permute-start(bf16[128,512]{1,0:T(8,128)(2,1)S(1)} %convolution_convert_fusion.1), channel_id=1, source_target_pairs={{0,8},{2,10},{4,12},{6,14},{8,16},{10,18},{12,20},{14,22},{16,24},... | collective-permute-start | bytes 393224 | tf_op jit(solution)/shard_map/ppermute | solution.py:19
  8.2 15.9 %collective-permute-start.15 = (bf16[128,512]{1,0:T(8,128)(2,1)S(1)}, bf16[128,512]{1,0:T(8,128)(2,1)S(1)}, u32[]{:S(2)}, u32[]{:S(2)}) collective-permute-start(bf16[128,512]{1,0:T(8,128)(2,1)S(1)} %convolution_convert_fusion.1), channel_id=1, source_target_pairs={{0,6},{2,8},{4,10},{6,12},{8,14},{10,16},{12,18},{14,20},{16,22},{... | collective-permute-start | bytes 393224 | tf_op jit(solution)/shard_map/ppermute | solution.py:19
  10.8 15.6 %collective-permute-start.16 = (bf16[128,512]{1,0:T(8,128)(2,1)S(1)}, bf16[128,512]{1,0:T(8,128)(2,1)S(1)}, u32[]{:S(2)}, u32[]{:S(2)}) collective-permute-start(bf16[128,512]{1,0:T(8,128)(2,1)S(1)} %convolution_convert_fusion.1), channel_id=1, source_target_pairs={{0,4},{2,6},{4,8},{6,10},{8,12},{10,14},{12,16},{14,18},{16,20},{1... | collective-permute-start | bytes 393224 | tf_op jit(solution)/shard_map/ppermute | solution.py:19
  13.6 14.8 %collective-permute-start.17 = (bf16[128,512]{1,0:T(8,128)(2,1)S(1)}, bf16[128,512]{1,0:T(8,128)(2,1)S(1)}, u32[]{:S(2)}, u32[]{:S(2)}) collective-permute-start(bf16[128,512]{1,0:T(8,128)(2,1)S(1)} %convolution_convert_fusion.1), channel_id=1, source_target_pairs={{0,2},{2,4},{4,6},{6,8},{8,10},{10,12},{12,14},{14,16},{16,18},{18... | collective-permute-start | bytes 393224 | tf_op jit(solution)/shard_map/ppermute | solution.py:19
  20.2 9.2 %copy-start.18 = (bf16[128,512]{0,1:T(8,128)(2,1)}, bf16[128,512]{0,1:T(8,128)(2,1)S(1)}, u32[]{:S(2)}) copy-start(bf16[128,512]{0,1:T(8,128)(2,1)S(1)} %copy.27) | copy-start | bytes 393220
  20.2 11.6 %collective-permute-start.10 = (bf16[128,512]{1,0:T(8,128)(2,1)S(1)}, bf16[128,512]{1,0:T(8,128)(2,1)S(1)}, u32[]{:S(2)}, u32[]{:S(2)}) collective-permute-start(bf16[128,512]{1,0:T(8,128)(2,1)S(1)} %convolution_convert_fusion.3), channel_id=1, source_target_pairs={{0,8},{2,10},{4,12},{6,14},{8,16},{10,18},{12,20},{14,22},{16,24},... | collective-permute-start | bytes 393224 | tf_op jit(solution)/shard_map/ppermute | solution.py:19
  22.2 10.3 %collective-permute-start.11 = (bf16[128,512]{1,0:T(8,128)(2,1)S(1)}, bf16[128,512]{1,0:T(8,128)(2,1)S(1)}, u32[]{:S(2)}, u32[]{:S(2)}) collective-permute-start(bf16[128,512]{1,0:T(8,128)(2,1)S(1)} %convolution_convert_fusion.3), channel_id=1, source_target_pairs={{0,6},{2,8},{4,10},{6,12},{8,14},{10,16},{12,18},{14,20},{16,22},{... | collective-permute-start | bytes 393224 | tf_op jit(solution)/shard_map/ppermute | solution.py:19
  24.1 10.2 %collective-permute-start.12 = (bf16[128,512]{1,0:T(8,128)(2,1)S(1)}, bf16[128,512]{1,0:T(8,128)(2,1)}, u32[]{:S(2)}, u32[]{:S(2)}) collective-permute-start(bf16[128,512]{1,0:T(8,128)(2,1)S(1)} %convolution_convert_fusion.3), channel_id=1, source_target_pairs={{0,4},{2,6},{4,8},{6,10},{8,12},{10,14},{12,16},{14,18},{16,20},{1... | collective-permute-start | bytes 393224 | tf_op jit(solution)/shard_map/ppermute | solution.py:19
  26.4 9.5 %collective-permute-start.13 = (bf16[128,512]{1,0:T(8,128)(2,1)S(1)}, bf16[128,512]{1,0:T(8,128)(2,1)}, u32[]{:S(2)}, u32[]{:S(2)}) collective-permute-start(bf16[128,512]{1,0:T(8,128)(2,1)S(1)} %convolution_convert_fusion.3), channel_id=1, source_target_pairs={{0,2},{2,4},{4,6},{6,8},{8,10},{10,12},{12,14},{14,16},{16,18},{18... | collective-permute-start | bytes 393224 | tf_op jit(solution)/shard_map/ppermute | solution.py:19
  28.7 1.4 copy-start.5
  40.3 10.4 %copy-start.23 = (f32[1,1,1024]{2,0,1:T(1,128)S(1)}, f32[1,1,1024]{2,0,1:T(1,128)}, u32[]{:S(2)}) copy-start(f32[1,1,1024]{2,0,1:T(1,128)} %get-tuple-element.684) | copy-start | bytes 12292
  42.4 8.2 %copy-start.16 = (bf16[8,64,128]{2,1,0:T(8,128)(2,1)}, bf16[8,64,128]{2,1,0:T(8,128)(2,1)S(1)}, u32[]{:S(2)}) copy-start(bf16[8,64,128]{2,1,0:T(8,128)(2,1)S(1)} %convolution_convert_fusion.4) | copy-start | bytes 393220
  44.1 6.5 %collective-permute-start.18 = (bf16[30,1024]{1,0:T(8,128)(2,1)S(1)}, bf16[30,1024]{1,0:T(8,128)(2,1)S(1)}, u32[]{:S(2)}, u32[]{:S(2)}) collective-permute-start(bf16[30,1024]{1,0:T(8,128)(2,1)S(1)} %slice.599), channel_id=1, source_target_pairs={{0,2},{2,4},{4,6},{6,8},{8,10},{10,12},{12,14},{14,16},{16,18},{18... | collective-permute-start | bytes 184328 | tf_op jit(solution)/shard_map/ppermute | solution.py:19
  50.7 3.8 %copy-start.8 = (bf16[128,1024]{1,0:T(8,128)(2,1)S(1)}, bf16[128,1024]{1,0:T(8,128)(2,1)}, u32[]{:S(2)}) copy-start(bf16[128,1024]{1,0:T(8,128)(2,1)} %param.18) | copy-start | bytes 786436
  54.6 3.8 %collective-permute-start = (bf16[30,1024]{1,0:T(8,128)(2,1)S(1)}, bf16[30,1024]{1,0:T(8,128)(2,1)S(1)}, u32[]{:S(2)}, u32[]{:S(2)}) collective-permute-start(bf16[30,1024]{1,0:T(8,128)(2,1)S(1)} %slice.1088), channel_id=1, source_target_pairs={{2,0},{4,2},{6,4},{8,6},{10,8},{12,10},{14,12},{16,14},{18,16},{20... | collective-permute-start | bytes 184328 | tf_op jit(solution)/shard_map/while/body/eval_jaxpr/ppermute | solution.py:19
  65.1 20.3 %collective-permute-start.1 = (bf16[128,512]{1,0:T(8,128)(2,1)}, bf16[128,512]{1,0:T(8,128)(2,1)S(1)}, u32[]{:S(2)}, u32[]{:S(2)}) collective-permute-start(bf16[128,512]{1,0:T(8,128)(2,1)} %get-tuple-element.856), channel_id=1, source_target_pairs={{2,0},{4,2},{6,4},{8,6},{10,8},{12,10},{14,12},{16,14},{18,16},{20... | collective-permute-start | bytes 393224 | tf_op jit(solution)/shard_map/while/body/eval_jaxpr/ppermute | solution.py:19
  69.7 17.6 %collective-permute-start.2 = (bf16[128,512]{1,0:T(8,128)(2,1)}, bf16[128,512]{1,0:T(8,128)(2,1)S(1)}, u32[]{:S(2)}, u32[]{:S(2)}) collective-permute-start(bf16[128,512]{1,0:T(8,128)(2,1)} %get-tuple-element.857), channel_id=1, source_target_pairs={{4,0},{6,2},{8,4},{10,6},{12,8},{14,10},{16,12},{18,14},{20,16},{2... | collective-permute-start | bytes 393224 | tf_op jit(solution)/shard_map/while/body/eval_jaxpr/ppermute | solution.py:19
  71.9 17.4 %collective-permute-start.3 = (bf16[128,512]{1,0:T(8,128)(2,1)}, bf16[128,512]{1,0:T(8,128)(2,1)}, u32[]{:S(2)}, u32[]{:S(2)}) collective-permute-start(bf16[128,512]{1,0:T(8,128)(2,1)} %get-tuple-element.858), channel_id=1, source_target_pairs={{6,0},{8,2},{10,4},{12,6},{14,8},{16,10},{18,12},{20,14},{22,16},{... | collective-permute-start | bytes 393224 | tf_op jit(solution)/shard_map/while/body/eval_jaxpr/ppermute | solution.py:19
  75.6 18.7 %collective-permute-start.4 = (bf16[128,512]{1,0:T(8,128)(2,1)}, bf16[128,512]{1,0:T(8,128)(2,1)S(1)}, u32[]{:S(2)}, u32[]{:S(2)}) collective-permute-start(bf16[128,512]{1,0:T(8,128)(2,1)} %get-tuple-element.859), channel_id=1, source_target_pairs={{8,0},{10,2},{12,4},{14,6},{16,8},{18,10},{20,12},{22,14},{24,16},... | collective-permute-start | bytes 393224 | tf_op jit(solution)/shard_map/while/body/eval_jaxpr/ppermute | solution.py:19
  80.4 19.6 %copy-start.24 = (f32[128,1]{0,1:T(1,128)S(1)}, f32[128,1]{0,1:T(1,128)}, u32[]{:S(2)}) copy-start(f32[128,1]{0,1:T(1,128)} %get-tuple-element.932) | copy-start | bytes 1540 | tf_op jit(solution)/shard_map/while
  82.3 12.8 %collective-permute-start.5 = (bf16[128,512]{1,0:T(8,128)(2,1)S(1)}, bf16[128,512]{1,0:T(8,128)(2,1)S(1)}, u32[]{:S(2)}, u32[]{:S(2)}) collective-permute-start(bf16[128,512]{1,0:T(8,128)(2,1)S(1)} %get-tuple-element.862), channel_id=1, source_target_pairs={{2,0},{4,2},{6,4},{8,6},{10,8},{12,10},{14,12},{16,14},{18,16},{20... | collective-permute-start | bytes 393224 | tf_op jit(solution)/shard_map/while/body/eval_jaxpr/ppermute | solution.py:19
  85.4 9.7 %collective-permute-start.6 = (bf16[128,512]{1,0:T(8,128)(2,1)S(1)}, bf16[128,512]{1,0:T(8,128)(2,1)S(1)}, u32[]{:S(2)}, u32[]{:S(2)}) collective-permute-start(bf16[128,512]{1,0:T(8,128)(2,1)S(1)} %get-tuple-element.863), channel_id=1, source_target_pairs={{4,0},{6,2},{8,4},{10,6},{12,8},{14,10},{16,12},{18,14},{20,16},{2... | collective-permute-start | bytes 393224 | tf_op jit(solution)/shard_map/while/body/eval_jaxpr/ppermute | solution.py:19
  87.3 8.5 %collective-permute-start.7 = (bf16[128,512]{1,0:T(8,128)(2,1)S(1)}, bf16[128,512]{1,0:T(8,128)(2,1)S(1)}, u32[]{:S(2)}, u32[]{:S(2)}) collective-permute-start(bf16[128,512]{1,0:T(8,128)(2,1)S(1)} %get-tuple-element.864), channel_id=1, source_target_pairs={{6,0},{8,2},{10,4},{12,6},{14,8},{16,10},{18,12},{20,14},{22,16},{... | collective-permute-start | bytes 393224 | tf_op jit(solution)/shard_map/while/body/eval_jaxpr/ppermute | solution.py:19
  89.3 10.0 %collective-permute-start.8 = (bf16[128,512]{1,0:T(8,128)(2,1)S(1)}, bf16[128,512]{1,0:T(8,128)(2,1)S(1)}, u32[]{:S(2)}, u32[]{:S(2)}) collective-permute-start(bf16[128,512]{1,0:T(8,128)(2,1)S(1)} %get-tuple-element.865), channel_id=1, source_target_pairs={{8,0},{10,2},{12,4},{14,6},{16,8},{18,10},{20,12},{22,14},{24,16},... | collective-permute-start | bytes 393224 | tf_op jit(solution)/shard_map/while/body/eval_jaxpr/ppermute | solution.py:19
  100.8 24.8 %collective-permute-start.9 = (bf16[128,1024]{1,0:T(8,128)(2,1)}, bf16[128,1024]{1,0:T(8,128)(2,1)S(1)}, u32[]{:S(2)}, u32[]{:S(2)}) collective-permute-start(bf16[128,1024]{1,0:T(8,128)(2,1)} %get-tuple-element.942), channel_id=1, source_target_pairs={{1,0},{3,2},{5,4},{7,6},{9,8},{11,10},{13,12},{15,14},{17,16},{19,... | collective-permute-start | bytes 786440 | tf_op jit(solution)/shard_map/while/body/eval_jaxpr/ppermute | solution.py:19
  126.7 3.8 %collective-permute-start = (bf16[30,1024]{1,0:T(8,128)(2,1)S(1)}, bf16[30,1024]{1,0:T(8,128)(2,1)S(1)}, u32[]{:S(2)}, u32[]{:S(2)}) collective-permute-start(bf16[30,1024]{1,0:T(8,128)(2,1)S(1)} %slice.1088), channel_id=1, source_target_pairs={{2,0},{4,2},{6,4},{8,6},{10,8},{12,10},{14,12},{16,14},{18,16},{20... | collective-permute-start | bytes 184328 | tf_op jit(solution)/shard_map/while/body/eval_jaxpr/ppermute | solution.py:19
  130.5 2.6 %copy-start.7 = (bf16[128,1024]{1,0:T(8,128)(2,1)}, bf16[128,1024]{1,0:T(8,128)(2,1)S(1)}, u32[]{:S(2)}) copy-start(bf16[128,1024]{1,0:T(8,128)(2,1)S(1)} %get-tuple-element.390) | copy-start | bytes 786436 | tf_op jit(solution)/shard_map/while/body/eval_jaxpr/cond
  133.1 3.2 %copy-start.4 = (bf16[512,1024]{1,0:T(8,128)(2,1)S(1)}, bf16[512,1024]{1,0:T(8,128)(2,1)}, u32[]{:S(2)}) copy-start(bf16[512,1024]{1,0:T(8,128)(2,1)} %get-tuple-element.396) | copy-start | bytes 3145732 | tf_op jit(solution)/shard_map/while/body/eval_jaxpr/cond
  133.1 3.8 %copy-start.17 = (bf16[128,512]{0,1:T(8,128)(2,1)S(1)}, bf16[128,512]{0,1:T(8,128)(2,1)}, u32[]{:S(2)}) copy-start(bf16[128,512]{0,1:T(8,128)(2,1)} %get-tuple-element.398) | copy-start | bytes 393220 | tf_op jit(solution)/shard_map/while/body/eval_jaxpr/cond
  136.2 2.5 %copy-start = (f32[128,1024]{1,0:T(8,128)}, f32[128,1024]{1,0:T(8,128)S(1)}, u32[]{:S(2)}) copy-start(f32[128,1024]{1,0:T(8,128)S(1)} %fusion.5) | copy-start | bytes 1572868 | tf_op jit(solution)/shard_map/while/body/eval_jaxpr/cond
  136.9 1.8 copy-start.19
  136.9 3.0 %copy-start.6 = (bf16[640,512]{0,1:T(8,128)(2,1)S(1)}, bf16[640,512]{0,1:T(8,128)(2,1)}, u32[]{:S(2)}) copy-start(bf16[640,512]{0,1:T(8,128)(2,1)} %get-tuple-element.399) | copy-start | bytes 1966084 | tf_op jit(solution)/shard_map/while/body/eval_jaxpr/cond
  138.7 2.5 %copy-start.2 = (bf16[8,128,640]{2,1,0:T(8,128)(2,1)S(1)}, bf16[8,128,640]{2,1,0:T(8,128)(2,1)}, u32[]{:S(2)}) copy-start(bf16[8,128,640]{2,1,0:T(8,128)(2,1)} %get-tuple-element.401) | copy-start | bytes 3932164 | tf_op jit(solution)/shard_map/while/body/eval_jaxpr/cond
  139.9 2.5 %copy-start.1 = (f32[128,1024]{1,0:T(8,128)S(1)}, f32[128,1024]{1,0:T(8,128)}, u32[]{:S(2)}) copy-start(f32[128,1024]{1,0:T(8,128)} %copy-done) | copy-start | bytes 1572868 | tf_op jit(solution)/shard_map/while/body/eval_jaxpr/cond
  146.6 16.7 %collective-permute-start.1 = (bf16[128,512]{1,0:T(8,128)(2,1)}, bf16[128,512]{1,0:T(8,128)(2,1)S(1)}, u32[]{:S(2)}, u32[]{:S(2)}) collective-permute-start(bf16[128,512]{1,0:T(8,128)(2,1)} %get-tuple-element.856), channel_id=1, source_target_pairs={{2,0},{4,2},{6,4},{8,6},{10,8},{12,10},{14,12},{16,14},{18,16},{20... | collective-permute-start | bytes 393224 | tf_op jit(solution)/shard_map/while/body/eval_jaxpr/ppermute | solution.py:19
  151.2 14.3 %collective-permute-start.2 = (bf16[128,512]{1,0:T(8,128)(2,1)}, bf16[128,512]{1,0:T(8,128)(2,1)S(1)}, u32[]{:S(2)}, u32[]{:S(2)}) collective-permute-start(bf16[128,512]{1,0:T(8,128)(2,1)} %get-tuple-element.857), channel_id=1, source_target_pairs={{4,0},{6,2},{8,4},{10,6},{12,8},{14,10},{16,12},{18,14},{20,16},{2... | collective-permute-start | bytes 393224 | tf_op jit(solution)/shard_map/while/body/eval_jaxpr/ppermute | solution.py:19
  153.2 14.3 %collective-permute-start.3 = (bf16[128,512]{1,0:T(8,128)(2,1)}, bf16[128,512]{1,0:T(8,128)(2,1)}, u32[]{:S(2)}, u32[]{:S(2)}) collective-permute-start(bf16[128,512]{1,0:T(8,128)(2,1)} %get-tuple-element.858), channel_id=1, source_target_pairs={{6,0},{8,2},{10,4},{12,6},{14,8},{16,10},{18,12},{20,14},{22,16},{... | collective-permute-start | bytes 393224 | tf_op jit(solution)/shard_map/while/body/eval_jaxpr/ppermute | solution.py:19
  155.1 17.5 %collective-permute-start.4 = (bf16[128,512]{1,0:T(8,128)(2,1)}, bf16[128,512]{1,0:T(8,128)(2,1)S(1)}, u32[]{:S(2)}, u32[]{:S(2)}) collective-permute-start(bf16[128,512]{1,0:T(8,128)(2,1)} %get-tuple-element.859), channel_id=1, source_target_pairs={{8,0},{10,2},{12,4},{14,6},{16,8},{18,10},{20,12},{22,14},{24,16},... | collective-permute-start | bytes 393224 | tf_op jit(solution)/shard_map/while/body/eval_jaxpr/ppermute | solution.py:19
  159.2 19.4 %copy-start.24 = (f32[128,1]{0,1:T(1,128)S(1)}, f32[128,1]{0,1:T(1,128)}, u32[]{:S(2)}) copy-start(f32[128,1]{0,1:T(1,128)} %get-tuple-element.932) | copy-start | bytes 1540 | tf_op jit(solution)/shard_map/while
  161.1 12.2 %collective-permute-start.5 = (bf16[128,512]{1,0:T(8,128)(2,1)S(1)}, bf16[128,512]{1,0:T(8,128)(2,1)S(1)}, u32[]{:S(2)}, u32[]{:S(2)}) collective-permute-start(bf16[128,512]{1,0:T(8,128)(2,1)S(1)} %get-tuple-element.862), channel_id=1, source_target_pairs={{2,0},{4,2},{6,4},{8,6},{10,8},{12,10},{14,12},{16,14},{18,16},{20... | collective-permute-start | bytes 393224 | tf_op jit(solution)/shard_map/while/body/eval_jaxpr/ppermute | solution.py:19
  163.4 10.0 %collective-permute-start.6 = (bf16[128,512]{1,0:T(8,128)(2,1)S(1)}, bf16[128,512]{1,0:T(8,128)(2,1)S(1)}, u32[]{:S(2)}, u32[]{:S(2)}) collective-permute-start(bf16[128,512]{1,0:T(8,128)(2,1)S(1)} %get-tuple-element.863), channel_id=1, source_target_pairs={{4,0},{6,2},{8,4},{10,6},{12,8},{14,10},{16,12},{18,14},{20,16},{2... | collective-permute-start | bytes 393224 | tf_op jit(solution)/shard_map/while/body/eval_jaxpr/ppermute | solution.py:19
  165.6 8.5 %collective-permute-start.7 = (bf16[128,512]{1,0:T(8,128)(2,1)S(1)}, bf16[128,512]{1,0:T(8,128)(2,1)S(1)}, u32[]{:S(2)}, u32[]{:S(2)}) collective-permute-start(bf16[128,512]{1,0:T(8,128)(2,1)S(1)} %get-tuple-element.864), channel_id=1, source_target_pairs={{6,0},{8,2},{10,4},{12,6},{14,8},{16,10},{18,12},{20,14},{22,16},{... | collective-permute-start | bytes 393224 | tf_op jit(solution)/shard_map/while/body/eval_jaxpr/ppermute | solution.py:19
  167.5 10.4 %collective-permute-start.8 = (bf16[128,512]{1,0:T(8,128)(2,1)S(1)}, bf16[128,512]{1,0:T(8,128)(2,1)S(1)}, u32[]{:S(2)}, u32[]{:S(2)}) collective-permute-start(bf16[128,512]{1,0:T(8,128)(2,1)S(1)} %get-tuple-element.865), channel_id=1, source_target_pairs={{8,0},{10,2},{12,4},{14,6},{16,8},{18,10},{20,12},{22,14},{24,16},... | collective-permute-start | bytes 393224 | tf_op jit(solution)/shard_map/while/body/eval_jaxpr/ppermute | solution.py:19
  178.6 4.1 %copy-start.3 = (f32[128,1024]{1,0:T(8,128)S(1)}, f32[128,1024]{1,0:T(8,128)}, u32[]{:S(2)}) copy-start(f32[128,1024]{1,0:T(8,128)} %get-tuple-element.419) | copy-start | bytes 1572868 | tf_op jit(solution)/shard_map/while/body/eval_jaxpr/cond
  178.6 4.1 %copy-start.10 = (bf16[1024,512]{1,0:T(8,128)(2,1)S(1)}, bf16[1024,512]{1,0:T(8,128)(2,1)}, u32[]{:S(2)}) copy-start(bf16[1024,512]{1,0:T(8,128)(2,1)} %get-tuple-element.417) | copy-start | bytes 3145732 | tf_op jit(solution)/shard_map/while/body/eval_jaxpr/cond
  178.6 4.1 %copy-start.11 = (f32[128,512]{1,0:T(8,128)S(1)}, f32[128,512]{1,0:T(8,128)}, u32[]{:S(2)}) copy-start(f32[128,512]{1,0:T(8,128)} %get-tuple-element.414) | copy-start | bytes 786436 | tf_op jit(solution)/shard_map/while/body/eval_jaxpr/cond
  178.6 4.1 %copy-start.12 = (f32[128,512]{1,0:T(8,128)S(1)}, f32[128,512]{1,0:T(8,128)}, u32[]{:S(2)}) copy-start(f32[128,512]{1,0:T(8,128)} %get-tuple-element.415) | copy-start | bytes 786436 | tf_op jit(solution)/shard_map/while/body/eval_jaxpr/cond
  178.6 4.1 %copy-start.13 = (f32[128,512]{1,0:T(8,128)S(1)}, f32[128,512]{1,0:T(8,128)}, u32[]{:S(2)}) copy-start(f32[128,512]{1,0:T(8,128)} %get-tuple-element.416) | copy-start | bytes 786436 | tf_op jit(solution)/shard_map/while/body/eval_jaxpr/cond
  178.7 4.1 %copy-start.14 = (f32[128,512]{1,0:T(8,128)S(1)}, f32[128,512]{1,0:T(8,128)}, u32[]{:S(2)}) copy-start(f32[128,512]{1,0:T(8,128)} %get-tuple-element.412) | copy-start | bytes 786436 | tf_op jit(solution)/shard_map/while/body/eval_jaxpr/cond
  184.2 9.8 %collective-permute-start.9 = (bf16[128,1024]{1,0:T(8,128)(2,1)}, bf16[128,1024]{1,0:T(8,128)(2,1)S(1)}, u32[]{:S(2)}, u32[]{:S(2)}) collective-permute-start(bf16[128,1024]{1,0:T(8,128)(2,1)} %get-tuple-element.942), channel_id=1, source_target_pairs={{1,0},{3,2},{5,4},{7,6},{9,8},{11,10},{13,12},{15,14},{17,16},{19,... | collective-permute-start | bytes 786440 | tf_op jit(solution)/shard_map/while/body/eval_jaxpr/ppermute | solution.py:19
where the time goes:
time: 196 us; the launch traced here: 194 us
  starting transfers between devices  67.9 us (35%)
  waiting for transfers between devices  42.6 us (22%)
  other arithmetic  40.7 us (21%)
  local copies, waits for them, and re-layouts  24.5 us (12%)
  matrix products  17.4 us (9%)
    ppermute x29, starting transfers between devices, shifted(): lax.ppermute(value, axis, [(source, source + steps) for source in range(i...  67.9 us
    ppermute x29, waiting for transfers between devices, shifted(): lax.ppermute(value, axis, [(source, source + steps) for source in range(i...  42.6 us
    cond x4, local copies, waits for them, and re-layouts, only_if(): return lax.cond(active, function, skipped, *operands)  8.68 us
    convert_element_type x8, other arithmetic, step(): key_sum = key_sum + back_keys.astype(jnp.float32)  7.73 us
    unnamed x31, local copies, waits for them, and re-layouts  5.22 us
    dot_general x4, matrix products, contract(): lax.dot_general(left_rows, weight, (((1,), (1,)), ((), ())), preferred_el...  5.09 us
    convert_element_type x8, other arithmetic, step(): value_sum = value_sum + back_values.astype(jnp.float32)  4.45 us
    slice x2, other arithmetic, step(): key_low[lower:lower + frames]  4.13 us
  transfers between devices with their start and end apart: 29, of which 8 were waited for; matrix products, arithmetic and copies ran while one was open for 18% of the time, Pallas kernels for 0%

commit v1 on v0

v1 whole, which is shorter than its diff:
```python
import functools

import jax
import jax.numpy as jnp
from jax import lax
from jax.experimental import pallas as pl
from jax.experimental.pallas import tpu as pltpu
from jax.sharding import PartitionSpec as P

HEAD_DIM = 64
PAIR = 128
ROWS = 128
LEFT = 4
EDGE = 32
SCALE = HEAD_DIM ** (-0.5)
NEGATIVE = -1e30
EPSILON = 1e-05
F32 = jnp.float32
BF16 = jnp.bfloat16
VMEM_LIMIT = 56 * 1024 * 1024


def dot_nn(a, b):
    return lax.dot_general(a, b, (((1,), (0,)), ((), ())), preferred_element_type=F32)


def dot_nt(a, b):
    return lax.dot_general(a, b, (((1,), (1,)), ((), ())), preferred_element_type=F32)


def valid_count(valid_ref, block):
    groups = valid_ref.shape[0]
    inside = (block >= 0) & (block < groups)
    return jnp.where(inside, valid_ref[jnp.clip(block, 0, groups - 1)], 0)


def even_half(rows):
    return lax.broadcasted_iota(jnp.int32, (rows, PAIR), 1) < HEAD_DIM


def unit_rows(values):
    center = values - jnp.mean(values, axis=-1, keepdims=True)
    spread = jnp.mean(center * center, axis=-1, keepdims=True)
    inverse = lax.rsqrt(spread + EPSILON)
    return center * inverse, inverse


def three_parts(value):
    first = value.astype(BF16)
    rest = value - first.astype(F32)
    second = rest.astype(BF16)
    third = (rest - second.astype(F32)).astype(BF16)
    return first, second, third


def shift_rows(value, amount):
    if amount == 0:
        return value
    return pltpu.roll(value, value.shape[0] - amount, 0)


def tap_sum(padded, kernel_ref, lanes, first, step, rows):
    taps = kernel_ref.shape[0]
    total = jnp.zeros((rows, padded.shape[1]), F32)
    for phase in range(8):
        moved = None
        for tap in range(taps):
            offset = first + step * tap
            if offset % 8 != phase:
                continue
            if moved is None:
                moved = shift_rows(padded, phase)
            base = offset - phase
            total = total + kernel_ref[tap : tap + 1, lanes] * moved[base : base + rows]
    return total


def forward_kernel(
    valid_ref,
    own_ref,
    back2_ref,
    back4_ref,
    back5_ref,
    next2_ref,
    next4_ref,
    peer_ref,
    peer_back2_ref,
    peer_back4_ref,
    peer_next2_ref,
    peer_next4_ref,
    w_query_ref,
    w_key_ref,
    w_value_ref,
    w_out_ref,
    kernel_ref,
    gain_ref,
    slope_ref,
    queries_ref,
    keys_ref,
    values_ref,
    attended_ref,
    log_ref,
    normed,
    key_all,
    value_all,
    query_all,
    attended_all,
    mixed,
):
    place = lax.axis_index("tm")
    odd = lax.rem(place, 2) == 1
    sources = (
        (peer_back4_ref, back5_ref),
        (back4_ref, back4_ref),
        (peer_back2_ref, peer_back4_ref),
        (back2_ref, back2_ref),
        (peer_ref, peer_back2_ref),
        (own_ref, own_ref),
        (peer_next2_ref, peer_ref),
        (next2_ref, next2_ref),
        (peer_next4_ref, peer_next2_ref),
        (next4_ref, next4_ref),
    )
    chunk = 16
    gain = gain_ref[...]

    def block_rows(index, rows):
        when_odd, when_even = sources[index]
        if when_odd is when_even:
            return when_odd[rows, :].astype(F32)
        return jnp.where(odd, when_odd[rows, :].astype(F32), when_even[rows, :].astype(F32))

    for index in range(len(sources)):

        def norm_step(step, carry, index=index):
            row = pl.multiple_of(step * chunk, chunk)
            unit, _ = unit_rows(block_rows(index, pl.ds(row, chunk)))
            normed[pl.ds(pl.multiple_of(index * ROWS + row, chunk), chunk), :] = (unit * gain).astype(BF16)
            return carry

        lax.fori_loop(0, ROWS // chunk, norm_step, 0, unroll=2)

    key_rows = 7 * ROWS
    lane_even = lax.rem(lax.broadcasted_iota(jnp.int32, (ROWS, w_key_ref.shape[1]), 1), PAIR) < HEAD_DIM
    zero = jnp.zeros((ROWS, w_key_ref.shape[1]), F32)
    keys = dot_nn(normed[0:key_rows, :], w_key_ref[...])
    for block in range(7):
        part = keys[block * ROWS : (block + 1) * ROWS]
        key_all[0, block * ROWS : (block + 1) * ROWS, :] = jnp.where(lane_even, part, zero).astype(BF16)
        key_all[1, block * ROWS : (block + 1) * ROWS, :] = jnp.where(lane_even, zero, part).astype(BF16)
        if 1 <= block <= 5:
            keys_ref[(block - 1) * ROWS : block * ROWS, :] = part.astype(BF16)
    values = dot_nn(normed[0:key_rows, :], w_value_ref[...])
    for block in range(7):
        part = values[block * ROWS : (block + 1) * ROWS]
        value_all[0, block * ROWS : (block + 1) * ROWS, :] = jnp.where(lane_even, part, zero).astype(BF16)
        value_all[1, block * ROWS : (block + 1) * ROWS, :] = jnp.where(lane_even, zero, part).astype(BF16)
        if 1 <= block <= 5:
            values_ref[(block - 1) * ROWS : block * ROWS, :] = part.astype(BF16)
    query_first = 5 * ROWS - EDGE
    query_all[...] = dot_nn(normed[query_first:, :], w_query_ref[...]).astype(BF16)
    queries_ref[...] = query_all[EDGE:, :]

    counts = [valid_count(valid_ref, place + block - 5) for block in range(7)]
    key_lane = lax.broadcasted_iota(jnp.int32, (1, ROWS), 1)
    allowed = jnp.concatenate([key_lane < count for count in counts], axis=1)
    span = (LEFT + 1) * ROWS
    groups = (
        (0, EDGE, 0),
        (EDGE, EDGE + ROWS, ROWS),
        (EDGE + ROWS, 2 * EDGE + ROWS, 2 * ROWS),
    )
    log_lane = lax.broadcasted_iota(jnp.int32, (ROWS, PAIR), 1)
    logs = jnp.zeros((ROWS, PAIR), F32)
    query_rows = ROWS + 2 * EDGE
    for pair in range(w_key_ref.shape[1] // PAIR):
        lanes = slice(pair * PAIR, (pair + 1) * PAIR)
        query_pair = query_all[0:query_rows, lanes]
        scores = [dot_nt(query_pair, key_all[half, :, lanes]) * SCALE for half in range(2)]
        for low, high, first in groups:
            total = None
            for half in range(2):
                part = jnp.where(
                    allowed[:, first : first + span],
                    scores[half][low:high, first : first + span],
                    NEGATIVE,
                )
                highest = jnp.max(part, axis=-1, keepdims=True)
                exped = jnp.exp(part - highest)
                summed = jnp.sum(exped, axis=-1, keepdims=True)
                shares_low = (exped * (1.0 / summed)).astype(BF16)
                product = dot_nn(shares_low, value_all[half, first : first + span, lanes])
                total = product if total is None else total + product
                if low == EDGE:
                    logs = jnp.where(log_lane == 2 * pair + half, highest + jnp.log(summed), logs)
            attended_all[low:high, lanes] = total.astype(BF16)
    log_ref[...] = logs
    attended_ref[...] = attended_all[EDGE : EDGE + ROWS, :]

    projected = dot_nn(attended_all[...], w_out_ref[...])
    row_ids = lax.broadcasted_iota(jnp.int32, (ROWS, 1), 0)
    edge_ids = lax.broadcasted_iota(jnp.int32, (EDGE, 1), 0)
    before = projected[0:EDGE] + block_rows(4, slice(ROWS - EDGE, ROWS))
    here = projected[EDGE : EDGE + ROWS] + own_ref[...].astype(F32)
    after = projected[EDGE + ROWS :] + block_rows(6, slice(0, EDGE))
    mixed[0:EDGE, :] = jnp.where(edge_ids + (ROWS - EDGE) < counts[4], before, 0.0).astype(BF16).astype(F32)
    mixed[EDGE : EDGE + ROWS, :] = jnp.where(row_ids < counts[5], here, 0.0).astype(BF16).astype(F32)
    mixed[EDGE + ROWS :, :] = jnp.where(edge_ids < counts[6], after, 0.0).astype(BF16).astype(F32)

    taps = kernel_ref.shape[0]

    def conv_step(step, carry):
        lanes = pl.ds(pl.multiple_of(step * PAIR, PAIR), PAIR)
        output = tap_sum(mixed[:, lanes], kernel_ref, lanes, EDGE - (taps - 1), 1, ROWS + EDGE)
        gate = 1.0 / (1.0 + jnp.exp(-output))
        slope_ref[:, lanes] = gate * (1.0 + output * (1.0 - gate))
        return carry

    lax.fori_loop(0, own_ref.shape[1] // PAIR, conv_step, 0)


def mixer_kernel(
    valid_ref,
    upstream_ref,
    next_ref,
    slope_ref,
    kernel_ref,
    w_out_ref,
    attended_ref,
    log_ref,
    total_ref,
    message_ref,
    dot_ref,
    total_low,
):
    place = lax.axis_index("tm")
    count = valid_count(valid_ref, place)
    row_ids = lax.broadcasted_iota(jnp.int32, (ROWS, PAIR), 0)
    taps = kernel_ref.shape[0]

    def conv_step(step, carry):
        lanes = pl.ds(pl.multiple_of(step * PAIR, PAIR), PAIR)
        upper = upstream_ref[:, lanes].astype(F32)
        stacked = jnp.concatenate([upper, next_ref[:, lanes].astype(F32)], axis=0)
        grads = (stacked * slope_ref[:, lanes]).astype(BF16).astype(F32)
        back = tap_sum(grads, kernel_ref, lanes, taps - 1, -1, ROWS)
        total = upper + jnp.where(row_ids < count, back, 0.0)
        total_ref[:, lanes] = total
        total_low[:, lanes] = total.astype(BF16)
        return carry

    lax.fori_loop(0, upstream_ref.shape[1] // PAIR, conv_step, 0)
    out_grad = dot_nt(total_low[...], w_out_ref[...]).astype(BF16)
    message_ref[0:ROWS, :] = out_grad
    product = out_grad.astype(F32) * attended_ref[...].astype(F32)
    high = product.astype(BF16)
    low = (product - high.astype(F32)).astype(BF16)
    width = product.shape[1]
    head_of = lax.broadcasted_iota(jnp.int32, (PAIR, width), 1) // HEAD_DIM
    chosen = (head_of == lax.broadcasted_iota(jnp.int32, (PAIR, width), 0)).astype(F32).astype(BF16)
    dots = dot_nt(high, chosen) + dot_nt(low, chosen)
    dot_ref[...] = dots
    stacked = jnp.concatenate([log_ref[...].T[0:8], dots.T[0:8]], axis=0)
    message_ref[ROWS : ROWS + 16, :] = jnp.zeros((16, width), BF16)
    for index, part in enumerate(three_parts(stacked)):
        message_ref[ROWS : ROWS + 16, index * PAIR : (index + 1) * PAIR] = part


def query_kernel(
    valid_ref,
    queries_ref,
    keys_ref,
    values_ref,
    message_ref,
    log_ref,
    dot_ref,
    w_query_ref,
    out_ref,
    query_grad,
):
    place = lax.axis_index("tm")
    key_lane = lax.broadcasted_iota(jnp.int32, (1, ROWS), 1)
    allowed = jnp.concatenate(
        [key_lane < valid_count(valid_ref, place + block - LEFT) for block in range(LEFT + 1)], axis=1
    )
    span = (LEFT + 1) * ROWS
    halves = even_half(span)
    nothing = jnp.zeros((span, PAIR), BF16)
    for pair in range(keys_ref.shape[1] // PAIR):
        lanes = slice(pair * PAIR, (pair + 1) * PAIR)
        query_pair = queries_ref[:, lanes]
        grad_pair = message_ref[0:ROWS, lanes]
        key_pair = keys_ref[:, lanes]
        value_pair = values_ref[:, lanes]
        total = None
        for half in range(2):
            keep = halves if half == 0 else jnp.logical_not(halves)
            key_half = jnp.where(keep, key_pair, nothing)
            value_half = jnp.where(keep, value_pair, nothing)
            head = 2 * pair + half
            scores = dot_nt(query_pair, key_half) * SCALE
            shares = jnp.exp(jnp.where(allowed, scores, NEGATIVE) - log_ref[:, head : head + 1])
            share_grad = dot_nt(grad_pair, value_half)
            score_grad = (shares * (share_grad - dot_ref[:, head : head + 1])).astype(BF16)
            product = dot_nn(score_grad, key_half)
            total = product if total is None else total + product
        query_grad[:, lanes] = (total * SCALE).astype(BF16)
    out_ref[...] = dot_nt(query_grad[...], w_query_ref[...])


def key_kernel(
    valid_ref,
    queries_ref,
    keys_ref,
    values_ref,
    message_ref,
    next2_ref,
    next4_ref,
    peer_ref,
    peer_next2_ref,
    peer_next4_ref,
    w_key_ref,
    w_value_ref,
    gain_ref,
    own_ref,
    total_ref,
    partial_ref,
    out_ref,
    grads,
    stats,
    key_grad,
    value_grad,
):
    place = lax.axis_index("tm")
    odd = lax.rem(place, 2) == 1
    count = valid_count(valid_ref, place)
    sources = (
        (message_ref, message_ref),
        (peer_next2_ref, peer_ref),
        (next2_ref, next2_ref),
        (peer_next4_ref, peer_next2_ref),
        (next4_ref, next4_ref),
    )
    for block, (when_odd, when_even) in enumerate(sources):
        if when_odd is when_even:
            part = when_odd[...]
        else:
            part = jnp.where(odd, when_odd[...].astype(F32), when_even[...].astype(F32)).astype(BF16)
        grads[block * ROWS : (block + 1) * ROWS, :] = part[0:ROWS]
        tail = part[ROWS : ROWS + 16].astype(F32)
        stats[:, block * ROWS : (block + 1) * ROWS] = (
            tail[:, 0:PAIR] + tail[:, PAIR : 2 * PAIR] + tail[:, 2 * PAIR : 3 * PAIR]
        )
    span = (LEFT + 1) * ROWS
    halves = even_half(span)
    nothing = jnp.zeros((span, PAIR), BF16)
    key_valid = lax.broadcasted_iota(jnp.int32, (ROWS, span), 0) < count
    for pair in range(keys_ref.shape[1] // PAIR):
        lanes = slice(pair * PAIR, (pair + 1) * PAIR)
        key_pair = keys_ref[span - ROWS : span, lanes]
        value_pair = values_ref[span - ROWS : span, lanes]
        query_pair = queries_ref[:, lanes]
        grad_pair = grads[:, lanes]
        query_halves = []
        grad_halves = []
        share_halves = []
        score_halves = []
        for half in range(2):
            keep = halves if half == 0 else jnp.logical_not(halves)
            query_half = jnp.where(keep, query_pair, nothing)
            grad_half = jnp.where(keep, grad_pair, nothing)
            head = 2 * pair + half
            scores = dot_nt(key_pair, query_half) * SCALE
            shares = jnp.exp(jnp.where(key_valid, scores, NEGATIVE) - stats[head : head + 1, :])
            share_grad = dot_nt(value_pair, grad_half)
            score_grad = (shares * (share_grad - stats[8 + head : 9 + head, :])).astype(BF16)
            query_halves.append(query_half)
            grad_halves.append(grad_half)
            share_halves.append(shares.astype(BF16))
            score_halves.append(score_grad)
        key_sum = None
        value_sum = None
        for block in range(LEFT + 1):
            rows = slice(block * ROWS, (block + 1) * ROWS)
            key_term = dot_nn(
                jnp.concatenate([score_halves[0][:, rows], score_halves[1][:, rows]], axis=1),
                jnp.concatenate([query_halves[0][rows], query_halves[1][rows]], axis=0),
            )
            value_term = dot_nn(
                jnp.concatenate([share_halves[0][:, rows], share_halves[1][:, rows]], axis=1),
                jnp.concatenate([grad_halves[0][rows], grad_halves[1][rows]], axis=0),
            )
            key_term = (key_term * SCALE).astype(BF16).astype(F32)
            value_term = value_term.astype(BF16).astype(F32)
            key_sum = key_term if key_sum is None else key_sum + key_term
            value_sum = value_term if value_sum is None else value_sum + value_term
        key_grad[:, lanes] = key_sum.astype(BF16)
        value_grad[:, lanes] = value_sum.astype(BF16)
    normed_grad = partial_ref[...] + dot_nt(key_grad[...], w_key_ref[...])
    normed_grad = normed_grad + dot_nt(value_grad[...], w_value_ref[...])
    scaled = normed_grad * gain_ref[...]
    unit, inverse = unit_rows(own_ref[...].astype(F32))
    back = inverse * (
        scaled
        - jnp.mean(scaled, axis=-1, keepdims=True)
        - unit * jnp.mean(scaled * unit, axis=-1, keepdims=True)
    )
    out_ref[...] = (total_ref[...] + back).astype(BF16)


def call(kernel, name, n_inputs, outs, scratch, flops):
    vmem = pl.BlockSpec(memory_space=pltpu.VMEM)
    return pl.pallas_call(
        kernel,
        name=name,
        in_specs=[pl.BlockSpec(memory_space=pltpu.SMEM)] + [vmem] * (n_inputs - 1),
        out_specs=[vmem] * len(outs),
        out_shape=[jax.ShapeDtypeStruct(shape, dtype) for shape, dtype in outs],
        scratch_shapes=[pltpu.VMEM(shape, dtype) for shape, dtype in scratch],
        compiler_params=pltpu.CompilerParams(vmem_limit_bytes=VMEM_LIMIT),
        cost_estimate=pl.CostEstimate(flops=flops, bytes_accessed=4 << 20, transcendentals=0),
    )


def shards(
    layer_inputs, top_grad, w_query, w_key, w_value, w_out, conv_kernel, norm_gain, group_valid
):
    own = layer_inputs[0]
    width = own.shape[1]
    heads_width = w_query.shape[2]
    query_weight = w_query[0]
    key_weight = w_key[0]
    value_weight = w_value[0]
    out_weight = w_out[0]
    kernel = conv_kernel[0]
    sections = lax.axis_size("section")
    count = lax.axis_size("tm")
    section_index = lax.axis_index("section")
    place = lax.axis_index("tm")
    odd = lax.rem(place, 2) == 1

    def at(layer, frame):
        return frame * sections + layer

    def moved(value, pairs):
        return lax.ppermute(value, ("tm", "section"), pairs)

    def across(steps, chosen):
        return [
            (at(section, source), at(section, source + steps))
            for section in chosen
            for source in range(max(0, -steps), min(count, count - steps))
        ]

    def swapped(chosen):
        return [
            (at(section, source), at(section, source ^ 1))
            for section in chosen
            for source in range(count)
        ]

    every = range(sections)
    next2 = moved(own, across(-2, every))
    back2 = moved(own, across(2, every))
    back4 = moved(own, across(4, every))
    next4 = moved(own, across(-4, every))
    mixed_pairs = []
    for section in every:
        for source in range(1, count - 5, 2):
            mixed_pairs.append((at(section, source), at(section, source + 5)))
        for source in range(2, count, 2):
            mixed_pairs.append((at(section, source), at(section, source - 1)))
    back5 = moved(jnp.where(odd, own, top_grad), mixed_pairs)
    swap = swapped(every)
    peer = moved(own, swap)
    peer_top = moved(top_grad[:EDGE], swap)
    peer_back2 = moved(back2, swap)
    peer_back4 = moved(back4, swap)
    peer_next2 = moved(next2, swap)
    peer_next4 = moved(next4, swap)
    top_next = jnp.where(odd, back5[:EDGE], peer_top)

    span = (LEFT + 1) * ROWS
    slope, queries, keys, values, attended, logs = call(
        forward_kernel,
        "forward",
        18,
        [
            ((ROWS + EDGE, width), F32),
            ((span, heads_width), BF16),
            ((span, heads_width), BF16),
            ((span, heads_width), BF16),
            ((ROWS, heads_width), BF16),
            ((ROWS, PAIR), F32),
        ],
        [
            ((10 * ROWS, width), BF16),
            ((2, 7 * ROWS, heads_width), BF16),
            ((2, 7 * ROWS, heads_width), BF16),
            ((span + EDGE, heads_width), BF16),
            ((ROWS + 2 * EDGE, heads_width), BF16),
            ((ROWS + 2 * EDGE, width), F32),
        ],
        4 << 30,
    )(
        group_valid,
        own,
        back2,
        back4,
        back5,
        next2,
        next4,
        peer,
        peer_back2,
        peer_back4,
        peer_next2,
        peer_next4,
        query_weight,
        key_weight,
        value_weight,
        out_weight,
        kernel,
        norm_gain,
    )

    upstream = top_grad
    upstream_next = top_next
    result = None
    for step in range(sections):
        layer = sections - 1 - step
        total, message, dots = call(
            mixer_kernel,
            "mixer",
            8,
            [((ROWS, width), F32), ((ROWS + 16, heads_width), BF16), ((ROWS, PAIR), F32)],
            [((ROWS, width), BF16)],
            1 << 30,
        )(group_valid, upstream, upstream_next, slope, kernel, out_weight, attended, logs)
        here = [layer]
        step_swap = swapped(here)
        grad2 = moved(message, across(-2, here))
        grad4 = moved(message, across(-4, here))
        peer_grad = moved(message, step_swap)
        peer_grad2 = moved(grad2, step_swap)
        peer_grad4 = moved(grad4, step_swap)
        (partial,) = call(
            query_kernel,
            "own_queries",
            8,
            [((ROWS, width), F32)],
            [((ROWS, heads_width), BF16)],
            1 << 30,
        )(group_valid, queries[:ROWS], keys, values, message, logs, dots, query_weight)
        (input_grad,) = call(
            key_kernel,
            "own_keys",
            16,
            [((ROWS, width), BF16)],
            [
                ((span, heads_width), BF16),
                ((16, span), F32),
                ((ROWS, heads_width), BF16),
                ((ROWS, heads_width), BF16),
            ],
            1 << 30,
        )(
            group_valid,
            queries,
            keys,
            values,
            message,
            grad2,
            grad4,
            peer_grad,
            peer_grad2,
            peer_grad4,
            key_weight,
            value_weight,
            norm_gain,
            own,
            total,
            partial,
        )
        result = input_grad if result is None else jnp.where(section_index == layer, input_grad, result)
        if layer > 0:
            upstream = moved(
                input_grad,
                [(at(layer, source), at(layer - 1, source)) for source in range(count)],
            )
            upstream_next = moved(
                input_grad[:EDGE],
                [(at(layer, source), at(layer - 1, source - 1)) for source in range(1, count)],
            )
    return result[None]


def solution(mesh):
    placed = (
        P("section", "tm", None),
        P("tm", None),
        P("section", None, None),
        P("section", None, None),
        P("section", None, None),
        P("section", None, None),
        P("section", None, None),
        P("section", None),
        P(),
    )
    return jax.shard_map(
        shards, mesh=mesh, in_specs=placed, out_specs=P("section", "tm", None), check_vma=False
    )
```

time: 196 us -> 130 us (0.66)
  the two profiles are of different devices: /device:TPU:16 before, /device:TPU:1 now
where the time goes in v1:
time: 130 us; the launch traced here: 129 us
  Pallas kernels  52.8 us (41%)
  starting transfers between devices  37.4 us (29%)
  waiting for transfers between devices  28.2 us (22%)
  local copies, waits for them, and re-layouts  7.17 us (6%)
  other arithmetic  3.36 us (3%)
    ppermute x23, starting transfers between devices, moved(): return lax.ppermute(value, ('tm', 'section'), pairs)  37.4 us
    ppermute x23, waiting for transfers between devices, moved(): return lax.ppermute(value, ('tm', 'section'), pairs)  28.2 us
    pallas_call x1, Pallas kernels, shards(): call(forward_kernel, 'forward', 18, [((ROWS + EDGE, width), F32), ((span,...  20.7 us
    pallas_call x2, Pallas kernels, shards(): call(key_kernel, 'own_keys', 16, [((ROWS, width), BF16)], [((span, heads_...  12.7 us
    pallas_call x2, Pallas kernels, shards(): call(mixer_kernel, 'mixer', 8, [((ROWS, width), F32), ((ROWS + 16, heads_...  9.95 us
    pallas_call x2, Pallas kernels, shards(): call(query_kernel, 'own_queries', 8, [((ROWS, width), F32)], [((ROWS, hea...  9.38 us
    unnamed x51, local copies, waits for them, and re-layouts  3.89 us
  transfers between devices with their start and end apart: 23, of which 6 were waited for; matrix products, arithmetic and copies ran while one was open for 4% of the time, Pallas kernels for 7%

profile of v1, /device:TPU:1, one launch (start us, length us, event | category | flops | bytes accessed | tf_op | source)
XLA Modules:
  0.0 129.3 jit_solution(16175162410778527396)
XLA Ops:
  0.0 0.8 slice.14
  0.8 0.1 collective-permute-start.10
  0.9 1.0 broadcast_select_fusion
  2.0 5.5 %collective-permute-start.2 = (bf16[128,1024]{1,0:T(8,128)(2,1)S(1)}, bf16[128,1024]{1,0:T(8,128)(2,1)S(1)}, u32[]{:S(2)}, u32[]{:S(2)}) collective-permute-start(bf16[128,1024]{1,0:T(8,128)(2,1)S(1)} %broadcast_select_fusion), channel_id=1, source_target_pairs={{2,12},{6,16},{10,20},{14,24},{18,28},{4,2},{8,6},{12,10},{16,14},... | collective-permute-start | bytes 786440 | tf_op jit(solution)/shard_map/ppermute | solution.py:446
  7.5 3.2 %collective-permute-start = (bf16[128,1024]{1,0:T(8,128)(2,1)S(1)}, bf16[128,1024]{1,0:T(8,128)(2,1)S(1)}, u32[]{:S(2)}, u32[]{:S(2)}) collective-permute-start(bf16[128,1024]{1,0:T(8,128)(2,1)S(1)} %bitcast.20), channel_id=1, source_target_pairs={{0,4},{2,6},{4,8},{6,10},{8,12},{10,14},{12,16},{14,18},{16,20},{1... | collective-permute-start | bytes 786440 | tf_op jit(solution)/shard_map/ppermute | solution.py:446
  10.7 3.2 %collective-permute-start.1 = (bf16[128,1024]{1,0:T(8,128)(2,1)S(1)}, bf16[128,1024]{1,0:T(8,128)(2,1)S(1)}, u32[]{:S(2)}, u32[]{:S(2)}) collective-permute-start(bf16[128,1024]{1,0:T(8,128)(2,1)S(1)} %bitcast.21), channel_id=1, source_target_pairs={{0,8},{2,10},{4,12},{6,14},{8,16},{10,18},{12,20},{14,22},{16,24},... | collective-permute-start | bytes 786440 | tf_op jit(solution)/shard_map/ppermute | solution.py:446
  13.9 1.3 collective-permute-start.3
  15.2 1.3 collective-permute-start.4
  16.5 0.0 collective-permute-done.2.back5_ref
  16.6 0.1 collective-permute-start.5
  16.6 0.4 collective-permute-done.back2_ref
  17.0 0.2 collective-permute-start.6
  17.2 1.9 %collective-permute-done.1.back4_ref = bf16[128,1024]{1,0:T(8,128)(2,1)S(1)} collective-permute-done((bf16[128,1024]{1,0:T(8,128)(2,1)S(1)}, bf16[128,1024]{1,0:T(8,128)(2,1)S(1)}, u32[]{:S(2)}, u32[]{:S(2)}) %collective-permute-start.1) | collective-permute-done | bytes 262176 | tf_op jit(solution)/shard_map/ppermute | solution.py:446
  19.2 0.0 collective-permute-start.7
  19.2 4.6 %collective-permute-done.3.next2_ref = bf16[128,1024]{1,0:T(8,128)(2,1)S(1)} collective-permute-done((bf16[128,1024]{1,0:T(8,128)(2,1)S(1)}, bf16[128,1024]{1,0:T(8,128)(2,1)S(1)}, u32[]{:S(2)}, u32[]{:S(2)}) %collective-permute-start.3) | collective-permute-done | bytes 262176 | tf_op jit(solution)/shard_map/ppermute | solution.py:446
  23.7 0.4 collective-permute-start.8
  24.1 6.2 %collective-permute-done.4.next4_ref = bf16[128,1024]{1,0:T(8,128)(2,1)S(1)} collective-permute-done((bf16[128,1024]{1,0:T(8,128)(2,1)S(1)}, bf16[128,1024]{1,0:T(8,128)(2,1)S(1)}, u32[]{:S(2)}, u32[]{:S(2)}) %collective-permute-start.4) | collective-permute-done | bytes 262176 | tf_op jit(solution)/shard_map/ppermute | solution.py:446
  30.4 0.7 collective-permute-start.9
  31.1 0.7 copy.12
  31.8 0.6 slice_select_fusion.next_ref
  32.4 0.0 collective-permute-done.5.peer_ref
  32.4 0.0 collective-permute-done.6.peer_back2_ref
  32.5 0.0 collective-permute-done.8.peer_next2_ref
  32.5 0.0 collective-permute-done.9.peer_next4_ref
  32.6 0.6 copy-done.18
  33.1 0.1 copy-done.19
  33.2 0.1 copy-done.20
  33.3 0.1 copy-done.21
  33.4 0.1 copy-done.22
  33.5 20.7 %forward.1 = (f32[160,1024]{1,0:T(8,128)}, bf16[640,512]{1,0:T(8,128)(2,1)}, bf16[640,512]{1,0:T(8,128)(2,1)}, bf16[640,512]{1,0:T(8,128)(2,1)}, bf16[128,512]{1,0:T(8,128)(2,1)}, /*index=5*/f32[128,128]{1,0:T(8,128)}) custom-call(s32[16]{0:T(128)} %valid_ref.13, bf16[128,1024]{1,0:T(8,128)(2,1)} %bitcast.17, bf16[128,1024]{1,0:T(8,128)(2,1)} %copy-done.14, ...), custom_call_target="tpu_custom_call" | custom-call | flops 4294967296 | bytes 4194304 | tf_op jit(solution)/shard_map/forward/pallas_call | solution.py:484
  54.3 5.0 %mixer.2 = (f32[128,1024]{1,0:T(8,128)}, bf16[144,512]{1,0:T(8,128)(2,1)}, f32[128,128]{1,0:T(8,128)}) custom-call(s32[16]{0:T(128)} %valid_ref.13, bf16[128,1024]{1,0:T(8,128)(2,1)} %upstream_ref.1, bf16[32,1024]{1,0:T(8,128)(2,1)} %slice_select_fusion.next_ref, f32[160,1024]{1,0:T(8,128)} %get-tuple-element.20.slope_ref, f32[31,1024]{1,0:T(8,128)} %bitcast.26, ...), custom_call_target="tpu_custom_call" | custom-call | flops 1073741824 | bytes 4194304 | tf_op jit(solution)/shard_map/mixer/pallas_call | solution.py:531
  59.2 0.7 collective-permute-start.11
  59.9 0.7 collective-permute-start.12
  60.6 0.7 collective-permute-start.13
  61.3 0.7 collective-permute-start.14
  62.0 0.9 collective-permute-start.15
  62.8 1.6 %slice.15.queries_ref = bf16[128,512]{1,0:T(8,128)(2,1)} slice(bf16[640,512]{1,0:T(8,128)(2,1)} %get-tuple-element.17.queries_ref), slice={[0:128], [0:512]} | slice | bytes 262144 | tf_op jit(solution)/shard_map/slice | solution.py:553
  64.4 4.7 %own_queries.2.partial_ref = f32[128,1024]{1,0:T(8,128)} custom-call(s32[16]{0:T(128)} %valid_ref.13, bf16[128,512]{1,0:T(8,128)(2,1)} %slice.15.queries_ref, bf16[640,512]{1,0:T(8,128)(2,1)} %get-tuple-element.18.keys_ref, bf16[640,512]{1,0:T(8,128)(2,1)} %get-tuple-element.19.values_ref, bf16[144,512]{1,0:T(8,128)(2,1)} %get-tuple-element.23.message_ref, ...), custom_call_target="tpu_custom_call" | custom-call | flops 1073741824 | bytes 4194304 | tf_op jit(solution)/shard_map/own_queries/pallas_call | solution.py:546
  69.1 0.0 collective-permute-done.13.peer_ref
  69.1 0.0 collective-permute-done.15.peer_next4_ref
  69.2 0.6 copy-done.8
  69.8 0.1 copy-done.10
  69.8 0.0 copy-done.11
  69.9 6.3 %own_keys.2 = bf16[128,1024]{1,0:T(8,128)(2,1)} custom-call(s32[16]{0:T(128)} %valid_ref.13, bf16[640,512]{1,0:T(8,128)(2,1)} %get-tuple-element.17.queries_ref, bf16[640,512]{1,0:T(8,128)(2,1)} %get-tuple-element.18.keys_ref, bf16[640,512]{1,0:T(8,128)(2,1)} %get-tuple-element.19.values_ref, bf16[144,512]{1,0:T(8,128)(2,1)} %get-tuple-element.23.message_ref, ...), custom_call_target="tpu_custom_call" | custom-call | flops 1073741824 | bytes 4194304 | tf_op jit(solution)/shard_map/own_keys/pallas_call | solution.py:554
  76.2 1.3 collective-permute-start.16
  77.5 0.8 slice.18
  78.4 1.3 collective-permute-start.17
  79.6 13.2 %collective-permute-done.17.next_ref = bf16[32,1024]{1,0:T(8,128)(2,1)S(1)} collective-permute-done((bf16[32,1024]{1,0:T(8,128)(2,1)S(1)}, bf16[32,1024]{1,0:T(8,128)(2,1)S(1)}, u32[]{:S(2)}, u32[]{:S(2)}) %collective-permute-start.17) | collective-permute-done | bytes 65568 | tf_op jit(solution)/shard_map/ppermute | solution.py:446
  92.8 1.8 %collective-permute-done.16.upstream_ref = bf16[128,1024]{1,0:T(8,128)(2,1)S(1)} collective-permute-done((bf16[128,1024]{1,0:T(8,128)(2,1)}, bf16[128,1024]{1,0:T(8,128)(2,1)S(1)}, u32[]{:S(2)}, u32[]{:S(2)}) %collective-permute-start.16) | collective-permute-done | bytes 262176 | tf_op jit(solution)/shard_map/ppermute | solution.py:446
  94.6 0.7 copy-done.23
  95.3 5.0 %mixer.3 = (f32[128,1024]{1,0:T(8,128)}, bf16[144,512]{1,0:T(8,128)(2,1)}, f32[128,128]{1,0:T(8,128)}) custom-call(s32[16]{0:T(128)} %valid_ref.13, bf16[128,1024]{1,0:T(8,128)(2,1)} %copy-done.23, bf16[32,1024]{1,0:T(8,128)(2,1)} %copy-done.24, f32[160,1024]{1,0:T(8,128)} %get-tuple-element.20.slope_ref, f32[31,1024]{1,0:T(8,128)} %bitcast.27, ...), custom_call_target="tpu_custom_call" | custom-call | flops 1073741824 | bytes 4194304 | tf_op jit(solution)/shard_map/mixer/pallas_call | solution.py:531
  100.3 1.3 collective-permute-start.18
  101.6 1.3 collective-permute-start.19
  102.9 4.3 %collective-permute-start.20 = (bf16[144,512]{1,0:T(8,128)(2,1)}, bf16[144,512]{1,0:T(8,128)(2,1)S(1)}, u32[]{:S(2)}, u32[]{:S(2)}) collective-permute-start(bf16[144,512]{1,0:T(8,128)(2,1)} %get-tuple-element.26.message_ref), channel_id=1, source_target_pairs={{0,2},{2,0},{4,6},{6,4},{8,10},{10,8},{12,14},{14,12},{16,18},{18,... | collective-permute-start | bytes 442376 | tf_op jit(solution)/shard_map/ppermute | solution.py:446
  107.2 0.0 collective-permute-done.18.next2_ref
  107.2 4.6 %collective-permute-start.21 = (bf16[144,512]{1,0:T(8,128)(2,1)S(1)}, bf16[144,512]{1,0:T(8,128)(2,1)S(1)}, u32[]{:S(2)}, u32[]{:S(2)}) collective-permute-start(bf16[144,512]{1,0:T(8,128)(2,1)S(1)} %collective-permute-done.18.next2_ref), channel_id=1, source_target_pairs={{0,2},{2,0},{4,6},{6,4},{8,10},{10,8},{12,14},{14,12},{16,18},{18,... | collective-permute-start | bytes 442376 | tf_op jit(solution)/shard_map/ppermute | solution.py:446
  111.9 3.9 %collective-permute-start.22 = (bf16[144,512]{1,0:T(8,128)(2,1)S(1)}, bf16[144,512]{1,0:T(8,128)(2,1)S(1)}, u32[]{:S(2)}, u32[]{:S(2)}) collective-permute-start(bf16[144,512]{1,0:T(8,128)(2,1)S(1)} %collective-permute-done.19.next4_ref), channel_id=1, source_target_pairs={{0,2},{2,0},{4,6},{6,4},{8,10},{10,8},{12,14},{14,12},{16,18},{18,... | collective-permute-start | bytes 442376 | tf_op jit(solution)/shard_map/ppermute | solution.py:446
  115.8 4.7 %own_queries.3.partial_ref = f32[128,1024]{1,0:T(8,128)} custom-call(s32[16]{0:T(128)} %valid_ref.13, bf16[128,512]{1,0:T(8,128)(2,1)} %slice.15.queries_ref, bf16[640,512]{1,0:T(8,128)(2,1)} %get-tuple-element.18.keys_ref, bf16[640,512]{1,0:T(8,128)(2,1)} %get-tuple-element.19.values_ref, bf16[144,512]{1,0:T(8,128)(2,1)} %get-tuple-element.26.message_ref, ...), custom_call_target="tpu_custom_call" | custom-call | flops 1073741824 | bytes 4194304 | tf_op jit(solution)/shard_map/own_queries/pallas_call | solution.py:546
  120.5 0.0 collective-permute-done.21.peer_next2_ref
  120.5 0.6 copy-done.4
  121.1 0.1 copy-done.6
  121.2 0.1 copy-done.9
  121.2 6.4 %own_keys.3 = bf16[128,1024]{1,0:T(8,128)(2,1)} custom-call(s32[16]{0:T(128)} %valid_ref.13, bf16[640,512]{1,0:T(8,128)(2,1)} %get-tuple-element.17.queries_ref, bf16[640,512]{1,0:T(8,128)(2,1)} %get-tuple-element.18.keys_ref, bf16[640,512]{1,0:T(8,128)(2,1)} %get-tuple-element.19.values_ref, bf16[144,512]{1,0:T(8,128)(2,1)} %get-tuple-element.26.message_ref, ...), custom_call_target="tpu_custom_call" | custom-call | flops 1073741824 | bytes 4194304 | tf_op jit(solution)/shard_map/own_keys/pallas_call | solution.py:554
  127.6 1.7 %select_bitcast_fusion = bf16[1,128,1024]{2,1,0:T(8,128)(2,1)} fusion(bf16[128,1024]{1,0:T(8,128)(2,1)} %own_keys.3, bf16[128,1024]{1,0:T(8,128)(2,1)S(1)} %copy-done.1, pred[]{:T(512)S(6)} %eq.6), kind=kLoop, calls=%fused_computation | loop fusion | flops 131072 | bytes 786433 | tf_op jit(solution)/shard_map/broadcast_in_dim | solution.py:594
  (46 shorter events, 0.1 us)
Async XLA Ops:
  0.8 14.4 %collective-permute-start.10 = (bf16[32,1024]{1,0:T(8,128)(2,1)S(1)}, bf16[32,1024]{1,0:T(8,128)(2,1)S(1)}, u32[]{:S(2)}, u32[]{:S(2)}) collective-permute-start(bf16[32,1024]{1,0:T(8,128)(2,1)S(1)} %slice.14), channel_id=1, source_target_pairs={{0,2},{2,0},{4,6},{6,4},{8,10},{10,8},{12,14},{14,12},{16,18},{18,... | collective-permute-start | bytes 196616 | tf_op jit(solution)/shard_map/ppermute | solution.py:446
  0.9 6.6 %copy-start = (bf16[1,128,1024]{2,1,0:T(8,128)(2,1)S(1)}, bf16[1,128,1024]{2,1,0:T(8,128)(2,1)}, u32[]{:S(2)}) copy-start(bf16[1,128,1024]{2,1,0:T(8,128)(2,1)} %param.9) | copy-start | bytes 786436
  0.9 30.2 %copy-start.12 = (f32[1,31,1024]{2,0,1:T(1,128)S(1)}, f32[1,31,1024]{2,0,1:T(1,128)}, u32[]{:S(2)}) copy-start(f32[1,31,1024]{2,0,1:T(1,128)} %param.15) | copy-start | bytes 380932
  2.0 14.6 %collective-permute-start.2 = (bf16[128,1024]{1,0:T(8,128)(2,1)S(1)}, bf16[128,1024]{1,0:T(8,128)(2,1)S(1)}, u32[]{:S(2)}, u32[]{:S(2)}) collective-permute-start(bf16[128,1024]{1,0:T(8,128)(2,1)S(1)} %broadcast_select_fusion), channel_id=1, source_target_pairs={{2,12},{6,16},{10,20},{14,24},{18,28},{4,2},{8,6},{12,10},{16,14},... | collective-permute-start | bytes 786440 | tf_op jit(solution)/shard_map/ppermute | solution.py:446
  7.5 9.5 %collective-permute-start = (bf16[128,1024]{1,0:T(8,128)(2,1)S(1)}, bf16[128,1024]{1,0:T(8,128)(2,1)S(1)}, u32[]{:S(2)}, u32[]{:S(2)}) collective-permute-start(bf16[128,1024]{1,0:T(8,128)(2,1)S(1)} %bitcast.20), channel_id=1, source_target_pairs={{0,4},{2,6},{4,8},{6,10},{8,12},{10,14},{12,16},{14,18},{16,20},{1... | collective-permute-start | bytes 786440 | tf_op jit(solution)/shard_map/ppermute | solution.py:446
  10.7 8.4 %collective-permute-start.1 = (bf16[128,1024]{1,0:T(8,128)(2,1)S(1)}, bf16[128,1024]{1,0:T(8,128)(2,1)S(1)}, u32[]{:S(2)}, u32[]{:S(2)}) collective-permute-start(bf16[128,1024]{1,0:T(8,128)(2,1)S(1)} %bitcast.21), channel_id=1, source_target_pairs={{0,8},{2,10},{4,12},{6,14},{8,16},{10,18},{12,20},{14,22},{16,24},... | collective-permute-start | bytes 786440 | tf_op jit(solution)/shard_map/ppermute | solution.py:446
  13.9 9.8 %collective-permute-start.3 = (bf16[128,1024]{1,0:T(8,128)(2,1)S(1)}, bf16[128,1024]{1,0:T(8,128)(2,1)S(1)}, u32[]{:S(2)}, u32[]{:S(2)}) collective-permute-start(bf16[128,1024]{1,0:T(8,128)(2,1)S(1)} %bitcast.22), channel_id=1, source_target_pairs={{4,0},{6,2},{8,4},{10,6},{12,8},{14,10},{16,12},{18,14},{20,16},{2... | collective-permute-start | bytes 786440 | tf_op jit(solution)/shard_map/ppermute | solution.py:446
  15.2 15.1 %collective-permute-start.4 = (bf16[128,1024]{1,0:T(8,128)(2,1)S(1)}, bf16[128,1024]{1,0:T(8,128)(2,1)S(1)}, u32[]{:S(2)}, u32[]{:S(2)}) collective-permute-start(bf16[128,1024]{1,0:T(8,128)(2,1)S(1)} %bitcast.23), channel_id=1, source_target_pairs={{8,0},{10,2},{12,4},{14,6},{16,8},{18,10},{20,12},{22,14},{24,16},... | collective-permute-start | bytes 786440 | tf_op jit(solution)/shard_map/ppermute | solution.py:446
  16.6 16.0 %copy-start.13 = (bf16[128,1024]{1,0:T(8,128)(2,1)}, bf16[128,1024]{1,0:T(8,128)(2,1)S(1)}, u32[]{:S(2)}) copy-start(bf16[128,1024]{1,0:T(8,128)(2,1)S(1)} %collective-permute-done.2.back5_ref) | copy-start | bytes 786436
  16.6 15.9 %collective-permute-start.5 = (bf16[128,1024]{1,0:T(8,128)(2,1)S(1)}, bf16[128,1024]{1,0:T(8,128)(2,1)S(1)}, u32[]{:S(2)}, u32[]{:S(2)}) collective-permute-start(bf16[128,1024]{1,0:T(8,128)(2,1)S(1)} %bitcast.24), channel_id=1, source_target_pairs={{0,2},{2,0},{4,6},{6,4},{8,10},{10,8},{12,14},{14,12},{16,18},{18,... | collective-permute-start | bytes 786440 | tf_op jit(solution)/shard_map/ppermute | solution.py:446
  17.0 15.5 %copy-start.14 = (bf16[128,1024]{1,0:T(8,128)(2,1)}, bf16[128,1024]{1,0:T(8,128)(2,1)S(1)}, u32[]{:S(2)}) copy-start(bf16[128,1024]{1,0:T(8,128)(2,1)S(1)} %collective-permute-done.back2_ref) | copy-start | bytes 786436
  17.0 15.4 %collective-permute-start.6 = (bf16[128,1024]{1,0:T(8,128)(2,1)S(1)}, bf16[128,1024]{1,0:T(8,128)(2,1)S(1)}, u32[]{:S(2)}, u32[]{:S(2)}) collective-permute-start(bf16[128,1024]{1,0:T(8,128)(2,1)S(1)} %collective-permute-done.back2_ref), channel_id=1, source_target_pairs={{0,2},{2,0},{4,6},{6,4},{8,10},{10,8},{12,14},{14,12},{16,18},{18,... | collective-permute-start | bytes 786440 | tf_op jit(solution)/shard_map/ppermute | solution.py:446
  19.2 13.4 %copy-start.15 = (bf16[128,1024]{1,0:T(8,128)(2,1)}, bf16[128,1024]{1,0:T(8,128)(2,1)S(1)}, u32[]{:S(2)}) copy-start(bf16[128,1024]{1,0:T(8,128)(2,1)S(1)} %collective-permute-done.1.back4_ref) | copy-start | bytes 786436
  19.2 13.3 %collective-permute-start.7 = (bf16[128,1024]{1,0:T(8,128)(2,1)S(1)}, bf16[128,1024]{1,0:T(8,128)(2,1)S(1)}, u32[]{:S(2)}, u32[]{:S(2)}) collective-permute-start(bf16[128,1024]{1,0:T(8,128)(2,1)S(1)} %collective-permute-done.1.back4_ref), channel_id=1, source_target_pairs={{0,2},{2,0},{4,6},{6,4},{8,10},{10,8},{12,14},{14,12},{16,18},{18,... | collective-permute-start | bytes 786440 | tf_op jit(solution)/shard_map/ppermute | solution.py:446
  23.7 8.8 %copy-start.16 = (bf16[128,1024]{1,0:T(8,128)(2,1)}, bf16[128,1024]{1,0:T(8,128)(2,1)S(1)}, u32[]{:S(2)}) copy-start(bf16[128,1024]{1,0:T(8,128)(2,1)S(1)} %collective-permute-done.3.next2_ref) | copy-start | bytes 786436
  23.7 8.7 %collective-permute-start.8 = (bf16[128,1024]{1,0:T(8,128)(2,1)S(1)}, bf16[128,1024]{1,0:T(8,128)(2,1)S(1)}, u32[]{:S(2)}, u32[]{:S(2)}) collective-permute-start(bf16[128,1024]{1,0:T(8,128)(2,1)S(1)} %collective-permute-done.3.next2_ref), channel_id=1, source_target_pairs={{0,2},{2,0},{4,6},{6,4},{8,10},{10,8},{12,14},{14,12},{16,18},{18,... | collective-permute-start | bytes 786440 | tf_op jit(solution)/shard_map/ppermute | solution.py:446
  30.4 2.2 %copy-start.17 = (bf16[128,1024]{1,0:T(8,128)(2,1)}, bf16[128,1024]{1,0:T(8,128)(2,1)S(1)}, u32[]{:S(2)}) copy-start(bf16[128,1024]{1,0:T(8,128)(2,1)S(1)} %collective-permute-done.4.next4_ref) | copy-start | bytes 786436
  30.4 2.1 %collective-permute-start.9 = (bf16[128,1024]{1,0:T(8,128)(2,1)S(1)}, bf16[128,1024]{1,0:T(8,128)(2,1)S(1)}, u32[]{:S(2)}, u32[]{:S(2)}) collective-permute-start(bf16[128,1024]{1,0:T(8,128)(2,1)S(1)} %collective-permute-done.4.next4_ref), channel_id=1, source_target_pairs={{0,2},{2,0},{4,6},{6,4},{8,10},{10,8},{12,14},{14,12},{16,18},{18,... | collective-permute-start | bytes 786440 | tf_op jit(solution)/shard_map/ppermute | solution.py:446
  32.4 0.7 copy-start.18
  32.4 0.8 copy-start.19
  32.5 0.9 copy-start.20
  32.5 0.9 copy-start.21
  32.5 1.0 copy-start.22
  59.2 2.0 %collective-permute-start.11 = (bf16[144,512]{1,0:T(8,128)(2,1)}, bf16[144,512]{1,0:T(8,128)(2,1)S(1)}, u32[]{:S(2)}, u32[]{:S(2)}) collective-permute-start(bf16[144,512]{1,0:T(8,128)(2,1)} %get-tuple-element.23.message_ref), channel_id=1, source_target_pairs={{5,1},{7,3},{9,5},{11,7},{13,9},{15,11},{17,13},{19,15},{21,17},{2... | collective-permute-start | bytes 442376 | tf_op jit(solution)/shard_map/ppermute | solution.py:446
  59.9 2.1 %collective-permute-start.12 = (bf16[144,512]{1,0:T(8,128)(2,1)}, bf16[144,512]{1,0:T(8,128)(2,1)S(1)}, u32[]{:S(2)}, u32[]{:S(2)}) collective-permute-start(bf16[144,512]{1,0:T(8,128)(2,1)} %get-tuple-element.23.message_ref), channel_id=1, source_target_pairs={{9,1},{11,3},{13,5},{15,7},{17,9},{19,11},{21,13},{23,15},{25,17},... | collective-permute-start | bytes 442376 | tf_op jit(solution)/shard_map/ppermute | solution.py:446
  60.6 8.5 %collective-permute-start.13 = (bf16[144,512]{1,0:T(8,128)(2,1)}, bf16[144,512]{1,0:T(8,128)(2,1)S(1)}, u32[]{:S(2)}, u32[]{:S(2)}) collective-permute-start(bf16[144,512]{1,0:T(8,128)(2,1)} %get-tuple-element.23.message_ref), channel_id=1, source_target_pairs={{1,3},{3,1},{5,7},{7,5},{9,11},{11,9},{13,15},{15,13},{17,19},{19,... | collective-permute-start | bytes 442376 | tf_op jit(solution)/shard_map/ppermute | solution.py:446
  61.3 7.8 %copy-start.5 = (bf16[144,512]{1,0:T(8,128)(2,1)}, bf16[144,512]{1,0:T(8,128)(2,1)S(1)}, u32[]{:S(2)}) copy-start(bf16[144,512]{1,0:T(8,128)(2,1)S(1)} %collective-permute-done.11.next2_ref) | copy-start | bytes 442372
  61.3 7.9 %collective-permute-start.14 = (bf16[144,512]{1,0:T(8,128)(2,1)S(1)}, bf16[144,512]{1,0:T(8,128)(2,1)S(1)}, u32[]{:S(2)}, u32[]{:S(2)}) collective-permute-start(bf16[144,512]{1,0:T(8,128)(2,1)S(1)} %collective-permute-done.11.next2_ref), channel_id=1, source_target_pairs={{1,3},{3,1},{5,7},{7,5},{9,11},{11,9},{13,15},{15,13},{17,19},{19,... | collective-permute-start | bytes 442376 | tf_op jit(solution)/shard_map/ppermute | solution.py:446
  62.0 7.1 %copy-start.7 = (bf16[144,512]{1,0:T(8,128)(2,1)}, bf16[144,512]{1,0:T(8,128)(2,1)S(1)}, u32[]{:S(2)}) copy-start(bf16[144,512]{1,0:T(8,128)(2,1)S(1)} %collective-permute-done.12.next4_ref) | copy-start | bytes 442372
  62.0 7.2 %collective-permute-start.15 = (bf16[144,512]{1,0:T(8,128)(2,1)S(1)}, bf16[144,512]{1,0:T(8,128)(2,1)S(1)}, u32[]{:S(2)}, u32[]{:S(2)}) collective-permute-start(bf16[144,512]{1,0:T(8,128)(2,1)S(1)} %collective-permute-done.12.next4_ref), channel_id=1, source_target_pairs={{1,3},{3,1},{5,7},{7,5},{9,11},{11,9},{13,15},{15,13},{17,19},{19,... | collective-permute-start | bytes 442376 | tf_op jit(solution)/shard_map/ppermute | solution.py:446
  69.1 0.7 copy-start.8
  69.1 0.7 copy-start.10
  69.2 0.7 copy-start.11
  76.2 18.4 %collective-permute-start.16 = (bf16[128,1024]{1,0:T(8,128)(2,1)}, bf16[128,1024]{1,0:T(8,128)(2,1)S(1)}, u32[]{:S(2)}, u32[]{:S(2)}) collective-permute-start(bf16[128,1024]{1,0:T(8,128)(2,1)} %own_keys.2), channel_id=1, source_target_pairs={{1,0},{3,2},{5,4},{7,6},{9,8},{11,10},{13,12},{15,14},{17,16},{19,... | collective-permute-start | bytes 786440 | tf_op jit(solution)/shard_map/ppermute | solution.py:446
  78.4 14.4 %collective-permute-start.17 = (bf16[32,1024]{1,0:T(8,128)(2,1)S(1)}, bf16[32,1024]{1,0:T(8,128)(2,1)S(1)}, u32[]{:S(2)}, u32[]{:S(2)}) collective-permute-start(bf16[32,1024]{1,0:T(8,128)(2,1)S(1)} %slice.18), channel_id=1, source_target_pairs={{3,0},{5,2},{7,4},{9,6},{11,8},{13,10},{15,12},{17,14},{19,16},{21... | collective-permute-start | bytes 196616 | tf_op jit(solution)/shard_map/ppermute | solution.py:446
  92.8 1.8 %copy-start.24 = (bf16[32,1024]{1,0:T(8,128)(2,1)}, bf16[32,1024]{1,0:T(8,128)(2,1)S(1)}, u32[]{:S(2)}) copy-start(bf16[32,1024]{1,0:T(8,128)(2,1)S(1)} %collective-permute-done.17.next_ref) | copy-start | bytes 196612
  94.6 0.7 copy-start.23
  100.3 6.9 %collective-permute-start.18 = (bf16[144,512]{1,0:T(8,128)(2,1)}, bf16[144,512]{1,0:T(8,128)(2,1)S(1)}, u32[]{:S(2)}, u32[]{:S(2)}) collective-permute-start(bf16[144,512]{1,0:T(8,128)(2,1)} %get-tuple-element.26.message_ref), channel_id=1, source_target_pairs={{4,0},{6,2},{8,4},{10,6},{12,8},{14,10},{16,12},{18,14},{20,16},{2... | collective-permute-start | bytes 442376 | tf_op jit(solution)/shard_map/ppermute | solution.py:446
  101.6 10.3 %collective-permute-start.19 = (bf16[144,512]{1,0:T(8,128)(2,1)}, bf16[144,512]{1,0:T(8,128)(2,1)S(1)}, u32[]{:S(2)}, u32[]{:S(2)}) collective-permute-start(bf16[144,512]{1,0:T(8,128)(2,1)} %get-tuple-element.26.message_ref), channel_id=1, source_target_pairs={{8,0},{10,2},{12,4},{14,6},{16,8},{18,10},{20,12},{22,14},{24,16},... | collective-permute-start | bytes 442376 | tf_op jit(solution)/shard_map/ppermute | solution.py:446
  102.9 17.6 %collective-permute-start.20 = (bf16[144,512]{1,0:T(8,128)(2,1)}, bf16[144,512]{1,0:T(8,128)(2,1)S(1)}, u32[]{:S(2)}, u32[]{:S(2)}) collective-permute-start(bf16[144,512]{1,0:T(8,128)(2,1)} %get-tuple-element.26.message_ref), channel_id=1, source_target_pairs={{0,2},{2,0},{4,6},{6,4},{8,10},{10,8},{12,14},{14,12},{16,18},{18,... | collective-permute-start | bytes 442376 | tf_op jit(solution)/shard_map/ppermute | solution.py:446
  107.2 13.2 %copy-start.2 = (bf16[144,512]{1,0:T(8,128)(2,1)}, bf16[144,512]{1,0:T(8,128)(2,1)S(1)}, u32[]{:S(2)}) copy-start(bf16[144,512]{1,0:T(8,128)(2,1)S(1)} %collective-permute-done.18.next2_ref) | copy-start | bytes 442372
  107.2 13.2 %collective-permute-start.21 = (bf16[144,512]{1,0:T(8,128)(2,1)S(1)}, bf16[144,512]{1,0:T(8,128)(2,1)S(1)}, u32[]{:S(2)}, u32[]{:S(2)}) collective-permute-start(bf16[144,512]{1,0:T(8,128)(2,1)S(1)} %collective-permute-done.18.next2_ref), channel_id=1, source_target_pairs={{0,2},{2,0},{4,6},{6,4},{8,10},{10,8},{12,14},{14,12},{16,18},{18,... | collective-permute-start | bytes 442376 | tf_op jit(solution)/shard_map/ppermute | solution.py:446
  111.9 8.6 %copy-start.3 = (bf16[144,512]{1,0:T(8,128)(2,1)}, bf16[144,512]{1,0:T(8,128)(2,1)S(1)}, u32[]{:S(2)}) copy-start(bf16[144,512]{1,0:T(8,128)(2,1)S(1)} %collective-permute-done.19.next4_ref) | copy-start | bytes 442372
  111.9 8.6 %collective-permute-start.22 = (bf16[144,512]{1,0:T(8,128)(2,1)S(1)}, bf16[144,512]{1,0:T(8,128)(2,1)S(1)}, u32[]{:S(2)}, u32[]{:S(2)}) collective-permute-start(bf16[144,512]{1,0:T(8,128)(2,1)S(1)} %collective-permute-done.19.next4_ref), channel_id=1, source_target_pairs={{0,2},{2,0},{4,6},{6,4},{8,10},{10,8},{12,14},{14,12},{16,18},{18,... | collective-permute-start | bytes 442376 | tf_op jit(solution)/shard_map/ppermute | solution.py:446
  120.5 0.7 copy-start.4
  120.5 0.7 copy-start.6
  120.5 0.7 copy-start.9
  121.2 6.4 %copy-start.1 = (bf16[128,1024]{1,0:T(8,128)(2,1)S(1)}, bf16[128,1024]{1,0:T(8,128)(2,1)}, u32[]{:S(2)}) copy-start(bf16[128,1024]{1,0:T(8,128)(2,1)} %own_keys.2) | copy-start | bytes 786436

commit v2 on v1

v2 whole, which is shorter than its diff:
```python
import jax
import jax.numpy as jnp
from jax import lax
from jax.experimental import pallas as pl
from jax.experimental.pallas import tpu as pltpu
from jax.sharding import PartitionSpec as P

HEAD_DIM = 64
PAIR = 128
ROWS = 128
LEFT = 4
EDGE = 32
SCALE = HEAD_DIM ** (-0.5)
NEGATIVE = -1e30
EPSILON = 1e-05
F32 = jnp.float32
BF16 = jnp.bfloat16
VMEM_LIMIT = 56 * 1024 * 1024


def dot_nn(a, b):
    return lax.dot_general(a, b, (((1,), (0,)), ((), ())), preferred_element_type=F32)


def dot_nt(a, b):
    return lax.dot_general(a, b, (((1,), (1,)), ((), ())), preferred_element_type=F32)


def valid_count(valid_ref, block):
    groups = valid_ref.shape[0]
    inside = (block >= 0) & (block < groups)
    return jnp.where(inside, valid_ref[jnp.clip(block, 0, groups - 1)], 0)


def even_half(rows):
    return lax.broadcasted_iota(jnp.int32, (rows, PAIR), 1) < HEAD_DIM


def unit_rows(values):
    center = values - jnp.mean(values, axis=-1, keepdims=True)
    spread = jnp.mean(center * center, axis=-1, keepdims=True)
    inverse = lax.rsqrt(spread + EPSILON)
    return center * inverse, inverse


def three_parts(value):
    first = value.astype(BF16)
    rest = value - first.astype(F32)
    second = rest.astype(BF16)
    third = (rest - second.astype(F32)).astype(BF16)
    return first, second, third


def shift_rows(value, amount):
    if amount == 0:
        return value
    return pltpu.roll(value, value.shape[0] - amount, 0)


def tap_sum(padded, kernel_ref, lanes, first, step, rows):
    taps = kernel_ref.shape[0]
    total = jnp.zeros((rows, padded.shape[1]), F32)
    for phase in range(8):
        moved = None
        for tap in range(taps):
            offset = first + step * tap
            if offset % 8 != phase:
                continue
            if moved is None:
                moved = shift_rows(padded, phase)
            base = offset - phase
            total = total + kernel_ref[tap : tap + 1, lanes] * moved[base : base + rows]
    return total


def project_kernel(
    own_ref,
    top_ref,
    gain_ref,
    w_query_ref,
    w_key_ref,
    w_value_ref,
    queries_ref,
    kept_ref,
    ahead_ref,
    behind_ref,
    normed,
):
    chunk = 16

    def norm_step(step, carry):
        rows = pl.ds(pl.multiple_of(step * chunk, chunk), chunk)
        unit, _ = unit_rows(own_ref[rows, :].astype(F32))
        normed[rows, :] = (unit * gain_ref[...]).astype(BF16)
        return carry

    lax.fori_loop(0, ROWS // chunk, norm_step, 0, unroll=2)
    wide = w_key_ref.shape[1]
    half = EDGE // 2
    keys = dot_nn(normed[...], w_key_ref[...]).astype(BF16)
    values = dot_nn(normed[...], w_value_ref[...]).astype(BF16)
    for ref in (kept_ref, ahead_ref, behind_ref):
        ref[0:ROWS, 0:wide] = keys
        ref[0:ROWS, wide : 2 * wide] = values
    queries = dot_nn(normed[...], w_query_ref[...]).astype(BF16)
    queries_ref[...] = queries
    ahead_ref[ROWS : ROWS + EDGE, :] = own_ref[ROWS - EDGE : ROWS, :]
    ahead_ref[ROWS + EDGE : ROWS + EDGE + half, 0:wide] = queries[ROWS - EDGE : ROWS - half]
    ahead_ref[ROWS + EDGE : ROWS + EDGE + half, wide : 2 * wide] = queries[ROWS - half : ROWS]
    behind_ref[ROWS : ROWS + EDGE, :] = own_ref[0:EDGE, :]
    behind_ref[ROWS + EDGE : ROWS + EDGE + half, 0:wide] = queries[0:half]
    behind_ref[ROWS + EDGE : ROWS + EDGE + half, wide : 2 * wide] = queries[half:EDGE]
    behind_ref[ROWS + EDGE + half : ROWS + 2 * EDGE + half, :] = top_ref[0:EDGE, :]


def chosen_rows(odd, when_odd, when_even, rows):
    if when_odd is when_even:
        return when_odd[rows, :]
    return jnp.where(odd, when_odd[rows, :].astype(F32), when_even[rows, :].astype(F32)).astype(BF16)


def gather_window(odd, sources, window):
    for index, (when_odd, when_even) in enumerate(sources):
        window[index * ROWS : (index + 1) * ROWS, :] = chosen_rows(odd, when_odd, when_even, slice(0, ROWS))


def masked_half(value, half):
    keep = even_half(value.shape[0])
    if half:
        keep = jnp.logical_not(keep)
    return jnp.where(keep, value, jnp.zeros_like(value))


def pair_shares(scores, allowed):
    part = jnp.where(allowed, scores, NEGATIVE)
    highest = jnp.max(part, axis=-1, keepdims=True)
    exped = jnp.exp(part - highest)
    summed = jnp.sum(exped, axis=-1, keepdims=True)
    return (exped * (1.0 / summed)).astype(BF16), highest, summed


def attend_kernel(
    valid_ref,
    queries_ref,
    kept_ref,
    back2_ref,
    back4_ref,
    peer_ref,
    peer_back2_ref,
    peer_back4_ref,
    after_ref,
    attended_ref,
    log_ref,
    window,
    query_all,
):
    place = lax.axis_index("tm")
    odd = lax.rem(place, 2) == 1
    wide = queries_ref.shape[1]
    half_edge = EDGE // 2
    gather_window(
        odd,
        (
            (back4_ref, back4_ref),
            (peer_back2_ref, peer_back4_ref),
            (back2_ref, back2_ref),
            (peer_ref, peer_back2_ref),
            (kept_ref, kept_ref),
            (after_ref, after_ref),
        ),
        window,
    )
    query_all[0:ROWS, :] = queries_ref[...]
    query_all[ROWS : ROWS + half_edge, :] = after_ref[ROWS + EDGE : ROWS + EDGE + half_edge, 0:wide]
    query_all[ROWS + half_edge : ROWS + EDGE, :] = after_ref[
        ROWS + EDGE : ROWS + EDGE + half_edge, wide : 2 * wide
    ]
    key_lane = lax.broadcasted_iota(jnp.int32, (1, ROWS), 1)
    allowed = jnp.concatenate(
        [key_lane < valid_count(valid_ref, place + block - LEFT) for block in range(LEFT + 2)], axis=1
    )
    span = (LEFT + 1) * ROWS
    log_lane = lax.broadcasted_iota(jnp.int32, (ROWS, PAIR), 1)
    logs = jnp.zeros((ROWS, PAIR), F32)
    for pair in range(wide // PAIR):
        lanes = slice(pair * PAIR, (pair + 1) * PAIR)
        value_lanes = slice(wide + pair * PAIR, wide + (pair + 1) * PAIR)
        totals = [None, None]
        for half in range(2):
            scores = dot_nt(query_all[:, lanes], masked_half(window[:, lanes], half)) * SCALE
            value_half = masked_half(window[:, value_lanes], half)
            for group, (low, high, first) in enumerate(((0, ROWS, 0), (ROWS, ROWS + EDGE, ROWS))):
                shares_low, highest, summed = pair_shares(
                    scores[low:high, first : first + span], allowed[:, first : first + span]
                )
                product = dot_nn(shares_low, value_half[first : first + span])
                totals[group] = product if totals[group] is None else totals[group] + product
                if group == 0:
                    logs = jnp.where(log_lane == 2 * pair + half, highest + jnp.log(summed), logs)
        attended_ref[0:ROWS, lanes] = totals[0].astype(BF16)
        attended_ref[ROWS : ROWS + EDGE, lanes] = totals[1].astype(BF16)
    log_ref[...] = logs


def mixer_body(
    count, upstream_ref, next_rows, slope_ref, kernel_ref, w_out_ref, attended, log_ref, total_ref, message_ref, dot_ref, total_low
):
    row_ids = lax.broadcasted_iota(jnp.int32, (ROWS, PAIR), 0)
    taps = kernel_ref.shape[0]

    def conv_step(step, carry):
        lanes = pl.ds(pl.multiple_of(step * PAIR, PAIR), PAIR)
        upper = upstream_ref[:, lanes].astype(F32)
        stacked = jnp.concatenate([upper, next_rows(lanes)], axis=0)
        grads = (stacked * slope_ref[:, lanes]).astype(BF16).astype(F32)
        back = tap_sum(grads, kernel_ref, lanes, taps - 1, -1, ROWS)
        total = upper + jnp.where(row_ids < count, back, 0.0)
        total_ref[:, lanes] = total
        total_low[:, lanes] = total.astype(BF16)
        return carry

    lax.fori_loop(0, upstream_ref.shape[1] // PAIR, conv_step, 0)
    out_grad = dot_nt(total_low[...], w_out_ref[...]).astype(BF16)
    message_ref[0:ROWS, :] = out_grad
    product = out_grad.astype(F32) * attended.astype(F32)
    high = product.astype(BF16)
    low = (product - high.astype(F32)).astype(BF16)
    width = product.shape[1]
    head_of = lax.broadcasted_iota(jnp.int32, (PAIR, width), 1) // HEAD_DIM
    chosen = (head_of == lax.broadcasted_iota(jnp.int32, (PAIR, width), 0)).astype(F32).astype(BF16)
    dots = dot_nt(high, chosen) + dot_nt(low, chosen)
    dot_ref[...] = dots
    stacked = jnp.concatenate([log_ref[...].T[0:8], dots.T[0:8]], axis=0)
    message_ref[ROWS : ROWS + 16, :] = jnp.zeros((16, width), BF16)
    for index, part in enumerate(three_parts(stacked)):
        message_ref[ROWS : ROWS + 16, index * PAIR : (index + 1) * PAIR] = part


def mix_kernel(
    valid_ref,
    own_ref,
    top_ref,
    attended_ref,
    log_ref,
    back2_ref,
    back4_ref,
    back5_ref,
    peer_ref,
    peer_back2_ref,
    peer_back4_ref,
    after_ref,
    w_out_ref,
    kernel_ref,
    slope_ref,
    total_ref,
    message_ref,
    dot_ref,
    window,
    query_tail,
    attended_all,
    mixed,
    total_low,
):
    place = lax.axis_index("tm")
    odd = lax.rem(place, 2) == 1
    wide = attended_ref.shape[1]
    half_edge = EDGE // 2
    counts = [valid_count(valid_ref, place + block - LEFT - 1) for block in range(LEFT + 3)]
    gather_window(
        odd,
        (
            (peer_back4_ref, back5_ref),
            (back4_ref, back4_ref),
            (peer_back2_ref, peer_back4_ref),
            (back2_ref, back2_ref),
            (peer_ref, peer_back2_ref),
        ),
        window,
    )
    packed = chosen_rows(odd, peer_ref, peer_back2_ref, slice(ROWS + EDGE, ROWS + EDGE + half_edge))
    query_tail[0:half_edge, :] = packed[:, 0:wide]
    query_tail[half_edge:EDGE, :] = packed[:, wide : 2 * wide]
    key_lane = lax.broadcasted_iota(jnp.int32, (1, ROWS), 1)
    allowed = jnp.concatenate([key_lane < count for count in counts[: LEFT + 1]], axis=1)
    for pair in range(wide // PAIR):
        lanes = slice(pair * PAIR, (pair + 1) * PAIR)
        value_lanes = slice(wide + pair * PAIR, wide + (pair + 1) * PAIR)
        total = None
        for half in range(2):
            scores = dot_nt(query_tail[:, lanes], masked_half(window[:, lanes], half)) * SCALE
            shares_low, _, _ = pair_shares(scores, allowed)
            product = dot_nn(shares_low, masked_half(window[:, value_lanes], half))
            total = product if total is None else total + product
        attended_all[0:EDGE, lanes] = total.astype(BF16)
    attended_all[EDGE:, :] = attended_ref[...]

    projected = dot_nn(attended_all[...], w_out_ref[...])
    row_ids = lax.broadcasted_iota(jnp.int32, (ROWS, 1), 0)
    edge_ids = lax.broadcasted_iota(jnp.int32, (EDGE, 1), 0)
    x_before = chosen_rows(odd, peer_ref, peer_back2_ref, slice(ROWS, ROWS + EDGE)).astype(F32)
    before = projected[0:EDGE] + x_before
    here = projected[EDGE : EDGE + ROWS] + own_ref[...].astype(F32)
    after = projected[EDGE + ROWS :] + after_ref[ROWS : ROWS + EDGE, :].astype(F32)
    before = jnp.where(edge_ids + (ROWS - EDGE) < counts[LEFT], before, 0.0)
    here = jnp.where(row_ids < counts[LEFT + 1], here, 0.0)
    after = jnp.where(edge_ids < counts[LEFT + 2], after, 0.0)
    mixed[0:EDGE, :] = before.astype(BF16).astype(F32)
    mixed[EDGE : EDGE + ROWS, :] = here.astype(BF16).astype(F32)
    mixed[EDGE + ROWS :, :] = after.astype(BF16).astype(F32)
    taps = kernel_ref.shape[0]

    def conv_step(step, carry):
        lanes = pl.ds(pl.multiple_of(step * PAIR, PAIR), PAIR)
        output = tap_sum(mixed[:, lanes], kernel_ref, lanes, EDGE - (taps - 1), 1, ROWS + EDGE)
        gate = 1.0 / (1.0 + jnp.exp(-output))
        slope_ref[:, lanes] = gate * (1.0 + output * (1.0 - gate))
        return carry

    lax.fori_loop(0, own_ref.shape[1] // PAIR, conv_step, 0)
    first = ROWS + EDGE + half_edge
    mixer_body(
        counts[LEFT + 1],
        top_ref,
        lambda lanes: after_ref[first : first + EDGE, lanes].astype(F32),
        slope_ref,
        kernel_ref,
        w_out_ref,
        attended_ref[0:ROWS, :],
        log_ref,
        total_ref,
        message_ref,
        dot_ref,
        total_low,
    )


def mixer_kernel(
    valid_ref,
    upstream_ref,
    next_ref,
    slope_ref,
    kernel_ref,
    w_out_ref,
    attended_ref,
    log_ref,
    total_ref,
    message_ref,
    dot_ref,
    total_low,
):
    mixer_body(
        valid_count(valid_ref, lax.axis_index("tm")),
        upstream_ref,
        lambda lanes: next_ref[:, lanes].astype(F32),
        slope_ref,
        kernel_ref,
        w_out_ref,
        attended_ref[0:ROWS, :],
        log_ref,
        total_ref,
        message_ref,
        dot_ref,
        total_low,
    )


def key_terms(key_pair, value_pair, query_pair, grad_pair, logs, dots, key_valid):
    share_halves = []
    score_halves = []
    query_halves = [masked_half(query_pair, half) for half in range(2)]
    grad_halves = [masked_half(grad_pair, half) for half in range(2)]
    for half in range(2):
        scores = dot_nt(key_pair, query_halves[half]) * SCALE
        shares = jnp.exp(jnp.where(key_valid, scores, NEGATIVE) - logs[half])
        share_grad = dot_nt(value_pair, grad_halves[half])
        score_halves.append((shares * (share_grad - dots[half])).astype(BF16))
        share_halves.append(shares.astype(BF16))
    key_sum = None
    value_sum = None
    for block in range(query_pair.shape[0] // ROWS):
        rows = slice(block * ROWS, (block + 1) * ROWS)
        key_term = dot_nn(
            jnp.concatenate([score[:, rows] for score in score_halves], axis=1),
            jnp.concatenate([query[rows] for query in query_halves], axis=0),
        )
        value_term = dot_nn(
            jnp.concatenate([share[:, rows] for share in share_halves], axis=1),
            jnp.concatenate([grad[rows] for grad in grad_halves], axis=0),
        )
        key_term = (key_term * SCALE).astype(BF16).astype(F32)
        value_term = value_term.astype(BF16).astype(F32)
        key_sum = key_term if key_sum is None else key_sum + key_term
        value_sum = value_term if value_sum is None else value_sum + value_term
    return key_sum, value_sum


def message_stats(tail):
    tail = tail.astype(F32)
    return tail[:, 0:PAIR] + tail[:, PAIR : 2 * PAIR] + tail[:, 2 * PAIR : 3 * PAIR]


def query_kernel(
    valid_ref,
    queries_ref,
    kept_ref,
    back2_ref,
    back4_ref,
    peer_ref,
    peer_back2_ref,
    peer_back4_ref,
    message_ref,
    log_ref,
    dot_ref,
    w_query_ref,
    out_ref,
    key_sum_ref,
    value_sum_ref,
    window,
    query_grad,
):
    place = lax.axis_index("tm")
    odd = lax.rem(place, 2) == 1
    wide = queries_ref.shape[1]
    gather_window(
        odd,
        (
            (back4_ref, back4_ref),
            (peer_back2_ref, peer_back4_ref),
            (back2_ref, back2_ref),
            (peer_ref, peer_back2_ref),
            (kept_ref, kept_ref),
        ),
        window,
    )
    key_lane = lax.broadcasted_iota(jnp.int32, (1, ROWS), 1)
    allowed = jnp.concatenate(
        [key_lane < valid_count(valid_ref, place + block - LEFT) for block in range(LEFT + 1)], axis=1
    )
    key_valid = lax.broadcasted_iota(jnp.int32, (ROWS, ROWS), 0) < valid_count(valid_ref, place)
    stats = message_stats(message_ref[ROWS : ROWS + 16, :])
    for pair in range(wide // PAIR):
        lanes = slice(pair * PAIR, (pair + 1) * PAIR)
        value_lanes = slice(wide + pair * PAIR, wide + (pair + 1) * PAIR)
        query_pair = queries_ref[:, lanes]
        grad_pair = message_ref[0:ROWS, lanes]
        total = None
        for half in range(2):
            key_half = masked_half(window[:, lanes], half)
            value_half = masked_half(window[:, value_lanes], half)
            head = 2 * pair + half
            scores = dot_nt(query_pair, key_half) * SCALE
            shares = jnp.exp(jnp.where(allowed, scores, NEGATIVE) - log_ref[:, head : head + 1])
            share_grad = dot_nt(grad_pair, value_half)
            score_grad = (shares * (share_grad - dot_ref[:, head : head + 1])).astype(BF16)
            product = dot_nn(score_grad, key_half)
            total = product if total is None else total + product
        query_grad[:, lanes] = (total * SCALE).astype(BF16)
        heads = (2 * pair, 2 * pair + 1)
        key_sum_ref[:, lanes], value_sum_ref[:, lanes] = key_terms(
            kept_ref[:, lanes],
            kept_ref[:, value_lanes],
            query_pair,
            grad_pair,
            [stats[head : head + 1] for head in heads],
            [stats[8 + head : 9 + head] for head in heads],
            key_valid,
        )
    out_ref[...] = dot_nt(query_grad[...], w_query_ref[...])


def key_kernel(
    valid_ref,
    kept_ref,
    query_next2_ref,
    query_next4_ref,
    query_peer_ref,
    query_peer_next2_ref,
    query_peer_next4_ref,
    next2_ref,
    next4_ref,
    peer_ref,
    peer_next2_ref,
    peer_next4_ref,
    w_key_ref,
    w_value_ref,
    gain_ref,
    own_ref,
    total_ref,
    partial_ref,
    key_sum_ref,
    value_sum_ref,
    result_ref,
    keep_ref,
    out_ref,
    held_ref,
    grads,
    queries,
    stats,
    key_grad,
    value_grad,
):
    place = lax.axis_index("tm")
    odd = lax.rem(place, 2) == 1
    count = valid_count(valid_ref, place)
    wide = grads.shape[1]
    messages = (
        (peer_next2_ref, peer_ref),
        (next2_ref, next2_ref),
        (peer_next4_ref, peer_next2_ref),
        (next4_ref, next4_ref),
    )
    gather_window(odd, messages, grads)
    gather_window(
        odd,
        (
            (query_peer_next2_ref, query_peer_ref),
            (query_next2_ref, query_next2_ref),
            (query_peer_next4_ref, query_peer_next2_ref),
            (query_next4_ref, query_next4_ref),
        ),
        queries,
    )
    for block, (when_odd, when_even) in enumerate(messages):
        stats[:, block * ROWS : (block + 1) * ROWS] = message_stats(
            chosen_rows(odd, when_odd, when_even, slice(ROWS, ROWS + 16))
        )
    key_valid = lax.broadcasted_iota(jnp.int32, (ROWS, LEFT * ROWS), 0) < count
    for pair in range(wide // PAIR):
        lanes = slice(pair * PAIR, (pair + 1) * PAIR)
        heads = (2 * pair, 2 * pair + 1)
        key_sum, value_sum = key_terms(
            kept_ref[:, lanes],
            kept_ref[:, slice(wide + pair * PAIR, wide + (pair + 1) * PAIR)],
            queries[:, lanes],
            grads[:, lanes],
            [stats[head : head + 1, :] for head in heads],
            [stats[8 + head : 9 + head, :] for head in heads],
            key_valid,
        )
        key_grad[:, lanes] = (key_sum_ref[:, lanes] + key_sum).astype(BF16)
        value_grad[:, lanes] = (value_sum_ref[:, lanes] + value_sum).astype(BF16)
    normed_grad = partial_ref[...] + dot_nt(key_grad[...], w_key_ref[...])
    normed_grad = normed_grad + dot_nt(value_grad[...], w_value_ref[...])
    scaled = normed_grad * gain_ref[...]
    unit, inverse = unit_rows(own_ref[...].astype(F32))
    back = inverse * (
        scaled
        - jnp.mean(scaled, axis=-1, keepdims=True)
        - unit * jnp.mean(scaled * unit, axis=-1, keepdims=True)
    )
    result = total_ref[...] + back
    out_ref[...] = result.astype(BF16)
    mine = lax.axis_index("section") == keep_ref[0]
    held_ref[...] = jnp.where(mine, result, result_ref[...].astype(F32)).astype(BF16)


def call(kernel, name, operands, outs, scratch, flops, scalars=(0,)):
    vmem = pl.BlockSpec(memory_space=pltpu.VMEM)
    smem = pl.BlockSpec(memory_space=pltpu.SMEM)
    return pl.pallas_call(
        kernel,
        name=name,
        in_specs=[smem if index in scalars else vmem for index in range(len(operands))],
        out_specs=[vmem] * len(outs),
        out_shape=[jax.ShapeDtypeStruct(shape, dtype) for shape, dtype in outs],
        scratch_shapes=[pltpu.VMEM(shape, dtype) for shape, dtype in scratch],
        compiler_params=pltpu.CompilerParams(vmem_limit_bytes=VMEM_LIMIT),
        cost_estimate=pl.CostEstimate(flops=flops, bytes_accessed=4 << 20, transcendentals=0),
    )(*operands)


def after(value, *others):
    return lax.optimization_barrier((value, *others))[0]


def shards(
    layer_inputs, top_grad, w_query, w_key, w_value, w_out, conv_kernel, norm_gain, group_valid
):
    own = layer_inputs[0]
    width = own.shape[1]
    wide = w_query.shape[2]
    query_weight = w_query[0]
    key_weight = w_key[0]
    value_weight = w_value[0]
    out_weight = w_out[0]
    kernel = conv_kernel[0]
    sections = lax.axis_size("section")
    count = lax.axis_size("tm")

    def moved(value, pairs):
        return lax.ppermute(value, ("tm", "section"), pairs)

    def at(layer, frame):
        return frame * sections + layer

    def across(steps, chosen):
        return [
            (at(section, source), at(section, source + steps))
            for section in chosen
            for source in range(max(0, -steps), min(count, count - steps))
        ]

    def swapped(chosen, parities):
        return [
            (at(section, source), at(section, source ^ 1))
            for section in chosen
            for source in range(count)
            if source % 2 in parities
        ]

    every = range(sections)
    half_edge = EDGE // 2
    queries, kept, ahead, behind = call(
        project_kernel,
        "project",
        (own, top_grad, norm_gain, query_weight, key_weight, value_weight),
        [
            ((ROWS, wide), BF16),
            ((ROWS, 2 * wide), BF16),
            ((ROWS + EDGE + half_edge, width), BF16),
            ((ROWS + 2 * EDGE + half_edge, width), BF16),
        ],
        [((ROWS, width), BF16)],
        1 << 30,
        scalars=(),
    )
    back2 = moved(ahead, across(2, every))
    back4 = moved(kept, across(4, every))
    peer = moved(ahead, swapped(every, (0,)))
    after1 = moved(behind, across(-1, every))
    peer_back2 = moved(back2, swapped(every, (0, 1)))
    peer_back4 = moved(back4, swapped(every, (0, 1)))
    far_pairs = [
        (at(section, source), at(section, source + 5))
        for section in every
        for source in range(1, count - 5, 2)
    ]
    back5 = moved(after(kept, back2), far_pairs)
    query_next2 = moved(after(queries, back2), across(-2, every))
    query_next4 = moved(after(queries, back2), across(-4, every))

    attended, logs = call(
        attend_kernel,
        "attend",
        (group_valid, queries, kept, back2, back4, peer, peer_back2, peer_back4, after1),
        [((ROWS + EDGE, wide), BF16), ((ROWS, PAIR), F32)],
        [(((LEFT + 2) * ROWS, 2 * wide), BF16), ((ROWS + EDGE, wide), BF16)],
        1 << 30,
    )
    back5 = after(back5, attended)
    span = (LEFT + 1) * ROWS
    step_outs = [((ROWS, width), F32), ((ROWS + 16, wide), BF16), ((ROWS, PAIR), F32)]
    slope, total, message, dots = call(
        mix_kernel,
        "mix",
        (
            group_valid,
            own,
            top_grad,
            attended,
            logs,
            back2,
            back4,
            back5,
            peer,
            peer_back2,
            peer_back4,
            after1,
            out_weight,
            kernel,
        ),
        [((ROWS + EDGE, width), F32)] + step_outs,
        [
            ((span, 2 * wide), BF16),
            ((EDGE, wide), BF16),
            ((ROWS + 2 * EDGE, wide), BF16),
            ((ROWS + 2 * EDGE, width), F32),
            ((ROWS, width), BF16),
        ],
        1 << 30,
    )
    query_peer = moved(queries, swapped(every, (1,)))
    query_peer_next2 = moved(query_next2, swapped(every, (0, 1)))
    query_peer_next4 = moved(query_next4, swapped(every, (0,)))

    result = own
    upstream = None
    upstream_next = None
    for step in range(sections):
        layer = sections - 1 - step
        if step > 0:
            total, message, dots = call(
                mixer_kernel,
                "mixer",
                (group_valid, upstream, upstream_next, slope, kernel, out_weight, attended, logs),
                step_outs,
                [((ROWS, width), BF16)],
                1 << 30,
            )
        here = [layer]
        grad2 = moved(message, across(-2, here))
        grad4 = moved(message, across(-4, here))
        peer_grad = moved(message, swapped(here, (1,)))
        partial, key_sum, value_sum = call(
            query_kernel,
            "own_queries",
            (
                group_valid,
                queries,
                kept,
                back2,
                back4,
                peer,
                peer_back2,
                peer_back4,
                message,
                logs,
                dots,
                query_weight,
            ),
            [((ROWS, width), F32), ((ROWS, wide), F32), ((ROWS, wide), F32)],
            [((span, 2 * wide), BF16), ((ROWS, wide), BF16)],
            1 << 30,
        )
        grad2, grad4, partial = lax.optimization_barrier((grad2, grad4, partial))
        peer_grad2 = moved(grad2, swapped(here, (0, 1)))
        peer_grad4 = moved(grad4, swapped(here, (0,)))
        operands = (
            group_valid,
            kept,
            query_next2,
            query_next4,
            query_peer,
            query_peer_next2,
            query_peer_next4,
            grad2,
            grad4,
            peer_grad,
            peer_grad2,
            peer_grad4,
            key_weight,
            value_weight,
            norm_gain,
            own,
            total,
            partial,
            key_sum,
            value_sum,
            result,
            jnp.full((1,), layer, jnp.int32),
        )
        input_grad, result = call(
            key_kernel,
            "own_keys",
            operands,
            [((ROWS, width), BF16), ((ROWS, width), BF16)],
            [
                ((LEFT * ROWS, wide), BF16),
                ((LEFT * ROWS, wide), BF16),
                ((16, LEFT * ROWS), F32),
                ((ROWS, wide), BF16),
                ((ROWS, wide), BF16),
            ],
            1 << 30,
            scalars=(0, len(operands) - 1),
        )
        if layer > 0:
            upstream = moved(
                input_grad, [(at(layer, source), at(layer - 1, source)) for source in range(count)]
            )
            upstream_next = moved(
                input_grad[:EDGE],
                [(at(layer, source), at(layer - 1, source - 1)) for source in range(1, count)],
            )
    return result[None]


def solution(mesh):
    placed = (
        P("section", "tm", None),
        P("tm", None),
        P("section", None, None),
        P("section", None, None),
        P("section", None, None),
        P("section", None, None),
        P("section", None, None),
        P("section", None),
        P(),
    )
    return jax.shard_map(
        shards, mesh=mesh, in_specs=placed, out_specs=P("section", "tm", None), check_vma=False
    )
```

time: 130 us -> 119 us (0.915)
  the two profiles are of different devices: /device:TPU:1 before, /device:TPU:19 now
where the time goes in v2:
time: 119 us; the launch traced here: 118 us
  Pallas kernels  48.7 us (41%)
  starting transfers between devices  46.5 us (39%)
  waiting for transfers between devices  16.6 us (14%)
  local copies, waits for them, and re-layouts  5.37 us (5%)
    pallas_call x8, Pallas kernels, call(): pl.pallas_call(kernel, name=name, in_specs=[smem if index in scalars else...  48.7 us
    ppermute x24, starting transfers between devices, moved(): return lax.ppermute(value, ('tm', 'section'), pairs)  46.5 us
    ppermute x24, waiting for transfers between devices, moved(): return lax.ppermute(value, ('tm', 'section'), pairs)  16.6 us
    unnamed x55, local copies, waits for them, and re-layouts  4.53 us
  transfers between devices with their start and end apart: 24, of which 6 were waited for; matrix products, arithmetic and copies ran while one was open for 1% of the time, Pallas kernels for 14%

profile of v2, /device:TPU:19, one launch (start us, length us, event | category | flops | bytes accessed | tf_op | source)
XLA Modules:
  0.0 117.7 jit_solution(14547875789727949088)
XLA Ops:
  0.0 4.4 %project.1 = (bf16[128,512]{1,0:T(8,128)(2,1)}, bf16[128,1024]{1,0:T(8,128)(2,1)}, bf16[176,1024]{1,0:T(8,128)(2,1)}, bf16[208,1024]{1,0:T(8,128)(2,1)}) custom-call(bf16[128,1024]{1,0:T(8,128)(2,1)} %bitcast.9, bf16[128,1024]{1,0:T(8,128)(2,1)} %top_ref.3, f32[1,1024]{1,0:T(1,128)} %gain_ref.5, bf16[1024,512]{1,0:T(8,128)(2,1)} %bitcast.24, ...), custom_call_target="tpu_custom_call" | custom-call | flops 1073741824 | bytes 4194304 | tf_op jit(solution)/shard_map/project/pallas_call | solution.py:560
  4.4 3.2 %collective-permute-start = (bf16[176,1024]{1,0:T(8,128)(2,1)}, bf16[176,1024]{1,0:T(8,128)(2,1)S(1)}, u32[]{:S(2)}, u32[]{:S(2)}) collective-permute-start(bf16[176,1024]{1,0:T(8,128)(2,1)} %get-tuple-element.38), channel_id=1, source_target_pairs={{0,4},{2,6},{4,8},{6,10},{8,12},{10,14},{12,16},{14,18},{16,20},{1... | collective-permute-start | bytes 1081352 | tf_op jit(solution)/shard_map/ppermute | solution.py:591
  7.5 1.9 %collective-permute-start.6 = (bf16[128,1024]{1,0:T(8,128)(2,1)}, bf16[128,1024]{1,0:T(8,128)(2,1)S(1)}, u32[]{:S(2)}, u32[]{:S(2)}) collective-permute-start(bf16[128,1024]{1,0:T(8,128)(2,1)} %get-tuple-element.43.kept_ref), channel_id=1, source_target_pairs={{0,8},{2,10},{4,12},{6,14},{8,16},{10,18},{12,20},{14,22},{16,24},... | collective-permute-start | bytes 786440 | tf_op jit(solution)/shard_map/ppermute | solution.py:591
  9.5 2.9 %collective-permute-start.10 = (bf16[208,1024]{1,0:T(8,128)(2,1)}, bf16[208,1024]{1,0:T(8,128)(2,1)S(1)}, u32[]{:S(2)}, u32[]{:S(2)}) collective-permute-start(bf16[208,1024]{1,0:T(8,128)(2,1)} %get-tuple-element.40), channel_id=1, source_target_pairs={{2,0},{4,2},{6,4},{8,6},{10,8},{12,10},{14,12},{16,14},{18,16},{20... | collective-permute-start | bytes 1277960 | tf_op jit(solution)/shard_map/ppermute | solution.py:591
  12.3 1.3 %collective-permute-start.7 = (bf16[176,1024]{1,0:T(8,128)(2,1)}, bf16[176,1024]{1,0:T(8,128)(2,1)S(1)}, u32[]{:S(2)}, u32[]{:S(2)}) collective-permute-start(bf16[176,1024]{1,0:T(8,128)(2,1)} %get-tuple-element.38), channel_id=1, source_target_pairs={{0,2},{4,6},{8,10},{12,14},{16,18},{20,22},{24,26},{28,30},{1,3},{... | collective-permute-start | bytes 1081352 | tf_op jit(solution)/shard_map/ppermute | solution.py:591
  13.6 2.1 %collective-permute-done.back2_ref = bf16[176,1024]{1,0:T(8,128)(2,1)S(1)} collective-permute-done((bf16[176,1024]{1,0:T(8,128)(2,1)}, bf16[176,1024]{1,0:T(8,128)(2,1)S(1)}, u32[]{:S(2)}, u32[]{:S(2)}) %collective-permute-start) | collective-permute-done | bytes 360480 | tf_op jit(solution)/shard_map/ppermute | solution.py:591
  15.7 6.1 %collective-permute-start.8 = (bf16[176,1024]{1,0:T(8,128)(2,1)S(1)}, bf16[176,1024]{1,0:T(8,128)(2,1)S(1)}, u32[]{:S(2)}, u32[]{:S(2)}) collective-permute-start(bf16[176,1024]{1,0:T(8,128)(2,1)S(1)} %collective-permute-done.back2_ref), channel_id=1, source_target_pairs={{0,2},{2,0},{4,6},{6,4},{8,10},{10,8},{12,14},{14,12},{16,18},{18,... | collective-permute-start | bytes 1081352 | tf_op jit(solution)/shard_map/ppermute | solution.py:591
  21.8 0.0 collective-permute-done.6.back4_ref
  21.8 1.0 collective-permute-start.9
  22.9 0.7 collective-permute-start.11
  23.6 0.7 copy.12
  24.2 0.0 collective-permute-done.7.peer_ref
  24.2 0.0 collective-permute-done.10.after_ref
  24.2 0.0 collective-permute-done.9.peer_back4_ref
  24.3 0.0 collective-permute-done.8.peer_back2_ref
  24.3 0.7 copy-done.7
  25.0 0.1 copy-done.5
  25.1 0.1 copy-done.10
  25.2 0.1 copy-done.8
  25.3 5.3 %attend.1 = (bf16[160,512]{1,0:T(8,128)(2,1)}, f32[128,128]{1,0:T(8,128)}) custom-call(s32[16]{0:T(128)} %valid_ref.13, bf16[128,512]{1,0:T(8,128)(2,1)} %get-tuple-element.39.queries_ref, bf16[128,1024]{1,0:T(8,128)(2,1)} %get-tuple-element.43.kept_ref, bf16[176,1024]{1,0:T(8,128)(2,1)} %copy-done.6, bf16[128,1024]{1,0:T(8,128)(2,1)} %copy-done.9, ...), custom_call_target="tpu_custom_call" | custom-call | flops 1073741824 | bytes 4194304 | tf_op jit(solution)/shard_map/attend/pallas_call | solution.py:560
  30.7 0.7 copy-done.11
  31.4 9.9 %mix.1 = (f32[160,1024]{1,0:T(8,128)}, f32[128,1024]{1,0:T(8,128)}, bf16[144,512]{1,0:T(8,128)(2,1)}, f32[128,128]{1,0:T(8,128)}) custom-call(s32[16]{0:T(128)} %valid_ref.13, bf16[128,1024]{1,0:T(8,128)(2,1)} %bitcast.10, bf16[128,1024]{1,0:T(8,128)(2,1)} %top_ref.3, bf16[160,512]{1,0:T(8,128)(2,1)} %get-tuple-element.41.attended_ref, ...), custom_call_target="tpu_custom_call" | custom-call | flops 1073741824 | bytes 4194304 | tf_op jit(solution)/shard_map/mix/pallas_call | solution.py:560
  41.3 0.7 collective-permute-start.13
  42.0 0.7 collective-permute-start.12
  42.6 2.9 %collective-permute-start.3 = (bf16[128,512]{1,0:T(8,128)(2,1)S(1)}, bf16[128,512]{1,0:T(8,128)(2,1)S(1)}, u32[]{:S(2)}, u32[]{:S(2)}) collective-permute-start(bf16[128,512]{1,0:T(8,128)(2,1)S(1)} %copy-done.25), channel_id=1, source_target_pairs={{2,0},{6,4},{10,8},{14,12},{18,16},{22,20},{26,24},{30,28},{3,1},{... | collective-permute-start | bytes 393224 | tf_op jit(solution)/shard_map/ppermute | solution.py:591
  45.6 2.1 %collective-permute-start.2 = (bf16[128,512]{1,0:T(8,128)(2,1)S(1)}, bf16[128,512]{1,0:T(8,128)(2,1)S(1)}, u32[]{:S(2)}, u32[]{:S(2)}) collective-permute-start(bf16[128,512]{1,0:T(8,128)(2,1)S(1)} %copy-done.25), channel_id=1, source_target_pairs={{8,0},{10,2},{12,4},{14,6},{16,8},{18,10},{20,12},{22,14},{24,16},... | collective-permute-start | bytes 393224 | tf_op jit(solution)/shard_map/ppermute | solution.py:591
  47.7 3.9 %collective-permute-start.1 = (bf16[128,512]{1,0:T(8,128)(2,1)S(1)}, bf16[128,512]{1,0:T(8,128)(2,1)S(1)}, u32[]{:S(2)}, u32[]{:S(2)}) collective-permute-start(bf16[128,512]{1,0:T(8,128)(2,1)S(1)} %copy-done.25), channel_id=1, source_target_pairs={{4,0},{6,2},{8,4},{10,6},{12,8},{14,10},{16,12},{18,14},{20,16},{2... | collective-permute-start | bytes 393224 | tf_op jit(solution)/shard_map/ppermute | solution.py:591
  51.6 5.9 %own_queries.2 = (f32[128,1024]{1,0:T(8,128)}, f32[128,512]{1,0:T(8,128)}, f32[128,512]{1,0:T(8,128)}) custom-call(s32[16]{0:T(128)} %valid_ref.13, bf16[128,512]{1,0:T(8,128)(2,1)} %get-tuple-element.39.queries_ref, bf16[128,1024]{1,0:T(8,128)(2,1)} %get-tuple-element.43.kept_ref, bf16[176,1024]{1,0:T(8,128)(2,1)} %copy-done.6, ...), custom_call_target="tpu_custom_call" | custom-call | flops 1073741824 | bytes 4194304 | tf_op jit(solution)/shard_map/own_queries/pallas_call | solution.py:560
  57.5 0.7 collective-permute-start.14
  58.1 0.7 collective-permute-start.15
  58.8 0.7 collective-permute-start.16
  59.5 1.5 %collective-permute-start.5 = (bf16[128,512]{1,0:T(8,128)(2,1)S(1)}, bf16[128,512]{1,0:T(8,128)(2,1)S(1)}, u32[]{:S(2)}, u32[]{:S(2)}) collective-permute-start(bf16[128,512]{1,0:T(8,128)(2,1)S(1)} %collective-permute-done.2.query_next4_ref), channel_id=1, source_target_pairs={{0,2},{4,6},{8,10},{12,14},{16,18},{20,22},{24,26},{28,30},{1,3},{... | collective-permute-start | bytes 393224 | tf_op jit(solution)/shard_map/ppermute | solution.py:591
  61.0 0.0 collective-permute-done.1.query_next2_ref
  61.0 1.2 %collective-permute-start.4 = (bf16[128,512]{1,0:T(8,128)(2,1)S(1)}, bf16[128,512]{1,0:T(8,128)(2,1)S(1)}, u32[]{:S(2)}, u32[]{:S(2)}) collective-permute-start(bf16[128,512]{1,0:T(8,128)(2,1)S(1)} %collective-permute-done.1.query_next2_ref), channel_id=1, source_target_pairs={{0,2},{2,0},{4,6},{6,4},{8,10},{10,8},{12,14},{14,12},{16,18},{18,... | collective-permute-start | bytes 393224 | tf_op jit(solution)/shard_map/ppermute | solution.py:591
  62.2 0.5 collective-permute-done.5.query_peer_next4_ref
  62.8 0.4 collective-permute-done.4.query_peer_next2_ref
  63.2 0.0 collective-permute-done.14.peer_ref
  63.2 0.0 collective-permute-done.15.peer_next2_ref
  63.3 0.0 collective-permute-done.16.peer_next4_ref
  63.3 0.1 copy-done.3
  63.4 0.4 copy-done.4
  63.9 0.1 copy-done.16
  63.9 0.1 copy-done.18
  64.0 0.1 copy-done.19
  64.0 6.2 %own_keys.2 = (bf16[128,1024]{1,0:T(8,128)(2,1)}, bf16[128,1024]{1,0:T(8,128)(2,1)}) custom-call(s32[16]{0:T(128)} %valid_ref.13, bf16[128,1024]{1,0:T(8,128)(2,1)} %get-tuple-element.43.kept_ref, bf16[128,512]{1,0:T(8,128)(2,1)} %copy-done.2, bf16[128,512]{1,0:T(8,128)(2,1)} %copy-done.1, bf16[128,512]{1,0:T(8,128)(2,1)} %copy-done, ...), custom_call_target="tpu_custom_call" | custom-call | flops 1073741824 | bytes 4194304 | tf_op jit(solution)/shard_map/own_keys/pallas_call | solution.py:560
  70.2 1.3 %collective-permute-start.17 = (bf16[128,1024]{1,0:T(8,128)(2,1)}, bf16[128,1024]{1,0:T(8,128)(2,1)S(1)}, u32[]{:S(2)}, u32[]{:S(2)}) collective-permute-start(bf16[128,1024]{1,0:T(8,128)(2,1)} %get-tuple-element.54), channel_id=1, source_target_pairs={{1,0},{3,2},{5,4},{7,6},{9,8},{11,10},{13,12},{15,14},{17,16},{19,... | collective-permute-start | bytes 786440 | tf_op jit(solution)/shard_map/ppermute | solution.py:591
  71.5 0.8 slice.3
  72.4 1.3 %collective-permute-start.18 = (bf16[32,1024]{1,0:T(8,128)(2,1)S(1)}, bf16[32,1024]{1,0:T(8,128)(2,1)S(1)}, u32[]{:S(2)}, u32[]{:S(2)}) collective-permute-start(bf16[32,1024]{1,0:T(8,128)(2,1)S(1)} %slice.3), channel_id=1, source_target_pairs={{3,0},{5,2},{7,4},{9,6},{11,8},{13,10},{15,12},{17,14},{19,16},{21... | collective-permute-start | bytes 196616 | tf_op jit(solution)/shard_map/ppermute | solution.py:591
  73.7 10.8 %collective-permute-done.18.next_ref = bf16[32,1024]{1,0:T(8,128)(2,1)S(1)} collective-permute-done((bf16[32,1024]{1,0:T(8,128)(2,1)S(1)}, bf16[32,1024]{1,0:T(8,128)(2,1)S(1)}, u32[]{:S(2)}, u32[]{:S(2)}) %collective-permute-start.18) | collective-permute-done | bytes 65568 | tf_op jit(solution)/shard_map/ppermute | solution.py:591
  84.4 0.8 collective-permute-done.17.upstream_ref
  85.2 0.7 copy-done.23
  85.9 5.0 %mixer.1 = (f32[128,1024]{1,0:T(8,128)}, bf16[144,512]{1,0:T(8,128)(2,1)}, f32[128,128]{1,0:T(8,128)}) custom-call(s32[16]{0:T(128)} %valid_ref.13, bf16[128,1024]{1,0:T(8,128)(2,1)} %copy-done.23, bf16[32,1024]{1,0:T(8,128)(2,1)} %copy-done.26, f32[160,1024]{1,0:T(8,128)} %get-tuple-element.55.slope_ref, f32[31,1024]{1,0:T(8,128)} %bitcast.23, ...), custom_call_target="tpu_custom_call" | custom-call | flops 1073741824 | bytes 4194304 | tf_op jit(solution)/shard_map/mixer/pallas_call | solution.py:560
  90.9 1.9 %collective-permute-start.20 = (bf16[144,512]{1,0:T(8,128)(2,1)}, bf16[144,512]{1,0:T(8,128)(2,1)S(1)}, u32[]{:S(2)}, u32[]{:S(2)}) collective-permute-start(bf16[144,512]{1,0:T(8,128)(2,1)} %get-tuple-element.56.message_ref), channel_id=1, source_target_pairs={{8,0},{10,2},{12,4},{14,6},{16,8},{18,10},{20,12},{22,14},{24,16},... | collective-permute-start | bytes 442376 | tf_op jit(solution)/shard_map/ppermute | solution.py:591
  92.9 3.1 %collective-permute-start.19 = (bf16[144,512]{1,0:T(8,128)(2,1)}, bf16[144,512]{1,0:T(8,128)(2,1)S(1)}, u32[]{:S(2)}, u32[]{:S(2)}) collective-permute-start(bf16[144,512]{1,0:T(8,128)(2,1)} %get-tuple-element.56.message_ref), channel_id=1, source_target_pairs={{4,0},{6,2},{8,4},{10,6},{12,8},{14,10},{16,12},{18,14},{20,16},{2... | collective-permute-start | bytes 442376 | tf_op jit(solution)/shard_map/ppermute | solution.py:591
  95.9 3.8 %collective-permute-start.21 = (bf16[144,512]{1,0:T(8,128)(2,1)}, bf16[144,512]{1,0:T(8,128)(2,1)S(1)}, u32[]{:S(2)}, u32[]{:S(2)}) collective-permute-start(bf16[144,512]{1,0:T(8,128)(2,1)} %get-tuple-element.56.message_ref), channel_id=1, source_target_pairs={{2,0},{6,4},{10,8},{14,12},{18,16},{22,20},{26,24},{30,28}} | collective-permute-start | bytes 442376 | tf_op jit(solution)/shard_map/ppermute | solution.py:591
  99.8 5.9 %own_queries.3 = (f32[128,1024]{1,0:T(8,128)}, f32[128,512]{1,0:T(8,128)}, f32[128,512]{1,0:T(8,128)}) custom-call(s32[16]{0:T(128)} %valid_ref.13, bf16[128,512]{1,0:T(8,128)(2,1)} %get-tuple-element.39.queries_ref, bf16[128,1024]{1,0:T(8,128)(2,1)} %get-tuple-element.43.kept_ref, bf16[176,1024]{1,0:T(8,128)(2,1)} %copy-done.6, ...), custom_call_target="tpu_custom_call" | custom-call | flops 1073741824 | bytes 4194304 | tf_op jit(solution)/shard_map/own_queries/pallas_call | solution.py:560
  105.6 0.0 collective-permute-done.20.next4_ref
  105.6 0.0 collective-permute-done.19.next2_ref
  105.6 1.9 %collective-permute-start.22 = (bf16[144,512]{1,0:T(8,128)(2,1)S(1)}, bf16[144,512]{1,0:T(8,128)(2,1)S(1)}, u32[]{:S(2)}, u32[]{:S(2)}) collective-permute-start(bf16[144,512]{1,0:T(8,128)(2,1)S(1)} %collective-permute-done.19.next2_ref), channel_id=1, source_target_pairs={{0,2},{2,0},{4,6},{6,4},{8,10},{10,8},{12,14},{14,12},{16,18},{18,... | collective-permute-start | bytes 442376 | tf_op jit(solution)/shard_map/ppermute | solution.py:591
  107.6 1.3 %collective-permute-start.23 = (bf16[144,512]{1,0:T(8,128)(2,1)S(1)}, bf16[144,512]{1,0:T(8,128)(2,1)S(1)}, u32[]{:S(2)}, u32[]{:S(2)}) collective-permute-start(bf16[144,512]{1,0:T(8,128)(2,1)S(1)} %collective-permute-done.20.next4_ref), channel_id=1, source_target_pairs={{0,2},{4,6},{8,10},{12,14},{16,18},{20,22},{24,26},{28,30}} | collective-permute-start | bytes 442376 | tf_op jit(solution)/shard_map/ppermute | solution.py:591
  108.9 0.0 collective-permute-done.22.peer_next2_ref
  108.9 1.9 %collective-permute-done.23.peer_next4_ref = bf16[144,512]{1,0:T(8,128)(2,1)S(1)} collective-permute-done((bf16[144,512]{1,0:T(8,128)(2,1)S(1)}, bf16[144,512]{1,0:T(8,128)(2,1)S(1)}, u32[]{:S(2)}, u32[]{:S(2)}) %collective-permute-start.23) | collective-permute-done | bytes 147488 | tf_op jit(solution)/shard_map/ppermute | solution.py:591
  110.9 0.6 copy-done.21
  111.5 6.2 %own_keys.3 = (bf16[128,1024]{1,0:T(8,128)(2,1)}, bf16[128,1024]{1,0:T(8,128)(2,1)}) custom-call(s32[16]{0:T(128)} %valid_ref.13, bf16[128,1024]{1,0:T(8,128)(2,1)} %get-tuple-element.43.kept_ref, bf16[128,512]{1,0:T(8,128)(2,1)} %copy-done.2, bf16[128,512]{1,0:T(8,128)(2,1)} %copy-done.1, bf16[128,512]{1,0:T(8,128)(2,1)} %copy-done, ...), custom_call_target="tpu_custom_call" | custom-call | flops 1073741824 | bytes 4194304 | tf_op jit(solution)/shard_map/own_keys/pallas_call | solution.py:560
  (48 shorter events, 0.1 us)
Async XLA Ops:
  0.0 23.5 %copy-start.22 = (f32[1,31,1024]{2,0,1:T(1,128)S(1)}, f32[1,31,1024]{2,0,1:T(1,128)}, u32[]{:S(2)}) copy-start(f32[1,31,1024]{2,0,1:T(1,128)} %param.15) | copy-start | bytes 380932
  4.4 11.4 %collective-permute-start = (bf16[176,1024]{1,0:T(8,128)(2,1)}, bf16[176,1024]{1,0:T(8,128)(2,1)S(1)}, u32[]{:S(2)}, u32[]{:S(2)}) collective-permute-start(bf16[176,1024]{1,0:T(8,128)(2,1)} %get-tuple-element.38), channel_id=1, source_target_pairs={{0,4},{2,6},{4,8},{6,10},{8,12},{10,14},{12,16},{14,18},{16,20},{1... | collective-permute-start | bytes 1081352 | tf_op jit(solution)/shard_map/ppermute | solution.py:591
  7.5 14.3 %collective-permute-start.6 = (bf16[128,1024]{1,0:T(8,128)(2,1)}, bf16[128,1024]{1,0:T(8,128)(2,1)S(1)}, u32[]{:S(2)}, u32[]{:S(2)}) collective-permute-start(bf16[128,1024]{1,0:T(8,128)(2,1)} %get-tuple-element.43.kept_ref), channel_id=1, source_target_pairs={{0,8},{2,10},{4,12},{6,14},{8,16},{10,18},{12,20},{14,22},{16,24},... | collective-permute-start | bytes 786440 | tf_op jit(solution)/shard_map/ppermute | solution.py:591
  9.5 14.8 %collective-permute-start.10 = (bf16[208,1024]{1,0:T(8,128)(2,1)}, bf16[208,1024]{1,0:T(8,128)(2,1)S(1)}, u32[]{:S(2)}, u32[]{:S(2)}) collective-permute-start(bf16[208,1024]{1,0:T(8,128)(2,1)} %get-tuple-element.40), channel_id=1, source_target_pairs={{2,0},{4,2},{6,4},{8,6},{10,8},{12,10},{14,12},{16,14},{18,16},{20... | collective-permute-start | bytes 1277960 | tf_op jit(solution)/shard_map/ppermute | solution.py:591
  12.3 11.9 %collective-permute-start.7 = (bf16[176,1024]{1,0:T(8,128)(2,1)}, bf16[176,1024]{1,0:T(8,128)(2,1)S(1)}, u32[]{:S(2)}, u32[]{:S(2)}) collective-permute-start(bf16[176,1024]{1,0:T(8,128)(2,1)} %get-tuple-element.38), channel_id=1, source_target_pairs={{0,2},{4,6},{8,10},{12,14},{16,18},{20,22},{24,26},{28,30},{1,3},{... | collective-permute-start | bytes 1081352 | tf_op jit(solution)/shard_map/ppermute | solution.py:591
  15.7 8.5 %copy-start.6 = (bf16[176,1024]{1,0:T(8,128)(2,1)}, bf16[176,1024]{1,0:T(8,128)(2,1)S(1)}, u32[]{:S(2)}) copy-start(bf16[176,1024]{1,0:T(8,128)(2,1)S(1)} %collective-permute-done.back2_ref) | copy-start | bytes 1081348
  15.7 8.5 %collective-permute-start.8 = (bf16[176,1024]{1,0:T(8,128)(2,1)S(1)}, bf16[176,1024]{1,0:T(8,128)(2,1)S(1)}, u32[]{:S(2)}, u32[]{:S(2)}) collective-permute-start(bf16[176,1024]{1,0:T(8,128)(2,1)S(1)} %collective-permute-done.back2_ref), channel_id=1, source_target_pairs={{0,2},{2,0},{4,6},{6,4},{8,10},{10,8},{12,14},{14,12},{16,18},{18,... | collective-permute-start | bytes 1081352 | tf_op jit(solution)/shard_map/ppermute | solution.py:591
  21.8 2.4 %copy-start.9 = (bf16[128,1024]{1,0:T(8,128)(2,1)}, bf16[128,1024]{1,0:T(8,128)(2,1)S(1)}, u32[]{:S(2)}) copy-start(bf16[128,1024]{1,0:T(8,128)(2,1)S(1)} %collective-permute-done.6.back4_ref) | copy-start | bytes 786436
  21.8 2.4 %collective-permute-start.9 = (bf16[128,1024]{1,0:T(8,128)(2,1)S(1)}, bf16[128,1024]{1,0:T(8,128)(2,1)S(1)}, u32[]{:S(2)}, u32[]{:S(2)}) collective-permute-start(bf16[128,1024]{1,0:T(8,128)(2,1)S(1)} %collective-permute-done.6.back4_ref), channel_id=1, source_target_pairs={{0,2},{2,0},{4,6},{6,4},{8,10},{10,8},{12,14},{14,12},{16,18},{18,... | collective-permute-start | bytes 786440 | tf_op jit(solution)/shard_map/ppermute | solution.py:591
  22.9 7.8 %collective-permute-start.11 = (bf16[128,1024]{1,0:T(8,128)(2,1)}, bf16[128,1024]{1,0:T(8,128)(2,1)S(1)}, u32[]{:S(2)}, u32[]{:S(2)}) collective-permute-start(bf16[128,1024]{1,0:T(8,128)(2,1)} %get-tuple-element.43.kept_ref), channel_id=1, source_target_pairs={{2,12},{6,16},{10,20},{14,24},{18,28},{3,13},{7,17},{11,21},{15,25... | collective-permute-start | bytes 786440 | tf_op jit(solution)/shard_map/ppermute | solution.py:591
  24.2 0.8 copy-start.7
  24.2 0.9 copy-start.5
  24.2 0.9 copy-start.10
  24.3 1.0 copy-start.8
  30.6 0.7 copy-start.11
  31.4 11.3 %copy-start.25 = (bf16[128,512]{1,0:T(8,128)(2,1)S(1)}, bf16[128,512]{1,0:T(8,128)(2,1)}, u32[]{:S(2)}) copy-start(bf16[128,512]{1,0:T(8,128)(2,1)} %get-tuple-element.39.queries_ref) | copy-start | bytes 393220
  41.3 16.1 %collective-permute-start.13 = (bf16[144,512]{1,0:T(8,128)(2,1)}, bf16[144,512]{1,0:T(8,128)(2,1)S(1)}, u32[]{:S(2)}, u32[]{:S(2)}) collective-permute-start(bf16[144,512]{1,0:T(8,128)(2,1)} %get-tuple-element.45.message_ref), channel_id=1, source_target_pairs={{9,1},{11,3},{13,5},{15,7},{17,9},{19,11},{21,13},{23,15},{25,17},... | collective-permute-start | bytes 442376 | tf_op jit(solution)/shard_map/ppermute | solution.py:591
  42.0 16.2 %collective-permute-start.12 = (bf16[144,512]{1,0:T(8,128)(2,1)}, bf16[144,512]{1,0:T(8,128)(2,1)S(1)}, u32[]{:S(2)}, u32[]{:S(2)}) collective-permute-start(bf16[144,512]{1,0:T(8,128)(2,1)} %get-tuple-element.45.message_ref), channel_id=1, source_target_pairs={{5,1},{7,3},{9,5},{11,7},{13,9},{15,11},{17,13},{19,15},{21,17},{2... | collective-permute-start | bytes 442376 | tf_op jit(solution)/shard_map/ppermute | solution.py:591
  42.6 16.2 %collective-permute-start.3 = (bf16[128,512]{1,0:T(8,128)(2,1)S(1)}, bf16[128,512]{1,0:T(8,128)(2,1)S(1)}, u32[]{:S(2)}, u32[]{:S(2)}) collective-permute-start(bf16[128,512]{1,0:T(8,128)(2,1)S(1)} %copy-done.25), channel_id=1, source_target_pairs={{2,0},{6,4},{10,8},{14,12},{18,16},{22,20},{26,24},{30,28},{3,1},{... | collective-permute-start | bytes 393224 | tf_op jit(solution)/shard_map/ppermute | solution.py:591
  45.6 14.0 %collective-permute-start.2 = (bf16[128,512]{1,0:T(8,128)(2,1)S(1)}, bf16[128,512]{1,0:T(8,128)(2,1)S(1)}, u32[]{:S(2)}, u32[]{:S(2)}) collective-permute-start(bf16[128,512]{1,0:T(8,128)(2,1)S(1)} %copy-done.25), channel_id=1, source_target_pairs={{8,0},{10,2},{12,4},{14,6},{16,8},{18,10},{20,12},{22,14},{24,16},... | collective-permute-start | bytes 393224 | tf_op jit(solution)/shard_map/ppermute | solution.py:591
  47.7 13.4 %collective-permute-start.1 = (bf16[128,512]{1,0:T(8,128)(2,1)S(1)}, bf16[128,512]{1,0:T(8,128)(2,1)S(1)}, u32[]{:S(2)}, u32[]{:S(2)}) collective-permute-start(bf16[128,512]{1,0:T(8,128)(2,1)S(1)} %copy-done.25), channel_id=1, source_target_pairs={{4,0},{6,2},{8,4},{10,6},{12,8},{14,10},{16,12},{18,14},{20,16},{2... | collective-permute-start | bytes 393224 | tf_op jit(solution)/shard_map/ppermute | solution.py:591
  51.6 5.9 %copy-start.24 = (bf16[144,512]{1,0:T(8,128)(2,1)S(1)}, bf16[144,512]{1,0:T(8,128)(2,1)}, u32[]{:S(2)}) copy-start(bf16[144,512]{1,0:T(8,128)(2,1)} %get-tuple-element.45.message_ref) | copy-start | bytes 442372
  57.4 5.8 %copy-start.12 = (bf16[144,512]{1,0:T(8,128)(2,1)}, bf16[144,512]{1,0:T(8,128)(2,1)S(1)}, u32[]{:S(2)}) copy-start(bf16[144,512]{1,0:T(8,128)(2,1)S(1)} %collective-permute-done.13.next4_ref) | copy-start | bytes 442372
  57.5 5.8 %collective-permute-start.14 = (bf16[144,512]{1,0:T(8,128)(2,1)S(1)}, bf16[144,512]{1,0:T(8,128)(2,1)S(1)}, u32[]{:S(2)}, u32[]{:S(2)}) collective-permute-start(bf16[144,512]{1,0:T(8,128)(2,1)S(1)} %copy-done.24), channel_id=1, source_target_pairs={{3,1},{7,5},{11,9},{15,13},{19,17},{23,21},{27,25},{31,29}} | collective-permute-start | bytes 442376 | tf_op jit(solution)/shard_map/ppermute | solution.py:591
  58.1 5.1 %copy-start.13 = (bf16[144,512]{1,0:T(8,128)(2,1)}, bf16[144,512]{1,0:T(8,128)(2,1)S(1)}, u32[]{:S(2)}) copy-start(bf16[144,512]{1,0:T(8,128)(2,1)S(1)} %collective-permute-done.12.next2_ref) | copy-start | bytes 442372
  58.1 5.1 %collective-permute-start.15 = (bf16[144,512]{1,0:T(8,128)(2,1)S(1)}, bf16[144,512]{1,0:T(8,128)(2,1)S(1)}, u32[]{:S(2)}, u32[]{:S(2)}) collective-permute-start(bf16[144,512]{1,0:T(8,128)(2,1)S(1)} %collective-permute-done.12.next2_ref), channel_id=1, source_target_pairs={{1,3},{3,1},{5,7},{7,5},{9,11},{11,9},{13,15},{15,13},{17,19},{19,... | collective-permute-start | bytes 442376 | tf_op jit(solution)/shard_map/ppermute | solution.py:591
  58.8 4.5 %copy-start = (bf16[128,512]{1,0:T(8,128)(2,1)}, bf16[128,512]{1,0:T(8,128)(2,1)S(1)}, u32[]{:S(2)}) copy-start(bf16[128,512]{1,0:T(8,128)(2,1)S(1)} %collective-permute-done.3.query_peer_ref) | copy-start | bytes 393220
  58.8 4.4 %collective-permute-start.16 = (bf16[144,512]{1,0:T(8,128)(2,1)S(1)}, bf16[144,512]{1,0:T(8,128)(2,1)S(1)}, u32[]{:S(2)}, u32[]{:S(2)}) collective-permute-start(bf16[144,512]{1,0:T(8,128)(2,1)S(1)} %collective-permute-done.13.next4_ref), channel_id=1, source_target_pairs={{1,3},{5,7},{9,11},{13,15},{17,19},{21,23},{25,27},{29,31}} | collective-permute-start | bytes 442376 | tf_op jit(solution)/shard_map/ppermute | solution.py:591
  59.5 3.8 %copy-start.1 = (bf16[128,512]{1,0:T(8,128)(2,1)}, bf16[128,512]{1,0:T(8,128)(2,1)S(1)}, u32[]{:S(2)}) copy-start(bf16[128,512]{1,0:T(8,128)(2,1)S(1)} %collective-permute-done.2.query_next4_ref) | copy-start | bytes 393220
  59.5 3.2 %collective-permute-start.5 = (bf16[128,512]{1,0:T(8,128)(2,1)S(1)}, bf16[128,512]{1,0:T(8,128)(2,1)S(1)}, u32[]{:S(2)}, u32[]{:S(2)}) collective-permute-start(bf16[128,512]{1,0:T(8,128)(2,1)S(1)} %collective-permute-done.2.query_next4_ref), channel_id=1, source_target_pairs={{0,2},{4,6},{8,10},{12,14},{16,18},{20,22},{24,26},{28,30},{1,3},{... | collective-permute-start | bytes 393224 | tf_op jit(solution)/shard_map/ppermute | solution.py:591
  61.0 2.3 %copy-start.2 = (bf16[128,512]{1,0:T(8,128)(2,1)}, bf16[128,512]{1,0:T(8,128)(2,1)S(1)}, u32[]{:S(2)}) copy-start(bf16[128,512]{1,0:T(8,128)(2,1)S(1)} %collective-permute-done.1.query_next2_ref) | copy-start | bytes 393220
  61.0 2.2 %collective-permute-start.4 = (bf16[128,512]{1,0:T(8,128)(2,1)S(1)}, bf16[128,512]{1,0:T(8,128)(2,1)S(1)}, u32[]{:S(2)}, u32[]{:S(2)}) collective-permute-start(bf16[128,512]{1,0:T(8,128)(2,1)S(1)} %collective-permute-done.1.query_next2_ref), channel_id=1, source_target_pairs={{0,2},{2,0},{4,6},{6,4},{8,10},{10,8},{12,14},{14,12},{16,18},{18,... | collective-permute-start | bytes 393224 | tf_op jit(solution)/shard_map/ppermute | solution.py:591
  62.8 0.7 copy-start.3
  63.2 0.6 copy-start.4
  63.2 0.7 copy-start.16
  63.2 0.7 copy-start.18
  63.3 0.8 copy-start.19
  70.2 15.0 %collective-permute-start.17 = (bf16[128,1024]{1,0:T(8,128)(2,1)}, bf16[128,1024]{1,0:T(8,128)(2,1)S(1)}, u32[]{:S(2)}, u32[]{:S(2)}) collective-permute-start(bf16[128,1024]{1,0:T(8,128)(2,1)} %get-tuple-element.54), channel_id=1, source_target_pairs={{1,0},{3,2},{5,4},{7,6},{9,8},{11,10},{13,12},{15,14},{17,16},{19,... | collective-permute-start | bytes 786440 | tf_op jit(solution)/shard_map/ppermute | solution.py:591
  72.4 12.1 %collective-permute-start.18 = (bf16[32,1024]{1,0:T(8,128)(2,1)S(1)}, bf16[32,1024]{1,0:T(8,128)(2,1)S(1)}, u32[]{:S(2)}, u32[]{:S(2)}) collective-permute-start(bf16[32,1024]{1,0:T(8,128)(2,1)S(1)} %slice.3), channel_id=1, source_target_pairs={{3,0},{5,2},{7,4},{9,6},{11,8},{13,10},{15,12},{17,14},{19,16},{21... | collective-permute-start | bytes 196616 | tf_op jit(solution)/shard_map/ppermute | solution.py:591
  84.4 0.8 copy-start.26
  85.2 0.7 copy-start.23
  90.9 14.7 %collective-permute-start.20 = (bf16[144,512]{1,0:T(8,128)(2,1)}, bf16[144,512]{1,0:T(8,128)(2,1)S(1)}, u32[]{:S(2)}, u32[]{:S(2)}) collective-permute-start(bf16[144,512]{1,0:T(8,128)(2,1)} %get-tuple-element.56.message_ref), channel_id=1, source_target_pairs={{8,0},{10,2},{12,4},{14,6},{16,8},{18,10},{20,12},{22,14},{24,16},... | collective-permute-start | bytes 442376 | tf_op jit(solution)/shard_map/ppermute | solution.py:591
  92.9 12.8 %collective-permute-start.19 = (bf16[144,512]{1,0:T(8,128)(2,1)}, bf16[144,512]{1,0:T(8,128)(2,1)S(1)}, u32[]{:S(2)}, u32[]{:S(2)}) collective-permute-start(bf16[144,512]{1,0:T(8,128)(2,1)} %get-tuple-element.56.message_ref), channel_id=1, source_target_pairs={{4,0},{6,2},{8,4},{10,6},{12,8},{14,10},{16,12},{18,14},{20,16},{2... | collective-permute-start | bytes 442376 | tf_op jit(solution)/shard_map/ppermute | solution.py:591
  95.9 12.9 %collective-permute-start.21 = (bf16[144,512]{1,0:T(8,128)(2,1)}, bf16[144,512]{1,0:T(8,128)(2,1)S(1)}, u32[]{:S(2)}, u32[]{:S(2)}) collective-permute-start(bf16[144,512]{1,0:T(8,128)(2,1)} %get-tuple-element.56.message_ref), channel_id=1, source_target_pairs={{2,0},{6,4},{10,8},{14,12},{18,16},{22,20},{26,24},{30,28}} | collective-permute-start | bytes 442376 | tf_op jit(solution)/shard_map/ppermute | solution.py:591
  105.6 5.2 %copy-start.14 = (bf16[144,512]{1,0:T(8,128)(2,1)}, bf16[144,512]{1,0:T(8,128)(2,1)S(1)}, u32[]{:S(2)}) copy-start(bf16[144,512]{1,0:T(8,128)(2,1)S(1)} %collective-permute-done.20.next4_ref) | copy-start | bytes 442372
  105.6 5.2 %copy-start.15 = (bf16[144,512]{1,0:T(8,128)(2,1)}, bf16[144,512]{1,0:T(8,128)(2,1)S(1)}, u32[]{:S(2)}) copy-start(bf16[144,512]{1,0:T(8,128)(2,1)S(1)} %collective-permute-done.19.next2_ref) | copy-start | bytes 442372
  105.6 3.3 %collective-permute-start.22 = (bf16[144,512]{1,0:T(8,128)(2,1)S(1)}, bf16[144,512]{1,0:T(8,128)(2,1)S(1)}, u32[]{:S(2)}, u32[]{:S(2)}) collective-permute-start(bf16[144,512]{1,0:T(8,128)(2,1)S(1)} %collective-permute-done.19.next2_ref), channel_id=1, source_target_pairs={{0,2},{2,0},{4,6},{6,4},{8,10},{10,8},{12,14},{14,12},{16,18},{18,... | collective-permute-start | bytes 442376 | tf_op jit(solution)/shard_map/ppermute | solution.py:591
  107.6 3.3 %collective-permute-start.23 = (bf16[144,512]{1,0:T(8,128)(2,1)S(1)}, bf16[144,512]{1,0:T(8,128)(2,1)S(1)}, u32[]{:S(2)}, u32[]{:S(2)}) collective-permute-start(bf16[144,512]{1,0:T(8,128)(2,1)S(1)} %collective-permute-done.20.next4_ref), channel_id=1, source_target_pairs={{0,2},{4,6},{8,10},{12,14},{16,18},{20,22},{24,26},{28,30}} | collective-permute-start | bytes 442376 | tf_op jit(solution)/shard_map/ppermute | solution.py:591
  108.9 2.0 %copy-start.17 = (bf16[144,512]{1,0:T(8,128)(2,1)}, bf16[144,512]{1,0:T(8,128)(2,1)S(1)}, u32[]{:S(2)}) copy-start(bf16[144,512]{1,0:T(8,128)(2,1)S(1)} %collective-permute-done.21.peer_ref) | copy-start | bytes 442372
  108.9 1.9 %copy-start.20 = (bf16[144,512]{1,0:T(8,128)(2,1)}, bf16[144,512]{1,0:T(8,128)(2,1)S(1)}, u32[]{:S(2)}) copy-start(bf16[144,512]{1,0:T(8,128)(2,1)S(1)} %collective-permute-done.22.peer_next2_ref) | copy-start | bytes 442372
  110.8 0.7 copy-start.21

commit v3 on v2

--- a/solution.py
+++ b/solution.py
@@ -85,8 +85,17 @@
     ahead_ref,
     behind_ref,
     normed,
+    w_query,
+    w_key,
+    w_value,
+    semaphores,
 ):
     chunk = 16
+    loader = Loader(semaphores, None)
+    loader.get(w_key, w_key_ref)
+    loader.get(w_value, w_value_ref)
+    late = Loader(semaphores.at[2:], None)
+    late.get(w_query, w_query_ref)
 
     def norm_step(step, carry):
         rows = pl.ds(pl.multiple_of(step * chunk, chunk), chunk)
@@ -97,12 +106,14 @@
     lax.fori_loop(0, ROWS // chunk, norm_step, 0, unroll=2)
     wide = w_key_ref.shape[1]
     half = EDGE // 2
-    keys = dot_nn(normed[...], w_key_ref[...]).astype(BF16)
-    values = dot_nn(normed[...], w_value_ref[...]).astype(BF16)
+    loader.wait()
+    keys = dot_nn(normed[...], w_key[...]).astype(BF16)
+    values = dot_nn(normed[...], w_value[...]).astype(BF16)
     for ref in (kept_ref, ahead_ref, behind_ref):
         ref[0:ROWS, 0:wide] = keys
         ref[0:ROWS, wide : 2 * wide] = values
-    queries = dot_nn(normed[...], w_query_ref[...]).astype(BF16)
+    late.wait()
+    queries = dot_nn(normed[...], w_query[...]).astype(BF16)
     queries_ref[...] = queries
     ahead_ref[ROWS : ROWS + EDGE, :] = own_ref[ROWS - EDGE : ROWS, :]
     ahead_ref[ROWS + EDGE : ROWS + EDGE + half, 0:wide] = queries[ROWS - EDGE : ROWS - half]
@@ -113,15 +124,43 @@
     behind_ref[ROWS + EDGE + half : ROWS + 2 * EDGE + half, :] = top_ref[0:EDGE, :]
 
 
-def chosen_rows(odd, when_odd, when_even, rows):
-    if when_odd is when_even:
-        return when_odd[rows, :]
-    return jnp.where(odd, when_odd[rows, :].astype(F32), when_even[rows, :].astype(F32)).astype(BF16)
-
-
-def gather_window(odd, sources, window):
-    for index, (when_odd, when_even) in enumerate(sources):
-        window[index * ROWS : (index + 1) * ROWS, :] = chosen_rows(odd, when_odd, when_even, slice(0, ROWS))
+class Loader:
+    def __init__(self, semaphores, odd):
+        self.semaphores = semaphores
+        self.odd = odd
+        self.used = 0
+        self.waiting = []
+
+    def get(self, target, when_odd, when_even=None, rows=None):
+        semaphore = self.semaphores.at[self.used]
+        self.used += 1
+
+        def copy(source):
+            view = source if rows is None else source.at[rows[0] : rows[1]]
+            return pltpu.make_async_copy(view, target, semaphore)
+
+        if when_even is None or when_even is when_odd:
+            copy(when_odd).start()
+        else:
+
+            @pl.when(self.odd)
+            def _():
+                copy(when_odd).start()
+
+            @pl.when(jnp.logical_not(self.odd))
+            def _():
+                copy(when_even).start()
+
+        self.waiting.append(copy(when_odd))
+
+    def window(self, target, sources):
+        for index, (when_odd, when_even) in enumerate(sources):
+            self.get(target.at[index * ROWS : (index + 1) * ROWS], when_odd, when_even, (0, ROWS))
+
+    def wait(self):
+        for copy in self.waiting:
+            copy.wait()
+        self.waiting = []
 
 
 def masked_half(value, half):
@@ -153,13 +192,18 @@
     log_ref,
     window,
     query_all,
+    packed,
+    semaphores,
 ):
     place = lax.axis_index("tm")
     odd = lax.rem(place, 2) == 1
     wide = queries_ref.shape[1]
     half_edge = EDGE // 2
-    gather_window(
-        odd,
+    loader = Loader(semaphores, odd)
+    loader.get(query_all.at[0:ROWS], queries_ref)
+    loader.get(packed, after_ref, rows=(ROWS + EDGE, ROWS + EDGE + half_edge))
+    loader.window(
+        window,
         (
             (back4_ref, back4_ref),
             (peer_back2_ref, peer_back4_ref),
@@ -168,13 +212,10 @@
             (kept_ref, kept_ref),
             (after_ref, after_ref),
         ),
-        window,
-    )
-    query_all[0:ROWS, :] = queries_ref[...]
-    query_all[ROWS : ROWS + half_edge, :] = after_ref[ROWS + EDGE : ROWS + EDGE + half_edge, 0:wide]
-    query_all[ROWS + half_edge : ROWS + EDGE, :] = after_ref[
-        ROWS + EDGE : ROWS + EDGE + half_edge, wide : 2 * wide
-    ]
+    )
+    loader.wait()
+    query_all[ROWS : ROWS + half_edge, :] = packed[:, 0:wide]
+    query_all[ROWS + half_edge : ROWS + EDGE, :] = packed[:, wide : 2 * wide]
     key_lane = lax.broadcasted_iota(jnp.int32, (1, ROWS), 1)
     allowed = jnp.concatenate(
         [key_lane < valid_count(valid_ref, place + block - LEFT) for block in range(LEFT + 2)], axis=1
@@ -203,7 +244,7 @@
 
 
 def mixer_body(
-    count, upstream_ref, next_rows, slope_ref, kernel_ref, w_out_ref, attended, log_ref, total_ref, message_ref, dot_ref, total_low
+    count, upstream_ref, next_rows, slope_ref, kernel_ref, w_out_ref, attended, log_ref, total_ref, message_ref, dot_ref, total_low, ready=lambda: None
 ):
     row_ids = lax.broadcasted_iota(jnp.int32, (ROWS, PAIR), 0)
     taps = kernel_ref.shape[0]
@@ -220,9 +261,10 @@
         return carry
 
     lax.fori_loop(0, upstream_ref.shape[1] // PAIR, conv_step, 0)
+    ready()
     out_grad = dot_nt(total_low[...], w_out_ref[...]).astype(BF16)
     message_ref[0:ROWS, :] = out_grad
-    product = out_grad.astype(F32) * attended.astype(F32)
+    product = out_grad.astype(F32) * attended[...].astype(F32)
     high = product.astype(BF16)
     low = (product - high.astype(F32)).astype(BF16)
     width = product.shape[1]
@@ -260,14 +302,22 @@
     attended_all,
     mixed,
     total_low,
+    before_rows,
+    after_rows,
+    own,
+    top,
+    w_out,
+    semaphores,
 ):
     place = lax.axis_index("tm")
     odd = lax.rem(place, 2) == 1
-    wide = attended_ref.shape[1]
+    wide = query_tail.shape[1]
     half_edge = EDGE // 2
     counts = [valid_count(valid_ref, place + block - LEFT - 1) for block in range(LEFT + 3)]
-    gather_window(
-        odd,
+    loader = Loader(semaphores, odd)
+    loader.get(before_rows, peer_ref, peer_back2_ref, (ROWS, ROWS + EDGE + half_edge))
+    loader.window(
+        window,
         (
             (peer_back4_ref, back5_ref),
             (back4_ref, back4_ref),
@@ -275,11 +325,16 @@
             (back2_ref, back2_ref),
             (peer_ref, peer_back2_ref),
         ),
-        window,
-    )
-    packed = chosen_rows(odd, peer_ref, peer_back2_ref, slice(ROWS + EDGE, ROWS + EDGE + half_edge))
-    query_tail[0:half_edge, :] = packed[:, 0:wide]
-    query_tail[half_edge:EDGE, :] = packed[:, wide : 2 * wide]
+    )
+    late = Loader(semaphores.at[LEFT + 2 :], odd)
+    late.get(attended_all.at[EDGE : 2 * EDGE + ROWS], attended_ref)
+    late.get(w_out, w_out_ref)
+    late.get(own, own_ref)
+    late.get(after_rows, after_ref, rows=(ROWS, ROWS + 2 * EDGE + half_edge))
+    late.get(top, top_ref)
+    loader.wait()
+    query_tail[0:half_edge, :] = before_rows[EDGE : EDGE + half_edge, 0:wide]
+    query_tail[half_edge:EDGE, :] = before_rows[EDGE : EDGE + half_edge, wide : 2 * wide]
     key_lane = lax.broadcasted_iota(jnp.int32, (1, ROWS), 1)
     allowed = jnp.concatenate([key_lane < count for count in counts[: LEFT + 1]], axis=1)
     for pair in range(wide // PAIR):
@@ -292,15 +347,13 @@
             product = dot_nn(shares_low, masked_half(window[:, value_lanes], half))
             total = product if total is None else total + product
         attended_all[0:EDGE, lanes] = total.astype(BF16)
-    attended_all[EDGE:, :] = attended_ref[...]
-
-    projected = dot_nn(attended_all[...], w_out_ref[...])
+    late.wait()
+    projected = dot_nn(attended_all[...], w_out[...])
     row_ids = lax.broadcasted_iota(jnp.int32, (ROWS, 1), 0)
     edge_ids = lax.broadcasted_iota(jnp.int32, (EDGE, 1), 0)
-    x_before = chosen_rows(odd, peer_ref, peer_back2_ref, slice(ROWS, ROWS + EDGE)).astype(F32)
-    before = projected[0:EDGE] + x_before
-    here = projected[EDGE : EDGE + ROWS] + own_ref[...].astype(F32)
-    after = projected[EDGE + ROWS :] + after_ref[ROWS : ROWS + EDGE, :].astype(F32)
+    before = projected[0:EDGE] + before_rows[0:EDGE, :].astype(F32)
+    here = projected[EDGE : EDGE + ROWS] + own[...].astype(F32)
+    after = projected[EDGE + ROWS :] + after_rows[0:EDGE, :].astype(F32)
     before = jnp.where(edge_ids + (ROWS - EDGE) < counts[LEFT], before, 0.0)
     here = jnp.where(row_ids < counts[LEFT + 1], here, 0.0)
     after = jnp.where(edge_ids < counts[LEFT + 2], after, 0.0)
@@ -316,16 +369,16 @@
         slope_ref[:, lanes] = gate * (1.0 + output * (1.0 - gate))
         return carry
 
-    lax.fori_loop(0, own_ref.shape[1] // PAIR, conv_step, 0)
-    first = ROWS + EDGE + half_edge
+    lax.fori_loop(0, own.shape[1] // PAIR, conv_step, 0)
+    first = EDGE + half_edge
     mixer_body(
         counts[LEFT + 1],
-        top_ref,
-        lambda lanes: after_ref[first : first + EDGE, lanes].astype(F32),
+        top,
+        lambda lanes: after_rows[first : first + EDGE, lanes].astype(F32),
         slope_ref,
         kernel_ref,
-        w_out_ref,
-        attended_ref[0:ROWS, :],
+        w_out,
+        attended_all[EDGE : EDGE + ROWS, :],
         log_ref,
         total_ref,
         message_ref,
@@ -347,20 +400,35 @@
     message_ref,
     dot_ref,
     total_low,
+    upstream,
+    next_rows,
+    slope,
+    w_out,
+    attended,
+    semaphores,
 ):
+    loader = Loader(semaphores, None)
+    loader.get(upstream, upstream_ref)
+    loader.get(next_rows, next_ref)
+    loader.get(slope, slope_ref)
+    late = Loader(semaphores.at[3:], None)
+    late.get(attended, attended_ref, rows=(0, ROWS))
+    late.get(w_out, w_out_ref)
+    loader.wait()
     mixer_body(
         valid_count(valid_ref, lax.axis_index("tm")),
-        upstream_ref,
-        lambda lanes: next_ref[:, lanes].astype(F32),
-        slope_ref,
+        upstream,
+        lambda lanes: next_rows[:, lanes].astype(F32),
+        slope,
         kernel_ref,
-        w_out_ref,
-        attended_ref[0:ROWS, :],
+        w_out,
+        attended,
         log_ref,
         total_ref,
         message_ref,
         dot_ref,
         total_low,
+        late.wait,
     )
 
 
@@ -417,12 +485,19 @@
     value_sum_ref,
     window,
     query_grad,
+    queries,
+    message,
+    w_query,
+    semaphores,
 ):
     place = lax.axis_index("tm")
     odd = lax.rem(place, 2) == 1
     wide = queries_ref.shape[1]
-    gather_window(
-        odd,
+    loader = Loader(semaphores, odd)
+    loader.get(queries, queries_ref)
+    loader.get(message, message_ref)
+    loader.window(
+        window,
         (
             (back4_ref, back4_ref),
             (peer_back2_ref, peer_back4_ref),
@@ -430,19 +505,22 @@
             (peer_ref, peer_back2_ref),
             (kept_ref, kept_ref),
         ),
-        window,
-    )
+    )
+    late = Loader(semaphores.at[LEFT + 3 :], odd)
+    late.get(w_query, w_query_ref)
+    loader.wait()
+    own_rows = slice(LEFT * ROWS, (LEFT + 1) * ROWS)
     key_lane = lax.broadcasted_iota(jnp.int32, (1, ROWS), 1)
     allowed = jnp.concatenate(
         [key_lane < valid_count(valid_ref, place + block - LEFT) for block in range(LEFT + 1)], axis=1
     )
     key_valid = lax.broadcasted_iota(jnp.int32, (ROWS, ROWS), 0) < valid_count(valid_ref, place)
-    stats = message_stats(message_ref[ROWS : ROWS + 16, :])
+    stats = message_stats(message[ROWS : ROWS + 16, :])
     for pair in range(wide // PAIR):
         lanes = slice(pair * PAIR, (pair + 1) * PAIR)
         value_lanes = slice(wide + pair * PAIR, wide + (pair + 1) * PAIR)
-        query_pair = queries_ref[:, lanes]
-        grad_pair = message_ref[0:ROWS, lanes]
+        query_pair = queries[:, lanes]
+        grad_pair = message[0:ROWS, lanes]
         total = None
         for half in range(2):
             key_half = masked_half(window[:, lanes], half)
@@ -457,15 +535,16 @@
         query_grad[:, lanes] = (total * SCALE).astype(BF16)
         heads = (2 * pair, 2 * pair + 1)
         key_sum_ref[:, lanes], value_sum_ref[:, lanes] = key_terms(
-            kept_ref[:, lanes],
-            kept_ref[:, value_lanes],
+            window[own_rows, lanes],
+            window[own_rows, value_lanes],
             query_pair,
             grad_pair,
             [stats[head : head + 1] for head in heads],
             [stats[8 + head : 9 + head] for head in heads],
             key_valid,
         )
-    out_ref[...] = dot_nt(query_grad[...], w_query_ref[...])
+    late.wait()
+    out_ref[...] = dot_nt(query_grad[...], w_query[...])
 
 
 def key_kernel(
@@ -492,45 +571,64 @@
     result_ref,
     keep_ref,
     out_ref,
+    edge_ref,
     held_ref,
     grads,
     queries,
+    tails,
     stats,
     key_grad,
     value_grad,
+    kept,
+    w_key,
+    w_value,
+    own,
+    total,
+    partial,
+    result,
+    semaphores,
 ):
     place = lax.axis_index("tm")
     odd = lax.rem(place, 2) == 1
     count = valid_count(valid_ref, place)
     wide = grads.shape[1]
+    loader = Loader(semaphores, odd)
     messages = (
         (peer_next2_ref, peer_ref),
         (next2_ref, next2_ref),
         (peer_next4_ref, peer_next2_ref),
         (next4_ref, next4_ref),
     )
-    gather_window(odd, messages, grads)
-    gather_window(
-        odd,
+    loader.get(kept, kept_ref)
+    loader.window(grads, messages)
+    for block, (when_odd, when_even) in enumerate(messages):
+        loader.get(tails.at[block * 16 : block * 16 + 16], when_odd, when_even, (ROWS, ROWS + 16))
+    loader.window(
+        queries,
         (
             (query_peer_next2_ref, query_peer_ref),
             (query_next2_ref, query_next2_ref),
             (query_peer_next4_ref, query_peer_next2_ref),
             (query_next4_ref, query_next4_ref),
         ),
-        queries,
-    )
-    for block, (when_odd, when_even) in enumerate(messages):
-        stats[:, block * ROWS : (block + 1) * ROWS] = message_stats(
-            chosen_rows(odd, when_odd, when_even, slice(ROWS, ROWS + 16))
-        )
+    )
+    late = Loader(semaphores.at[loader.used :], odd)
+    late.get(w_key, w_key_ref)
+    late.get(w_value, w_value_ref)
+    late.get(own, own_ref)
+    late.get(total, total_ref)
+    late.get(partial, partial_ref)
+    late.get(result, result_ref)
+    loader.wait()
+    for block in range(LEFT):
+        stats[:, block * ROWS : (block + 1) * ROWS] = message_stats(tails[block * 16 : block * 16 + 16, :])
     key_valid = lax.broadcasted_iota(jnp.int32, (ROWS, LEFT * ROWS), 0) < count
     for pair in range(wide // PAIR):
         lanes = slice(pair * PAIR, (pair + 1) * PAIR)
         heads = (2 * pair, 2 * pair + 1)
         key_sum, value_sum = key_terms(
-            kept_ref[:, lanes],
-            kept_ref[:, slice(wide + pair * PAIR, wide + (pair + 1) * PAIR)],
+            kept[:, lanes],
+            kept[:, slice(wide + pair * PAIR, wide + (pair + 1) * PAIR)],
             queries[:, lanes],
             grads[:, lanes],
             [stats[head : head + 1, :] for head in heads],
@@ -539,34 +637,44 @@
         )
         key_grad[:, lanes] = (key_sum_ref[:, lanes] + key_sum).astype(BF16)
         value_grad[:, lanes] = (value_sum_ref[:, lanes] + value_sum).astype(BF16)
-    normed_grad = partial_ref[...] + dot_nt(key_grad[...], w_key_ref[...])
-    normed_grad = normed_grad + dot_nt(value_grad[...], w_value_ref[...])
+    late.wait()
+    normed_grad = partial[...] + dot_nt(key_grad[...], w_key[...])
+    normed_grad = normed_grad + dot_nt(value_grad[...], w_value[...])
     scaled = normed_grad * gain_ref[...]
-    unit, inverse = unit_rows(own_ref[...].astype(F32))
+    unit, inverse = unit_rows(own[...].astype(F32))
     back = inverse * (
         scaled
         - jnp.mean(scaled, axis=-1, keepdims=True)
         - unit * jnp.mean(scaled * unit, axis=-1, keepdims=True)
     )
-    result = total_ref[...] + back
-    out_ref[...] = result.astype(BF16)
+    grad = total[...] + back
+    out_ref[...] = grad.astype(BF16)
+    edge_ref[...] = grad[0:EDGE].astype(BF16)
     mine = lax.axis_index("section") == keep_ref[0]
-    held_ref[...] = jnp.where(mine, result, result_ref[...].astype(F32)).astype(BF16)
-
-
-def call(kernel, name, operands, outs, scratch, flops, scalars=(0,)):
-    vmem = pl.BlockSpec(memory_space=pltpu.VMEM)
-    smem = pl.BlockSpec(memory_space=pltpu.SMEM)
+    held_ref[...] = jnp.where(mine, grad, result[...].astype(F32)).astype(BF16)
+
+
+def call(kernel, name, operands, outs, scratch, copies, flops):
+    kinds = {
+        "s": pl.BlockSpec(memory_space=pltpu.SMEM),
+        "v": pl.BlockSpec(memory_space=pltpu.VMEM),
+        "a": pl.BlockSpec(memory_space=pl.ANY),
+    }
     return pl.pallas_call(
         kernel,
         name=name,
-        in_specs=[smem if index in scalars else vmem for index in range(len(operands))],
-        out_specs=[vmem] * len(outs),
+        in_specs=[kinds[place] for _, place in operands],
+        out_specs=[kinds["v"]] * len(outs),
         out_shape=[jax.ShapeDtypeStruct(shape, dtype) for shape, dtype in outs],
-        scratch_shapes=[pltpu.VMEM(shape, dtype) for shape, dtype in scratch],
+        scratch_shapes=[pltpu.VMEM(shape, dtype) for shape, dtype in scratch]
+        + [pltpu.SemaphoreType.DMA((copies,))],
         compiler_params=pltpu.CompilerParams(vmem_limit_bytes=VMEM_LIMIT),
         cost_estimate=pl.CostEstimate(flops=flops, bytes_accessed=4 << 20, transcendentals=0),
-    )(*operands)
+    )(*[array for array, _ in operands])
+
+
+def placed(kinds, *arrays):
+    return list(zip(arrays, kinds, strict=True))
 
 
 def after(value, *others):
@@ -600,60 +708,64 @@
             for source in range(max(0, -steps), min(count, count - steps))
         ]
 
-    def swapped(chosen, parities):
-        return [
-            (at(section, source), at(section, source ^ 1))
-            for section in chosen
-            for source in range(count)
-            if source % 2 in parities
-        ]
-
     every = range(sections)
     half_edge = EDGE // 2
+    swap = [(at(section, source), at(section, source ^ 1)) for section in every for source in range(count)]
+    weight = ((width, wide), BF16)
     queries, kept, ahead, behind = call(
         project_kernel,
         "project",
-        (own, top_grad, norm_gain, query_weight, key_weight, value_weight),
+        placed("vvvaaa", own, top_grad, norm_gain, query_weight, key_weight, value_weight),
         [
             ((ROWS, wide), BF16),
             ((ROWS, 2 * wide), BF16),
             ((ROWS + EDGE + half_edge, width), BF16),
             ((ROWS + 2 * EDGE + half_edge, width), BF16),
         ],
-        [((ROWS, width), BF16)],
+        [((ROWS, width), BF16), weight, weight, weight],
+        3,
         1 << 30,
-        scalars=(),
     )
     back2 = moved(ahead, across(2, every))
     back4 = moved(kept, across(4, every))
-    peer = moved(ahead, swapped(every, (0,)))
     after1 = moved(behind, across(-1, every))
-    peer_back2 = moved(back2, swapped(every, (0, 1)))
-    peer_back4 = moved(back4, swapped(every, (0, 1)))
+    query_next2 = moved(queries, across(-2, every))
+    query_next4 = moved(queries, across(-4, every))
+    peer = moved(ahead, swap)
+    query_peer = moved(queries, swap)
+    peer_back2 = moved(back2, swap)
+    peer_back4 = moved(back4, swap)
+    query_peer_next2 = moved(query_next2, swap)
+    query_peer_next4 = moved(query_next4, swap)
     far_pairs = [
         (at(section, source), at(section, source + 5))
         for section in every
         for source in range(1, count - 5, 2)
     ]
     back5 = moved(after(kept, back2), far_pairs)
-    query_next2 = moved(after(queries, back2), across(-2, every))
-    query_next4 = moved(after(queries, back2), across(-4, every))
-
+    query_next2, query_next4, query_peer, query_peer_next2, query_peer_next4, after1 = (
+        lax.optimization_barrier(
+            (query_next2, query_next4, query_peer, query_peer_next2, query_peer_next4, after1)
+        )
+    )
+
+    span = (LEFT + 1) * ROWS
     attended, logs = call(
         attend_kernel,
         "attend",
-        (group_valid, queries, kept, back2, back4, peer, peer_back2, peer_back4, after1),
+        placed("saaaaaaaa", group_valid, queries, kept, back2, back4, peer, peer_back2, peer_back4, after1),
         [((ROWS + EDGE, wide), BF16), ((ROWS, PAIR), F32)],
-        [(((LEFT + 2) * ROWS, 2 * wide), BF16), ((ROWS + EDGE, wide), BF16)],
+        [(((LEFT + 2) * ROWS, 2 * wide), BF16), ((ROWS + EDGE, wide), BF16), ((half_edge, 2 * wide), BF16)],
+        LEFT + 4,
         1 << 30,
     )
     back5 = after(back5, attended)
-    span = (LEFT + 1) * ROWS
     step_outs = [((ROWS, width), F32), ((ROWS + 16, wide), BF16), ((ROWS, PAIR), F32)]
     slope, total, message, dots = call(
         mix_kernel,
         "mix",
-        (
+        placed(
+            "saaavaaaaaaaav",
             group_valid,
             own,
             top_grad,
@@ -676,12 +788,15 @@
             ((ROWS + 2 * EDGE, wide), BF16),
             ((ROWS + 2 * EDGE, width), F32),
             ((ROWS, width), BF16),
+            ((EDGE + half_edge, width), BF16),
+            ((2 * EDGE + half_edge, width), BF16),
+            ((ROWS, width), BF16),
+            ((ROWS, width), BF16),
+            ((wide, width), BF16),
         ],
+        LEFT + 7,
         1 << 30,
     )
-    query_peer = moved(queries, swapped(every, (1,)))
-    query_peer_next2 = moved(query_next2, swapped(every, (0, 1)))
-    query_peer_next4 = moved(query_next4, swapped(every, (0,)))
 
     result = own
     upstream = None
@@ -692,19 +807,30 @@
             total, message, dots = call(
                 mixer_kernel,
                 "mixer",
-                (group_valid, upstream, upstream_next, slope, kernel, out_weight, attended, logs),
+                placed(
+                    "saaavaav", group_valid, upstream, upstream_next, slope, kernel, out_weight, attended, logs
+                ),
                 step_outs,
-                [((ROWS, width), BF16)],
+                [
+                    ((ROWS, width), BF16),
+                    ((ROWS, width), BF16),
+                    ((EDGE, width), BF16),
+                    ((ROWS + EDGE, width), F32),
+                    ((wide, width), BF16),
+                    ((ROWS, wide), BF16),
+                ],
+                5,
                 1 << 30,
             )
         here = [layer]
         grad2 = moved(message, across(-2, here))
         grad4 = moved(message, across(-4, here))
-        peer_grad = moved(message, swapped(here, (1,)))
+        peer_grad = moved(message, swap)
         partial, key_sum, value_sum = call(
             query_kernel,
             "own_queries",
-            (
+            placed(
+                "saaaaaaaavva",
                 group_valid,
                 queries,
                 kept,
@@ -719,58 +845,74 @@
                 query_weight,
             ),
             [((ROWS, width), F32), ((ROWS, wide), F32), ((ROWS, wide), F32)],
-            [((span, 2 * wide), BF16), ((ROWS, wide), BF16)],
+            [
+                ((span, 2 * wide), BF16),
+                ((ROWS, wide), BF16),
+                ((ROWS, wide), BF16),
+                ((ROWS + 16, wide), BF16),
+                weight,
+            ],
+            LEFT + 4,
             1 << 30,
         )
         grad2, grad4, partial = lax.optimization_barrier((grad2, grad4, partial))
-        peer_grad2 = moved(grad2, swapped(here, (0, 1)))
-        peer_grad4 = moved(grad4, swapped(here, (0,)))
-        operands = (
-            group_valid,
-            kept,
-            query_next2,
-            query_next4,
-            query_peer,
-            query_peer_next2,
-            query_peer_next4,
-            grad2,
-            grad4,
-            peer_grad,
-            peer_grad2,
-            peer_grad4,
-            key_weight,
-            value_weight,
-            norm_gain,
-            own,
-            total,
-            partial,
-            key_sum,
-            value_sum,
-            result,
-            jnp.full((1,), layer, jnp.int32),
-        )
-        input_grad, result = call(
+        peer_grad2 = moved(grad2, swap)
+        peer_grad4 = moved(grad4, swap)
+        input_grad, edge, result = call(
             key_kernel,
             "own_keys",
-            operands,
-            [((ROWS, width), BF16), ((ROWS, width), BF16)],
+            placed(
+                "saaaaaaaaaaaaavaaavvas",
+                group_valid,
+                kept,
+                query_next2,
+                query_next4,
+                query_peer,
+                query_peer_next2,
+                query_peer_next4,
+                grad2,
+                grad4,
+                peer_grad,
+                peer_grad2,
+                peer_grad4,
+                key_weight,
+                value_weight,
+                norm_gain,
+                own,
+                total,
+                partial,
+                key_sum,
+                value_sum,
+                result,
+                jnp.full((1,), layer, jnp.int32),
+            ),
+            [((ROWS, width), BF16), ((EDGE, width), BF16), ((ROWS, width), BF16)],
             [
                 ((LEFT * ROWS, wide), BF16),
                 ((LEFT * ROWS, wide), BF16),
+                ((LEFT * 16, wide), BF16),
                 ((16, LEFT * ROWS), F32),
                 ((ROWS, wide), BF16),
                 ((ROWS, wide), BF16),
+                ((ROWS, 2 * wide), BF16),
+                weight,
+                weight,
+                ((ROWS, width), BF16),
+                ((ROWS, width), F32),
+                ((ROWS, width), F32),
+                ((ROWS, width), BF16),
             ],
+            3 * LEFT + 7,
             1 << 30,
-            scalars=(0, len(operands) - 1),
         )
         if layer > 0:
             upstream = moved(
-                input_grad, [(at(layer, source), at(layer - 1, source)) for source in range(count)]
+                input_grad,
+                [(at(layer, source), at(layer - 1, source)) for source in range(count)]
+                + [(at(layer - 1, source), at(layer, source)) for source in range(count)],
             )
             upstream_next = moved(
-                input_grad[:EDGE],
-                [(at(layer, source), at(layer - 1, source - 1)) for source in range(1, count)],
+                edge, [(at(layer, source), at(layer - 1, source - 1)) for source in range(1, count)]
             )
     return result[None]
 

time: 119 us -> 106 us (0.89)
  starting transfers between devices: 46.5 us -> 35.2 us
  waiting for transfers between devices: 16.6 us -> 12.4 us
  Pallas kernels: 48.7 us -> 50.6 us
    ppermute x24, starting transfers between devices: 46.5 us -> 35.2 us  [moved(): return lax.ppermute(value, ('tm', 'section'), pairs)]
    ppermute x24, waiting for transfers between devices: 16.6 us -> 12.4 us  [moved(): return lax.ppermute(value, ('tm', 'section'), pairs)]
    pallas_call x8, Pallas kernels: 48.7 us -> 50.6 us  [call(): pl.pallas_call(kernel, name=name, in_specs=[kinds[place] for _, place in...]
    unnamed x55 -> x51, local copies, waits for them, and re-layouts: 4.53 us -> 5.2 us
  transfers between devices with their start and end apart: 24 -> 24, of which waited for: 6 -> 8; matrix products, arithmetic and copies ran while one was open for 1% -> 1% of each run, Pallas kernels for 14% -> 18%
where the time goes in v3:
time: 106 us; the launch traced here: 104 us
  Pallas kernels  50.6 us (48%)
  starting transfers between devices  35.2 us (33%)
  waiting for transfers between devices  12.4 us (12%)
  local copies, waits for them, and re-layouts  5.2 us (5%)
    pallas_call x8, Pallas kernels, call(): pl.pallas_call(kernel, name=name, in_specs=[kinds[place] for _, place in...  50.6 us
    ppermute x24, starting transfers between devices, moved(): return lax.ppermute(value, ('tm', 'section'), pairs)  35.2 us
    ppermute x24, waiting for transfers between devices, moved(): return lax.ppermute(value, ('tm', 'section'), pairs)  12.4 us
    unnamed x51, local copies, waits for them, and re-layouts  5.2 us
  transfers between devices with their start and end apart: 24, of which 8 were waited for; matrix products, arithmetic and copies ran while one was open for 1% of the time, Pallas kernels for 18%

profile of v3, /device:TPU:19, one launch (start us, length us, event | category | flops | bytes accessed | tf_op | source)
XLA Modules:
  0.0 103.9 jit_solution(162994539231175189)
XLA Ops:
  0.0 4.3 %project.1 = (bf16[128,512]{1,0:T(8,128)(2,1)}, bf16[128,1024]{1,0:T(8,128)(2,1)}, bf16[176,1024]{1,0:T(8,128)(2,1)}, bf16[208,1024]{1,0:T(8,128)(2,1)}) custom-call(bf16[128,1024]{1,0:T(8,128)(2,1)} %bitcast.9, bf16[128,1024]{1,0:T(8,128)(2,1)} %top_ref.3, f32[1,1024]{1,0:T(1,128)} %gain_ref.5, bf16[1024,512]{1,0:T(8,128)(2,1)} %bitcast.24, ...), custom_call_target="tpu_custom_call" | custom-call | flops 1073741824 | bytes 4194304 | tf_op jit(solution)/shard_map/project/pallas_call | solution.py:663
  4.3 3.2 %collective-permute-start.6 = (bf16[176,1024]{1,0:T(8,128)(2,1)}, bf16[176,1024]{1,0:T(8,128)(2,1)S(1)}, u32[]{:S(2)}, u32[]{:S(2)}) collective-permute-start(bf16[176,1024]{1,0:T(8,128)(2,1)} %get-tuple-element.50), channel_id=1, source_target_pairs={{0,4},{2,6},{4,8},{6,10},{8,12},{10,14},{12,16},{14,18},{16,20},{1... | collective-permute-start | bytes 1081352 | tf_op jit(solution)/shard_map/ppermute | solution.py:699
  7.5 1.0 collective-permute-start.2
  8.5 2.1 %collective-permute-start.1 = (bf16[128,512]{1,0:T(8,128)(2,1)}, bf16[128,512]{1,0:T(8,128)(2,1)S(1)}, u32[]{:S(2)}, u32[]{:S(2)}) collective-permute-start(bf16[128,512]{1,0:T(8,128)(2,1)} %get-tuple-element.43.queries_ref), channel_id=1, source_target_pairs={{8,0},{10,2},{12,4},{14,6},{16,8},{18,10},{20,12},{22,14},{24,16},... | collective-permute-start | bytes 393224 | tf_op jit(solution)/shard_map/ppermute | solution.py:699
  10.6 3.2 %collective-permute-start.7 = (bf16[128,1024]{1,0:T(8,128)(2,1)}, bf16[128,1024]{1,0:T(8,128)(2,1)S(1)}, u32[]{:S(2)}, u32[]{:S(2)}) collective-permute-start(bf16[128,1024]{1,0:T(8,128)(2,1)} %get-tuple-element.54.kept_ref), channel_id=1, source_target_pairs={{0,8},{2,10},{4,12},{6,14},{8,16},{10,18},{12,20},{14,22},{16,24},... | collective-permute-start | bytes 786440 | tf_op jit(solution)/shard_map/ppermute | solution.py:699
  13.8 2.1 %collective-permute-start = (bf16[128,512]{1,0:T(8,128)(2,1)}, bf16[128,512]{1,0:T(8,128)(2,1)S(1)}, u32[]{:S(2)}, u32[]{:S(2)}) collective-permute-start(bf16[128,512]{1,0:T(8,128)(2,1)} %get-tuple-element.43.queries_ref), channel_id=1, source_target_pairs={{4,0},{6,2},{8,4},{10,6},{12,8},{14,10},{16,12},{18,14},{20,16},{2... | collective-permute-start | bytes 393224 | tf_op jit(solution)/shard_map/ppermute | solution.py:699
  15.9 0.0 collective-permute-done.2.query_peer_ref
  16.0 2.8 %collective-permute-start.5 = (bf16[208,1024]{1,0:T(8,128)(2,1)}, bf16[208,1024]{1,0:T(8,128)(2,1)S(1)}, u32[]{:S(2)}, u32[]{:S(2)}) collective-permute-start(bf16[208,1024]{1,0:T(8,128)(2,1)} %get-tuple-element.44), channel_id=1, source_target_pairs={{2,0},{4,2},{6,4},{8,6},{10,8},{12,10},{14,12},{16,14},{18,16},{20... | collective-permute-start | bytes 1277960 | tf_op jit(solution)/shard_map/ppermute | solution.py:699
  18.7 0.0 collective-permute-done.1.query_next4_ref
  18.8 0.7 collective-permute-start.4
  19.5 1.8 %collective-permute-done.query_next2_ref = bf16[128,512]{1,0:T(8,128)(2,1)S(1)} collective-permute-done((bf16[128,512]{1,0:T(8,128)(2,1)}, bf16[128,512]{1,0:T(8,128)(2,1)S(1)}, u32[]{:S(2)}, u32[]{:S(2)}) %collective-permute-start) | collective-permute-done | bytes 131104 | tf_op jit(solution)/shard_map/ppermute | solution.py:699
  21.3 1.4 %collective-permute-start.8 = (bf16[176,1024]{1,0:T(8,128)(2,1)}, bf16[176,1024]{1,0:T(8,128)(2,1)S(1)}, u32[]{:S(2)}, u32[]{:S(2)}) collective-permute-start(bf16[176,1024]{1,0:T(8,128)(2,1)} %get-tuple-element.50), channel_id=1, source_target_pairs={{0,2},{2,0},{4,6},{6,4},{8,10},{10,8},{12,14},{14,12},{16,18},{18,... | collective-permute-start | bytes 1081352 | tf_op jit(solution)/shard_map/ppermute | solution.py:699
  22.7 0.0 collective-permute-done.6.back2_ref
  22.8 0.1 collective-permute-start.9
  22.8 0.0 collective-permute-done.4.query_peer_next4_ref
  22.8 0.4 collective-permute-start.3
  23.3 0.0 collective-permute-done.7.back4_ref
  23.3 0.1 collective-permute-start.10
  23.4 1.4 %collective-permute-done.3.query_peer_next2_ref = bf16[128,512]{1,0:T(8,128)(2,1)S(1)} collective-permute-done((bf16[128,512]{1,0:T(8,128)(2,1)S(1)}, bf16[128,512]{1,0:T(8,128)(2,1)S(1)}, u32[]{:S(2)}, u32[]{:S(2)}) %collective-permute-start.3) | collective-permute-done | bytes 131104 | tf_op jit(solution)/shard_map/ppermute | solution.py:699
  24.8 0.7 collective-permute-start.11
  25.4 0.7 copy.12
  26.1 0.7 collective-permute-done.5.after_ref
  26.8 0.0 collective-permute-done.8.peer_ref
  26.8 0.0 collective-permute-done.9.peer_back2_ref
  26.9 0.7 copy-done.5
  27.6 0.2 copy-done.7
  27.7 0.1 copy-done.10
  27.8 0.7 copy-done.8
  28.6 5.8 %attend.1 = (bf16[160,512]{1,0:T(8,128)(2,1)}, f32[128,128]{1,0:T(8,128)}) custom-call(s32[16]{0:T(128)} %valid_ref.13, bf16[128,512]{1,0:T(8,128)(2,1)} %get-tuple-element.43.queries_ref, bf16[128,1024]{1,0:T(8,128)(2,1)} %get-tuple-element.54.kept_ref, bf16[176,1024]{1,0:T(8,128)(2,1)} %copy-done.6, bf16[128,1024]{1,0:T(8,128)(2,1)} %copy-done.9, ...), custom_call_target="tpu_custom_call" | custom-call | flops 1073741824 | bytes 4194304 | tf_op jit(solution)/shard_map/attend/pallas_call | solution.py:663
  34.4 0.0 collective-permute-done.11.back5_ref
  34.4 0.7 copy-done.11
  35.1 10.2 %mix.1 = (f32[160,1024]{1,0:T(8,128)}, f32[128,1024]{1,0:T(8,128)}, bf16[144,512]{1,0:T(8,128)(2,1)}, f32[128,128]{1,0:T(8,128)}) custom-call(s32[16]{0:T(128)} %valid_ref.13, bf16[128,1024]{1,0:T(8,128)(2,1)} %bitcast.10, bf16[128,1024]{1,0:T(8,128)(2,1)} %top_ref.3, bf16[160,512]{1,0:T(8,128)(2,1)} %get-tuple-element.52.attended_ref, ...), custom_call_target="tpu_custom_call" | custom-call | flops 1073741824 | bytes 4194304 | tf_op jit(solution)/shard_map/mix/pallas_call | solution.py:663
  45.3 0.7 collective-permute-start.13
  46.0 0.9 collective-permute-start.12
  46.9 0.4 collective-permute-start.14
  47.2 6.3 %own_queries.2 = (f32[128,1024]{1,0:T(8,128)}, f32[128,512]{1,0:T(8,128)}, f32[128,512]{1,0:T(8,128)}) custom-call(s32[16]{0:T(128)} %valid_ref.13, bf16[128,512]{1,0:T(8,128)(2,1)} %get-tuple-element.43.queries_ref, bf16[128,1024]{1,0:T(8,128)(2,1)} %get-tuple-element.54.kept_ref, bf16[176,1024]{1,0:T(8,128)(2,1)} %copy-done.6, ...), custom_call_target="tpu_custom_call" | custom-call | flops 1073741824 | bytes 4194304 | tf_op jit(solution)/shard_map/own_queries/pallas_call | solution.py:663
  53.6 0.0 collective-permute-done.13.next4_ref
  53.6 0.3 collective-permute-start.15
  53.9 0.3 collective-permute-start.16
  54.2 0.9 collective-permute-done.15.peer_next2_ref
  55.0 0.2 collective-permute-done.16.peer_next4_ref
  55.3 0.4 copy-done.20
  55.7 0.2 copy-done.21
  55.9 6.1 %own_keys.2 = (bf16[128,1024]{1,0:T(8,128)(2,1)}, bf16[32,1024]{1,0:T(8,128)(2,1)}, bf16[128,1024]{1,0:T(8,128)(2,1)}) custom-call(s32[16]{0:T(128)} %valid_ref.13, bf16[128,1024]{1,0:T(8,128)(2,1)} %get-tuple-element.54.kept_ref, bf16[128,512]{1,0:T(8,128)(2,1)} %copy-done.2, bf16[128,512]{1,0:T(8,128)(2,1)} %copy-done.1, bf16[128,512]{1,0:T(8,128)(2,1)} %copy-done, ...), custom_call_target="tpu_custom_call" | custom-call | flops 1073741824 | bytes 4194304 | tf_op jit(solution)/shard_map/own_keys/pallas_call | solution.py:663
  62.0 7.2 %collective-permute-start.17 = (bf16[128,1024]{1,0:T(8,128)(2,1)}, bf16[128,1024]{1,0:T(8,128)(2,1)S(1)}, u32[]{:S(2)}, u32[]{:S(2)}) collective-permute-start(bf16[128,1024]{1,0:T(8,128)(2,1)} %get-tuple-element.65), channel_id=1, source_target_pairs={{1,0},{3,2},{5,4},{7,6},{9,8},{11,10},{13,12},{15,14},{17,16},{19,... | collective-permute-start | bytes 786440 | tf_op jit(solution)/shard_map/ppermute | solution.py:699
  69.2 1.3 %collective-permute-start.18 = (bf16[32,1024]{1,0:T(8,128)(2,1)}, bf16[32,1024]{1,0:T(8,128)(2,1)S(1)}, u32[]{:S(2)}, u32[]{:S(2)}) collective-permute-start(bf16[32,1024]{1,0:T(8,128)(2,1)} %get-tuple-element.66), channel_id=1, source_target_pairs={{3,0},{5,2},{7,4},{9,6},{11,8},{13,10},{15,12},{17,14},{19,16},{21... | collective-permute-start | bytes 196616 | tf_op jit(solution)/shard_map/ppermute | solution.py:699
  70.5 6.4 %collective-permute-done.18.next_ref = bf16[32,1024]{1,0:T(8,128)(2,1)S(1)} collective-permute-done((bf16[32,1024]{1,0:T(8,128)(2,1)}, bf16[32,1024]{1,0:T(8,128)(2,1)S(1)}, u32[]{:S(2)}, u32[]{:S(2)}) %collective-permute-start.18) | collective-permute-done | bytes 65568 | tf_op jit(solution)/shard_map/ppermute | solution.py:699
  76.9 0.0 collective-permute-done.17.upstream_ref
  76.9 0.6 copy-done.24
  77.5 0.2 copy-done.23
  77.7 5.4 %mixer.1 = (f32[128,1024]{1,0:T(8,128)}, bf16[144,512]{1,0:T(8,128)(2,1)}, f32[128,128]{1,0:T(8,128)}) custom-call(s32[16]{0:T(128)} %valid_ref.13, bf16[128,1024]{1,0:T(8,128)(2,1)} %copy-done.23, bf16[32,1024]{1,0:T(8,128)(2,1)} %copy-done.24, f32[160,1024]{1,0:T(8,128)} %get-tuple-element.67.slope_ref, f32[31,1024]{1,0:T(8,128)} %bitcast.23, ...), custom_call_target="tpu_custom_call" | custom-call | flops 1073741824 | bytes 4194304 | tf_op jit(solution)/shard_map/mixer/pallas_call | solution.py:663
  83.2 2.1 %collective-permute-start.20 = (bf16[144,512]{1,0:T(8,128)(2,1)}, bf16[144,512]{1,0:T(8,128)(2,1)S(1)}, u32[]{:S(2)}, u32[]{:S(2)}) collective-permute-start(bf16[144,512]{1,0:T(8,128)(2,1)} %get-tuple-element.68.message_ref), channel_id=1, source_target_pairs={{8,0},{10,2},{12,4},{14,6},{16,8},{18,10},{20,12},{22,14},{24,16},... | collective-permute-start | bytes 442376 | tf_op jit(solution)/shard_map/ppermute | solution.py:699
  85.3 1.9 %collective-permute-start.19 = (bf16[144,512]{1,0:T(8,128)(2,1)}, bf16[144,512]{1,0:T(8,128)(2,1)S(1)}, u32[]{:S(2)}, u32[]{:S(2)}) collective-permute-start(bf16[144,512]{1,0:T(8,128)(2,1)} %get-tuple-element.68.message_ref), channel_id=1, source_target_pairs={{4,0},{6,2},{8,4},{10,6},{12,8},{14,10},{16,12},{18,14},{20,16},{2... | collective-permute-start | bytes 442376 | tf_op jit(solution)/shard_map/ppermute | solution.py:699
  87.2 1.8 %collective-permute-start.21 = (bf16[144,512]{1,0:T(8,128)(2,1)}, bf16[144,512]{1,0:T(8,128)(2,1)S(1)}, u32[]{:S(2)}, u32[]{:S(2)}) collective-permute-start(bf16[144,512]{1,0:T(8,128)(2,1)} %get-tuple-element.68.message_ref), channel_id=1, source_target_pairs={{0,2},{2,0},{4,6},{6,4},{8,10},{10,8},{12,14},{14,12},{16,18},{18,... | collective-permute-start | bytes 442376 | tf_op jit(solution)/shard_map/ppermute | solution.py:699
  89.0 6.3 %own_queries.3 = (f32[128,1024]{1,0:T(8,128)}, f32[128,512]{1,0:T(8,128)}, f32[128,512]{1,0:T(8,128)}) custom-call(s32[16]{0:T(128)} %valid_ref.13, bf16[128,512]{1,0:T(8,128)(2,1)} %get-tuple-element.43.queries_ref, bf16[128,1024]{1,0:T(8,128)(2,1)} %get-tuple-element.54.kept_ref, bf16[176,1024]{1,0:T(8,128)(2,1)} %copy-done.6, ...), custom_call_target="tpu_custom_call" | custom-call | flops 1073741824 | bytes 4194304 | tf_op jit(solution)/shard_map/own_queries/pallas_call | solution.py:663
  95.4 0.0 collective-permute-done.19.next2_ref
  95.4 0.1 collective-permute-start.22
  95.5 0.5 collective-permute-start.23
  96.0 0.0 collective-permute-done.21.peer_ref
  96.0 0.9 collective-permute-done.22.peer_next2_ref
  96.8 0.2 collective-permute-done.23.peer_next4_ref
  97.0 0.4 copy-done.18
  97.5 0.2 copy-done.19
  97.7 6.1 %own_keys.3 = (bf16[128,1024]{1,0:T(8,128)(2,1)}, bf16[32,1024]{1,0:T(8,128)(2,1)}, bf16[128,1024]{1,0:T(8,128)(2,1)}) custom-call(s32[16]{0:T(128)} %valid_ref.13, bf16[128,1024]{1,0:T(8,128)(2,1)} %get-tuple-element.54.kept_ref, bf16[128,512]{1,0:T(8,128)(2,1)} %copy-done.2, bf16[128,512]{1,0:T(8,128)(2,1)} %copy-done.1, bf16[128,512]{1,0:T(8,128)(2,1)} %copy-done, ...), custom_call_target="tpu_custom_call" | custom-call | flops 1073741824 | bytes 4194304 | tf_op jit(solution)/shard_map/own_keys/pallas_call | solution.py:663
  (43 shorter events, 0.1 us)
Async XLA Ops:
  0.0 25.4 %copy-start.22 = (f32[1,31,1024]{2,0,1:T(1,128)S(1)}, f32[1,31,1024]{2,0,1:T(1,128)}, u32[]{:S(2)}) copy-start(f32[1,31,1024]{2,0,1:T(1,128)} %param.15) | copy-start | bytes 380932
  4.3 18.4 %collective-permute-start.6 = (bf16[176,1024]{1,0:T(8,128)(2,1)}, bf16[176,1024]{1,0:T(8,128)(2,1)S(1)}, u32[]{:S(2)}, u32[]{:S(2)}) collective-permute-start(bf16[176,1024]{1,0:T(8,128)(2,1)} %get-tuple-element.50), channel_id=1, source_target_pairs={{0,4},{2,6},{4,8},{6,10},{8,12},{10,14},{12,16},{14,18},{16,20},{1... | collective-permute-start | bytes 1081352 | tf_op jit(solution)/shard_map/ppermute | solution.py:699
  7.5 8.4 %collective-permute-start.2 = (bf16[128,512]{1,0:T(8,128)(2,1)}, bf16[128,512]{1,0:T(8,128)(2,1)S(1)}, u32[]{:S(2)}, u32[]{:S(2)}) collective-permute-start(bf16[128,512]{1,0:T(8,128)(2,1)} %get-tuple-element.43.queries_ref), channel_id=1, source_target_pairs={{0,2},{2,0},{4,6},{6,4},{8,10},{10,8},{12,14},{14,12},{16,18},{18,... | collective-permute-start | bytes 393224 | tf_op jit(solution)/shard_map/ppermute | solution.py:699
  8.5 10.2 %collective-permute-start.1 = (bf16[128,512]{1,0:T(8,128)(2,1)}, bf16[128,512]{1,0:T(8,128)(2,1)S(1)}, u32[]{:S(2)}, u32[]{:S(2)}) collective-permute-start(bf16[128,512]{1,0:T(8,128)(2,1)} %get-tuple-element.43.queries_ref), channel_id=1, source_target_pairs={{8,0},{10,2},{12,4},{14,6},{16,8},{18,10},{20,12},{22,14},{24,16},... | collective-permute-start | bytes 393224 | tf_op jit(solution)/shard_map/ppermute | solution.py:699
  10.6 12.7 %collective-permute-start.7 = (bf16[128,1024]{1,0:T(8,128)(2,1)}, bf16[128,1024]{1,0:T(8,128)(2,1)S(1)}, u32[]{:S(2)}, u32[]{:S(2)}) collective-permute-start(bf16[128,1024]{1,0:T(8,128)(2,1)} %get-tuple-element.54.kept_ref), channel_id=1, source_target_pairs={{0,8},{2,10},{4,12},{6,14},{8,16},{10,18},{12,20},{14,22},{16,24},... | collective-permute-start | bytes 786440 | tf_op jit(solution)/shard_map/ppermute | solution.py:699
  13.8 7.5 %collective-permute-start = (bf16[128,512]{1,0:T(8,128)(2,1)}, bf16[128,512]{1,0:T(8,128)(2,1)S(1)}, u32[]{:S(2)}, u32[]{:S(2)}) collective-permute-start(bf16[128,512]{1,0:T(8,128)(2,1)} %get-tuple-element.43.queries_ref), channel_id=1, source_target_pairs={{4,0},{6,2},{8,4},{10,6},{12,8},{14,10},{16,12},{18,14},{20,16},{2... | collective-permute-start | bytes 393224 | tf_op jit(solution)/shard_map/ppermute | solution.py:699
  16.0 18.4 %copy-start = (bf16[128,512]{1,0:T(8,128)(2,1)}, bf16[128,512]{1,0:T(8,128)(2,1)S(1)}, u32[]{:S(2)}) copy-start(bf16[128,512]{1,0:T(8,128)(2,1)S(1)} %collective-permute-done.2.query_peer_ref) | copy-start | bytes 393220
  16.0 10.8 %collective-permute-start.5 = (bf16[208,1024]{1,0:T(8,128)(2,1)}, bf16[208,1024]{1,0:T(8,128)(2,1)S(1)}, u32[]{:S(2)}, u32[]{:S(2)}) collective-permute-start(bf16[208,1024]{1,0:T(8,128)(2,1)} %get-tuple-element.44), channel_id=1, source_target_pairs={{2,0},{4,2},{6,4},{8,6},{10,8},{12,10},{14,12},{16,14},{18,16},{20... | collective-permute-start | bytes 1277960 | tf_op jit(solution)/shard_map/ppermute | solution.py:699
  18.8 15.6 %copy-start.1 = (bf16[128,512]{1,0:T(8,128)(2,1)}, bf16[128,512]{1,0:T(8,128)(2,1)S(1)}, u32[]{:S(2)}) copy-start(bf16[128,512]{1,0:T(8,128)(2,1)S(1)} %collective-permute-done.1.query_next4_ref) | copy-start | bytes 393220
  18.8 4.1 %collective-permute-start.4 = (bf16[128,512]{1,0:T(8,128)(2,1)S(1)}, bf16[128,512]{1,0:T(8,128)(2,1)S(1)}, u32[]{:S(2)}, u32[]{:S(2)}) collective-permute-start(bf16[128,512]{1,0:T(8,128)(2,1)S(1)} %collective-permute-done.1.query_next4_ref), channel_id=1, source_target_pairs={{0,2},{2,0},{4,6},{6,4},{8,10},{10,8},{12,14},{14,12},{16,18},{18,... | collective-permute-start | bytes 393224 | tf_op jit(solution)/shard_map/ppermute | solution.py:699
  21.3 13.1 %copy-start.2 = (bf16[128,512]{1,0:T(8,128)(2,1)}, bf16[128,512]{1,0:T(8,128)(2,1)S(1)}, u32[]{:S(2)}) copy-start(bf16[128,512]{1,0:T(8,128)(2,1)S(1)} %collective-permute-done.query_next2_ref) | copy-start | bytes 393220
  21.3 5.5 %collective-permute-start.8 = (bf16[176,1024]{1,0:T(8,128)(2,1)}, bf16[176,1024]{1,0:T(8,128)(2,1)S(1)}, u32[]{:S(2)}, u32[]{:S(2)}) collective-permute-start(bf16[176,1024]{1,0:T(8,128)(2,1)} %get-tuple-element.50), channel_id=1, source_target_pairs={{0,2},{2,0},{4,6},{6,4},{8,10},{10,8},{12,14},{14,12},{16,18},{18,... | collective-permute-start | bytes 1081352 | tf_op jit(solution)/shard_map/ppermute | solution.py:699
  22.7 4.1 %copy-start.6 = (bf16[176,1024]{1,0:T(8,128)(2,1)}, bf16[176,1024]{1,0:T(8,128)(2,1)S(1)}, u32[]{:S(2)}) copy-start(bf16[176,1024]{1,0:T(8,128)(2,1)S(1)} %collective-permute-done.6.back2_ref) | copy-start | bytes 1081348
  22.8 4.1 %collective-permute-start.9 = (bf16[176,1024]{1,0:T(8,128)(2,1)S(1)}, bf16[176,1024]{1,0:T(8,128)(2,1)S(1)}, u32[]{:S(2)}, u32[]{:S(2)}) collective-permute-start(bf16[176,1024]{1,0:T(8,128)(2,1)S(1)} %collective-permute-done.6.back2_ref), channel_id=1, source_target_pairs={{0,2},{2,0},{4,6},{6,4},{8,10},{10,8},{12,14},{14,12},{16,18},{18,... | collective-permute-start | bytes 1081352 | tf_op jit(solution)/shard_map/ppermute | solution.py:699
  22.8 11.6 %copy-start.3 = (bf16[128,512]{1,0:T(8,128)(2,1)}, bf16[128,512]{1,0:T(8,128)(2,1)S(1)}, u32[]{:S(2)}) copy-start(bf16[128,512]{1,0:T(8,128)(2,1)S(1)} %collective-permute-done.4.query_peer_next4_ref) | copy-start | bytes 393220
  22.8 1.9 %collective-permute-start.3 = (bf16[128,512]{1,0:T(8,128)(2,1)S(1)}, bf16[128,512]{1,0:T(8,128)(2,1)S(1)}, u32[]{:S(2)}, u32[]{:S(2)}) collective-permute-start(bf16[128,512]{1,0:T(8,128)(2,1)S(1)} %collective-permute-done.query_next2_ref), channel_id=1, source_target_pairs={{0,2},{2,0},{4,6},{6,4},{8,10},{10,8},{12,14},{14,12},{16,18},{18,... | collective-permute-start | bytes 393224 | tf_op jit(solution)/shard_map/ppermute | solution.py:699
  23.3 3.6 %copy-start.9 = (bf16[128,1024]{1,0:T(8,128)(2,1)}, bf16[128,1024]{1,0:T(8,128)(2,1)S(1)}, u32[]{:S(2)}) copy-start(bf16[128,1024]{1,0:T(8,128)(2,1)S(1)} %collective-permute-done.7.back4_ref) | copy-start | bytes 786436
  23.3 3.5 %collective-permute-start.10 = (bf16[128,1024]{1,0:T(8,128)(2,1)S(1)}, bf16[128,1024]{1,0:T(8,128)(2,1)S(1)}, u32[]{:S(2)}, u32[]{:S(2)}) collective-permute-start(bf16[128,1024]{1,0:T(8,128)(2,1)S(1)} %collective-permute-done.7.back4_ref), channel_id=1, source_target_pairs={{0,2},{2,0},{4,6},{6,4},{8,10},{10,8},{12,14},{14,12},{16,18},{18,... | collective-permute-start | bytes 786440 | tf_op jit(solution)/shard_map/ppermute | solution.py:699
  24.8 9.7 %copy-start.4 = (bf16[128,512]{1,0:T(8,128)(2,1)}, bf16[128,512]{1,0:T(8,128)(2,1)S(1)}, u32[]{:S(2)}) copy-start(bf16[128,512]{1,0:T(8,128)(2,1)S(1)} %collective-permute-done.3.query_peer_next2_ref) | copy-start | bytes 393220
  24.8 9.7 %collective-permute-start.11 = (bf16[128,1024]{1,0:T(8,128)(2,1)}, bf16[128,1024]{1,0:T(8,128)(2,1)S(1)}, u32[]{:S(2)}, u32[]{:S(2)}) collective-permute-start(bf16[128,1024]{1,0:T(8,128)(2,1)} %get-tuple-element.54.kept_ref), channel_id=1, source_target_pairs={{2,12},{6,16},{10,20},{14,24},{18,28},{3,13},{7,17},{11,21},{15,25... | collective-permute-start | bytes 786440 | tf_op jit(solution)/shard_map/ppermute | solution.py:699
  26.8 0.8 copy-start.5
  26.8 0.9 copy-start.7
  26.8 1.0 copy-start.10
  27.8 0.7 copy-start.8
  34.4 0.7 copy-start.11
  45.3 8.2 %collective-permute-start.13 = (bf16[144,512]{1,0:T(8,128)(2,1)}, bf16[144,512]{1,0:T(8,128)(2,1)S(1)}, u32[]{:S(2)}, u32[]{:S(2)}) collective-permute-start(bf16[144,512]{1,0:T(8,128)(2,1)} %get-tuple-element.56.message_ref), channel_id=1, source_target_pairs={{9,1},{11,3},{13,5},{15,7},{17,9},{19,11},{21,13},{23,15},{25,17},... | collective-permute-start | bytes 442376 | tf_op jit(solution)/shard_map/ppermute | solution.py:699
  46.0 7.6 %collective-permute-start.12 = (bf16[144,512]{1,0:T(8,128)(2,1)}, bf16[144,512]{1,0:T(8,128)(2,1)S(1)}, u32[]{:S(2)}, u32[]{:S(2)}) collective-permute-start(bf16[144,512]{1,0:T(8,128)(2,1)} %get-tuple-element.56.message_ref), channel_id=1, source_target_pairs={{5,1},{7,3},{9,5},{11,7},{13,9},{15,11},{17,13},{19,15},{21,17},{2... | collective-permute-start | bytes 442376 | tf_op jit(solution)/shard_map/ppermute | solution.py:699
  46.9 7.3 %collective-permute-start.14 = (bf16[144,512]{1,0:T(8,128)(2,1)}, bf16[144,512]{1,0:T(8,128)(2,1)S(1)}, u32[]{:S(2)}, u32[]{:S(2)}) collective-permute-start(bf16[144,512]{1,0:T(8,128)(2,1)} %get-tuple-element.56.message_ref), channel_id=1, source_target_pairs={{0,2},{2,0},{4,6},{6,4},{8,10},{10,8},{12,14},{14,12},{16,18},{18,... | collective-permute-start | bytes 442376 | tf_op jit(solution)/shard_map/ppermute | solution.py:699
  53.6 1.7 %copy-start.15 = (bf16[144,512]{1,0:T(8,128)(2,1)}, bf16[144,512]{1,0:T(8,128)(2,1)S(1)}, u32[]{:S(2)}) copy-start(bf16[144,512]{1,0:T(8,128)(2,1)S(1)} %collective-permute-done.13.next4_ref) | copy-start | bytes 442372
  53.6 1.7 %copy-start.16 = (bf16[144,512]{1,0:T(8,128)(2,1)}, bf16[144,512]{1,0:T(8,128)(2,1)S(1)}, u32[]{:S(2)}) copy-start(bf16[144,512]{1,0:T(8,128)(2,1)S(1)} %collective-permute-done.12.next2_ref) | copy-start | bytes 442372
  53.6 1.4 %collective-permute-start.15 = (bf16[144,512]{1,0:T(8,128)(2,1)S(1)}, bf16[144,512]{1,0:T(8,128)(2,1)S(1)}, u32[]{:S(2)}, u32[]{:S(2)}) collective-permute-start(bf16[144,512]{1,0:T(8,128)(2,1)S(1)} %collective-permute-done.12.next2_ref), channel_id=1, source_target_pairs={{0,2},{2,0},{4,6},{6,4},{8,10},{10,8},{12,14},{14,12},{16,18},{18,... | collective-permute-start | bytes 442376 | tf_op jit(solution)/shard_map/ppermute | solution.py:699
  53.9 1.4 %collective-permute-start.16 = (bf16[144,512]{1,0:T(8,128)(2,1)S(1)}, bf16[144,512]{1,0:T(8,128)(2,1)S(1)}, u32[]{:S(2)}, u32[]{:S(2)}) collective-permute-start(bf16[144,512]{1,0:T(8,128)(2,1)S(1)} %collective-permute-done.13.next4_ref), channel_id=1, source_target_pairs={{0,2},{2,0},{4,6},{6,4},{8,10},{10,8},{12,14},{14,12},{16,18},{18,... | collective-permute-start | bytes 442376 | tf_op jit(solution)/shard_map/ppermute | solution.py:699
  54.2 1.1 %copy-start.17 = (bf16[144,512]{1,0:T(8,128)(2,1)}, bf16[144,512]{1,0:T(8,128)(2,1)S(1)}, u32[]{:S(2)}) copy-start(bf16[144,512]{1,0:T(8,128)(2,1)S(1)} %collective-permute-done.14.peer_ref) | copy-start | bytes 442372
  55.0 0.7 copy-start.20
  55.2 0.7 copy-start.21
  62.0 14.9 %collective-permute-start.17 = (bf16[128,1024]{1,0:T(8,128)(2,1)}, bf16[128,1024]{1,0:T(8,128)(2,1)S(1)}, u32[]{:S(2)}, u32[]{:S(2)}) collective-permute-start(bf16[128,1024]{1,0:T(8,128)(2,1)} %get-tuple-element.65), channel_id=1, source_target_pairs={{1,0},{3,2},{5,4},{7,6},{9,8},{11,10},{13,12},{15,14},{17,16},{19,... | collective-permute-start | bytes 786440 | tf_op jit(solution)/shard_map/ppermute | solution.py:699
  69.2 7.7 %collective-permute-start.18 = (bf16[32,1024]{1,0:T(8,128)(2,1)}, bf16[32,1024]{1,0:T(8,128)(2,1)S(1)}, u32[]{:S(2)}, u32[]{:S(2)}) collective-permute-start(bf16[32,1024]{1,0:T(8,128)(2,1)} %get-tuple-element.66), channel_id=1, source_target_pairs={{3,0},{5,2},{7,4},{9,6},{11,8},{13,10},{15,12},{17,14},{19,16},{21... | collective-permute-start | bytes 196616 | tf_op jit(solution)/shard_map/ppermute | solution.py:699
  76.9 0.6 copy-start.24
  76.9 0.8 copy-start.23
  83.2 12.2 %collective-permute-start.20 = (bf16[144,512]{1,0:T(8,128)(2,1)}, bf16[144,512]{1,0:T(8,128)(2,1)S(1)}, u32[]{:S(2)}, u32[]{:S(2)}) collective-permute-start(bf16[144,512]{1,0:T(8,128)(2,1)} %get-tuple-element.68.message_ref), channel_id=1, source_target_pairs={{8,0},{10,2},{12,4},{14,6},{16,8},{18,10},{20,12},{22,14},{24,16},... | collective-permute-start | bytes 442376 | tf_op jit(solution)/shard_map/ppermute | solution.py:699
  85.3 10.1 %collective-permute-start.19 = (bf16[144,512]{1,0:T(8,128)(2,1)}, bf16[144,512]{1,0:T(8,128)(2,1)S(1)}, u32[]{:S(2)}, u32[]{:S(2)}) collective-permute-start(bf16[144,512]{1,0:T(8,128)(2,1)} %get-tuple-element.68.message_ref), channel_id=1, source_target_pairs={{4,0},{6,2},{8,4},{10,6},{12,8},{14,10},{16,12},{18,14},{20,16},{2... | collective-permute-start | bytes 442376 | tf_op jit(solution)/shard_map/ppermute | solution.py:699
  87.2 8.8 %collective-permute-start.21 = (bf16[144,512]{1,0:T(8,128)(2,1)}, bf16[144,512]{1,0:T(8,128)(2,1)S(1)}, u32[]{:S(2)}, u32[]{:S(2)}) collective-permute-start(bf16[144,512]{1,0:T(8,128)(2,1)} %get-tuple-element.68.message_ref), channel_id=1, source_target_pairs={{0,2},{2,0},{4,6},{6,4},{8,10},{10,8},{12,14},{14,12},{16,18},{18,... | collective-permute-start | bytes 442376 | tf_op jit(solution)/shard_map/ppermute | solution.py:699
  95.3 1.7 %copy-start.12 = (bf16[144,512]{1,0:T(8,128)(2,1)}, bf16[144,512]{1,0:T(8,128)(2,1)S(1)}, u32[]{:S(2)}) copy-start(bf16[144,512]{1,0:T(8,128)(2,1)S(1)} %collective-permute-done.20.next4_ref) | copy-start | bytes 442372
  95.4 1.7 %copy-start.13 = (bf16[144,512]{1,0:T(8,128)(2,1)}, bf16[144,512]{1,0:T(8,128)(2,1)S(1)}, u32[]{:S(2)}) copy-start(bf16[144,512]{1,0:T(8,128)(2,1)S(1)} %collective-permute-done.19.next2_ref) | copy-start | bytes 442372
  95.4 1.4 %collective-permute-start.22 = (bf16[144,512]{1,0:T(8,128)(2,1)S(1)}, bf16[144,512]{1,0:T(8,128)(2,1)S(1)}, u32[]{:S(2)}, u32[]{:S(2)}) collective-permute-start(bf16[144,512]{1,0:T(8,128)(2,1)S(1)} %collective-permute-done.19.next2_ref), channel_id=1, source_target_pairs={{0,2},{2,0},{4,6},{6,4},{8,10},{10,8},{12,14},{14,12},{16,18},{18,... | collective-permute-start | bytes 442376 | tf_op jit(solution)/shard_map/ppermute | solution.py:699
  95.5 1.6 %collective-permute-start.23 = (bf16[144,512]{1,0:T(8,128)(2,1)S(1)}, bf16[144,512]{1,0:T(8,128)(2,1)S(1)}, u32[]{:S(2)}, u32[]{:S(2)}) collective-permute-start(bf16[144,512]{1,0:T(8,128)(2,1)S(1)} %collective-permute-done.20.next4_ref), channel_id=1, source_target_pairs={{0,2},{2,0},{4,6},{6,4},{8,10},{10,8},{12,14},{14,12},{16,18},{18,... | collective-permute-start | bytes 442376 | tf_op jit(solution)/shard_map/ppermute | solution.py:699
  96.0 1.1 %copy-start.14 = (bf16[144,512]{1,0:T(8,128)(2,1)}, bf16[144,512]{1,0:T(8,128)(2,1)S(1)}, u32[]{:S(2)}) copy-start(bf16[144,512]{1,0:T(8,128)(2,1)S(1)} %collective-permute-done.21.peer_ref) | copy-start | bytes 442372
  96.8 0.7 copy-start.18
  97.0 0.7 copy-start.19

commit v4 on v3

--- a/solution.py
+++ b/solution.py
@@ -15,7 +15,8 @@
 EPSILON = 1e-05
 F32 = jnp.float32
 BF16 = jnp.bfloat16
-VMEM_LIMIT = 56 * 1024 * 1024
+VMEM_LIMIT = 20 << 20
+VMEM_WHOLE = 56 << 20
 
 
 def dot_nn(a, b):
@@ -654,7 +655,7 @@
     held_ref[...] = jnp.where(mine, grad, result[...].astype(F32)).astype(BF16)
 
 
-def call(kernel, name, operands, outs, scratch, copies, flops):
+def call(kernel, name, operands, outs, scratch, copies, flops, limit=VMEM_LIMIT):
     kinds = {
         "s": pl.BlockSpec(memory_space=pltpu.SMEM),
         "v": pl.BlockSpec(memory_space=pltpu.VMEM),
@@ -668,7 +669,7 @@
         out_shape=[jax.ShapeDtypeStruct(shape, dtype) for shape, dtype in outs],
         scratch_shapes=[pltpu.VMEM(shape, dtype) for shape, dtype in scratch]
         + [pltpu.SemaphoreType.DMA((copies,))],
-        compiler_params=pltpu.CompilerParams(vmem_limit_bytes=VMEM_LIMIT),
+        compiler_params=pltpu.CompilerParams(vmem_limit_bytes=limit),
         cost_estimate=pl.CostEstimate(flops=flops, bytes_accessed=4 << 20, transcendentals=0),
     )(*[array for array, _ in operands])
 
@@ -725,6 +726,7 @@
         [((ROWS, width), BF16), weight, weight, weight],
         3,
         1 << 30,
+        VMEM_WHOLE,
     )
     back2 = moved(ahead, across(2, every))
     back4 = moved(kept, across(4, every))

time: 106 us -> 93.3 us (0.88); the launches traced: 104 us -> 92.9 us
  Pallas kernels: 50.6 us -> 41 us
  local copies, waits for them, and re-layouts: 5.2 us -> 0.98 us
  starting transfers between devices: 35.2 us -> 37.3 us
    pallas_call x8, Pallas kernels: 50.6 us -> 41 us  [call(): pl.pallas_call(kernel, name=name, in_specs=[kinds[place] for _, place in...]
    unnamed x51 -> x23, local copies, waits for them, and re-layouts: 5.2 us -> 0.98 us
    ppermute x24, starting transfers between devices: 35.2 us -> 37.3 us  [moved(): return lax.ppermute(value, ('tm', 'section'), pairs)]
  transfers between devices with their start and end apart: 24 -> 24, of which waited for: 8 -> 8; matrix products, arithmetic and copies ran while one was open for 1% -> 0% of each run, Pallas kernels for 18% -> 14%
where the time goes in v4:
time: 93.3 us; the launch traced here: 92.9 us
  Pallas kernels  41 us (44%)
  starting transfers between devices  37.3 us (40%)
  waiting for transfers between devices  13.2 us (14%)
  local copies, waits for them, and re-layouts  0.98 us (1%)
    pallas_call x8, Pallas kernels, call(): pl.pallas_call(kernel, name=name, in_specs=[kinds[place] for _, place in...  41 us
    ppermute x24, starting transfers between devices, moved(): return lax.ppermute(value, ('tm', 'section'), pairs)  37.3 us
    ppermute x24, waiting for transfers between devices, moved(): return lax.ppermute(value, ('tm', 'section'), pairs)  13.2 us
  transfers between devices with their start and end apart: 24, of which 8 were waited for; matrix products, arithmetic and copies ran while one was open for 0% of the time, Pallas kernels for 14%

profile of v4, /device:TPU:19, one launch (start us, length us, event | category | flops | bytes accessed | tf_op | source)
XLA Modules:
  0.0 92.9 jit_solution(12163415683492365669)
XLA Ops:
  0.0 4.3 %project.1 = (bf16[128,512]{1,0:T(8,128)(2,1)}, bf16[128,1024]{1,0:T(8,128)(2,1)}, bf16[176,1024]{1,0:T(8,128)(2,1)}, bf16[208,1024]{1,0:T(8,128)(2,1)}) custom-call(bf16[128,1024]{1,0:T(8,128)(2,1)} %bitcast.9, bf16[128,1024]{1,0:T(8,128)(2,1)} %top_ref.3, f32[1,1024]{1,0:T(1,128)} %gain_ref.5, bf16[1024,512]{1,0:T(8,128)(2,1)} %bitcast.24, ...), custom_call_target="tpu_custom_call" | custom-call | flops 1073741824 | bytes 4194304 | tf_op jit(solution)/shard_map/project/pallas_call | solution.py:664
  4.3 0.0 copy-start.4
  4.3 3.3 %collective-permute-start.6 = (bf16[176,1024]{1,0:T(8,128)(2,1)}, bf16[176,1024]{1,0:T(8,128)(2,1)S(1)}, u32[]{:S(2)}, u32[]{:S(2)}) collective-permute-start(bf16[176,1024]{1,0:T(8,128)(2,1)} %get-tuple-element.50), channel_id=1, source_target_pairs={{0,4},{2,6},{4,8},{6,10},{8,12},{10,14},{12,16},{14,18},{16,20},{1... | collective-permute-start | bytes 1081352 | tf_op jit(solution)/shard_map/ppermute | solution.py:700
  7.6 1.0 %collective-permute-start.2 = (bf16[128,512]{1,0:T(8,128)(2,1)}, bf16[128,512]{1,0:T(8,128)(2,1)S(1)}, u32[]{:S(2)}, u32[]{:S(2)}) collective-permute-start(bf16[128,512]{1,0:T(8,128)(2,1)} %get-tuple-element.43.queries_ref), channel_id=1, source_target_pairs={{0,2},{2,0},{4,6},{6,4},{8,10},{10,8},{12,14},{14,12},{16,18},{18,... | collective-permute-start | bytes 393224 | tf_op jit(solution)/shard_map/ppermute | solution.py:700
  8.7 2.1 %collective-permute-start.1 = (bf16[128,512]{1,0:T(8,128)(2,1)}, bf16[128,512]{1,0:T(8,128)(2,1)S(1)}, u32[]{:S(2)}, u32[]{:S(2)}) collective-permute-start(bf16[128,512]{1,0:T(8,128)(2,1)} %get-tuple-element.43.queries_ref), channel_id=1, source_target_pairs={{8,0},{10,2},{12,4},{14,6},{16,8},{18,10},{20,12},{22,14},{24,16},... | collective-permute-start | bytes 393224 | tf_op jit(solution)/shard_map/ppermute | solution.py:700
  10.7 3.2 %collective-permute-start.7 = (bf16[128,1024]{1,0:T(8,128)(2,1)}, bf16[128,1024]{1,0:T(8,128)(2,1)S(1)}, u32[]{:S(2)}, u32[]{:S(2)}) collective-permute-start(bf16[128,1024]{1,0:T(8,128)(2,1)} %get-tuple-element.54.kept_ref), channel_id=1, source_target_pairs={{0,8},{2,10},{4,12},{6,14},{8,16},{10,18},{12,20},{14,22},{16,24},... | collective-permute-start | bytes 786440 | tf_op jit(solution)/shard_map/ppermute | solution.py:700
  13.9 2.1 %collective-permute-start = (bf16[128,512]{1,0:T(8,128)(2,1)}, bf16[128,512]{1,0:T(8,128)(2,1)S(1)}, u32[]{:S(2)}, u32[]{:S(2)}) collective-permute-start(bf16[128,512]{1,0:T(8,128)(2,1)} %get-tuple-element.43.queries_ref), channel_id=1, source_target_pairs={{4,0},{6,2},{8,4},{10,6},{12,8},{14,10},{16,12},{18,14},{20,16},{2... | collective-permute-start | bytes 393224 | tf_op jit(solution)/shard_map/ppermute | solution.py:700
  16.1 0.0 collective-permute-done.2.query_peer_ref
  16.1 0.0 copy-start.7
  16.1 2.8 %collective-permute-start.5 = (bf16[208,1024]{1,0:T(8,128)(2,1)}, bf16[208,1024]{1,0:T(8,128)(2,1)S(1)}, u32[]{:S(2)}, u32[]{:S(2)}) collective-permute-start(bf16[208,1024]{1,0:T(8,128)(2,1)} %get-tuple-element.44), channel_id=1, source_target_pairs={{2,0},{4,2},{6,4},{8,6},{10,8},{12,10},{14,12},{16,14},{18,16},{20... | collective-permute-start | bytes 1277960 | tf_op jit(solution)/shard_map/ppermute | solution.py:700
  18.9 0.0 collective-permute-done.1.query_next4_ref
  18.9 0.7 collective-permute-start.4
  19.6 1.8 %collective-permute-done.query_next2_ref = bf16[128,512]{1,0:T(8,128)(2,1)S(1)} collective-permute-done((bf16[128,512]{1,0:T(8,128)(2,1)}, bf16[128,512]{1,0:T(8,128)(2,1)S(1)}, u32[]{:S(2)}, u32[]{:S(2)}) %collective-permute-start) | collective-permute-done | bytes 131104 | tf_op jit(solution)/shard_map/ppermute | solution.py:700
  21.4 1.4 %collective-permute-start.8 = (bf16[176,1024]{1,0:T(8,128)(2,1)}, bf16[176,1024]{1,0:T(8,128)(2,1)S(1)}, u32[]{:S(2)}, u32[]{:S(2)}) collective-permute-start(bf16[176,1024]{1,0:T(8,128)(2,1)} %get-tuple-element.50), channel_id=1, source_target_pairs={{0,2},{2,0},{4,6},{6,4},{8,10},{10,8},{12,14},{14,12},{16,18},{18,... | collective-permute-start | bytes 1081352 | tf_op jit(solution)/shard_map/ppermute | solution.py:700
  22.9 0.0 collective-permute-done.6.back2_ref
  22.9 0.0 collective-permute-start.9
  22.9 0.0 collective-permute-done.4.query_peer_next4_ref
  22.9 0.5 collective-permute-start.3
  23.4 0.0 collective-permute-done.7.back4_ref
  23.4 0.1 collective-permute-start.10
  23.5 1.4 %collective-permute-done.3.query_peer_next2_ref = bf16[128,512]{1,0:T(8,128)(2,1)S(1)} collective-permute-done((bf16[128,512]{1,0:T(8,128)(2,1)S(1)}, bf16[128,512]{1,0:T(8,128)(2,1)S(1)}, u32[]{:S(2)}, u32[]{:S(2)}) %collective-permute-start.3) | collective-permute-done | bytes 131104 | tf_op jit(solution)/shard_map/ppermute | solution.py:700
  24.9 0.7 collective-permute-start.11
  25.6 0.0 copy-start
  25.6 0.0 copy-start.3
  25.6 0.0 copy-start.5
  25.6 1.3 %collective-permute-done.5.after_ref = bf16[208,1024]{1,0:T(8,128)(2,1)S(1)} collective-permute-done((bf16[208,1024]{1,0:T(8,128)(2,1)}, bf16[208,1024]{1,0:T(8,128)(2,1)S(1)}, u32[]{:S(2)}, u32[]{:S(2)}) %collective-permute-start.5) | collective-permute-done | bytes 426016 | tf_op jit(solution)/shard_map/ppermute | solution.py:700
  26.9 0.0 collective-permute-done.8.peer_ref
  26.9 0.0 collective-permute-done.10.peer_back4_ref
  26.9 0.0 collective-permute-done.9.peer_back2_ref
  27.0 0.9 copy-done.9
  27.9 3.9 %attend.1 = (bf16[160,512]{1,0:T(8,128)(2,1)S(1)}, f32[128,128]{1,0:T(8,128)S(1)}) custom-call(s32[16]{0:T(128)S(1)} %copy-done.7, bf16[128,512]{1,0:T(8,128)(2,1)S(1)} %copy-done.9, bf16[128,1024]{1,0:T(8,128)(2,1)S(1)} %copy-done.4, bf16[176,1024]{1,0:T(8,128)(2,1)S(1)} %collective-permute-done.6.back2_ref, ...), custom_call_target="tpu_custom_call" | custom-call | flops 1073741824 | bytes 4194304 | tf_op jit(solution)/shard_map/attend/pallas_call | solution.py:664
  31.8 0.0 collective-permute-done.11.back5_ref
  31.8 0.0 copy-start.8
  31.9 8.6 %mix.1 = (f32[160,1024]{1,0:T(8,128)S(1)}, f32[128,1024]{1,0:T(8,128)S(1)}, bf16[144,512]{1,0:T(8,128)(2,1)S(1)}, f32[128,128]{1,0:T(8,128)S(1)}) custom-call(s32[16]{0:T(128)S(1)} %copy-done.7, bf16[128,1024]{1,0:T(8,128)(2,1)S(1)} %bitcast.10, bf16[128,1024]{1,0:T(8,128)(2,1)S(1)} %copy-done.5, bf16[160,512]{1,0:T(8,128)(2,1)S(1)} %get-tuple-element.52.attended_ref, ...), custom_call_target="tpu_custom_call" | custom-call | flops 1073741824 | bytes 4194304 | tf_op jit(solution)/shard_map/mix/pallas_call | solution.py:664
  40.5 0.7 collective-permute-start.13
  41.1 0.7 collective-permute-start.12
  41.8 2.3 %collective-permute-start.14 = (bf16[144,512]{1,0:T(8,128)(2,1)S(1)}, bf16[144,512]{1,0:T(8,128)(2,1)S(1)}, u32[]{:S(2)}, u32[]{:S(2)}) collective-permute-start(bf16[144,512]{1,0:T(8,128)(2,1)S(1)} %get-tuple-element.56.message_ref), channel_id=1, source_target_pairs={{0,2},{2,0},{4,6},{6,4},{8,10},{10,8},{12,14},{14,12},{16,18},{18,... | collective-permute-start | bytes 442376 | tf_op jit(solution)/shard_map/ppermute | solution.py:700
  44.1 4.3 %own_queries.2 = (f32[128,1024]{1,0:T(8,128)S(1)}, f32[128,512]{1,0:T(8,128)S(1)}, f32[128,512]{1,0:T(8,128)S(1)}) custom-call(s32[16]{0:T(128)S(1)} %copy-done.7, bf16[128,512]{1,0:T(8,128)(2,1)S(1)} %copy-done.9, bf16[128,1024]{1,0:T(8,128)(2,1)S(1)} %copy-done.4, bf16[176,1024]{1,0:T(8,128)(2,1)S(1)} %collective-permute-done.6.back2_ref, ...), custom_call_target="tpu_custom_call" | custom-call | flops 1073741824 | bytes 4194304 | tf_op jit(solution)/shard_map/own_queries/pallas_call | solution.py:664
  48.4 0.0 copy-start.6
  48.4 0.0 collective-permute-done.13.next4_ref
  48.4 0.0 collective-permute-done.12.next2_ref
  48.4 0.1 collective-permute-start.15
  48.6 0.5 collective-permute-start.16
  49.0 0.0 collective-permute-done.14.peer_ref
  49.0 0.9 collective-permute-done.15.peer_next2_ref
  49.9 0.2 collective-permute-done.16.peer_next4_ref
  50.1 5.6 %own_keys.2 = (bf16[128,1024]{1,0:T(8,128)(2,1)S(1)}, bf16[32,1024]{1,0:T(8,128)(2,1)S(1)}, bf16[128,1024]{1,0:T(8,128)(2,1)S(1)}) custom-call(s32[16]{0:T(128)S(1)} %copy-done.7, bf16[128,1024]{1,0:T(8,128)(2,1)S(1)} %copy-done.4, bf16[128,512]{1,0:T(8,128)(2,1)S(1)} %collective-permute-done.query_next2_ref, ...), custom_call_target="tpu_custom_call" | custom-call | flops 1073741824 | bytes 4194304 | tf_op jit(solution)/shard_map/own_keys/pallas_call | solution.py:664
  55.7 6.3 %collective-permute-start.17 = (bf16[128,1024]{1,0:T(8,128)(2,1)S(1)}, bf16[128,1024]{1,0:T(8,128)(2,1)S(1)}, u32[]{:S(2)}, u32[]{:S(2)}) collective-permute-start(bf16[128,1024]{1,0:T(8,128)(2,1)S(1)} %get-tuple-element.65), channel_id=1, source_target_pairs={{1,0},{3,2},{5,4},{7,6},{9,8},{11,10},{13,12},{15,14},{17,16},{19,... | collective-permute-start | bytes 786440 | tf_op jit(solution)/shard_map/ppermute | solution.py:700
  62.1 1.3 %collective-permute-start.18 = (bf16[32,1024]{1,0:T(8,128)(2,1)S(1)}, bf16[32,1024]{1,0:T(8,128)(2,1)S(1)}, u32[]{:S(2)}, u32[]{:S(2)}) collective-permute-start(bf16[32,1024]{1,0:T(8,128)(2,1)S(1)} %get-tuple-element.66), channel_id=1, source_target_pairs={{3,0},{5,2},{7,4},{9,6},{11,8},{13,10},{15,12},{17,14},{19,16},{21... | collective-permute-start | bytes 196616 | tf_op jit(solution)/shard_map/ppermute | solution.py:700
  63.3 6.2 %collective-permute-done.18.next_ref = bf16[32,1024]{1,0:T(8,128)(2,1)S(1)} collective-permute-done((bf16[32,1024]{1,0:T(8,128)(2,1)S(1)}, bf16[32,1024]{1,0:T(8,128)(2,1)S(1)}, u32[]{:S(2)}, u32[]{:S(2)}) %collective-permute-start.18) | collective-permute-done | bytes 65568 | tf_op jit(solution)/shard_map/ppermute | solution.py:700
  69.5 0.0 collective-permute-done.17.upstream_ref
  69.5 3.7 %mixer.1 = (f32[128,1024]{1,0:T(8,128)S(1)}, bf16[144,512]{1,0:T(8,128)(2,1)S(1)}, f32[128,128]{1,0:T(8,128)S(1)}) custom-call(s32[16]{0:T(128)S(1)} %copy-done.7, bf16[128,1024]{1,0:T(8,128)(2,1)S(1)} %collective-permute-done.17.upstream_ref, bf16[32,1024]{1,0:T(8,128)(2,1)S(1)} %collective-permute-done.18.next_ref, ...), custom_call_target="tpu_custom_call" | custom-call | flops 1073741824 | bytes 4194304 | tf_op jit(solution)/shard_map/mixer/pallas_call | solution.py:664
  73.3 2.5 %collective-permute-start.20 = (bf16[144,512]{1,0:T(8,128)(2,1)S(1)}, bf16[144,512]{1,0:T(8,128)(2,1)S(1)}, u32[]{:S(2)}, u32[]{:S(2)}) collective-permute-start(bf16[144,512]{1,0:T(8,128)(2,1)S(1)} %get-tuple-element.68.message_ref), channel_id=1, source_target_pairs={{8,0},{10,2},{12,4},{14,6},{16,8},{18,10},{20,12},{22,14},{24,16},... | collective-permute-start | bytes 442376 | tf_op jit(solution)/shard_map/ppermute | solution.py:700
  75.8 1.9 %collective-permute-start.19 = (bf16[144,512]{1,0:T(8,128)(2,1)S(1)}, bf16[144,512]{1,0:T(8,128)(2,1)S(1)}, u32[]{:S(2)}, u32[]{:S(2)}) collective-permute-start(bf16[144,512]{1,0:T(8,128)(2,1)S(1)} %get-tuple-element.68.message_ref), channel_id=1, source_target_pairs={{4,0},{6,2},{8,4},{10,6},{12,8},{14,10},{16,12},{18,14},{20,16},{2... | collective-permute-start | bytes 442376 | tf_op jit(solution)/shard_map/ppermute | solution.py:700
  77.7 1.5 %collective-permute-start.21 = (bf16[144,512]{1,0:T(8,128)(2,1)S(1)}, bf16[144,512]{1,0:T(8,128)(2,1)S(1)}, u32[]{:S(2)}, u32[]{:S(2)}) collective-permute-start(bf16[144,512]{1,0:T(8,128)(2,1)S(1)} %get-tuple-element.68.message_ref), channel_id=1, source_target_pairs={{0,2},{2,0},{4,6},{6,4},{8,10},{10,8},{12,14},{14,12},{16,18},{18,... | collective-permute-start | bytes 442376 | tf_op jit(solution)/shard_map/ppermute | solution.py:700
  79.2 4.3 %own_queries.3 = (f32[128,1024]{1,0:T(8,128)S(1)}, f32[128,512]{1,0:T(8,128)S(1)}, f32[128,512]{1,0:T(8,128)S(1)}) custom-call(s32[16]{0:T(128)S(1)} %copy-done.7, bf16[128,512]{1,0:T(8,128)(2,1)S(1)} %copy-done.9, bf16[128,1024]{1,0:T(8,128)(2,1)S(1)} %copy-done.4, bf16[176,1024]{1,0:T(8,128)(2,1)S(1)} %collective-permute-done.6.back2_ref, ...), custom_call_target="tpu_custom_call" | custom-call | flops 1073741824 | bytes 4194304 | tf_op jit(solution)/shard_map/own_queries/pallas_call | solution.py:664
  83.6 0.0 collective-permute-done.20.next4_ref
  83.6 0.0 collective-permute-done.19.next2_ref
  83.6 1.6 %collective-permute-start.22 = (bf16[144,512]{1,0:T(8,128)(2,1)S(1)}, bf16[144,512]{1,0:T(8,128)(2,1)S(1)}, u32[]{:S(2)}, u32[]{:S(2)}) collective-permute-start(bf16[144,512]{1,0:T(8,128)(2,1)S(1)} %collective-permute-done.19.next2_ref), channel_id=1, source_target_pairs={{0,2},{2,0},{4,6},{6,4},{8,10},{10,8},{12,14},{14,12},{16,18},{18,... | collective-permute-start | bytes 442376 | tf_op jit(solution)/shard_map/ppermute | solution.py:700
  85.2 0.0 collective-permute-start.23
  85.2 0.0 collective-permute-done.21.peer_ref
  85.2 1.0 %collective-permute-done.22.peer_next2_ref = bf16[144,512]{1,0:T(8,128)(2,1)S(1)} collective-permute-done((bf16[144,512]{1,0:T(8,128)(2,1)S(1)}, bf16[144,512]{1,0:T(8,128)(2,1)S(1)}, u32[]{:S(2)}, u32[]{:S(2)}) %collective-permute-start.22) | collective-permute-done | bytes 147488 | tf_op jit(solution)/shard_map/ppermute | solution.py:700
  86.2 0.4 collective-permute-done.23.peer_next4_ref
  86.6 6.2 %own_keys.3 = (bf16[128,1024]{1,0:T(8,128)(2,1)}, bf16[32,1024]{1,0:T(8,128)(2,1)}, bf16[128,1024]{1,0:T(8,128)(2,1)}) custom-call(s32[16]{0:T(128)S(1)} %copy-done.7, bf16[128,1024]{1,0:T(8,128)(2,1)S(1)} %copy-done.4, bf16[128,512]{1,0:T(8,128)(2,1)S(1)} %collective-permute-done.query_next2_ref, ...), custom_call_target="tpu_custom_call" | custom-call | flops 1073741824 | bytes 4194304 | tf_op jit(solution)/shard_map/own_keys/pallas_call | solution.py:664
  (15 shorter events, 0.1 us)
Async XLA Ops:
  0.0 25.5 %copy-start.10 = (f32[1,31,1024]{2,0,1:T(1,128)S(1)}, f32[1,31,1024]{2,0,1:T(1,128)}, u32[]{:S(2)}) copy-start(f32[1,31,1024]{2,0,1:T(1,128)} %param.15) | copy-start | bytes 380932
  4.3 22.6 %copy-start.4 = (bf16[128,1024]{1,0:T(8,128)(2,1)S(1)}, bf16[128,1024]{1,0:T(8,128)(2,1)}, u32[]{:S(2)}) copy-start(bf16[128,1024]{1,0:T(8,128)(2,1)} %get-tuple-element.54.kept_ref) | copy-start | bytes 786436
  4.3 18.5 %collective-permute-start.6 = (bf16[176,1024]{1,0:T(8,128)(2,1)}, bf16[176,1024]{1,0:T(8,128)(2,1)S(1)}, u32[]{:S(2)}, u32[]{:S(2)}) collective-permute-start(bf16[176,1024]{1,0:T(8,128)(2,1)} %get-tuple-element.50), channel_id=1, source_target_pairs={{0,4},{2,6},{4,8},{6,10},{8,12},{10,14},{12,16},{14,18},{16,20},{1... | collective-permute-start | bytes 1081352 | tf_op jit(solution)/shard_map/ppermute | solution.py:700
  7.6 8.4 %collective-permute-start.2 = (bf16[128,512]{1,0:T(8,128)(2,1)}, bf16[128,512]{1,0:T(8,128)(2,1)S(1)}, u32[]{:S(2)}, u32[]{:S(2)}) collective-permute-start(bf16[128,512]{1,0:T(8,128)(2,1)} %get-tuple-element.43.queries_ref), channel_id=1, source_target_pairs={{0,2},{2,0},{4,6},{6,4},{8,10},{10,8},{12,14},{14,12},{16,18},{18,... | collective-permute-start | bytes 393224 | tf_op jit(solution)/shard_map/ppermute | solution.py:700
  8.7 10.2 %collective-permute-start.1 = (bf16[128,512]{1,0:T(8,128)(2,1)}, bf16[128,512]{1,0:T(8,128)(2,1)S(1)}, u32[]{:S(2)}, u32[]{:S(2)}) collective-permute-start(bf16[128,512]{1,0:T(8,128)(2,1)} %get-tuple-element.43.queries_ref), channel_id=1, source_target_pairs={{8,0},{10,2},{12,4},{14,6},{16,8},{18,10},{20,12},{22,14},{24,16},... | collective-permute-start | bytes 393224 | tf_op jit(solution)/shard_map/ppermute | solution.py:700
  10.7 12.7 %collective-permute-start.7 = (bf16[128,1024]{1,0:T(8,128)(2,1)}, bf16[128,1024]{1,0:T(8,128)(2,1)S(1)}, u32[]{:S(2)}, u32[]{:S(2)}) collective-permute-start(bf16[128,1024]{1,0:T(8,128)(2,1)} %get-tuple-element.54.kept_ref), channel_id=1, source_target_pairs={{0,8},{2,10},{4,12},{6,14},{8,16},{10,18},{12,20},{14,22},{16,24},... | collective-permute-start | bytes 786440 | tf_op jit(solution)/shard_map/ppermute | solution.py:700
  13.9 7.5 %collective-permute-start = (bf16[128,512]{1,0:T(8,128)(2,1)}, bf16[128,512]{1,0:T(8,128)(2,1)S(1)}, u32[]{:S(2)}, u32[]{:S(2)}) collective-permute-start(bf16[128,512]{1,0:T(8,128)(2,1)} %get-tuple-element.43.queries_ref), channel_id=1, source_target_pairs={{4,0},{6,2},{8,4},{10,6},{12,8},{14,10},{16,12},{18,14},{20,16},{2... | collective-permute-start | bytes 393224 | tf_op jit(solution)/shard_map/ppermute | solution.py:700
  16.1 10.9 %copy-start.7 = (s32[16]{0:T(128)S(1)}, s32[16]{0:T(128)}, u32[]{:S(2)}) copy-start(s32[16]{0:T(128)} %valid_ref.13) | copy-start | bytes 196
  16.1 10.8 %collective-permute-start.5 = (bf16[208,1024]{1,0:T(8,128)(2,1)}, bf16[208,1024]{1,0:T(8,128)(2,1)S(1)}, u32[]{:S(2)}, u32[]{:S(2)}) collective-permute-start(bf16[208,1024]{1,0:T(8,128)(2,1)} %get-tuple-element.44), channel_id=1, source_target_pairs={{2,0},{4,2},{6,4},{8,6},{10,8},{12,10},{14,12},{16,14},{18,16},{20... | collective-permute-start | bytes 1277960 | tf_op jit(solution)/shard_map/ppermute | solution.py:700
  18.9 4.0 %collective-permute-start.4 = (bf16[128,512]{1,0:T(8,128)(2,1)S(1)}, bf16[128,512]{1,0:T(8,128)(2,1)S(1)}, u32[]{:S(2)}, u32[]{:S(2)}) collective-permute-start(bf16[128,512]{1,0:T(8,128)(2,1)S(1)} %collective-permute-done.1.query_next4_ref), channel_id=1, source_target_pairs={{0,2},{2,0},{4,6},{6,4},{8,10},{10,8},{12,14},{14,12},{16,18},{18,... | collective-permute-start | bytes 393224 | tf_op jit(solution)/shard_map/ppermute | solution.py:700
  21.4 5.5 %collective-permute-start.8 = (bf16[176,1024]{1,0:T(8,128)(2,1)}, bf16[176,1024]{1,0:T(8,128)(2,1)S(1)}, u32[]{:S(2)}, u32[]{:S(2)}) collective-permute-start(bf16[176,1024]{1,0:T(8,128)(2,1)} %get-tuple-element.50), channel_id=1, source_target_pairs={{0,2},{2,0},{4,6},{6,4},{8,10},{10,8},{12,14},{14,12},{16,18},{18,... | collective-permute-start | bytes 1081352 | tf_op jit(solution)/shard_map/ppermute | solution.py:700
  22.9 4.1 %collective-permute-start.9 = (bf16[176,1024]{1,0:T(8,128)(2,1)S(1)}, bf16[176,1024]{1,0:T(8,128)(2,1)S(1)}, u32[]{:S(2)}, u32[]{:S(2)}) collective-permute-start(bf16[176,1024]{1,0:T(8,128)(2,1)S(1)} %collective-permute-done.6.back2_ref), channel_id=1, source_target_pairs={{0,2},{2,0},{4,6},{6,4},{8,10},{10,8},{12,14},{14,12},{16,18},{18,... | collective-permute-start | bytes 1081352 | tf_op jit(solution)/shard_map/ppermute | solution.py:700
  22.9 2.0 %collective-permute-start.3 = (bf16[128,512]{1,0:T(8,128)(2,1)S(1)}, bf16[128,512]{1,0:T(8,128)(2,1)S(1)}, u32[]{:S(2)}, u32[]{:S(2)}) collective-permute-start(bf16[128,512]{1,0:T(8,128)(2,1)S(1)} %collective-permute-done.query_next2_ref), channel_id=1, source_target_pairs={{0,2},{2,0},{4,6},{6,4},{8,10},{10,8},{12,14},{14,12},{16,18},{18,... | collective-permute-start | bytes 393224 | tf_op jit(solution)/shard_map/ppermute | solution.py:700
  23.4 3.5 %collective-permute-start.10 = (bf16[128,1024]{1,0:T(8,128)(2,1)S(1)}, bf16[128,1024]{1,0:T(8,128)(2,1)S(1)}, u32[]{:S(2)}, u32[]{:S(2)}) collective-permute-start(bf16[128,1024]{1,0:T(8,128)(2,1)S(1)} %collective-permute-done.7.back4_ref), channel_id=1, source_target_pairs={{0,2},{2,0},{4,6},{6,4},{8,10},{10,8},{12,14},{14,12},{16,18},{18,... | collective-permute-start | bytes 786440 | tf_op jit(solution)/shard_map/ppermute | solution.py:700
  24.9 6.9 %collective-permute-start.11 = (bf16[128,1024]{1,0:T(8,128)(2,1)}, bf16[128,1024]{1,0:T(8,128)(2,1)S(1)}, u32[]{:S(2)}, u32[]{:S(2)}) collective-permute-start(bf16[128,1024]{1,0:T(8,128)(2,1)} %get-tuple-element.54.kept_ref), channel_id=1, source_target_pairs={{2,12},{6,16},{10,20},{14,24},{18,28},{3,13},{7,17},{11,21},{15,25... | collective-permute-start | bytes 786440 | tf_op jit(solution)/shard_map/ppermute | solution.py:700
  25.6 6.2 %copy-start = (bf16[1,128,1024]{2,1,0:T(8,128)(2,1)S(1)}, bf16[1,128,1024]{2,1,0:T(8,128)(2,1)}, u32[]{:S(2)}) copy-start(bf16[1,128,1024]{2,1,0:T(8,128)(2,1)} %param.9) | copy-start | bytes 786436
  25.6 6.2 %copy-start.3 = (bf16[1,512,1024]{2,1,0:T(8,128)(2,1)S(1)}, bf16[1,512,1024]{2,1,0:T(8,128)(2,1)}, u32[]{:S(2)}) copy-start(bf16[1,512,1024]{2,1,0:T(8,128)(2,1)} %param.14) | copy-start | bytes 3145732
  25.6 6.2 %copy-start.5 = (bf16[128,1024]{1,0:T(8,128)(2,1)S(1)}, bf16[128,1024]{1,0:T(8,128)(2,1)}, u32[]{:S(2)}) copy-start(bf16[128,1024]{1,0:T(8,128)(2,1)} %top_ref.3) | copy-start | bytes 786436
  27.0 0.9 copy-start.9
  31.8 12.2 %copy-start.8 = (bf16[1,1024,512]{2,1,0:T(8,128)(2,1)S(1)}, bf16[1,1024,512]{2,1,0:T(8,128)(2,1)}, u32[]{:S(2)}) copy-start(bf16[1,1024,512]{2,1,0:T(8,128)(2,1)} %param.11) | copy-start | bytes 3145732
  40.5 8.0 %collective-permute-start.13 = (bf16[144,512]{1,0:T(8,128)(2,1)S(1)}, bf16[144,512]{1,0:T(8,128)(2,1)S(1)}, u32[]{:S(2)}, u32[]{:S(2)}) collective-permute-start(bf16[144,512]{1,0:T(8,128)(2,1)S(1)} %get-tuple-element.56.message_ref), channel_id=1, source_target_pairs={{9,1},{11,3},{13,5},{15,7},{17,9},{19,11},{21,13},{23,15},{25,17},... | collective-permute-start | bytes 442376 | tf_op jit(solution)/shard_map/ppermute | solution.py:700
  41.1 7.3 %collective-permute-start.12 = (bf16[144,512]{1,0:T(8,128)(2,1)S(1)}, bf16[144,512]{1,0:T(8,128)(2,1)S(1)}, u32[]{:S(2)}, u32[]{:S(2)}) collective-permute-start(bf16[144,512]{1,0:T(8,128)(2,1)S(1)} %get-tuple-element.56.message_ref), channel_id=1, source_target_pairs={{5,1},{7,3},{9,5},{11,7},{13,9},{15,11},{17,13},{19,15},{21,17},{2... | collective-permute-start | bytes 442376 | tf_op jit(solution)/shard_map/ppermute | solution.py:700
  41.8 7.2 %collective-permute-start.14 = (bf16[144,512]{1,0:T(8,128)(2,1)S(1)}, bf16[144,512]{1,0:T(8,128)(2,1)S(1)}, u32[]{:S(2)}, u32[]{:S(2)}) collective-permute-start(bf16[144,512]{1,0:T(8,128)(2,1)S(1)} %get-tuple-element.56.message_ref), channel_id=1, source_target_pairs={{0,2},{2,0},{4,6},{6,4},{8,10},{10,8},{12,14},{14,12},{16,18},{18,... | collective-permute-start | bytes 442376 | tf_op jit(solution)/shard_map/ppermute | solution.py:700
  44.1 6.0 %copy-start.1 = (bf16[1,1024,512]{2,1,0:T(8,128)(2,1)S(1)}, bf16[1,1024,512]{2,1,0:T(8,128)(2,1)}, u32[]{:S(2)}) copy-start(bf16[1,1024,512]{2,1,0:T(8,128)(2,1)} %param.12) | copy-start | bytes 3145732
  44.1 6.0 %copy-start.2 = (bf16[1,1024,512]{2,1,0:T(8,128)(2,1)S(1)}, bf16[1,1024,512]{2,1,0:T(8,128)(2,1)}, u32[]{:S(2)}) copy-start(bf16[1,1024,512]{2,1,0:T(8,128)(2,1)} %param.13) | copy-start | bytes 3145732
  48.4 1.7 %copy-start.6 = (f32[1,1024]{1,0:T(1,128)S(1)}, f32[1,1024]{1,0:T(1,128)}, u32[]{:S(2)}) copy-start(f32[1,1024]{1,0:T(1,128)} %gain_ref.5) | copy-start | bytes 12292
  48.4 1.4 %collective-permute-start.15 = (bf16[144,512]{1,0:T(8,128)(2,1)S(1)}, bf16[144,512]{1,0:T(8,128)(2,1)S(1)}, u32[]{:S(2)}, u32[]{:S(2)}) collective-permute-start(bf16[144,512]{1,0:T(8,128)(2,1)S(1)} %collective-permute-done.12.next2_ref), channel_id=1, source_target_pairs={{0,2},{2,0},{4,6},{6,4},{8,10},{10,8},{12,14},{14,12},{16,18},{18,... | collective-permute-start | bytes 442376 | tf_op jit(solution)/shard_map/ppermute | solution.py:700
  48.6 1.5 %collective-permute-start.16 = (bf16[144,512]{1,0:T(8,128)(2,1)S(1)}, bf16[144,512]{1,0:T(8,128)(2,1)S(1)}, u32[]{:S(2)}, u32[]{:S(2)}) collective-permute-start(bf16[144,512]{1,0:T(8,128)(2,1)S(1)} %collective-permute-done.13.next4_ref), channel_id=1, source_target_pairs={{0,2},{2,0},{4,6},{6,4},{8,10},{10,8},{12,14},{14,12},{16,18},{18,... | collective-permute-start | bytes 442376 | tf_op jit(solution)/shard_map/ppermute | solution.py:700
  55.7 13.8 %collective-permute-start.17 = (bf16[128,1024]{1,0:T(8,128)(2,1)S(1)}, bf16[128,1024]{1,0:T(8,128)(2,1)S(1)}, u32[]{:S(2)}, u32[]{:S(2)}) collective-permute-start(bf16[128,1024]{1,0:T(8,128)(2,1)S(1)} %get-tuple-element.65), channel_id=1, source_target_pairs={{1,0},{3,2},{5,4},{7,6},{9,8},{11,10},{13,12},{15,14},{17,16},{19,... | collective-permute-start | bytes 786440 | tf_op jit(solution)/shard_map/ppermute | solution.py:700
  62.1 7.5 %collective-permute-start.18 = (bf16[32,1024]{1,0:T(8,128)(2,1)S(1)}, bf16[32,1024]{1,0:T(8,128)(2,1)S(1)}, u32[]{:S(2)}, u32[]{:S(2)}) collective-permute-start(bf16[32,1024]{1,0:T(8,128)(2,1)S(1)} %get-tuple-element.66), channel_id=1, source_target_pairs={{3,0},{5,2},{7,4},{9,6},{11,8},{13,10},{15,12},{17,14},{19,16},{21... | collective-permute-start | bytes 196616 | tf_op jit(solution)/shard_map/ppermute | solution.py:700
  73.3 10.3 %collective-permute-start.20 = (bf16[144,512]{1,0:T(8,128)(2,1)S(1)}, bf16[144,512]{1,0:T(8,128)(2,1)S(1)}, u32[]{:S(2)}, u32[]{:S(2)}) collective-permute-start(bf16[144,512]{1,0:T(8,128)(2,1)S(1)} %get-tuple-element.68.message_ref), channel_id=1, source_target_pairs={{8,0},{10,2},{12,4},{14,6},{16,8},{18,10},{20,12},{22,14},{24,16},... | collective-permute-start | bytes 442376 | tf_op jit(solution)/shard_map/ppermute | solution.py:700
  75.8 7.8 %collective-permute-start.19 = (bf16[144,512]{1,0:T(8,128)(2,1)S(1)}, bf16[144,512]{1,0:T(8,128)(2,1)S(1)}, u32[]{:S(2)}, u32[]{:S(2)}) collective-permute-start(bf16[144,512]{1,0:T(8,128)(2,1)S(1)} %get-tuple-element.68.message_ref), channel_id=1, source_target_pairs={{4,0},{6,2},{8,4},{10,6},{12,8},{14,10},{16,12},{18,14},{20,16},{2... | collective-permute-start | bytes 442376 | tf_op jit(solution)/shard_map/ppermute | solution.py:700
  77.7 7.5 %collective-permute-start.21 = (bf16[144,512]{1,0:T(8,128)(2,1)S(1)}, bf16[144,512]{1,0:T(8,128)(2,1)S(1)}, u32[]{:S(2)}, u32[]{:S(2)}) collective-permute-start(bf16[144,512]{1,0:T(8,128)(2,1)S(1)} %get-tuple-element.68.message_ref), channel_id=1, source_target_pairs={{0,2},{2,0},{4,6},{6,4},{8,10},{10,8},{12,14},{14,12},{16,18},{18,... | collective-permute-start | bytes 442376 | tf_op jit(solution)/shard_map/ppermute | solution.py:700
  83.6 2.6 %collective-permute-start.22 = (bf16[144,512]{1,0:T(8,128)(2,1)S(1)}, bf16[144,512]{1,0:T(8,128)(2,1)S(1)}, u32[]{:S(2)}, u32[]{:S(2)}) collective-permute-start(bf16[144,512]{1,0:T(8,128)(2,1)S(1)} %collective-permute-done.19.next2_ref), channel_id=1, source_target_pairs={{0,2},{2,0},{4,6},{6,4},{8,10},{10,8},{12,14},{14,12},{16,18},{18,... | collective-permute-start | bytes 442376 | tf_op jit(solution)/shard_map/ppermute | solution.py:700
  85.2 1.4 %collective-permute-start.23 = (bf16[144,512]{1,0:T(8,128)(2,1)S(1)}, bf16[144,512]{1,0:T(8,128)(2,1)S(1)}, u32[]{:S(2)}, u32[]{:S(2)}) collective-permute-start(bf16[144,512]{1,0:T(8,128)(2,1)S(1)} %collective-permute-done.20.next4_ref), channel_id=1, source_target_pairs={{0,2},{2,0},{4,6},{6,4},{8,10},{10,8},{12,14},{14,12},{16,18},{18,... | collective-permute-start | bytes 442376 | tf_op jit(solution)/shard_map/ppermute | solution.py:700

commit v5 on v4

--- a/solution.py
+++ b/solution.py
@@ -16,7 +16,7 @@
 F32 = jnp.float32
 BF16 = jnp.bfloat16
 VMEM_LIMIT = 20 << 20
-VMEM_WHOLE = 56 << 20
+VMEM_WHOLE = 60 << 20
 
 
 def dot_nn(a, b):
@@ -86,82 +86,76 @@
     ahead_ref,
     behind_ref,
     normed,
+    own,
+    top,
     w_query,
     w_key,
     w_value,
     semaphores,
 ):
     chunk = 16
-    loader = Loader(semaphores, None)
-    loader.get(w_key, w_key_ref)
-    loader.get(w_value, w_value_ref)
-    late = Loader(semaphores.at[2:], None)
-    late.get(w_query, w_query_ref)
+    loads = [
+        pltpu.make_async_copy(source, target, semaphores.at[index])
+        for index, (source, target) in enumerate(
+            (
+                (own_ref, own),
+                (w_key_ref, w_key),
+                (w_value_ref, w_value),
+                (w_query_ref, w_query),
+                (top_ref.at[0:EDGE], top),
+            )
+        )
+    ]
+    for load in loads:
+        load.start()
+    loads[0].wait()
 
     def norm_step(step, carry):
         rows = pl.ds(pl.multiple_of(step * chunk, chunk), chunk)
-        unit, _ = unit_rows(own_ref[rows, :].astype(F32))
+        unit, _ = unit_rows(own[rows, :].astype(F32))
         normed[rows, :] = (unit * gain_ref[...]).astype(BF16)
         return carry
 
     lax.fori_loop(0, ROWS // chunk, norm_step, 0, unroll=2)
     wide = w_key_ref.shape[1]
     half = EDGE // 2
-    loader.wait()
+    loads[1].wait()
     keys = dot_nn(normed[...], w_key[...]).astype(BF16)
+    loads[2].wait()
     values = dot_nn(normed[...], w_value[...]).astype(BF16)
     for ref in (kept_ref, ahead_ref, behind_ref):
         ref[0:ROWS, 0:wide] = keys
         ref[0:ROWS, wide : 2 * wide] = values
-    late.wait()
+    loads[3].wait()
+    loads[4].wait()
     queries = dot_nn(normed[...], w_query[...]).astype(BF16)
     queries_ref[...] = queries
-    ahead_ref[ROWS : ROWS + EDGE, :] = own_ref[ROWS - EDGE : ROWS, :]
+    ahead_ref[ROWS : ROWS + EDGE, :] = own[ROWS - EDGE : ROWS, :]
     ahead_ref[ROWS + EDGE : ROWS + EDGE + half, 0:wide] = queries[ROWS - EDGE : ROWS - half]
     ahead_ref[ROWS + EDGE : ROWS + EDGE + half, wide : 2 * wide] = queries[ROWS - half : ROWS]
-    behind_ref[ROWS : ROWS + EDGE, :] = own_ref[0:EDGE, :]
+    behind_ref[ROWS : ROWS + EDGE, :] = own[0:EDGE, :]
     behind_ref[ROWS + EDGE : ROWS + EDGE + half, 0:wide] = queries[0:half]
     behind_ref[ROWS + EDGE : ROWS + EDGE + half, wide : 2 * wide] = queries[half:EDGE]
-    behind_ref[ROWS + EDGE + half : ROWS + 2 * EDGE + half, :] = top_ref[0:EDGE, :]
-
-
-class Loader:
-    def __init__(self, semaphores, odd):
-        self.semaphores = semaphores
-        self.odd = odd
-        self.used = 0
-        self.waiting = []
-
-    def get(self, target, when_odd, when_even=None, rows=None):
-        semaphore = self.semaphores.at[self.used]
-        self.used += 1
-
-        def copy(source):
-            view = source if rows is None else source.at[rows[0] : rows[1]]
-            return pltpu.make_async_copy(view, target, semaphore)
-
-        if when_even is None or when_even is when_odd:
-            copy(when_odd).start()
-        else:
-
-            @pl.when(self.odd)
-            def _():
-                copy(when_odd).start()
-
-            @pl.when(jnp.logical_not(self.odd))
-            def _():
-                copy(when_even).start()
-
-        self.waiting.append(copy(when_odd))
-
-    def window(self, target, sources):
-        for index, (when_odd, when_even) in enumerate(sources):
-            self.get(target.at[index * ROWS : (index + 1) * ROWS], when_odd, when_even, (0, ROWS))
-
-    def wait(self):
-        for copy in self.waiting:
-            copy.wait()
-        self.waiting = []
+    behind_ref[ROWS + EDGE + half : ROWS + 2 * EDGE + half, :] = top[...]
+
+
+def choose_rows(target, odd, when_odd, when_even, rows):
+    if when_even is when_odd:
+        target[...] = when_odd[rows, :]
+        return
+
+    @pl.when(odd)
+    def _():
+        target[...] = when_odd[rows, :]
+
+    @pl.when(jnp.logical_not(odd))
+    def _():
+        target[...] = when_even[rows, :]
+
+
+def choose_blocks(target, odd, sources):
+    for index, (when_odd, when_even) in enumerate(sources):
+        choose_rows(target.at[index * ROWS : (index + 1) * ROWS], odd, when_odd, when_even, slice(0, ROWS))
 
 
 def masked_half(value, half):
@@ -193,18 +187,16 @@
     log_ref,
     window,
     query_all,
-    packed,
-    semaphores,
 ):
     place = lax.axis_index("tm")
     odd = lax.rem(place, 2) == 1
     wide = queries_ref.shape[1]
     half_edge = EDGE // 2
-    loader = Loader(semaphores, odd)
-    loader.get(query_all.at[0:ROWS], queries_ref)
-    loader.get(packed, after_ref, rows=(ROWS + EDGE, ROWS + EDGE + half_edge))
-    loader.window(
+    packed = after_ref[ROWS + EDGE : ROWS + EDGE + half_edge, :]
+    query_all[0:ROWS, :] = queries_ref[...]
+    choose_blocks(
         window,
+        odd,
         (
             (back4_ref, back4_ref),
             (peer_back2_ref, peer_back4_ref),
@@ -214,7 +206,6 @@
             (after_ref, after_ref),
         ),
     )
-    loader.wait()
     query_all[ROWS : ROWS + half_edge, :] = packed[:, 0:wide]
     query_all[ROWS + half_edge : ROWS + EDGE, :] = packed[:, wide : 2 * wide]
     key_lane = lax.broadcasted_iota(jnp.int32, (1, ROWS), 1)
@@ -245,7 +236,7 @@
 
 
 def mixer_body(
-    count, upstream_ref, next_rows, slope_ref, kernel_ref, w_out_ref, attended, log_ref, total_ref, message_ref, dot_ref, total_low, ready=lambda: None
+    count, upstream_ref, next_rows, slope_ref, kernel_ref, w_out_ref, attended, log_ref, total_ref, message_ref, dot_ref, total_low
 ):
     row_ids = lax.broadcasted_iota(jnp.int32, (ROWS, PAIR), 0)
     taps = kernel_ref.shape[0]
@@ -262,7 +253,6 @@
         return carry
 
     lax.fori_loop(0, upstream_ref.shape[1] // PAIR, conv_step, 0)
-    ready()
     out_grad = dot_nt(total_low[...], w_out_ref[...]).astype(BF16)
     message_ref[0:ROWS, :] = out_grad
     product = out_grad.astype(F32) * attended[...].astype(F32)
@@ -304,21 +294,16 @@
     mixed,
     total_low,
     before_rows,
-    after_rows,
-    own,
-    top,
-    w_out,
-    semaphores,
 ):
     place = lax.axis_index("tm")
     odd = lax.rem(place, 2) == 1
     wide = query_tail.shape[1]
     half_edge = EDGE // 2
     counts = [valid_count(valid_ref, place + block - LEFT - 1) for block in range(LEFT + 3)]
-    loader = Loader(semaphores, odd)
-    loader.get(before_rows, peer_ref, peer_back2_ref, (ROWS, ROWS + EDGE + half_edge))
-    loader.window(
+    choose_rows(before_rows, odd, peer_ref, peer_back2_ref, slice(ROWS, ROWS + EDGE + half_edge))
+    choose_blocks(
         window,
+        odd,
         (
             (peer_back4_ref, back5_ref),
             (back4_ref, back4_ref),
@@ -327,13 +312,7 @@
             (peer_ref, peer_back2_ref),
         ),
     )
-    late = Loader(semaphores.at[LEFT + 2 :], odd)
-    late.get(attended_all.at[EDGE : 2 * EDGE + ROWS], attended_ref)
-    late.get(w_out, w_out_ref)
-    late.get(own, own_ref)
-    late.get(after_rows, after_ref, rows=(ROWS, ROWS + 2 * EDGE + half_edge))
-    late.get(top, top_ref)
-    loader.wait()
+    attended_all[EDGE:, :] = attended_ref[...]
     query_tail[0:half_edge, :] = before_rows[EDGE : EDGE + half_edge, 0:wide]
     query_tail[half_edge:EDGE, :] = before_rows[EDGE : EDGE + half_edge, wide : 2 * wide]
     key_lane = lax.broadcasted_iota(jnp.int32, (1, ROWS), 1)
@@ -348,13 +327,12 @@
             product = dot_nn(shares_low, masked_half(window[:, value_lanes], half))
             total = product if total is None else total + product
         attended_all[0:EDGE, lanes] = total.astype(BF16)
-    late.wait()
-    projected = dot_nn(attended_all[...], w_out[...])
+    projected = dot_nn(attended_all[...], w_out_ref[...])
     row_ids = lax.broadcasted_iota(jnp.int32, (ROWS, 1), 0)
     edge_ids = lax.broadcasted_iota(jnp.int32, (EDGE, 1), 0)
     before = projected[0:EDGE] + before_rows[0:EDGE, :].astype(F32)
-    here = projected[EDGE : EDGE + ROWS] + own[...].astype(F32)
-    after = projected[EDGE + ROWS :] + after_rows[0:EDGE, :].astype(F32)
+    here = projected[EDGE : EDGE + ROWS] + own_ref[...].astype(F32)
+    after = projected[EDGE + ROWS :] + after_ref[ROWS : ROWS + EDGE, :].astype(F32)
     before = jnp.where(edge_ids + (ROWS - EDGE) < counts[LEFT], before, 0.0)
     here = jnp.where(row_ids < counts[LEFT + 1], here, 0.0)
     after = jnp.where(edge_ids < counts[LEFT + 2], after, 0.0)
@@ -370,15 +348,15 @@
         slope_ref[:, lanes] = gate * (1.0 + output * (1.0 - gate))
         return carry
 
-    lax.fori_loop(0, own.shape[1] // PAIR, conv_step, 0)
-    first = EDGE + half_edge
+    lax.fori_loop(0, own_ref.shape[1] // PAIR, conv_step, 0)
+    first = ROWS + EDGE + half_edge
     mixer_body(
         counts[LEFT + 1],
-        top,
-        lambda lanes: after_rows[first : first + EDGE, lanes].astype(F32),
+        top_ref,
+        lambda lanes: after_ref[first : first + EDGE, lanes].astype(F32),
         slope_ref,
         kernel_ref,
-        w_out,
+        w_out_ref,
         attended_all[EDGE : EDGE + ROWS, :],
         log_ref,
         total_ref,
@@ -401,35 +379,20 @@
     message_ref,
     dot_ref,
     total_low,
-    upstream,
-    next_rows,
-    slope,
-    w_out,
-    attended,
-    semaphores,
 ):
-    loader = Loader(semaphores, None)
-    loader.get(upstream, upstream_ref)
-    loader.get(next_rows, next_ref)
-    loader.get(slope, slope_ref)
-    late = Loader(semaphores.at[3:], None)
-    late.get(attended, attended_ref, rows=(0, ROWS))
-    late.get(w_out, w_out_ref)
-    loader.wait()
     mixer_body(
         valid_count(valid_ref, lax.axis_index("tm")),
-        upstream,
-        lambda lanes: next_rows[:, lanes].astype(F32),
-        slope,
+        upstream_ref,
+        lambda lanes: next_ref[:, lanes].astype(F32),
+        slope_ref,
         kernel_ref,
-        w_out,
-        attended,
+        w_out_ref,
+        attended_ref[0:ROWS, :],
         log_ref,
         total_ref,
         message_ref,
         dot_ref,
         total_low,
-        late.wait,
     )
 
 
@@ -486,19 +449,13 @@
     value_sum_ref,
     window,
     query_grad,
-    queries,
-    message,
-    w_query,
-    semaphores,
 ):
     place = lax.axis_index("tm")
     odd = lax.rem(place, 2) == 1
     wide = queries_ref.shape[1]
-    loader = Loader(semaphores, odd)
-    loader.get(queries, queries_ref)
-    loader.get(message, message_ref)
-    loader.window(
+    choose_blocks(
         window,
+        odd,
         (
             (back4_ref, back4_ref),
             (peer_back2_ref, peer_back4_ref),
@@ -507,21 +464,18 @@
             (kept_ref, kept_ref),
         ),
     )
-    late = Loader(semaphores.at[LEFT + 3 :], odd)
-    late.get(w_query, w_query_ref)
-    loader.wait()
     own_rows = slice(LEFT * ROWS, (LEFT + 1) * ROWS)
     key_lane = lax.broadcasted_iota(jnp.int32, (1, ROWS), 1)
     allowed = jnp.concatenate(
         [key_lane < valid_count(valid_ref, place + block - LEFT) for block in range(LEFT + 1)], axis=1
     )
     key_valid = lax.broadcasted_iota(jnp.int32, (ROWS, ROWS), 0) < valid_count(valid_ref, place)
-    stats = message_stats(message[ROWS : ROWS + 16, :])
+    stats = message_stats(message_ref[ROWS : ROWS + 16, :])
     for pair in range(wide // PAIR):
         lanes = slice(pair * PAIR, (pair + 1) * PAIR)
         value_lanes = slice(wide + pair * PAIR, wide + (pair + 1) * PAIR)
-        query_pair = queries[:, lanes]
-        grad_pair = message[0:ROWS, lanes]
+        query_pair = queries_ref[:, lanes]
+        grad_pair = message_ref[0:ROWS, lanes]
         total = None
         for half in range(2):
             key_half = masked_half(window[:, lanes], half)
@@ -544,8 +498,7 @@
             [stats[8 + head : 9 + head] for head in heads],
             key_valid,
         )
-    late.wait()
-    out_ref[...] = dot_nt(query_grad[...], w_query[...])
+    out_ref[...] = dot_nt(query_grad[...], w_query_ref[...])
 
 
 def key_kernel(
@@ -580,32 +533,24 @@
     stats,
     key_grad,
     value_grad,
-    kept,
-    w_key,
-    w_value,
-    own,
-    total,
-    partial,
-    result,
-    semaphores,
 ):
     place = lax.axis_index("tm")
     odd = lax.rem(place, 2) == 1
     count = valid_count(valid_ref, place)
     wide = grads.shape[1]
-    loader = Loader(semaphores, odd)
     messages = (
         (peer_next2_ref, peer_ref),
         (next2_ref, next2_ref),
         (peer_next4_ref, peer_next2_ref),
         (next4_ref, next4_ref),
     )
-    loader.get(kept, kept_ref)
-    loader.window(grads, messages)
+    choose_blocks(grads, odd, messages)
     for block, (when_odd, when_even) in enumerate(messages):
-        loader.get(tails.at[block * 16 : block * 16 + 16], when_odd, when_even, (ROWS, ROWS + 16))
-    loader.window(
+        target = tails.at[block * 16 : block * 16 + 16]
+        choose_rows(target, odd, when_odd, when_even, slice(ROWS, ROWS + 16))
+    choose_blocks(
         queries,
+        odd,
         (
             (query_peer_next2_ref, query_peer_ref),
             (query_next2_ref, query_next2_ref),
@@ -613,14 +558,6 @@
             (query_next4_ref, query_next4_ref),
         ),
     )
-    late = Loader(semaphores.at[loader.used :], odd)
-    late.get(w_key, w_key_ref)
-    late.get(w_value, w_value_ref)
-    late.get(own, own_ref)
-    late.get(total, total_ref)
-    late.get(partial, partial_ref)
-    late.get(result, result_ref)
-    loader.wait()
     for block in range(LEFT):
         stats[:, block * ROWS : (block + 1) * ROWS] = message_stats(tails[block * 16 : block * 16 + 16, :])
     key_valid = lax.broadcasted_iota(jnp.int32, (ROWS, LEFT * ROWS), 0) < count
@@ -628,8 +565,8 @@
         lanes = slice(pair * PAIR, (pair + 1) * PAIR)
         heads = (2 * pair, 2 * pair + 1)
         key_sum, value_sum = key_terms(
-            kept[:, lanes],
-            kept[:, slice(wide + pair * PAIR, wide + (pair + 1) * PAIR)],
+            kept_ref[:, lanes],
+            kept_ref[:, slice(wide + pair * PAIR, wide + (pair + 1) * PAIR)],
             queries[:, lanes],
             grads[:, lanes],
             [stats[head : head + 1, :] for head in heads],
@@ -638,28 +575,27 @@
         )
         key_grad[:, lanes] = (key_sum_ref[:, lanes] + key_sum).astype(BF16)
         value_grad[:, lanes] = (value_sum_ref[:, lanes] + value_sum).astype(BF16)
-    late.wait()
-    normed_grad = partial[...] + dot_nt(key_grad[...], w_key[...])
-    normed_grad = normed_grad + dot_nt(value_grad[...], w_value[...])
+    normed_grad = partial_ref[...] + dot_nt(key_grad[...], w_key_ref[...])
+    normed_grad = normed_grad + dot_nt(value_grad[...], w_value_ref[...])
     scaled = normed_grad * gain_ref[...]
-    unit, inverse = unit_rows(own[...].astype(F32))
+    unit, inverse = unit_rows(own_ref[...].astype(F32))
     back = inverse * (
         scaled
         - jnp.mean(scaled, axis=-1, keepdims=True)
         - unit * jnp.mean(scaled * unit, axis=-1, keepdims=True)
     )
-    grad = total[...] + back
+    grad = total_ref[...] + back
     out_ref[...] = grad.astype(BF16)
     edge_ref[...] = grad[0:EDGE].astype(BF16)
     mine = lax.axis_index("section") == keep_ref[0]
-    held_ref[...] = jnp.where(mine, grad, result[...].astype(F32)).astype(BF16)
-
-
-def call(kernel, name, operands, outs, scratch, copies, flops, limit=VMEM_LIMIT):
+    held_ref[...] = jnp.where(mine, grad, result_ref[...].astype(F32)).astype(BF16)
+
+
+def call(kernel, name, operands, outs, scratch, copies=0, limit=VMEM_LIMIT):
     kinds = {
         "s": pl.BlockSpec(memory_space=pltpu.SMEM),
         "v": pl.BlockSpec(memory_space=pltpu.VMEM),
-        "a": pl.BlockSpec(memory_space=pl.ANY),
+        "h": pl.BlockSpec(memory_space=pltpu.HBM),
     }
     return pl.pallas_call(
         kernel,
@@ -668,9 +604,9 @@
         out_specs=[kinds["v"]] * len(outs),
         out_shape=[jax.ShapeDtypeStruct(shape, dtype) for shape, dtype in outs],
         scratch_shapes=[pltpu.VMEM(shape, dtype) for shape, dtype in scratch]
-        + [pltpu.SemaphoreType.DMA((copies,))],
+        + [pltpu.SemaphoreType.DMA((copies,))] * (copies > 0),
         compiler_params=pltpu.CompilerParams(vmem_limit_bytes=limit),
-        cost_estimate=pl.CostEstimate(flops=flops, bytes_accessed=4 << 20, transcendentals=0),
+        cost_estimate=pl.CostEstimate(flops=1 << 30, bytes_accessed=4 << 20, transcendentals=0),
     )(*[array for array, _ in operands])
 
 
@@ -716,16 +652,15 @@
     queries, kept, ahead, behind = call(
         project_kernel,
         "project",
-        placed("vvvaaa", own, top_grad, norm_gain, query_weight, key_weight, value_weight),
+        placed("hhvhhh", own, top_grad, norm_gain, query_weight, key_weight, value_weight),
         [
             ((ROWS, wide), BF16),
             ((ROWS, 2 * wide), BF16),
             ((ROWS + EDGE + half_edge, width), BF16),
             ((ROWS + 2 * EDGE + half_edge, width), BF16),
         ],
-        [((ROWS, width), BF16), weight, weight, weight],
-        3,
-        1 << 30,
+        [((ROWS, width), BF16), ((ROWS, width), BF16), ((EDGE, width), BF16), weight, weight, weight],
+        5,
         VMEM_WHOLE,
     )
     back2 = moved(ahead, across(2, every))
@@ -755,11 +690,9 @@
     attended, logs = call(
         attend_kernel,
         "attend",
-        placed("saaaaaaaa", group_valid, queries, kept, back2, back4, peer, peer_back2, peer_back4, after1),
+        placed("svvvvvvvv", group_valid, queries, kept, back2, back4, peer, peer_back2, peer_back4, after1),
         [((ROWS + EDGE, wide), BF16), ((ROWS, PAIR), F32)],
-        [(((LEFT + 2) * ROWS, 2 * wide), BF16), ((ROWS + EDGE, wide), BF16), ((half_edge, 2 * wide), BF16)],
-        LEFT + 4,
-        1 << 30,
+        [(((LEFT + 2) * ROWS, 2 * wide), BF16), ((ROWS + EDGE, wide), BF16)],
     )
     back5 = after(back5, attended)
     step_outs = [((ROWS, width), F32), ((ROWS + 16, wide), BF16), ((ROWS, PAIR), F32)]
@@ -767,7 +700,7 @@
         mix_kernel,
         "mix",
         placed(
-            "saaavaaaaaaaav",
+            "svvvvvvvvvvvvv",
             group_valid,
             own,
             top_grad,
@@ -791,13 +724,7 @@
             ((ROWS + 2 * EDGE, width), F32),
             ((ROWS, width), BF16),
             ((EDGE + half_edge, width), BF16),
-            ((2 * EDGE + half_edge, width), BF16),
-            ((ROWS, width), BF16),
-            ((ROWS, width), BF16),
-            ((wide, width), BF16),
         ],
-        LEFT + 7,
-        1 << 30,
     )
 
     result = own
@@ -810,20 +737,11 @@
                 mixer_kernel,
                 "mixer",
                 placed(
-                    "saaavaav", group_valid, upstream, upstream_next, slope, kernel, out_weight, attended, logs
+                    "svvvvvvv", group_valid, upstream, upstream_next, slope, kernel, out_weight, attended, logs
                 ),
                 step_outs,
-                [
-                    ((ROWS, width), BF16),
-                    ((ROWS, width), BF16),
-                    ((EDGE, width), BF16),
-                    ((ROWS + EDGE, width), F32),
-                    ((wide, width), BF16),
-                    ((ROWS, wide), BF16),
-                ],
-                5,
-                1 << 30,
-            )
+                [((ROWS, width), BF16)],
+                    )
         here = [layer]
         grad2 = moved(message, across(-2, here))
         grad4 = moved(message, across(-4, here))
@@ -832,7 +750,7 @@
             query_kernel,
             "own_queries",
             placed(
-                "saaaaaaaavva",
+                "svvvvvvvvvvv",
                 group_valid,
                 queries,
                 kept,
@@ -850,13 +768,8 @@
             [
                 ((span, 2 * wide), BF16),
                 ((ROWS, wide), BF16),
-                ((ROWS, wide), BF16),
-                ((ROWS + 16, wide), BF16),
-                weight,
             ],
-            LEFT + 4,
-            1 << 30,
-        )
+            )
         grad2, grad4, partial = lax.optimization_barrier((grad2, grad4, partial))
         peer_grad2 = moved(grad2, swap)
         peer_grad4 = moved(grad4, swap)
@@ -864,7 +777,7 @@
             key_kernel,
             "own_keys",
             placed(
-                "saaaaaaaaaaaaavaaavvas",
+                "svvvvvvvvvvvvvvvvvvvvs",
                 group_valid,
                 kept,
                 query_next2,
@@ -896,17 +809,8 @@
                 ((16, LEFT * ROWS), F32),
                 ((ROWS, wide), BF16),
                 ((ROWS, wide), BF16),
-                ((ROWS, 2 * wide), BF16),
-                weight,
-                weight,
-                ((ROWS, width), BF16),
-                ((ROWS, width), F32),
-                ((ROWS, width), F32),
-                ((ROWS, width), BF16),
             ],
-            3 * LEFT + 7,
-            1 << 30,
-        )
+            )
         if layer > 0:
             upstream = moved(
                 input_grad,

time: 93.3 us -> 87.1 us (0.934)
  Pallas kernels: 41 us -> 33.5 us
  starting transfers between devices: 37.3 us -> 38.7 us
    pallas_call x8, Pallas kernels: 41 us -> 33.5 us  [call(): pl.pallas_call(kernel, name=name, in_specs=[kinds[place] for _, place in...]
    ppermute x24, starting transfers between devices: 37.3 us -> 38.7 us  [moved(): return lax.ppermute(value, ('tm', 'section'), pairs)]
  transfers between devices with their start and end apart: 24 -> 24, of which waited for: 8 -> 8; matrix products, arithmetic and copies ran while one was open for 0% -> 0% of each run, Pallas kernels for 14% -> 13%
where the time goes in v5:
time: 87.1 us; the launch traced here: 86.7 us
  starting transfers between devices  38.7 us (44%)
  Pallas kernels  33.5 us (38%)
  waiting for transfers between devices  13.2 us (15%)
  local copies, waits for them, and re-layouts  0.98 us (1%)
    ppermute x24, starting transfers between devices, moved(): return lax.ppermute(value, ('tm', 'section'), pairs)  38.7 us
    pallas_call x8, Pallas kernels, call(): pl.pallas_call(kernel, name=name, in_specs=[kinds[place] for _, place in...  33.5 us
    ppermute x24, waiting for transfers between devices, moved(): return lax.ppermute(value, ('tm', 'section'), pairs)  13.2 us
  transfers between devices with their start and end apart: 24, of which 8 were waited for; matrix products, arithmetic and copies ran while one was open for 0% of the time, Pallas kernels for 13%

profile of v5, /device:TPU:19, one launch (start us, length us, event | category | flops | bytes accessed | tf_op | source)
XLA Modules:
  0.0 86.7 jit_solution(18265637459603321234)
XLA Ops:
  0.0 4.4 %project.1 = (bf16[128,512]{1,0:T(8,128)(2,1)}, bf16[128,1024]{1,0:T(8,128)(2,1)}, bf16[176,1024]{1,0:T(8,128)(2,1)}, bf16[208,1024]{1,0:T(8,128)(2,1)}) custom-call(bf16[128,1024]{1,0:T(8,128)(2,1)} %bitcast.9, bf16[128,1024]{1,0:T(8,128)(2,1)} %top_ref.3, f32[1,1024]{1,0:T(1,128)} %gain_ref.5, bf16[1024,512]{1,0:T(8,128)(2,1)} %bitcast.24, ...), custom_call_target="tpu_custom_call" | custom-call | flops 1073741824 | bytes 4194304 | tf_op jit(solution)/shard_map/project/pallas_call | solution.py:600
  4.4 0.0 copy-start.4
  4.4 3.3 %collective-permute-start.6 = (bf16[176,1024]{1,0:T(8,128)(2,1)}, bf16[176,1024]{1,0:T(8,128)(2,1)S(1)}, u32[]{:S(2)}, u32[]{:S(2)}) collective-permute-start(bf16[176,1024]{1,0:T(8,128)(2,1)} %get-tuple-element.50), channel_id=1, source_target_pairs={{0,4},{2,6},{4,8},{6,10},{8,12},{10,14},{12,16},{14,18},{16,20},{1... | collective-permute-start | bytes 1081352 | tf_op jit(solution)/shard_map/ppermute | solution.py:636
  7.7 1.0 %collective-permute-start.2 = (bf16[128,512]{1,0:T(8,128)(2,1)}, bf16[128,512]{1,0:T(8,128)(2,1)S(1)}, u32[]{:S(2)}, u32[]{:S(2)}) collective-permute-start(bf16[128,512]{1,0:T(8,128)(2,1)} %get-tuple-element.43.queries_ref), channel_id=1, source_target_pairs={{0,2},{2,0},{4,6},{6,4},{8,10},{10,8},{12,14},{14,12},{16,18},{18,... | collective-permute-start | bytes 393224 | tf_op jit(solution)/shard_map/ppermute | solution.py:636
  8.7 2.1 %collective-permute-start.1 = (bf16[128,512]{1,0:T(8,128)(2,1)}, bf16[128,512]{1,0:T(8,128)(2,1)S(1)}, u32[]{:S(2)}, u32[]{:S(2)}) collective-permute-start(bf16[128,512]{1,0:T(8,128)(2,1)} %get-tuple-element.43.queries_ref), channel_id=1, source_target_pairs={{8,0},{10,2},{12,4},{14,6},{16,8},{18,10},{20,12},{22,14},{24,16},... | collective-permute-start | bytes 393224 | tf_op jit(solution)/shard_map/ppermute | solution.py:636
  10.8 3.2 %collective-permute-start.7 = (bf16[128,1024]{1,0:T(8,128)(2,1)}, bf16[128,1024]{1,0:T(8,128)(2,1)S(1)}, u32[]{:S(2)}, u32[]{:S(2)}) collective-permute-start(bf16[128,1024]{1,0:T(8,128)(2,1)} %get-tuple-element.54.kept_ref), channel_id=1, source_target_pairs={{0,8},{2,10},{4,12},{6,14},{8,16},{10,18},{12,20},{14,22},{16,24},... | collective-permute-start | bytes 786440 | tf_op jit(solution)/shard_map/ppermute | solution.py:636
  14.0 2.1 %collective-permute-start = (bf16[128,512]{1,0:T(8,128)(2,1)}, bf16[128,512]{1,0:T(8,128)(2,1)S(1)}, u32[]{:S(2)}, u32[]{:S(2)}) collective-permute-start(bf16[128,512]{1,0:T(8,128)(2,1)} %get-tuple-element.43.queries_ref), channel_id=1, source_target_pairs={{4,0},{6,2},{8,4},{10,6},{12,8},{14,10},{16,12},{18,14},{20,16},{2... | collective-permute-start | bytes 393224 | tf_op jit(solution)/shard_map/ppermute | solution.py:636
  16.1 0.0 collective-permute-done.2.query_peer_ref
  16.1 0.0 copy-start.7
  16.1 2.8 %collective-permute-start.5 = (bf16[208,1024]{1,0:T(8,128)(2,1)}, bf16[208,1024]{1,0:T(8,128)(2,1)S(1)}, u32[]{:S(2)}, u32[]{:S(2)}) collective-permute-start(bf16[208,1024]{1,0:T(8,128)(2,1)} %get-tuple-element.44), channel_id=1, source_target_pairs={{2,0},{4,2},{6,4},{8,6},{10,8},{12,10},{14,12},{16,14},{18,16},{20... | collective-permute-start | bytes 1277960 | tf_op jit(solution)/shard_map/ppermute | solution.py:636
  18.9 0.0 collective-permute-done.1.query_next4_ref
  18.9 0.7 collective-permute-start.4
  19.7 1.8 %collective-permute-done.query_next2_ref = bf16[128,512]{1,0:T(8,128)(2,1)S(1)} collective-permute-done((bf16[128,512]{1,0:T(8,128)(2,1)}, bf16[128,512]{1,0:T(8,128)(2,1)S(1)}, u32[]{:S(2)}, u32[]{:S(2)}) %collective-permute-start) | collective-permute-done | bytes 131104 | tf_op jit(solution)/shard_map/ppermute | solution.py:636
  21.5 1.4 %collective-permute-start.8 = (bf16[176,1024]{1,0:T(8,128)(2,1)}, bf16[176,1024]{1,0:T(8,128)(2,1)S(1)}, u32[]{:S(2)}, u32[]{:S(2)}) collective-permute-start(bf16[176,1024]{1,0:T(8,128)(2,1)} %get-tuple-element.50), channel_id=1, source_target_pairs={{0,2},{2,0},{4,6},{6,4},{8,10},{10,8},{12,14},{14,12},{16,18},{18,... | collective-permute-start | bytes 1081352 | tf_op jit(solution)/shard_map/ppermute | solution.py:636
  22.9 0.0 collective-permute-done.6.back2_ref
  22.9 0.0 collective-permute-start.9
  22.9 0.0 collective-permute-done.4.query_peer_next4_ref
  22.9 0.5 collective-permute-start.3
  23.4 0.0 collective-permute-done.7.back4_ref
  23.4 0.1 collective-permute-start.10
  23.5 1.4 %collective-permute-done.3.query_peer_next2_ref = bf16[128,512]{1,0:T(8,128)(2,1)S(1)} collective-permute-done((bf16[128,512]{1,0:T(8,128)(2,1)S(1)}, bf16[128,512]{1,0:T(8,128)(2,1)S(1)}, u32[]{:S(2)}, u32[]{:S(2)}) %collective-permute-start.3) | collective-permute-done | bytes 131104 | tf_op jit(solution)/shard_map/ppermute | solution.py:636
  24.9 0.7 collective-permute-start.11
  25.6 0.0 copy-start
  25.6 0.0 copy-start.3
  25.7 0.0 copy-start.5
  25.7 1.3 %collective-permute-done.5.after_ref = bf16[208,1024]{1,0:T(8,128)(2,1)S(1)} collective-permute-done((bf16[208,1024]{1,0:T(8,128)(2,1)}, bf16[208,1024]{1,0:T(8,128)(2,1)S(1)}, u32[]{:S(2)}, u32[]{:S(2)}) %collective-permute-start.5) | collective-permute-done | bytes 426016 | tf_op jit(solution)/shard_map/ppermute | solution.py:636
  27.0 0.0 collective-permute-done.8.peer_ref
  27.0 0.0 collective-permute-done.10.peer_back4_ref
  27.0 0.0 collective-permute-done.9.peer_back2_ref
  27.0 0.9 %copy-done.9 = bf16[128,512]{1,0:T(8,128)(2,1)S(1)} copy-done((bf16[128,512]{1,0:T(8,128)(2,1)S(1)}, bf16[128,512]{1,0:T(8,128)(2,1)}, u32[]{:S(2)}) %copy-start.9) | copy-done | bytes 131096
  27.9 3.6 %attend.1 = (bf16[160,512]{1,0:T(8,128)(2,1)S(1)}, f32[128,128]{1,0:T(8,128)S(1)}) custom-call(s32[16]{0:T(128)S(1)} %copy-done.7, bf16[128,512]{1,0:T(8,128)(2,1)S(1)} %copy-done.9, bf16[128,1024]{1,0:T(8,128)(2,1)S(1)} %copy-done.4, bf16[176,1024]{1,0:T(8,128)(2,1)S(1)} %collective-permute-done.6.back2_ref, ...), custom_call_target="tpu_custom_call" | custom-call | flops 1073741824 | bytes 4194304 | tf_op jit(solution)/shard_map/attend/pallas_call | solution.py:600
  31.5 0.0 collective-permute-done.11.back5_ref
  31.5 0.0 copy-start.8
  31.5 7.7 %mix.1 = (f32[160,1024]{1,0:T(8,128)S(1)}, f32[128,1024]{1,0:T(8,128)S(1)}, bf16[144,512]{1,0:T(8,128)(2,1)S(1)}, f32[128,128]{1,0:T(8,128)S(1)}) custom-call(s32[16]{0:T(128)S(1)} %copy-done.7, bf16[128,1024]{1,0:T(8,128)(2,1)S(1)} %bitcast.10, bf16[128,1024]{1,0:T(8,128)(2,1)S(1)} %copy-done.5, bf16[160,512]{1,0:T(8,128)(2,1)S(1)} %get-tuple-element.52.attended_ref, ...), custom_call_target="tpu_custom_call" | custom-call | flops 1073741824 | bytes 4194304 | tf_op jit(solution)/shard_map/mix/pallas_call | solution.py:600
  39.3 0.7 collective-permute-start.13
  39.9 0.7 collective-permute-start.12
  40.6 2.6 %collective-permute-start.14 = (bf16[144,512]{1,0:T(8,128)(2,1)S(1)}, bf16[144,512]{1,0:T(8,128)(2,1)S(1)}, u32[]{:S(2)}, u32[]{:S(2)}) collective-permute-start(bf16[144,512]{1,0:T(8,128)(2,1)S(1)} %get-tuple-element.56.message_ref), channel_id=1, source_target_pairs={{0,2},{2,0},{4,6},{6,4},{8,10},{10,8},{12,14},{14,12},{16,18},{18,... | collective-permute-start | bytes 442376 | tf_op jit(solution)/shard_map/ppermute | solution.py:636
  43.2 3.7 %own_queries.2 = (f32[128,1024]{1,0:T(8,128)S(1)}, f32[128,512]{1,0:T(8,128)S(1)}, f32[128,512]{1,0:T(8,128)S(1)}) custom-call(s32[16]{0:T(128)S(1)} %copy-done.7, bf16[128,512]{1,0:T(8,128)(2,1)S(1)} %copy-done.9, bf16[128,1024]{1,0:T(8,128)(2,1)S(1)} %copy-done.4, bf16[176,1024]{1,0:T(8,128)(2,1)S(1)} %collective-permute-done.6.back2_ref, ...), custom_call_target="tpu_custom_call" | custom-call | flops 1073741824 | bytes 4194304 | tf_op jit(solution)/shard_map/own_queries/pallas_call | solution.py:600
  46.9 0.0 copy-start.6
  46.9 0.0 collective-permute-done.13.next4_ref
  46.9 0.0 collective-permute-done.12.next2_ref
  46.9 0.1 collective-permute-start.15
  47.0 0.5 collective-permute-start.16
  47.5 0.0 collective-permute-done.14.peer_ref
  47.5 0.9 collective-permute-done.15.peer_next2_ref
  48.4 0.2 collective-permute-done.16.peer_next4_ref
  48.6 3.4 %own_keys.2 = (bf16[128,1024]{1,0:T(8,128)(2,1)S(1)}, bf16[32,1024]{1,0:T(8,128)(2,1)S(1)}, bf16[128,1024]{1,0:T(8,128)(2,1)S(1)}) custom-call(s32[16]{0:T(128)S(1)} %copy-done.7, bf16[128,1024]{1,0:T(8,128)(2,1)S(1)} %copy-done.4, bf16[128,512]{1,0:T(8,128)(2,1)S(1)} %collective-permute-done.query_next2_ref, ...), custom_call_target="tpu_custom_call" | custom-call | flops 1073741824 | bytes 4194304 | tf_op jit(solution)/shard_map/own_keys/pallas_call | solution.py:600
  52.0 7.0 %collective-permute-start.17 = (bf16[128,1024]{1,0:T(8,128)(2,1)S(1)}, bf16[128,1024]{1,0:T(8,128)(2,1)S(1)}, u32[]{:S(2)}, u32[]{:S(2)}) collective-permute-start(bf16[128,1024]{1,0:T(8,128)(2,1)S(1)} %get-tuple-element.65), channel_id=1, source_target_pairs={{1,0},{3,2},{5,4},{7,6},{9,8},{11,10},{13,12},{15,14},{17,16},{19,... | collective-permute-start | bytes 786440 | tf_op jit(solution)/shard_map/ppermute | solution.py:636
  59.0 1.3 %collective-permute-start.18 = (bf16[32,1024]{1,0:T(8,128)(2,1)S(1)}, bf16[32,1024]{1,0:T(8,128)(2,1)S(1)}, u32[]{:S(2)}, u32[]{:S(2)}) collective-permute-start(bf16[32,1024]{1,0:T(8,128)(2,1)S(1)} %get-tuple-element.66), channel_id=1, source_target_pairs={{3,0},{5,2},{7,4},{9,6},{11,8},{13,10},{15,12},{17,14},{19,16},{21... | collective-permute-start | bytes 196616 | tf_op jit(solution)/shard_map/ppermute | solution.py:636
  60.3 6.2 %collective-permute-done.18.next_ref = bf16[32,1024]{1,0:T(8,128)(2,1)S(1)} collective-permute-done((bf16[32,1024]{1,0:T(8,128)(2,1)S(1)}, bf16[32,1024]{1,0:T(8,128)(2,1)S(1)}, u32[]{:S(2)}, u32[]{:S(2)}) %collective-permute-start.18) | collective-permute-done | bytes 65568 | tf_op jit(solution)/shard_map/ppermute | solution.py:636
  66.5 0.0 collective-permute-done.17.upstream_ref
  66.5 3.1 %mixer.1 = (f32[128,1024]{1,0:T(8,128)S(1)}, bf16[144,512]{1,0:T(8,128)(2,1)S(1)}, f32[128,128]{1,0:T(8,128)S(1)}) custom-call(s32[16]{0:T(128)S(1)} %copy-done.7, bf16[128,1024]{1,0:T(8,128)(2,1)S(1)} %collective-permute-done.17.upstream_ref, bf16[32,1024]{1,0:T(8,128)(2,1)S(1)} %collective-permute-done.18.next_ref, ...), custom_call_target="tpu_custom_call" | custom-call | flops 1073741824 | bytes 4194304 | tf_op jit(solution)/shard_map/mixer/pallas_call | solution.py:600
  69.7 2.3 %collective-permute-start.20 = (bf16[144,512]{1,0:T(8,128)(2,1)S(1)}, bf16[144,512]{1,0:T(8,128)(2,1)S(1)}, u32[]{:S(2)}, u32[]{:S(2)}) collective-permute-start(bf16[144,512]{1,0:T(8,128)(2,1)S(1)} %get-tuple-element.68.message_ref), channel_id=1, source_target_pairs={{8,0},{10,2},{12,4},{14,6},{16,8},{18,10},{20,12},{22,14},{24,16},... | collective-permute-start | bytes 442376 | tf_op jit(solution)/shard_map/ppermute | solution.py:636
  71.9 1.9 %collective-permute-start.19 = (bf16[144,512]{1,0:T(8,128)(2,1)S(1)}, bf16[144,512]{1,0:T(8,128)(2,1)S(1)}, u32[]{:S(2)}, u32[]{:S(2)}) collective-permute-start(bf16[144,512]{1,0:T(8,128)(2,1)S(1)} %get-tuple-element.68.message_ref), channel_id=1, source_target_pairs={{4,0},{6,2},{8,4},{10,6},{12,8},{14,10},{16,12},{18,14},{20,16},{2... | collective-permute-start | bytes 442376 | tf_op jit(solution)/shard_map/ppermute | solution.py:636
  73.9 1.5 %collective-permute-start.21 = (bf16[144,512]{1,0:T(8,128)(2,1)S(1)}, bf16[144,512]{1,0:T(8,128)(2,1)S(1)}, u32[]{:S(2)}, u32[]{:S(2)}) collective-permute-start(bf16[144,512]{1,0:T(8,128)(2,1)S(1)} %get-tuple-element.68.message_ref), channel_id=1, source_target_pairs={{0,2},{2,0},{4,6},{6,4},{8,10},{10,8},{12,14},{14,12},{16,18},{18,... | collective-permute-start | bytes 442376 | tf_op jit(solution)/shard_map/ppermute | solution.py:636
  75.4 3.7 %own_queries.3 = (f32[128,1024]{1,0:T(8,128)S(1)}, f32[128,512]{1,0:T(8,128)S(1)}, f32[128,512]{1,0:T(8,128)S(1)}) custom-call(s32[16]{0:T(128)S(1)} %copy-done.7, bf16[128,512]{1,0:T(8,128)(2,1)S(1)} %copy-done.9, bf16[128,1024]{1,0:T(8,128)(2,1)S(1)} %copy-done.4, bf16[176,1024]{1,0:T(8,128)(2,1)S(1)} %collective-permute-done.6.back2_ref, ...), custom_call_target="tpu_custom_call" | custom-call | flops 1073741824 | bytes 4194304 | tf_op jit(solution)/shard_map/own_queries/pallas_call | solution.py:600
  79.1 0.0 collective-permute-done.20.next4_ref
  79.1 0.0 collective-permute-done.19.next2_ref
  79.1 2.3 %collective-permute-start.22 = (bf16[144,512]{1,0:T(8,128)(2,1)S(1)}, bf16[144,512]{1,0:T(8,128)(2,1)S(1)}, u32[]{:S(2)}, u32[]{:S(2)}) collective-permute-start(bf16[144,512]{1,0:T(8,128)(2,1)S(1)} %collective-permute-done.19.next2_ref), channel_id=1, source_target_pairs={{0,2},{2,0},{4,6},{6,4},{8,10},{10,8},{12,14},{14,12},{16,18},{18,... | collective-permute-start | bytes 442376 | tf_op jit(solution)/shard_map/ppermute | solution.py:636
  81.3 0.0 collective-permute-start.23
  81.3 0.0 collective-permute-done.21.peer_ref
  81.3 1.0 %collective-permute-done.22.peer_next2_ref = bf16[144,512]{1,0:T(8,128)(2,1)S(1)} collective-permute-done((bf16[144,512]{1,0:T(8,128)(2,1)S(1)}, bf16[144,512]{1,0:T(8,128)(2,1)S(1)}, u32[]{:S(2)}, u32[]{:S(2)}) %collective-permute-start.22) | collective-permute-done | bytes 147488 | tf_op jit(solution)/shard_map/ppermute | solution.py:636
  82.3 0.4 collective-permute-done.23.peer_next4_ref
  82.7 4.0 %own_keys.3 = (bf16[128,1024]{1,0:T(8,128)(2,1)}, bf16[32,1024]{1,0:T(8,128)(2,1)}, bf16[128,1024]{1,0:T(8,128)(2,1)}) custom-call(s32[16]{0:T(128)S(1)} %copy-done.7, bf16[128,1024]{1,0:T(8,128)(2,1)S(1)} %copy-done.4, bf16[128,512]{1,0:T(8,128)(2,1)S(1)} %collective-permute-done.query_next2_ref, ...), custom_call_target="tpu_custom_call" | custom-call | flops 1073741824 | bytes 4194304 | tf_op jit(solution)/shard_map/own_keys/pallas_call | solution.py:600
  (15 shorter events, 0.1 us)
Async XLA Ops:
  0.0 25.6 %copy-start.10 = (f32[1,31,1024]{2,0,1:T(1,128)S(1)}, f32[1,31,1024]{2,0,1:T(1,128)}, u32[]{:S(2)}) copy-start(f32[1,31,1024]{2,0,1:T(1,128)} %param.15) | copy-start | bytes 380932
  4.4 22.6 %copy-start.4 = (bf16[128,1024]{1,0:T(8,128)(2,1)S(1)}, bf16[128,1024]{1,0:T(8,128)(2,1)}, u32[]{:S(2)}) copy-start(bf16[128,1024]{1,0:T(8,128)(2,1)} %get-tuple-element.54.kept_ref) | copy-start | bytes 786436
  4.4 18.5 %collective-permute-start.6 = (bf16[176,1024]{1,0:T(8,128)(2,1)}, bf16[176,1024]{1,0:T(8,128)(2,1)S(1)}, u32[]{:S(2)}, u32[]{:S(2)}) collective-permute-start(bf16[176,1024]{1,0:T(8,128)(2,1)} %get-tuple-element.50), channel_id=1, source_target_pairs={{0,4},{2,6},{4,8},{6,10},{8,12},{10,14},{12,16},{14,18},{16,20},{1... | collective-permute-start | bytes 1081352 | tf_op jit(solution)/shard_map/ppermute | solution.py:636
  7.7 8.4 %collective-permute-start.2 = (bf16[128,512]{1,0:T(8,128)(2,1)}, bf16[128,512]{1,0:T(8,128)(2,1)S(1)}, u32[]{:S(2)}, u32[]{:S(2)}) collective-permute-start(bf16[128,512]{1,0:T(8,128)(2,1)} %get-tuple-element.43.queries_ref), channel_id=1, source_target_pairs={{0,2},{2,0},{4,6},{6,4},{8,10},{10,8},{12,14},{14,12},{16,18},{18,... | collective-permute-start | bytes 393224 | tf_op jit(solution)/shard_map/ppermute | solution.py:636
  8.7 10.2 %collective-permute-start.1 = (bf16[128,512]{1,0:T(8,128)(2,1)}, bf16[128,512]{1,0:T(8,128)(2,1)S(1)}, u32[]{:S(2)}, u32[]{:S(2)}) collective-permute-start(bf16[128,512]{1,0:T(8,128)(2,1)} %get-tuple-element.43.queries_ref), channel_id=1, source_target_pairs={{8,0},{10,2},{12,4},{14,6},{16,8},{18,10},{20,12},{22,14},{24,16},... | collective-permute-start | bytes 393224 | tf_op jit(solution)/shard_map/ppermute | solution.py:636
  10.8 12.7 %collective-permute-start.7 = (bf16[128,1024]{1,0:T(8,128)(2,1)}, bf16[128,1024]{1,0:T(8,128)(2,1)S(1)}, u32[]{:S(2)}, u32[]{:S(2)}) collective-permute-start(bf16[128,1024]{1,0:T(8,128)(2,1)} %get-tuple-element.54.kept_ref), channel_id=1, source_target_pairs={{0,8},{2,10},{4,12},{6,14},{8,16},{10,18},{12,20},{14,22},{16,24},... | collective-permute-start | bytes 786440 | tf_op jit(solution)/shard_map/ppermute | solution.py:636
  14.0 7.5 %collective-permute-start = (bf16[128,512]{1,0:T(8,128)(2,1)}, bf16[128,512]{1,0:T(8,128)(2,1)S(1)}, u32[]{:S(2)}, u32[]{:S(2)}) collective-permute-start(bf16[128,512]{1,0:T(8,128)(2,1)} %get-tuple-element.43.queries_ref), channel_id=1, source_target_pairs={{4,0},{6,2},{8,4},{10,6},{12,8},{14,10},{16,12},{18,14},{20,16},{2... | collective-permute-start | bytes 393224 | tf_op jit(solution)/shard_map/ppermute | solution.py:636
  16.1 10.9 %copy-start.7 = (s32[16]{0:T(128)S(1)}, s32[16]{0:T(128)}, u32[]{:S(2)}) copy-start(s32[16]{0:T(128)} %valid_ref.13) | copy-start | bytes 196
  16.1 10.8 %collective-permute-start.5 = (bf16[208,1024]{1,0:T(8,128)(2,1)}, bf16[208,1024]{1,0:T(8,128)(2,1)S(1)}, u32[]{:S(2)}, u32[]{:S(2)}) collective-permute-start(bf16[208,1024]{1,0:T(8,128)(2,1)} %get-tuple-element.44), channel_id=1, source_target_pairs={{2,0},{4,2},{6,4},{8,6},{10,8},{12,10},{14,12},{16,14},{18,16},{20... | collective-permute-start | bytes 1277960 | tf_op jit(solution)/shard_map/ppermute | solution.py:636
  18.9 4.0 %collective-permute-start.4 = (bf16[128,512]{1,0:T(8,128)(2,1)S(1)}, bf16[128,512]{1,0:T(8,128)(2,1)S(1)}, u32[]{:S(2)}, u32[]{:S(2)}) collective-permute-start(bf16[128,512]{1,0:T(8,128)(2,1)S(1)} %collective-permute-done.1.query_next4_ref), channel_id=1, source_target_pairs={{0,2},{2,0},{4,6},{6,4},{8,10},{10,8},{12,14},{14,12},{16,18},{18,... | collective-permute-start | bytes 393224 | tf_op jit(solution)/shard_map/ppermute | solution.py:636
  21.5 5.5 %collective-permute-start.8 = (bf16[176,1024]{1,0:T(8,128)(2,1)}, bf16[176,1024]{1,0:T(8,128)(2,1)S(1)}, u32[]{:S(2)}, u32[]{:S(2)}) collective-permute-start(bf16[176,1024]{1,0:T(8,128)(2,1)} %get-tuple-element.50), channel_id=1, source_target_pairs={{0,2},{2,0},{4,6},{6,4},{8,10},{10,8},{12,14},{14,12},{16,18},{18,... | collective-permute-start | bytes 1081352 | tf_op jit(solution)/shard_map/ppermute | solution.py:636
  22.9 4.1 %collective-permute-start.9 = (bf16[176,1024]{1,0:T(8,128)(2,1)S(1)}, bf16[176,1024]{1,0:T(8,128)(2,1)S(1)}, u32[]{:S(2)}, u32[]{:S(2)}) collective-permute-start(bf16[176,1024]{1,0:T(8,128)(2,1)S(1)} %collective-permute-done.6.back2_ref), channel_id=1, source_target_pairs={{0,2},{2,0},{4,6},{6,4},{8,10},{10,8},{12,14},{14,12},{16,18},{18,... | collective-permute-start | bytes 1081352 | tf_op jit(solution)/shard_map/ppermute | solution.py:636
  22.9 2.0 %collective-permute-start.3 = (bf16[128,512]{1,0:T(8,128)(2,1)S(1)}, bf16[128,512]{1,0:T(8,128)(2,1)S(1)}, u32[]{:S(2)}, u32[]{:S(2)}) collective-permute-start(bf16[128,512]{1,0:T(8,128)(2,1)S(1)} %collective-permute-done.query_next2_ref), channel_id=1, source_target_pairs={{0,2},{2,0},{4,6},{6,4},{8,10},{10,8},{12,14},{14,12},{16,18},{18,... | collective-permute-start | bytes 393224 | tf_op jit(solution)/shard_map/ppermute | solution.py:636
  23.4 3.5 %collective-permute-start.10 = (bf16[128,1024]{1,0:T(8,128)(2,1)S(1)}, bf16[128,1024]{1,0:T(8,128)(2,1)S(1)}, u32[]{:S(2)}, u32[]{:S(2)}) collective-permute-start(bf16[128,1024]{1,0:T(8,128)(2,1)S(1)} %collective-permute-done.7.back4_ref), channel_id=1, source_target_pairs={{0,2},{2,0},{4,6},{6,4},{8,10},{10,8},{12,14},{14,12},{16,18},{18,... | collective-permute-start | bytes 786440 | tf_op jit(solution)/shard_map/ppermute | solution.py:636
  24.9 6.6 %collective-permute-start.11 = (bf16[128,1024]{1,0:T(8,128)(2,1)}, bf16[128,1024]{1,0:T(8,128)(2,1)S(1)}, u32[]{:S(2)}, u32[]{:S(2)}) collective-permute-start(bf16[128,1024]{1,0:T(8,128)(2,1)} %get-tuple-element.54.kept_ref), channel_id=1, source_target_pairs={{2,12},{6,16},{10,20},{14,24},{18,28},{3,13},{7,17},{11,21},{15,25... | collective-permute-start | bytes 786440 | tf_op jit(solution)/shard_map/ppermute | solution.py:636
  25.6 5.9 %copy-start = (bf16[1,128,1024]{2,1,0:T(8,128)(2,1)S(1)}, bf16[1,128,1024]{2,1,0:T(8,128)(2,1)}, u32[]{:S(2)}) copy-start(bf16[1,128,1024]{2,1,0:T(8,128)(2,1)} %param.9) | copy-start | bytes 786436
  25.6 5.9 %copy-start.3 = (bf16[1,512,1024]{2,1,0:T(8,128)(2,1)S(1)}, bf16[1,512,1024]{2,1,0:T(8,128)(2,1)}, u32[]{:S(2)}) copy-start(bf16[1,512,1024]{2,1,0:T(8,128)(2,1)} %param.14) | copy-start | bytes 3145732
  25.7 5.9 %copy-start.5 = (bf16[128,1024]{1,0:T(8,128)(2,1)S(1)}, bf16[128,1024]{1,0:T(8,128)(2,1)}, u32[]{:S(2)}) copy-start(bf16[128,1024]{1,0:T(8,128)(2,1)} %top_ref.3) | copy-start | bytes 786436
  27.0 0.9 %copy-start.9 = (bf16[128,512]{1,0:T(8,128)(2,1)S(1)}, bf16[128,512]{1,0:T(8,128)(2,1)}, u32[]{:S(2)}) copy-start(bf16[128,512]{1,0:T(8,128)(2,1)} %get-tuple-element.43.queries_ref) | copy-start | bytes 393220
  31.5 11.7 %copy-start.8 = (bf16[1,1024,512]{2,1,0:T(8,128)(2,1)S(1)}, bf16[1,1024,512]{2,1,0:T(8,128)(2,1)}, u32[]{:S(2)}) copy-start(bf16[1,1024,512]{2,1,0:T(8,128)(2,1)} %param.11) | copy-start | bytes 3145732
  39.3 7.6 %collective-permute-start.13 = (bf16[144,512]{1,0:T(8,128)(2,1)S(1)}, bf16[144,512]{1,0:T(8,128)(2,1)S(1)}, u32[]{:S(2)}, u32[]{:S(2)}) collective-permute-start(bf16[144,512]{1,0:T(8,128)(2,1)S(1)} %get-tuple-element.56.message_ref), channel_id=1, source_target_pairs={{9,1},{11,3},{13,5},{15,7},{17,9},{19,11},{21,13},{23,15},{25,17},... | collective-permute-start | bytes 442376 | tf_op jit(solution)/shard_map/ppermute | solution.py:636
  39.9 7.0 %collective-permute-start.12 = (bf16[144,512]{1,0:T(8,128)(2,1)S(1)}, bf16[144,512]{1,0:T(8,128)(2,1)S(1)}, u32[]{:S(2)}, u32[]{:S(2)}) collective-permute-start(bf16[144,512]{1,0:T(8,128)(2,1)S(1)} %get-tuple-element.56.message_ref), channel_id=1, source_target_pairs={{5,1},{7,3},{9,5},{11,7},{13,9},{15,11},{17,13},{19,15},{21,17},{2... | collective-permute-start | bytes 442376 | tf_op jit(solution)/shard_map/ppermute | solution.py:636
  40.6 6.9 %collective-permute-start.14 = (bf16[144,512]{1,0:T(8,128)(2,1)S(1)}, bf16[144,512]{1,0:T(8,128)(2,1)S(1)}, u32[]{:S(2)}, u32[]{:S(2)}) collective-permute-start(bf16[144,512]{1,0:T(8,128)(2,1)S(1)} %get-tuple-element.56.message_ref), channel_id=1, source_target_pairs={{0,2},{2,0},{4,6},{6,4},{8,10},{10,8},{12,14},{14,12},{16,18},{18,... | collective-permute-start | bytes 442376 | tf_op jit(solution)/shard_map/ppermute | solution.py:636
  43.2 5.3 %copy-start.1 = (bf16[1,1024,512]{2,1,0:T(8,128)(2,1)S(1)}, bf16[1,1024,512]{2,1,0:T(8,128)(2,1)}, u32[]{:S(2)}) copy-start(bf16[1,1024,512]{2,1,0:T(8,128)(2,1)} %param.12) | copy-start | bytes 3145732
  43.2 5.3 %copy-start.2 = (bf16[1,1024,512]{2,1,0:T(8,128)(2,1)S(1)}, bf16[1,1024,512]{2,1,0:T(8,128)(2,1)}, u32[]{:S(2)}) copy-start(bf16[1,1024,512]{2,1,0:T(8,128)(2,1)} %param.13) | copy-start | bytes 3145732
  46.9 1.7 %copy-start.6 = (f32[1,1024]{1,0:T(1,128)S(1)}, f32[1,1024]{1,0:T(1,128)}, u32[]{:S(2)}) copy-start(f32[1,1024]{1,0:T(1,128)} %gain_ref.5) | copy-start | bytes 12292
  46.9 1.4 %collective-permute-start.15 = (bf16[144,512]{1,0:T(8,128)(2,1)S(1)}, bf16[144,512]{1,0:T(8,128)(2,1)S(1)}, u32[]{:S(2)}, u32[]{:S(2)}) collective-permute-start(bf16[144,512]{1,0:T(8,128)(2,1)S(1)} %collective-permute-done.12.next2_ref), channel_id=1, source_target_pairs={{0,2},{2,0},{4,6},{6,4},{8,10},{10,8},{12,14},{14,12},{16,18},{18,... | collective-permute-start | bytes 442376 | tf_op jit(solution)/shard_map/ppermute | solution.py:636
  47.0 1.5 %collective-permute-start.16 = (bf16[144,512]{1,0:T(8,128)(2,1)S(1)}, bf16[144,512]{1,0:T(8,128)(2,1)S(1)}, u32[]{:S(2)}, u32[]{:S(2)}) collective-permute-start(bf16[144,512]{1,0:T(8,128)(2,1)S(1)} %collective-permute-done.13.next4_ref), channel_id=1, source_target_pairs={{0,2},{2,0},{4,6},{6,4},{8,10},{10,8},{12,14},{14,12},{16,18},{18,... | collective-permute-start | bytes 442376 | tf_op jit(solution)/shard_map/ppermute | solution.py:636
  52.0 14.5 %collective-permute-start.17 = (bf16[128,1024]{1,0:T(8,128)(2,1)S(1)}, bf16[128,1024]{1,0:T(8,128)(2,1)S(1)}, u32[]{:S(2)}, u32[]{:S(2)}) collective-permute-start(bf16[128,1024]{1,0:T(8,128)(2,1)S(1)} %get-tuple-element.65), channel_id=1, source_target_pairs={{1,0},{3,2},{5,4},{7,6},{9,8},{11,10},{13,12},{15,14},{17,16},{19,... | collective-permute-start | bytes 786440 | tf_op jit(solution)/shard_map/ppermute | solution.py:636
  59.0 7.5 %collective-permute-start.18 = (bf16[32,1024]{1,0:T(8,128)(2,1)S(1)}, bf16[32,1024]{1,0:T(8,128)(2,1)S(1)}, u32[]{:S(2)}, u32[]{:S(2)}) collective-permute-start(bf16[32,1024]{1,0:T(8,128)(2,1)S(1)} %get-tuple-element.66), channel_id=1, source_target_pairs={{3,0},{5,2},{7,4},{9,6},{11,8},{13,10},{15,12},{17,14},{19,16},{21... | collective-permute-start | bytes 196616 | tf_op jit(solution)/shard_map/ppermute | solution.py:636
  69.7 9.4 %collective-permute-start.20 = (bf16[144,512]{1,0:T(8,128)(2,1)S(1)}, bf16[144,512]{1,0:T(8,128)(2,1)S(1)}, u32[]{:S(2)}, u32[]{:S(2)}) collective-permute-start(bf16[144,512]{1,0:T(8,128)(2,1)S(1)} %get-tuple-element.68.message_ref), channel_id=1, source_target_pairs={{8,0},{10,2},{12,4},{14,6},{16,8},{18,10},{20,12},{22,14},{24,16},... | collective-permute-start | bytes 442376 | tf_op jit(solution)/shard_map/ppermute | solution.py:636
  71.9 7.1 %collective-permute-start.19 = (bf16[144,512]{1,0:T(8,128)(2,1)S(1)}, bf16[144,512]{1,0:T(8,128)(2,1)S(1)}, u32[]{:S(2)}, u32[]{:S(2)}) collective-permute-start(bf16[144,512]{1,0:T(8,128)(2,1)S(1)} %get-tuple-element.68.message_ref), channel_id=1, source_target_pairs={{4,0},{6,2},{8,4},{10,6},{12,8},{14,10},{16,12},{18,14},{20,16},{2... | collective-permute-start | bytes 442376 | tf_op jit(solution)/shard_map/ppermute | solution.py:636
  73.9 7.5 %collective-permute-start.21 = (bf16[144,512]{1,0:T(8,128)(2,1)S(1)}, bf16[144,512]{1,0:T(8,128)(2,1)S(1)}, u32[]{:S(2)}, u32[]{:S(2)}) collective-permute-start(bf16[144,512]{1,0:T(8,128)(2,1)S(1)} %get-tuple-element.68.message_ref), channel_id=1, source_target_pairs={{0,2},{2,0},{4,6},{6,4},{8,10},{10,8},{12,14},{14,12},{16,18},{18,... | collective-permute-start | bytes 442376 | tf_op jit(solution)/shard_map/ppermute | solution.py:636
  79.1 3.3 %collective-permute-start.22 = (bf16[144,512]{1,0:T(8,128)(2,1)S(1)}, bf16[144,512]{1,0:T(8,128)(2,1)S(1)}, u32[]{:S(2)}, u32[]{:S(2)}) collective-permute-start(bf16[144,512]{1,0:T(8,128)(2,1)S(1)} %collective-permute-done.19.next2_ref), channel_id=1, source_target_pairs={{0,2},{2,0},{4,6},{6,4},{8,10},{10,8},{12,14},{14,12},{16,18},{18,... | collective-permute-start | bytes 442376 | tf_op jit(solution)/shard_map/ppermute | solution.py:636
  81.3 1.4 %collective-permute-start.23 = (bf16[144,512]{1,0:T(8,128)(2,1)S(1)}, bf16[144,512]{1,0:T(8,128)(2,1)S(1)}, u32[]{:S(2)}, u32[]{:S(2)}) collective-permute-start(bf16[144,512]{1,0:T(8,128)(2,1)S(1)} %collective-permute-done.20.next4_ref), channel_id=1, source_target_pairs={{0,2},{2,0},{4,6},{6,4},{8,10},{10,8},{12,14},{14,12},{16,18},{18,... | collective-permute-start | bytes 442376 | tf_op jit(solution)/shard_map/ppermute | solution.py:636

commit v6 on v5

--- a/solution.py
+++ b/solution.py
@@ -1,3 +1,5 @@
+import functools
+
 import jax
 import jax.numpy as jnp
 from jax import lax
@@ -252,7 +254,7 @@
         total_low[:, lanes] = total.astype(BF16)
         return carry
 
-    lax.fori_loop(0, upstream_ref.shape[1] // PAIR, conv_step, 0)
+    lax.fori_loop(0, upstream_ref.shape[1] // PAIR, conv_step, 0, unroll=True)
     out_grad = dot_nt(total_low[...], w_out_ref[...]).astype(BF16)
     message_ref[0:ROWS, :] = out_grad
     product = out_grad.astype(F32) * attended[...].astype(F32)
@@ -348,7 +350,7 @@
         slope_ref[:, lanes] = gate * (1.0 + output * (1.0 - gate))
         return carry
 
-    lax.fori_loop(0, own_ref.shape[1] // PAIR, conv_step, 0)
+    lax.fori_loop(0, own_ref.shape[1] // PAIR, conv_step, 0, unroll=True)
     first = ROWS + EDGE + half_edge
     mixer_body(
         counts[LEFT + 1],
@@ -585,10 +587,15 @@
         - unit * jnp.mean(scaled * unit, axis=-1, keepdims=True)
     )
     grad = total_ref[...] + back
-    out_ref[...] = grad.astype(BF16)
-    edge_ref[...] = grad[0:EDGE].astype(BF16)
+    if out_ref is not None:
+        out_ref[...] = grad.astype(BF16)
+        edge_ref[...] = grad[0:EDGE].astype(BF16)
     mine = lax.axis_index("section") == keep_ref[0]
     held_ref[...] = jnp.where(mine, grad, result_ref[...].astype(F32)).astype(BF16)
+
+
+def last_key_kernel(operands, *refs):
+    key_kernel(*refs[:operands], None, None, *refs[operands:])
 
 
 def call(kernel, name, operands, outs, scratch, copies=0, limit=VMEM_LIMIT):
@@ -770,46 +777,55 @@
                 ((ROWS, wide), BF16),
             ],
             )
-        grad2, grad4, partial = lax.optimization_barrier((grad2, grad4, partial))
+        grad2 = after(grad2, partial)
+        grad4 = after(grad4, partial)
         peer_grad2 = moved(grad2, swap)
         peer_grad4 = moved(grad4, swap)
-        input_grad, edge, result = call(
-            key_kernel,
-            "own_keys",
-            placed(
-                "svvvvvvvvvvvvvvvvvvvvs",
-                group_valid,
-                kept,
-                query_next2,
-                query_next4,
-                query_peer,
-                query_peer_next2,
-                query_peer_next4,
-                grad2,
-                grad4,
-                peer_grad,
-                peer_grad2,
-                peer_grad4,
-                key_weight,
-                value_weight,
-                norm_gain,
-                own,
-                total,
-                partial,
-                key_sum,
-                value_sum,
-                result,
-                jnp.full((1,), layer, jnp.int32),
-            ),
-            [((ROWS, width), BF16), ((EDGE, width), BF16), ((ROWS, width), BF16)],
-            [
-                ((LEFT * ROWS, wide), BF16),
-                ((LEFT * ROWS, wide), BF16),
-                ((LEFT * 16, wide), BF16),
-                ((16, LEFT * ROWS), F32),
-                ((ROWS, wide), BF16),
-                ((ROWS, wide), BF16),
-            ],
+        key_operands = placed(
+            "svvvvvvvvvvvvvvvvvvvvs",
+            group_valid,
+            kept,
+            query_next2,
+            query_next4,
+            query_peer,
+            query_peer_next2,
+            query_peer_next4,
+            grad2,
+            grad4,
+            peer_grad,
+            peer_grad2,
+            peer_grad4,
+            key_weight,
+            value_weight,
+            norm_gain,
+            own,
+            total,
+            partial,
+            key_sum,
+            value_sum,
+            result,
+            jnp.full((1,), layer, jnp.int32),
+            )
+        key_scratch = [
+            ((LEFT * ROWS, wide), BF16),
+            ((LEFT * ROWS, wide), BF16),
+            ((LEFT * 16, wide), BF16),
+            ((16, LEFT * ROWS), F32),
+            ((ROWS, wide), BF16),
+            ((ROWS, wide), BF16),
+        ]
+        whole = ((ROWS, width), BF16)
+        if layer > 0:
+            input_grad, edge, result = call(
+                key_kernel, "own_keys", key_operands, [whole, ((EDGE, width), BF16), whole], key_scratch
+            )
+        else:
+            (result,) = call(
+                functools.partial(last_key_kernel, len(key_operands)),
+                "last_keys",
+                key_operands,
+                [whole],
+                key_scratch,
             )
         if layer > 0:
             upstream = moved(

time: 87.1 us -> 85.6 us (0.983)
  Pallas kernels: 33.5 us -> 32.6 us
    pallas_call x8, Pallas kernels: 33.5 us -> 32.6 us  [call(): pl.pallas_call(kernel, name=name, in_specs=[kinds[place] for _, place in...]
  transfers between devices with their start and end apart: 24 -> 24, of which waited for: 8 -> 7; matrix products, arithmetic and copies ran while one was open for 0% -> 0% of each run, Pallas kernels for 13% -> 13%
where the time goes in v6:
time: 85.6 us; the launch traced here: 85.3 us
  starting transfers between devices  38.6 us (45%)
  Pallas kernels  32.6 us (38%)
  waiting for transfers between devices  12.8 us (15%)
  local copies, waits for them, and re-layouts  0.98 us (1%)
    ppermute x24, starting transfers between devices, moved(): return lax.ppermute(value, ('tm', 'section'), pairs)  38.6 us
    pallas_call x8, Pallas kernels, call(): pl.pallas_call(kernel, name=name, in_specs=[kinds[place] for _, place in...  32.6 us
    ppermute x24, waiting for transfers between devices, moved(): return lax.ppermute(value, ('tm', 'section'), pairs)  12.8 us
  transfers between devices with their start and end apart: 24, of which 7 were waited for; matrix products, arithmetic and copies ran while one was open for 0% of the time, Pallas kernels for 13%

profile of v6, /device:TPU:19, one launch (start us, length us, event | category | flops | bytes accessed | tf_op | source)
XLA Modules:
  0.0 85.3 jit_solution(1413895074665574239)
XLA Ops:
  0.0 4.4 %project.1 = (bf16[128,512]{1,0:T(8,128)(2,1)}, bf16[128,1024]{1,0:T(8,128)(2,1)}, bf16[176,1024]{1,0:T(8,128)(2,1)}, bf16[208,1024]{1,0:T(8,128)(2,1)}) custom-call(bf16[128,1024]{1,0:T(8,128)(2,1)} %bitcast.9, bf16[128,1024]{1,0:T(8,128)(2,1)} %top_ref.3, f32[1,1024]{1,0:T(1,128)} %refs_14_.1, bf16[1024,512]{1,0:T(8,128)(2,1)} %bitcast.24, ...), custom_call_target="tpu_custom_call" | custom-call | flops 1073741824 | bytes 4194304 | tf_op jit(solution)/shard_map/project/pallas_call | solution.py:607
  4.4 0.0 copy-start.4
  4.4 3.3 %collective-permute-start.6 = (bf16[176,1024]{1,0:T(8,128)(2,1)}, bf16[176,1024]{1,0:T(8,128)(2,1)S(1)}, u32[]{:S(2)}, u32[]{:S(2)}) collective-permute-start(bf16[176,1024]{1,0:T(8,128)(2,1)} %get-tuple-element.47), channel_id=1, source_target_pairs={{0,4},{2,6},{4,8},{6,10},{8,12},{10,14},{12,16},{14,18},{16,20},{1... | collective-permute-start | bytes 1081352 | tf_op jit(solution)/shard_map/ppermute | solution.py:643
  7.7 1.0 %collective-permute-start.2 = (bf16[128,512]{1,0:T(8,128)(2,1)}, bf16[128,512]{1,0:T(8,128)(2,1)S(1)}, u32[]{:S(2)}, u32[]{:S(2)}) collective-permute-start(bf16[128,512]{1,0:T(8,128)(2,1)} %get-tuple-element.40.queries_ref), channel_id=1, source_target_pairs={{0,2},{2,0},{4,6},{6,4},{8,10},{10,8},{12,14},{14,12},{16,18},{18,... | collective-permute-start | bytes 393224 | tf_op jit(solution)/shard_map/ppermute | solution.py:643
  8.7 2.1 %collective-permute-start.1 = (bf16[128,512]{1,0:T(8,128)(2,1)}, bf16[128,512]{1,0:T(8,128)(2,1)S(1)}, u32[]{:S(2)}, u32[]{:S(2)}) collective-permute-start(bf16[128,512]{1,0:T(8,128)(2,1)} %get-tuple-element.40.queries_ref), channel_id=1, source_target_pairs={{8,0},{10,2},{12,4},{14,6},{16,8},{18,10},{20,12},{22,14},{24,16},... | collective-permute-start | bytes 393224 | tf_op jit(solution)/shard_map/ppermute | solution.py:643
  10.8 3.2 %collective-permute-start.7 = (bf16[128,1024]{1,0:T(8,128)(2,1)}, bf16[128,1024]{1,0:T(8,128)(2,1)S(1)}, u32[]{:S(2)}, u32[]{:S(2)}) collective-permute-start(bf16[128,1024]{1,0:T(8,128)(2,1)} %get-tuple-element.51.kept_ref.refs_1_), channel_id=1, source_target_pairs={{0,8},{2,10},{4,12},{6,14},{8,16},{10,18},{12,20},{14,22},{16,24},... | collective-permute-start | bytes 786440 | tf_op jit(solution)/shard_map/ppermute | solution.py:643
  14.0 2.1 %collective-permute-start = (bf16[128,512]{1,0:T(8,128)(2,1)}, bf16[128,512]{1,0:T(8,128)(2,1)S(1)}, u32[]{:S(2)}, u32[]{:S(2)}) collective-permute-start(bf16[128,512]{1,0:T(8,128)(2,1)} %get-tuple-element.40.queries_ref), channel_id=1, source_target_pairs={{4,0},{6,2},{8,4},{10,6},{12,8},{14,10},{16,12},{18,14},{20,16},{2... | collective-permute-start | bytes 393224 | tf_op jit(solution)/shard_map/ppermute | solution.py:643
  16.1 0.0 collective-permute-done.2.query_peer_ref.refs_4_
  16.1 0.0 copy-start.7
  16.1 2.8 %collective-permute-start.5 = (bf16[208,1024]{1,0:T(8,128)(2,1)}, bf16[208,1024]{1,0:T(8,128)(2,1)S(1)}, u32[]{:S(2)}, u32[]{:S(2)}) collective-permute-start(bf16[208,1024]{1,0:T(8,128)(2,1)} %get-tuple-element.41), channel_id=1, source_target_pairs={{2,0},{4,2},{6,4},{8,6},{10,8},{12,10},{14,12},{16,14},{18,16},{20... | collective-permute-start | bytes 1277960 | tf_op jit(solution)/shard_map/ppermute | solution.py:643
  18.9 0.0 collective-permute-done.1.query_next4_ref.refs_3_
  18.9 0.7 collective-permute-start.4
  19.7 1.8 %collective-permute-done.query_next2_ref.refs_2_ = bf16[128,512]{1,0:T(8,128)(2,1)S(1)} collective-permute-done((bf16[128,512]{1,0:T(8,128)(2,1)}, bf16[128,512]{1,0:T(8,128)(2,1)S(1)}, u32[]{:S(2)}, u32[]{:S(2)}) %collective-permute-start) | collective-permute-done | bytes 131104 | tf_op jit(solution)/shard_map/ppermute | solution.py:643
  21.5 1.4 %collective-permute-start.8 = (bf16[176,1024]{1,0:T(8,128)(2,1)}, bf16[176,1024]{1,0:T(8,128)(2,1)S(1)}, u32[]{:S(2)}, u32[]{:S(2)}) collective-permute-start(bf16[176,1024]{1,0:T(8,128)(2,1)} %get-tuple-element.47), channel_id=1, source_target_pairs={{0,2},{2,0},{4,6},{6,4},{8,10},{10,8},{12,14},{14,12},{16,18},{18,... | collective-permute-start | bytes 1081352 | tf_op jit(solution)/shard_map/ppermute | solution.py:643
  22.9 0.0 collective-permute-done.6.back2_ref
  22.9 0.0 collective-permute-start.9
  22.9 0.0 collective-permute-done.4.query_peer_next4_ref.refs_6_
  22.9 0.5 collective-permute-start.3
  23.4 0.0 collective-permute-done.7.back4_ref
  23.4 0.1 collective-permute-start.10
  23.5 1.4 %collective-permute-done.3.query_peer_next2_ref.refs_5_ = bf16[128,512]{1,0:T(8,128)(2,1)S(1)} collective-permute-done((bf16[128,512]{1,0:T(8,128)(2,1)S(1)}, bf16[128,512]{1,0:T(8,128)(2,1)S(1)}, u32[]{:S(2)}, u32[]{:S(2)}) %collective-permute-start.3) | collective-permute-done | bytes 131104 | tf_op jit(solution)/shard_map/ppermute | solution.py:643
  24.9 0.7 collective-permute-start.11
  25.6 0.0 copy-start
  25.6 0.0 copy-start.3
  25.7 0.0 copy-start.5
  25.7 1.3 %collective-permute-done.5.after_ref = bf16[208,1024]{1,0:T(8,128)(2,1)S(1)} collective-permute-done((bf16[208,1024]{1,0:T(8,128)(2,1)}, bf16[208,1024]{1,0:T(8,128)(2,1)S(1)}, u32[]{:S(2)}, u32[]{:S(2)}) %collective-permute-start.5) | collective-permute-done | bytes 426016 | tf_op jit(solution)/shard_map/ppermute | solution.py:643
  27.0 0.0 collective-permute-done.8.peer_ref
  27.0 0.0 collective-permute-done.10.peer_back4_ref
  27.0 0.0 collective-permute-done.9.peer_back2_ref
  27.0 0.9 %copy-done.9 = bf16[128,512]{1,0:T(8,128)(2,1)S(1)} copy-done((bf16[128,512]{1,0:T(8,128)(2,1)S(1)}, bf16[128,512]{1,0:T(8,128)(2,1)}, u32[]{:S(2)}) %copy-start.9) | copy-done | bytes 131096
  27.9 3.6 %attend.1 = (bf16[160,512]{1,0:T(8,128)(2,1)S(1)}, f32[128,128]{1,0:T(8,128)S(1)}) custom-call(s32[16]{0:T(128)S(1)} %copy-done.7, bf16[128,512]{1,0:T(8,128)(2,1)S(1)} %copy-done.9, bf16[128,1024]{1,0:T(8,128)(2,1)S(1)} %copy-done.4, bf16[176,1024]{1,0:T(8,128)(2,1)S(1)} %collective-permute-done.6.back2_ref, ...), custom_call_target="tpu_custom_call" | custom-call | flops 1073741824 | bytes 4194304 | tf_op jit(solution)/shard_map/attend/pallas_call | solution.py:607
  31.5 0.0 collective-permute-done.11.back5_ref
  31.5 0.0 copy-start.8
  31.5 7.2 %mix.1 = (f32[160,1024]{1,0:T(8,128)S(1)}, f32[128,1024]{1,0:T(8,128)S(1)}, bf16[144,512]{1,0:T(8,128)(2,1)S(1)}, f32[128,128]{1,0:T(8,128)S(1)}) custom-call(s32[16]{0:T(128)S(1)} %copy-done.7, bf16[128,1024]{1,0:T(8,128)(2,1)S(1)} %bitcast.10, bf16[128,1024]{1,0:T(8,128)(2,1)S(1)} %copy-done.5, bf16[160,512]{1,0:T(8,128)(2,1)S(1)} %get-tuple-element.49.attended_ref, ...), custom_call_target="tpu_custom_call" | custom-call | flops 1073741824 | bytes 4194304 | tf_op jit(solution)/shard_map/mix/pallas_call | solution.py:607
  38.7 0.7 collective-permute-start.13
  39.4 0.7 collective-permute-start.12
  40.1 2.6 %collective-permute-start.14 = (bf16[144,512]{1,0:T(8,128)(2,1)S(1)}, bf16[144,512]{1,0:T(8,128)(2,1)S(1)}, u32[]{:S(2)}, u32[]{:S(2)}) collective-permute-start(bf16[144,512]{1,0:T(8,128)(2,1)S(1)} %get-tuple-element.53.message_ref), channel_id=1, source_target_pairs={{0,2},{2,0},{4,6},{6,4},{8,10},{10,8},{12,14},{14,12},{16,18},{18,... | collective-permute-start | bytes 442376 | tf_op jit(solution)/shard_map/ppermute | solution.py:643
  42.7 3.8 %own_queries.2 = (f32[128,1024]{1,0:T(8,128)S(1)}, f32[128,512]{1,0:T(8,128)S(1)}, f32[128,512]{1,0:T(8,128)S(1)}) custom-call(s32[16]{0:T(128)S(1)} %copy-done.7, bf16[128,512]{1,0:T(8,128)(2,1)S(1)} %copy-done.9, bf16[128,1024]{1,0:T(8,128)(2,1)S(1)} %copy-done.4, bf16[176,1024]{1,0:T(8,128)(2,1)S(1)} %collective-permute-done.6.back2_ref, ...), custom_call_target="tpu_custom_call" | custom-call | flops 1073741824 | bytes 4194304 | tf_op jit(solution)/shard_map/own_queries/pallas_call | solution.py:607
  46.5 0.0 copy-start.6
  46.5 0.0 collective-permute-done.13.next4_ref
  46.6 0.0 collective-permute-done.12.next2_ref
  46.6 0.1 collective-permute-start.15
  46.7 0.5 collective-permute-start.16
  47.1 0.0 collective-permute-done.14.peer_ref
  47.1 0.9 %collective-permute-done.15.peer_next2_ref = bf16[144,512]{1,0:T(8,128)(2,1)S(1)} collective-permute-done((bf16[144,512]{1,0:T(8,128)(2,1)S(1)}, bf16[144,512]{1,0:T(8,128)(2,1)S(1)}, u32[]{:S(2)}, u32[]{:S(2)}) %collective-permute-start.15) | collective-permute-done | bytes 147488 | tf_op jit(solution)/shard_map/ppermute | solution.py:643
  48.0 0.2 collective-permute-done.16.peer_next4_ref
  48.2 3.3 %own_keys.1 = (bf16[128,1024]{1,0:T(8,128)(2,1)S(1)}, bf16[32,1024]{1,0:T(8,128)(2,1)S(1)}, bf16[128,1024]{1,0:T(8,128)(2,1)S(1)}) custom-call(s32[16]{0:T(128)S(1)} %copy-done.7, bf16[128,1024]{1,0:T(8,128)(2,1)S(1)} %copy-done.4, bf16[128,512]{1,0:T(8,128)(2,1)S(1)} %collective-permute-done.query_next2_ref.refs_2_, ...), custom_call_target="tpu_custom_call" | custom-call | flops 1073741824 | bytes 4194304 | tf_op jit(solution)/shard_map/own_keys/pallas_call | solution.py:607
  51.5 6.8 %collective-permute-start.17 = (bf16[128,1024]{1,0:T(8,128)(2,1)S(1)}, bf16[128,1024]{1,0:T(8,128)(2,1)S(1)}, u32[]{:S(2)}, u32[]{:S(2)}) collective-permute-start(bf16[128,1024]{1,0:T(8,128)(2,1)S(1)} %get-tuple-element.61), channel_id=1, source_target_pairs={{1,0},{3,2},{5,4},{7,6},{9,8},{11,10},{13,12},{15,14},{17,16},{19,... | collective-permute-start | bytes 786440 | tf_op jit(solution)/shard_map/ppermute | solution.py:643
  58.3 1.3 %collective-permute-start.18 = (bf16[32,1024]{1,0:T(8,128)(2,1)S(1)}, bf16[32,1024]{1,0:T(8,128)(2,1)S(1)}, u32[]{:S(2)}, u32[]{:S(2)}) collective-permute-start(bf16[32,1024]{1,0:T(8,128)(2,1)S(1)} %get-tuple-element.62), channel_id=1, source_target_pairs={{3,0},{5,2},{7,4},{9,6},{11,8},{13,10},{15,12},{17,14},{19,16},{21... | collective-permute-start | bytes 196616 | tf_op jit(solution)/shard_map/ppermute | solution.py:643
  59.6 6.2 %collective-permute-done.18.next_ref = bf16[32,1024]{1,0:T(8,128)(2,1)S(1)} collective-permute-done((bf16[32,1024]{1,0:T(8,128)(2,1)S(1)}, bf16[32,1024]{1,0:T(8,128)(2,1)S(1)}, u32[]{:S(2)}, u32[]{:S(2)}) %collective-permute-start.18) | collective-permute-done | bytes 65568 | tf_op jit(solution)/shard_map/ppermute | solution.py:643
  65.8 0.0 collective-permute-done.17.upstream_ref
  65.8 2.8 %mixer.1 = (f32[128,1024]{1,0:T(8,128)S(1)}, bf16[144,512]{1,0:T(8,128)(2,1)S(1)}, f32[128,128]{1,0:T(8,128)S(1)}) custom-call(s32[16]{0:T(128)S(1)} %copy-done.7, bf16[128,1024]{1,0:T(8,128)(2,1)S(1)} %collective-permute-done.17.upstream_ref, bf16[32,1024]{1,0:T(8,128)(2,1)S(1)} %collective-permute-done.18.next_ref, ...), custom_call_target="tpu_custom_call" | custom-call | flops 1073741824 | bytes 4194304 | tf_op jit(solution)/shard_map/mixer/pallas_call | solution.py:607
  68.6 2.3 %collective-permute-start.20 = (bf16[144,512]{1,0:T(8,128)(2,1)S(1)}, bf16[144,512]{1,0:T(8,128)(2,1)S(1)}, u32[]{:S(2)}, u32[]{:S(2)}) collective-permute-start(bf16[144,512]{1,0:T(8,128)(2,1)S(1)} %get-tuple-element.64.message_ref), channel_id=1, source_target_pairs={{8,0},{10,2},{12,4},{14,6},{16,8},{18,10},{20,12},{22,14},{24,16},... | collective-permute-start | bytes 442376 | tf_op jit(solution)/shard_map/ppermute | solution.py:643
  70.9 1.9 %collective-permute-start.19 = (bf16[144,512]{1,0:T(8,128)(2,1)S(1)}, bf16[144,512]{1,0:T(8,128)(2,1)S(1)}, u32[]{:S(2)}, u32[]{:S(2)}) collective-permute-start(bf16[144,512]{1,0:T(8,128)(2,1)S(1)} %get-tuple-element.64.message_ref), channel_id=1, source_target_pairs={{4,0},{6,2},{8,4},{10,6},{12,8},{14,10},{16,12},{18,14},{20,16},{2... | collective-permute-start | bytes 442376 | tf_op jit(solution)/shard_map/ppermute | solution.py:643
  72.8 1.5 %collective-permute-start.21 = (bf16[144,512]{1,0:T(8,128)(2,1)S(1)}, bf16[144,512]{1,0:T(8,128)(2,1)S(1)}, u32[]{:S(2)}, u32[]{:S(2)}) collective-permute-start(bf16[144,512]{1,0:T(8,128)(2,1)S(1)} %get-tuple-element.64.message_ref), channel_id=1, source_target_pairs={{0,2},{2,0},{4,6},{6,4},{8,10},{10,8},{12,14},{14,12},{16,18},{18,... | collective-permute-start | bytes 442376 | tf_op jit(solution)/shard_map/ppermute | solution.py:643
  74.4 3.7 %own_queries.3 = (f32[128,1024]{1,0:T(8,128)S(1)}, f32[128,512]{1,0:T(8,128)S(1)}, f32[128,512]{1,0:T(8,128)S(1)}) custom-call(s32[16]{0:T(128)S(1)} %copy-done.7, bf16[128,512]{1,0:T(8,128)(2,1)S(1)} %copy-done.10, bf16[128,1024]{1,0:T(8,128)(2,1)S(1)} %copy-done.4, bf16[176,1024]{1,0:T(8,128)(2,1)S(1)} %collective-permute-done.6.back2_ref, ...), custom_call_target="tpu_custom_call" | custom-call | flops 1073741824 | bytes 4194304 | tf_op jit(solution)/shard_map/own_queries/pallas_call | solution.py:607
  78.0 0.0 collective-permute-done.20.refs_8_
  78.0 0.1 collective-permute-start.23
  78.1 0.0 collective-permute-done.19.refs_7_
  78.1 2.2 %collective-permute-start.22 = (bf16[144,512]{1,0:T(8,128)(2,1)S(1)}, bf16[144,512]{1,0:T(8,128)(2,1)S(1)}, u32[]{:S(2)}, u32[]{:S(2)}) collective-permute-start(bf16[144,512]{1,0:T(8,128)(2,1)S(1)} %collective-permute-done.19.refs_7_), channel_id=1, source_target_pairs={{0,2},{2,0},{4,6},{6,4},{8,10},{10,8},{12,14},{14,12},{16,18},{18,... | collective-permute-start | bytes 442376 | tf_op jit(solution)/shard_map/ppermute | solution.py:643
  80.3 0.0 collective-permute-done.21.refs_9_
  80.3 0.0 collective-permute-done.23.refs_11_
  80.3 1.0 %collective-permute-done.22.refs_10_ = bf16[144,512]{1,0:T(8,128)(2,1)S(1)} collective-permute-done((bf16[144,512]{1,0:T(8,128)(2,1)S(1)}, bf16[144,512]{1,0:T(8,128)(2,1)S(1)}, u32[]{:S(2)}, u32[]{:S(2)}) %collective-permute-start.22) | collective-permute-done | bytes 147488 | tf_op jit(solution)/shard_map/ppermute | solution.py:643
  81.3 3.9 %last_keys.1 = bf16[128,1024]{1,0:T(8,128)(2,1)} custom-call(s32[16]{0:T(128)S(1)} %copy-done.7, bf16[128,1024]{1,0:T(8,128)(2,1)S(1)} %copy-done.4, bf16[128,512]{1,0:T(8,128)(2,1)S(1)} %collective-permute-done.query_next2_ref.refs_2_, bf16[128,512]{1,0:T(8,128)(2,1)S(1)} %collective-permute-done.1.query_next4_ref.refs_3_, ...), custom_call_target="tpu_custom_call" | custom-call | flops 1073741824 | bytes 4194304 | tf_op jit(solution)/shard_map/last_keys/pallas_call | solution.py:607
  (17 shorter events, 0.1 us)
Async XLA Ops:
  0.0 25.6 %copy-start.11 = (f32[1,31,1024]{2,0,1:T(1,128)S(1)}, f32[1,31,1024]{2,0,1:T(1,128)}, u32[]{:S(2)}) copy-start(f32[1,31,1024]{2,0,1:T(1,128)} %param.15) | copy-start | bytes 380932
  4.4 22.6 %copy-start.4 = (bf16[128,1024]{1,0:T(8,128)(2,1)S(1)}, bf16[128,1024]{1,0:T(8,128)(2,1)}, u32[]{:S(2)}) copy-start(bf16[128,1024]{1,0:T(8,128)(2,1)} %get-tuple-element.51.kept_ref.refs_1_) | copy-start | bytes 786436
  4.4 18.5 %collective-permute-start.6 = (bf16[176,1024]{1,0:T(8,128)(2,1)}, bf16[176,1024]{1,0:T(8,128)(2,1)S(1)}, u32[]{:S(2)}, u32[]{:S(2)}) collective-permute-start(bf16[176,1024]{1,0:T(8,128)(2,1)} %get-tuple-element.47), channel_id=1, source_target_pairs={{0,4},{2,6},{4,8},{6,10},{8,12},{10,14},{12,16},{14,18},{16,20},{1... | collective-permute-start | bytes 1081352 | tf_op jit(solution)/shard_map/ppermute | solution.py:643
  7.7 8.4 %collective-permute-start.2 = (bf16[128,512]{1,0:T(8,128)(2,1)}, bf16[128,512]{1,0:T(8,128)(2,1)S(1)}, u32[]{:S(2)}, u32[]{:S(2)}) collective-permute-start(bf16[128,512]{1,0:T(8,128)(2,1)} %get-tuple-element.40.queries_ref), channel_id=1, source_target_pairs={{0,2},{2,0},{4,6},{6,4},{8,10},{10,8},{12,14},{14,12},{16,18},{18,... | collective-permute-start | bytes 393224 | tf_op jit(solution)/shard_map/ppermute | solution.py:643
  8.7 10.2 %collective-permute-start.1 = (bf16[128,512]{1,0:T(8,128)(2,1)}, bf16[128,512]{1,0:T(8,128)(2,1)S(1)}, u32[]{:S(2)}, u32[]{:S(2)}) collective-permute-start(bf16[128,512]{1,0:T(8,128)(2,1)} %get-tuple-element.40.queries_ref), channel_id=1, source_target_pairs={{8,0},{10,2},{12,4},{14,6},{16,8},{18,10},{20,12},{22,14},{24,16},... | collective-permute-start | bytes 393224 | tf_op jit(solution)/shard_map/ppermute | solution.py:643
  10.8 12.7 %collective-permute-start.7 = (bf16[128,1024]{1,0:T(8,128)(2,1)}, bf16[128,1024]{1,0:T(8,128)(2,1)S(1)}, u32[]{:S(2)}, u32[]{:S(2)}) collective-permute-start(bf16[128,1024]{1,0:T(8,128)(2,1)} %get-tuple-element.51.kept_ref.refs_1_), channel_id=1, source_target_pairs={{0,8},{2,10},{4,12},{6,14},{8,16},{10,18},{12,20},{14,22},{16,24},... | collective-permute-start | bytes 786440 | tf_op jit(solution)/shard_map/ppermute | solution.py:643
  14.0 7.5 %collective-permute-start = (bf16[128,512]{1,0:T(8,128)(2,1)}, bf16[128,512]{1,0:T(8,128)(2,1)S(1)}, u32[]{:S(2)}, u32[]{:S(2)}) collective-permute-start(bf16[128,512]{1,0:T(8,128)(2,1)} %get-tuple-element.40.queries_ref), channel_id=1, source_target_pairs={{4,0},{6,2},{8,4},{10,6},{12,8},{14,10},{16,12},{18,14},{20,16},{2... | collective-permute-start | bytes 393224 | tf_op jit(solution)/shard_map/ppermute | solution.py:643
  16.1 10.9 %copy-start.7 = (s32[16]{0:T(128)S(1)}, s32[16]{0:T(128)}, u32[]{:S(2)}) copy-start(s32[16]{0:T(128)} %refs_0_.1) | copy-start | bytes 196
  16.1 10.8 %collective-permute-start.5 = (bf16[208,1024]{1,0:T(8,128)(2,1)}, bf16[208,1024]{1,0:T(8,128)(2,1)S(1)}, u32[]{:S(2)}, u32[]{:S(2)}) collective-permute-start(bf16[208,1024]{1,0:T(8,128)(2,1)} %get-tuple-element.41), channel_id=1, source_target_pairs={{2,0},{4,2},{6,4},{8,6},{10,8},{12,10},{14,12},{16,14},{18,16},{20... | collective-permute-start | bytes 1277960 | tf_op jit(solution)/shard_map/ppermute | solution.py:643
  18.9 4.0 %collective-permute-start.4 = (bf16[128,512]{1,0:T(8,128)(2,1)S(1)}, bf16[128,512]{1,0:T(8,128)(2,1)S(1)}, u32[]{:S(2)}, u32[]{:S(2)}) collective-permute-start(bf16[128,512]{1,0:T(8,128)(2,1)S(1)} %collective-permute-done.1.query_next4_ref.refs_3_), channel_id=1, source_target_pairs={{0,2},{2,0},{4,6},{6,4},{8,10},{10,8},{12,14},{14,12},{16,18},{18,... | collective-permute-start | bytes 393224 | tf_op jit(solution)/shard_map/ppermute | solution.py:643
  21.5 5.5 %collective-permute-start.8 = (bf16[176,1024]{1,0:T(8,128)(2,1)}, bf16[176,1024]{1,0:T(8,128)(2,1)S(1)}, u32[]{:S(2)}, u32[]{:S(2)}) collective-permute-start(bf16[176,1024]{1,0:T(8,128)(2,1)} %get-tuple-element.47), channel_id=1, source_target_pairs={{0,2},{2,0},{4,6},{6,4},{8,10},{10,8},{12,14},{14,12},{16,18},{18,... | collective-permute-start | bytes 1081352 | tf_op jit(solution)/shard_map/ppermute | solution.py:643
  22.9 4.1 %collective-permute-start.9 = (bf16[176,1024]{1,0:T(8,128)(2,1)S(1)}, bf16[176,1024]{1,0:T(8,128)(2,1)S(1)}, u32[]{:S(2)}, u32[]{:S(2)}) collective-permute-start(bf16[176,1024]{1,0:T(8,128)(2,1)S(1)} %collective-permute-done.6.back2_ref), channel_id=1, source_target_pairs={{0,2},{2,0},{4,6},{6,4},{8,10},{10,8},{12,14},{14,12},{16,18},{18,... | collective-permute-start | bytes 1081352 | tf_op jit(solution)/shard_map/ppermute | solution.py:643
  22.9 2.0 %collective-permute-start.3 = (bf16[128,512]{1,0:T(8,128)(2,1)S(1)}, bf16[128,512]{1,0:T(8,128)(2,1)S(1)}, u32[]{:S(2)}, u32[]{:S(2)}) collective-permute-start(bf16[128,512]{1,0:T(8,128)(2,1)S(1)} %collective-permute-done.query_next2_ref.refs_2_), channel_id=1, source_target_pairs={{0,2},{2,0},{4,6},{6,4},{8,10},{10,8},{12,14},{14,12},{16,18},{18,... | collective-permute-start | bytes 393224 | tf_op jit(solution)/shard_map/ppermute | solution.py:643
  23.4 3.5 %collective-permute-start.10 = (bf16[128,1024]{1,0:T(8,128)(2,1)S(1)}, bf16[128,1024]{1,0:T(8,128)(2,1)S(1)}, u32[]{:S(2)}, u32[]{:S(2)}) collective-permute-start(bf16[128,1024]{1,0:T(8,128)(2,1)S(1)} %collective-permute-done.7.back4_ref), channel_id=1, source_target_pairs={{0,2},{2,0},{4,6},{6,4},{8,10},{10,8},{12,14},{14,12},{16,18},{18,... | collective-permute-start | bytes 786440 | tf_op jit(solution)/shard_map/ppermute | solution.py:643
  24.9 6.6 %collective-permute-start.11 = (bf16[128,1024]{1,0:T(8,128)(2,1)}, bf16[128,1024]{1,0:T(8,128)(2,1)S(1)}, u32[]{:S(2)}, u32[]{:S(2)}) collective-permute-start(bf16[128,1024]{1,0:T(8,128)(2,1)} %get-tuple-element.51.kept_ref.refs_1_), channel_id=1, source_target_pairs={{2,12},{6,16},{10,20},{14,24},{18,28},{3,13},{7,17},{11,21},{15,25... | collective-permute-start | bytes 786440 | tf_op jit(solution)/shard_map/ppermute | solution.py:643
  25.6 5.9 %copy-start = (bf16[1,128,1024]{2,1,0:T(8,128)(2,1)S(1)}, bf16[1,128,1024]{2,1,0:T(8,128)(2,1)}, u32[]{:S(2)}) copy-start(bf16[1,128,1024]{2,1,0:T(8,128)(2,1)} %param.9) | copy-start | bytes 786436
  25.6 5.9 %copy-start.3 = (bf16[1,512,1024]{2,1,0:T(8,128)(2,1)S(1)}, bf16[1,512,1024]{2,1,0:T(8,128)(2,1)}, u32[]{:S(2)}) copy-start(bf16[1,512,1024]{2,1,0:T(8,128)(2,1)} %param.14) | copy-start | bytes 3145732
  25.7 5.9 %copy-start.5 = (bf16[128,1024]{1,0:T(8,128)(2,1)S(1)}, bf16[128,1024]{1,0:T(8,128)(2,1)}, u32[]{:S(2)}) copy-start(bf16[128,1024]{1,0:T(8,128)(2,1)} %top_ref.3) | copy-start | bytes 786436
  27.0 0.9 %copy-start.9 = (bf16[128,512]{1,0:T(8,128)(2,1)S(1)}, bf16[128,512]{1,0:T(8,128)(2,1)}, u32[]{:S(2)}) copy-start(bf16[128,512]{1,0:T(8,128)(2,1)} %get-tuple-element.40.queries_ref) | copy-start | bytes 393220
  31.5 11.2 %copy-start.8 = (bf16[1,1024,512]{2,1,0:T(8,128)(2,1)S(1)}, bf16[1,1024,512]{2,1,0:T(8,128)(2,1)}, u32[]{:S(2)}) copy-start(bf16[1,1024,512]{2,1,0:T(8,128)(2,1)} %param.11) | copy-start | bytes 3145732
  38.7 7.8 %collective-permute-start.13 = (bf16[144,512]{1,0:T(8,128)(2,1)S(1)}, bf16[144,512]{1,0:T(8,128)(2,1)S(1)}, u32[]{:S(2)}, u32[]{:S(2)}) collective-permute-start(bf16[144,512]{1,0:T(8,128)(2,1)S(1)} %get-tuple-element.53.message_ref), channel_id=1, source_target_pairs={{9,1},{11,3},{13,5},{15,7},{17,9},{19,11},{21,13},{23,15},{25,17},... | collective-permute-start | bytes 442376 | tf_op jit(solution)/shard_map/ppermute | solution.py:643
  39.4 7.2 %collective-permute-start.12 = (bf16[144,512]{1,0:T(8,128)(2,1)S(1)}, bf16[144,512]{1,0:T(8,128)(2,1)S(1)}, u32[]{:S(2)}, u32[]{:S(2)}) collective-permute-start(bf16[144,512]{1,0:T(8,128)(2,1)S(1)} %get-tuple-element.53.message_ref), channel_id=1, source_target_pairs={{5,1},{7,3},{9,5},{11,7},{13,9},{15,11},{17,13},{19,15},{21,17},{2... | collective-permute-start | bytes 442376 | tf_op jit(solution)/shard_map/ppermute | solution.py:643
  40.1 7.1 %collective-permute-start.14 = (bf16[144,512]{1,0:T(8,128)(2,1)S(1)}, bf16[144,512]{1,0:T(8,128)(2,1)S(1)}, u32[]{:S(2)}, u32[]{:S(2)}) collective-permute-start(bf16[144,512]{1,0:T(8,128)(2,1)S(1)} %get-tuple-element.53.message_ref), channel_id=1, source_target_pairs={{0,2},{2,0},{4,6},{6,4},{8,10},{10,8},{12,14},{14,12},{16,18},{18,... | collective-permute-start | bytes 442376 | tf_op jit(solution)/shard_map/ppermute | solution.py:643
  42.7 5.5 %copy-start.1 = (bf16[1,1024,512]{2,1,0:T(8,128)(2,1)S(1)}, bf16[1,1024,512]{2,1,0:T(8,128)(2,1)}, u32[]{:S(2)}) copy-start(bf16[1,1024,512]{2,1,0:T(8,128)(2,1)} %param.12) | copy-start | bytes 3145732
  42.7 5.5 %copy-start.2 = (bf16[1,1024,512]{2,1,0:T(8,128)(2,1)S(1)}, bf16[1,1024,512]{2,1,0:T(8,128)(2,1)}, u32[]{:S(2)}) copy-start(bf16[1,1024,512]{2,1,0:T(8,128)(2,1)} %param.13) | copy-start | bytes 3145732
  46.5 1.7 %copy-start.6 = (f32[1,1024]{1,0:T(1,128)S(1)}, f32[1,1024]{1,0:T(1,128)}, u32[]{:S(2)}) copy-start(f32[1,1024]{1,0:T(1,128)} %refs_14_.1) | copy-start | bytes 12292
  46.6 1.4 %collective-permute-start.15 = (bf16[144,512]{1,0:T(8,128)(2,1)S(1)}, bf16[144,512]{1,0:T(8,128)(2,1)S(1)}, u32[]{:S(2)}, u32[]{:S(2)}) collective-permute-start(bf16[144,512]{1,0:T(8,128)(2,1)S(1)} %collective-permute-done.12.next2_ref), channel_id=1, source_target_pairs={{0,2},{2,0},{4,6},{6,4},{8,10},{10,8},{12,14},{14,12},{16,18},{18,... | collective-permute-start | bytes 442376 | tf_op jit(solution)/shard_map/ppermute | solution.py:643
  46.7 1.5 %collective-permute-start.16 = (bf16[144,512]{1,0:T(8,128)(2,1)S(1)}, bf16[144,512]{1,0:T(8,128)(2,1)S(1)}, u32[]{:S(2)}, u32[]{:S(2)}) collective-permute-start(bf16[144,512]{1,0:T(8,128)(2,1)S(1)} %collective-permute-done.13.next4_ref), channel_id=1, source_target_pairs={{0,2},{2,0},{4,6},{6,4},{8,10},{10,8},{12,14},{14,12},{16,18},{18,... | collective-permute-start | bytes 442376 | tf_op jit(solution)/shard_map/ppermute | solution.py:643
  51.5 14.3 %collective-permute-start.17 = (bf16[128,1024]{1,0:T(8,128)(2,1)S(1)}, bf16[128,1024]{1,0:T(8,128)(2,1)S(1)}, u32[]{:S(2)}, u32[]{:S(2)}) collective-permute-start(bf16[128,1024]{1,0:T(8,128)(2,1)S(1)} %get-tuple-element.61), channel_id=1, source_target_pairs={{1,0},{3,2},{5,4},{7,6},{9,8},{11,10},{13,12},{15,14},{17,16},{19,... | collective-permute-start | bytes 786440 | tf_op jit(solution)/shard_map/ppermute | solution.py:643
  58.3 7.5 %collective-permute-start.18 = (bf16[32,1024]{1,0:T(8,128)(2,1)S(1)}, bf16[32,1024]{1,0:T(8,128)(2,1)S(1)}, u32[]{:S(2)}, u32[]{:S(2)}) collective-permute-start(bf16[32,1024]{1,0:T(8,128)(2,1)S(1)} %get-tuple-element.62), channel_id=1, source_target_pairs={{3,0},{5,2},{7,4},{9,6},{11,8},{13,10},{15,12},{17,14},{19,16},{21... | collective-permute-start | bytes 196616 | tf_op jit(solution)/shard_map/ppermute | solution.py:643
  65.8 8.6 %copy-start.10 = (bf16[128,512]{1,0:T(8,128)(2,1)S(1)}, bf16[128,512]{1,0:T(8,128)(2,1)}, u32[]{:S(2)}) copy-start(bf16[128,512]{1,0:T(8,128)(2,1)} %get-tuple-element.40.queries_ref) | copy-start | bytes 393220
  68.6 9.4 %collective-permute-start.20 = (bf16[144,512]{1,0:T(8,128)(2,1)S(1)}, bf16[144,512]{1,0:T(8,128)(2,1)S(1)}, u32[]{:S(2)}, u32[]{:S(2)}) collective-permute-start(bf16[144,512]{1,0:T(8,128)(2,1)S(1)} %get-tuple-element.64.message_ref), channel_id=1, source_target_pairs={{8,0},{10,2},{12,4},{14,6},{16,8},{18,10},{20,12},{22,14},{24,16},... | collective-permute-start | bytes 442376 | tf_op jit(solution)/shard_map/ppermute | solution.py:643
  70.9 7.2 %collective-permute-start.19 = (bf16[144,512]{1,0:T(8,128)(2,1)S(1)}, bf16[144,512]{1,0:T(8,128)(2,1)S(1)}, u32[]{:S(2)}, u32[]{:S(2)}) collective-permute-start(bf16[144,512]{1,0:T(8,128)(2,1)S(1)} %get-tuple-element.64.message_ref), channel_id=1, source_target_pairs={{4,0},{6,2},{8,4},{10,6},{12,8},{14,10},{16,12},{18,14},{20,16},{2... | collective-permute-start | bytes 442376 | tf_op jit(solution)/shard_map/ppermute | solution.py:643
  72.8 7.5 %collective-permute-start.21 = (bf16[144,512]{1,0:T(8,128)(2,1)S(1)}, bf16[144,512]{1,0:T(8,128)(2,1)S(1)}, u32[]{:S(2)}, u32[]{:S(2)}) collective-permute-start(bf16[144,512]{1,0:T(8,128)(2,1)S(1)} %get-tuple-element.64.message_ref), channel_id=1, source_target_pairs={{0,2},{2,0},{4,6},{6,4},{8,10},{10,8},{12,14},{14,12},{16,18},{18,... | collective-permute-start | bytes 442376 | tf_op jit(solution)/shard_map/ppermute | solution.py:643
  78.0 2.3 %collective-permute-start.23 = (bf16[144,512]{1,0:T(8,128)(2,1)S(1)}, bf16[144,512]{1,0:T(8,128)(2,1)S(1)}, u32[]{:S(2)}, u32[]{:S(2)}) collective-permute-start(bf16[144,512]{1,0:T(8,128)(2,1)S(1)} %collective-permute-done.20.refs_8_), channel_id=1, source_target_pairs={{0,2},{2,0},{4,6},{6,4},{8,10},{10,8},{12,14},{14,12},{16,18},{18,... | collective-permute-start | bytes 442376 | tf_op jit(solution)/shard_map/ppermute | solution.py:643
  78.1 3.2 %collective-permute-start.22 = (bf16[144,512]{1,0:T(8,128)(2,1)S(1)}, bf16[144,512]{1,0:T(8,128)(2,1)S(1)}, u32[]{:S(2)}, u32[]{:S(2)}) collective-permute-start(bf16[144,512]{1,0:T(8,128)(2,1)S(1)} %collective-permute-done.19.refs_7_), channel_id=1, source_target_pairs={{0,2},{2,0},{4,6},{6,4},{8,10},{10,8},{12,14},{14,12},{16,18},{18,... | collective-permute-start | bytes 442376 | tf_op jit(solution)/shard_map/ppermute | solution.py:643

commit v7 on v6

--- a/solution.py
+++ b/solution.py
@@ -506,11 +506,9 @@
 def key_kernel(
     valid_ref,
     kept_ref,
-    query_next2_ref,
-    query_next4_ref,
     query_peer_ref,
-    query_peer_next2_ref,
-    query_peer_next4_ref,
+    query_far_ref,
+    query_peer_far_ref,
     next2_ref,
     next4_ref,
     peer_ref,
@@ -554,10 +552,10 @@
         queries,
         odd,
         (
-            (query_peer_next2_ref, query_peer_ref),
-            (query_next2_ref, query_next2_ref),
-            (query_peer_next4_ref, query_peer_next2_ref),
-            (query_next4_ref, query_next4_ref),
+            (query_peer_far_ref.at[0:ROWS], query_peer_ref),
+            (query_peer_far_ref.at[ROWS : 2 * ROWS], query_far_ref.at[0:ROWS]),
+            (query_far_ref.at[ROWS : 2 * ROWS], query_far_ref.at[ROWS : 2 * ROWS]),
+            (query_far_ref.at[0:ROWS], query_peer_far_ref.at[ROWS : 2 * ROWS]),
         ),
     )
     for block in range(LEFT):
@@ -673,24 +671,26 @@
     back2 = moved(ahead, across(2, every))
     back4 = moved(kept, across(4, every))
     after1 = moved(behind, across(-1, every))
-    query_next2 = moved(queries, across(-2, every))
-    query_next4 = moved(queries, across(-4, every))
     peer = moved(ahead, swap)
     query_peer = moved(queries, swap)
     peer_back2 = moved(back2, swap)
     peer_back4 = moved(back4, swap)
-    query_peer_next2 = moved(query_next2, swap)
-    query_peer_next4 = moved(query_next4, swap)
+    chip_pairs = [
+        (at(section, source), at(section, source - 2 - 2 * (source % 2)))
+        for section in every
+        for source in range(count)
+        if source >= 2 + 2 * (source % 2)
+    ]
+    query_far = moved(jnp.concatenate([queries, after(query_peer, peer)]), chip_pairs)
+    query_peer_far = moved(query_far, swap)
     far_pairs = [
         (at(section, source), at(section, source + 5))
         for section in every
         for source in range(1, count - 5, 2)
     ]
     back5 = moved(after(kept, back2), far_pairs)
-    query_next2, query_next4, query_peer, query_peer_next2, query_peer_next4, after1 = (
-        lax.optimization_barrier(
-            (query_next2, query_next4, query_peer, query_peer_next2, query_peer_next4, after1)
-        )
+    query_peer, query_far, query_peer_far, after1 = lax.optimization_barrier(
+        (query_peer, query_far, query_peer_far, after1)
     )
 
     span = (LEFT + 1) * ROWS
@@ -782,14 +782,12 @@
         peer_grad2 = moved(grad2, swap)
         peer_grad4 = moved(grad4, swap)
         key_operands = placed(
-            "svvvvvvvvvvvvvvvvvvvvs",
+            "svvvvvvvvvvvvvvvvvvs",
             group_valid,
             kept,
-            query_next2,
-            query_next4,
             query_peer,
-            query_peer_next2,
-            query_peer_next4,
+            query_far,
+            query_peer_far,
             grad2,
             grad4,
             peer_grad,

time: 85.6 us -> 83.7 us (0.978)
  starting transfers between devices: 38.6 us -> 36.6 us
  other arithmetic: 0 us -> 0.92 us
  local copies, waits for them, and re-layouts: 0.98 us -> 0.08 us
    ppermute x24 -> x22, starting transfers between devices: 38.6 us -> 36.6 us  [moved(): return lax.ppermute(value, ('tm', 'section'), pairs)]
    concatenate x0 -> x1, other arithmetic: none -> 0.92 us  [shards(): jnp.concatenate([queries, after(query_peer, peer)])]
    unnamed x25 -> x23, local copies, waits for them, and re-layouts: 0.98 us -> 0.08 us
    ppermute x24 -> x22, waiting for transfers between devices: 12.8 us -> 12.8 us  [moved(): return lax.ppermute(value, ('tm', 'section'), pairs)]
  transfers between devices with their start and end apart: 24 -> 22, of which waited for: 7 -> 7; matrix products, arithmetic and copies ran while one was open for 0% -> 1% of each run, Pallas kernels for 13% -> 13%
where the time goes in v7:
time: 83.7 us; the launch traced here: 83.4 us
  starting transfers between devices  36.6 us (44%)
  Pallas kernels  32.6 us (39%)
  waiting for transfers between devices  12.8 us (15%)
  other arithmetic  0.92 us (1%)
    ppermute x22, starting transfers between devices, moved(): return lax.ppermute(value, ('tm', 'section'), pairs)  36.6 us
    pallas_call x8, Pallas kernels, call(): pl.pallas_call(kernel, name=name, in_specs=[kinds[place] for _, place in...  32.6 us
    ppermute x22, waiting for transfers between devices, moved(): return lax.ppermute(value, ('tm', 'section'), pairs)  12.8 us
  transfers between devices with their start and end apart: 22, of which 7 were waited for; matrix products, arithmetic and copies ran while one was open for 1% of the time, Pallas kernels for 13%

profile of v7, /device:TPU:19, one launch (start us, length us, event | category | flops | bytes accessed | tf_op | source)
XLA Modules:
  0.0 83.4 jit_solution(11122572974429979849)
XLA Ops:
  0.0 4.3 %project.1 = (bf16[128,512]{1,0:T(8,128)(2,1)}, bf16[128,1024]{1,0:T(8,128)(2,1)}, bf16[176,1024]{1,0:T(8,128)(2,1)}, bf16[208,1024]{1,0:T(8,128)(2,1)}) custom-call(bf16[128,1024]{1,0:T(8,128)(2,1)} %bitcast.9, bf16[128,1024]{1,0:T(8,128)(2,1)} %top_ref.3, f32[1,1024]{1,0:T(1,128)} %refs_12_.1, bf16[1024,512]{1,0:T(8,128)(2,1)} %bitcast.24, ...), custom_call_target="tpu_custom_call" | custom-call | flops 1073741824 | bytes 4194304 | tf_op jit(solution)/shard_map/project/pallas_call | solution.py:605
  4.3 0.7 collective-permute-start.1
  5.1 0.1 collective-permute-start
  5.2 3.3 %collective-permute-start.5 = (bf16[176,1024]{1,0:T(8,128)(2,1)}, bf16[176,1024]{1,0:T(8,128)(2,1)S(1)}, u32[]{:S(2)}, u32[]{:S(2)}) collective-permute-start(bf16[176,1024]{1,0:T(8,128)(2,1)} %get-tuple-element.40), channel_id=1, source_target_pairs={{0,4},{2,6},{4,8},{6,10},{8,12},{10,14},{12,16},{14,18},{16,20},{1... | collective-permute-start | bytes 1081352 | tf_op jit(solution)/shard_map/ppermute | solution.py:641
  8.5 0.0 collective-permute-done.query_peer_ref.refs_2_
  8.5 0.0 collective-permute-done.1.peer_ref
  8.5 0.9 %pad_maximum_fusion = bf16[256,512]{1,0:T(8,128)(2,1)S(1)} fusion(bf16[128,512]{1,0:T(8,128)(2,1)S(1)} %collective-permute-done.query_peer_ref.refs_2_, bf16[128,512]{1,0:T(8,128)(2,1)} %get-tuple-element.39.queries_ref), kind=kLoop, calls=%fused_computation | loop fusion | flops 524288 | bytes 524288 | tf_op jit(solution)/shard_map/concatenate | solution.py:684
  9.4 0.0 copy-start.6
  9.4 2.2 %collective-permute-start.2 = (bf16[256,512]{1,0:T(8,128)(2,1)S(1)}, bf16[256,512]{1,0:T(8,128)(2,1)S(1)}, u32[]{:S(2)}, u32[]{:S(2)}) collective-permute-start(bf16[256,512]{1,0:T(8,128)(2,1)S(1)} %pad_maximum_fusion), channel_id=1, source_target_pairs={{4,0},{8,4},{10,2},{12,8},{14,6},{16,12},{18,10},{20,16},{22,14},{... | collective-permute-start | bytes 786440 | tf_op jit(solution)/shard_map/ppermute | solution.py:641
  11.6 0.0 copy-done.4
  11.6 3.2 %collective-permute-start.6 = (bf16[128,1024]{1,0:T(8,128)(2,1)S(1)}, bf16[128,1024]{1,0:T(8,128)(2,1)S(1)}, u32[]{:S(2)}, u32[]{:S(2)}) collective-permute-start(bf16[128,1024]{1,0:T(8,128)(2,1)S(1)} %copy-done.4), channel_id=1, source_target_pairs={{0,8},{2,10},{4,12},{6,14},{8,16},{10,18},{12,20},{14,22},{16,24},... | collective-permute-start | bytes 786440 | tf_op jit(solution)/shard_map/ppermute | solution.py:641
  14.9 0.0 copy-start.8
  14.9 3.1 %collective-permute-start.4 = (bf16[208,1024]{1,0:T(8,128)(2,1)}, bf16[208,1024]{1,0:T(8,128)(2,1)S(1)}, u32[]{:S(2)}, u32[]{:S(2)}) collective-permute-start(bf16[208,1024]{1,0:T(8,128)(2,1)} %get-tuple-element.42), channel_id=1, source_target_pairs={{2,0},{4,2},{6,4},{8,6},{10,8},{12,10},{14,12},{16,14},{18,16},{20... | collective-permute-start | bytes 1277960 | tf_op jit(solution)/shard_map/ppermute | solution.py:641
  17.9 2.0 %collective-permute-done.5.back2_ref = bf16[176,1024]{1,0:T(8,128)(2,1)S(1)} collective-permute-done((bf16[176,1024]{1,0:T(8,128)(2,1)}, bf16[176,1024]{1,0:T(8,128)(2,1)S(1)}, u32[]{:S(2)}, u32[]{:S(2)}) %collective-permute-start.5) | collective-permute-done | bytes 360480 | tf_op jit(solution)/shard_map/ppermute | solution.py:641
  19.9 1.1 %collective-permute-start.7 = (bf16[176,1024]{1,0:T(8,128)(2,1)S(1)}, bf16[176,1024]{1,0:T(8,128)(2,1)S(1)}, u32[]{:S(2)}, u32[]{:S(2)}) collective-permute-start(bf16[176,1024]{1,0:T(8,128)(2,1)S(1)} %collective-permute-done.5.back2_ref), channel_id=1, source_target_pairs={{0,2},{2,0},{4,6},{6,4},{8,10},{10,8},{12,14},{14,12},{16,18},{18,... | collective-permute-start | bytes 1081352 | tf_op jit(solution)/shard_map/ppermute | solution.py:641
  21.0 0.0 collective-permute-done.2.query_far_ref.refs_3_
  21.0 0.0 collective-permute-start.3
  21.0 1.7 %collective-permute-done.6.back4_ref = bf16[128,1024]{1,0:T(8,128)(2,1)S(1)} collective-permute-done((bf16[128,1024]{1,0:T(8,128)(2,1)S(1)}, bf16[128,1024]{1,0:T(8,128)(2,1)S(1)}, u32[]{:S(2)}, u32[]{:S(2)}) %collective-permute-start.6) | collective-permute-done | bytes 262176 | tf_op jit(solution)/shard_map/ppermute | solution.py:641
  22.7 1.1 %collective-permute-start.8 = (bf16[128,1024]{1,0:T(8,128)(2,1)S(1)}, bf16[128,1024]{1,0:T(8,128)(2,1)S(1)}, u32[]{:S(2)}, u32[]{:S(2)}) collective-permute-start(bf16[128,1024]{1,0:T(8,128)(2,1)S(1)} %collective-permute-done.6.back4_ref), channel_id=1, source_target_pairs={{0,2},{2,0},{4,6},{6,4},{8,10},{10,8},{12,14},{14,12},{16,18},{18,... | collective-permute-start | bytes 786440 | tf_op jit(solution)/shard_map/ppermute | solution.py:641
  23.8 0.7 collective-permute-start.9
  24.6 0.0 copy-start
  24.6 0.0 copy-start.3
  24.6 0.0 copy-start.5
  24.6 0.8 %collective-permute-done.4.after_ref = bf16[208,1024]{1,0:T(8,128)(2,1)S(1)} collective-permute-done((bf16[208,1024]{1,0:T(8,128)(2,1)}, bf16[208,1024]{1,0:T(8,128)(2,1)S(1)}, u32[]{:S(2)}, u32[]{:S(2)}) %collective-permute-start.4) | collective-permute-done | bytes 426016 | tf_op jit(solution)/shard_map/ppermute | solution.py:641
  25.4 0.0 collective-permute-done.3.query_peer_far_ref.refs_4_
  25.4 0.0 collective-permute-done.8.peer_back4_ref
  25.4 0.0 collective-permute-done.7.peer_back2_ref
  25.5 3.6 %attend.1 = (bf16[160,512]{1,0:T(8,128)(2,1)S(1)}, f32[128,128]{1,0:T(8,128)S(1)}) custom-call(s32[16]{0:T(128)S(1)} %copy-done.8, bf16[128,512]{1,0:T(8,128)(2,1)S(1)} %copy-done.6, bf16[128,1024]{1,0:T(8,128)(2,1)S(1)} %copy-done.4, bf16[176,1024]{1,0:T(8,128)(2,1)S(1)} %collective-permute-done.5.back2_ref, ...), custom_call_target="tpu_custom_call" | custom-call | flops 1073741824 | bytes 4194304 | tf_op jit(solution)/shard_map/attend/pallas_call | solution.py:605
  29.0 0.0 collective-permute-done.9.back5_ref
  29.1 0.0 copy-start.9
  29.1 7.2 %mix.1 = (f32[160,1024]{1,0:T(8,128)S(1)}, f32[128,1024]{1,0:T(8,128)S(1)}, bf16[144,512]{1,0:T(8,128)(2,1)S(1)}, f32[128,128]{1,0:T(8,128)S(1)}) custom-call(s32[16]{0:T(128)S(1)} %copy-done.8, bf16[128,1024]{1,0:T(8,128)(2,1)S(1)} %bitcast.10, bf16[128,1024]{1,0:T(8,128)(2,1)S(1)} %copy-done.5, bf16[160,512]{1,0:T(8,128)(2,1)S(1)} %get-tuple-element.47.attended_ref, ...), custom_call_target="tpu_custom_call" | custom-call | flops 1073741824 | bytes 4194304 | tf_op jit(solution)/shard_map/mix/pallas_call | solution.py:605
  36.3 0.7 collective-permute-start.11
  37.0 0.7 collective-permute-start.10
  37.6 3.4 %collective-permute-start.12 = (bf16[144,512]{1,0:T(8,128)(2,1)S(1)}, bf16[144,512]{1,0:T(8,128)(2,1)S(1)}, u32[]{:S(2)}, u32[]{:S(2)}) collective-permute-start(bf16[144,512]{1,0:T(8,128)(2,1)S(1)} %get-tuple-element.51.message_ref), channel_id=1, source_target_pairs={{0,2},{2,0},{4,6},{6,4},{8,10},{10,8},{12,14},{14,12},{16,18},{18,... | collective-permute-start | bytes 442376 | tf_op jit(solution)/shard_map/ppermute | solution.py:641
  41.0 0.0 copy-done.9
  41.0 3.8 %own_queries.2 = (f32[128,1024]{1,0:T(8,128)S(1)}, f32[128,512]{1,0:T(8,128)S(1)}, f32[128,512]{1,0:T(8,128)S(1)}) custom-call(s32[16]{0:T(128)S(1)} %copy-done.8, bf16[128,512]{1,0:T(8,128)(2,1)S(1)} %copy-done.6, bf16[128,1024]{1,0:T(8,128)(2,1)S(1)} %copy-done.4, bf16[176,1024]{1,0:T(8,128)(2,1)S(1)} %collective-permute-done.5.back2_ref, ...), custom_call_target="tpu_custom_call" | custom-call | flops 1073741824 | bytes 4194304 | tf_op jit(solution)/shard_map/own_queries/pallas_call | solution.py:605
  44.9 0.0 copy-start.7
  44.9 0.0 collective-permute-done.11.next4_ref
  44.9 0.0 collective-permute-done.10.next2_ref
  44.9 0.1 collective-permute-start.13
  45.0 0.5 collective-permute-start.14
  45.5 0.0 collective-permute-done.12.peer_ref
  45.5 0.9 %collective-permute-done.13.peer_next2_ref = bf16[144,512]{1,0:T(8,128)(2,1)S(1)} collective-permute-done((bf16[144,512]{1,0:T(8,128)(2,1)S(1)}, bf16[144,512]{1,0:T(8,128)(2,1)S(1)}, u32[]{:S(2)}, u32[]{:S(2)}) %collective-permute-start.13) | collective-permute-done | bytes 147488 | tf_op jit(solution)/shard_map/ppermute | solution.py:641
  46.4 0.2 collective-permute-done.14.peer_next4_ref
  46.6 0.0 copy-done.1
  46.6 0.0 copy-done.7
  46.6 3.3 %own_keys.1 = (bf16[128,1024]{1,0:T(8,128)(2,1)S(1)}, bf16[32,1024]{1,0:T(8,128)(2,1)S(1)}, bf16[128,1024]{1,0:T(8,128)(2,1)S(1)}) custom-call(s32[16]{0:T(128)S(1)} %copy-done.8, bf16[128,1024]{1,0:T(8,128)(2,1)S(1)} %copy-done.4, bf16[128,512]{1,0:T(8,128)(2,1)S(1)} %collective-permute-done.query_peer_ref.refs_2_, ...), custom_call_target="tpu_custom_call" | custom-call | flops 1073741824 | bytes 4194304 | tf_op jit(solution)/shard_map/own_keys/pallas_call | solution.py:605
  49.9 7.0 %collective-permute-start.15 = (bf16[128,1024]{1,0:T(8,128)(2,1)S(1)}, bf16[128,1024]{1,0:T(8,128)(2,1)S(1)}, u32[]{:S(2)}, u32[]{:S(2)}) collective-permute-start(bf16[128,1024]{1,0:T(8,128)(2,1)S(1)} %get-tuple-element.59), channel_id=1, source_target_pairs={{1,0},{3,2},{5,4},{7,6},{9,8},{11,10},{13,12},{15,14},{17,16},{19,... | collective-permute-start | bytes 786440 | tf_op jit(solution)/shard_map/ppermute | solution.py:641
  56.9 1.3 %collective-permute-start.16 = (bf16[32,1024]{1,0:T(8,128)(2,1)S(1)}, bf16[32,1024]{1,0:T(8,128)(2,1)S(1)}, u32[]{:S(2)}, u32[]{:S(2)}) collective-permute-start(bf16[32,1024]{1,0:T(8,128)(2,1)S(1)} %get-tuple-element.60), channel_id=1, source_target_pairs={{3,0},{5,2},{7,4},{9,6},{11,8},{13,10},{15,12},{17,14},{19,16},{21... | collective-permute-start | bytes 196616 | tf_op jit(solution)/shard_map/ppermute | solution.py:641
  58.2 6.2 %collective-permute-done.16.next_ref = bf16[32,1024]{1,0:T(8,128)(2,1)S(1)} collective-permute-done((bf16[32,1024]{1,0:T(8,128)(2,1)S(1)}, bf16[32,1024]{1,0:T(8,128)(2,1)S(1)}, u32[]{:S(2)}, u32[]{:S(2)}) %collective-permute-start.16) | collective-permute-done | bytes 65568 | tf_op jit(solution)/shard_map/ppermute | solution.py:641
  64.3 0.0 collective-permute-done.15.upstream_ref
  64.3 2.8 %mixer.1 = (f32[128,1024]{1,0:T(8,128)S(1)}, bf16[144,512]{1,0:T(8,128)(2,1)S(1)}, f32[128,128]{1,0:T(8,128)S(1)}) custom-call(s32[16]{0:T(128)S(1)} %copy-done.8, bf16[128,1024]{1,0:T(8,128)(2,1)S(1)} %collective-permute-done.15.upstream_ref, bf16[32,1024]{1,0:T(8,128)(2,1)S(1)} %collective-permute-done.16.next_ref, ...), custom_call_target="tpu_custom_call" | custom-call | flops 1073741824 | bytes 4194304 | tf_op jit(solution)/shard_map/mixer/pallas_call | solution.py:605
  67.2 1.9 %collective-permute-start.18 = (bf16[144,512]{1,0:T(8,128)(2,1)S(1)}, bf16[144,512]{1,0:T(8,128)(2,1)S(1)}, u32[]{:S(2)}, u32[]{:S(2)}) collective-permute-start(bf16[144,512]{1,0:T(8,128)(2,1)S(1)} %get-tuple-element.62.message_ref), channel_id=1, source_target_pairs={{8,0},{10,2},{12,4},{14,6},{16,8},{18,10},{20,12},{22,14},{24,16},... | collective-permute-start | bytes 442376 | tf_op jit(solution)/shard_map/ppermute | solution.py:641
  69.1 1.9 %collective-permute-start.17 = (bf16[144,512]{1,0:T(8,128)(2,1)S(1)}, bf16[144,512]{1,0:T(8,128)(2,1)S(1)}, u32[]{:S(2)}, u32[]{:S(2)}) collective-permute-start(bf16[144,512]{1,0:T(8,128)(2,1)S(1)} %get-tuple-element.62.message_ref), channel_id=1, source_target_pairs={{4,0},{6,2},{8,4},{10,6},{12,8},{14,10},{16,12},{18,14},{20,16},{2... | collective-permute-start | bytes 442376 | tf_op jit(solution)/shard_map/ppermute | solution.py:641
  71.0 1.5 %collective-permute-start.19 = (bf16[144,512]{1,0:T(8,128)(2,1)S(1)}, bf16[144,512]{1,0:T(8,128)(2,1)S(1)}, u32[]{:S(2)}, u32[]{:S(2)}) collective-permute-start(bf16[144,512]{1,0:T(8,128)(2,1)S(1)} %get-tuple-element.62.message_ref), channel_id=1, source_target_pairs={{0,2},{2,0},{4,6},{6,4},{8,10},{10,8},{12,14},{14,12},{16,18},{18,... | collective-permute-start | bytes 442376 | tf_op jit(solution)/shard_map/ppermute | solution.py:641
  72.5 3.7 %own_queries.3 = (f32[128,1024]{1,0:T(8,128)S(1)}, f32[128,512]{1,0:T(8,128)S(1)}, f32[128,512]{1,0:T(8,128)S(1)}) custom-call(s32[16]{0:T(128)S(1)} %copy-done.8, bf16[128,512]{1,0:T(8,128)(2,1)S(1)} %copy-done.6, bf16[128,1024]{1,0:T(8,128)(2,1)S(1)} %copy-done.4, bf16[176,1024]{1,0:T(8,128)(2,1)S(1)} %collective-permute-done.5.back2_ref, ...), custom_call_target="tpu_custom_call" | custom-call | flops 1073741824 | bytes 4194304 | tf_op jit(solution)/shard_map/own_queries/pallas_call | solution.py:605
  76.2 0.0 collective-permute-done.18.refs_6_
  76.2 0.1 collective-permute-start.21
  76.2 0.0 collective-permute-done.17.refs_5_
  76.3 2.2 %collective-permute-start.20 = (bf16[144,512]{1,0:T(8,128)(2,1)S(1)}, bf16[144,512]{1,0:T(8,128)(2,1)S(1)}, u32[]{:S(2)}, u32[]{:S(2)}) collective-permute-start(bf16[144,512]{1,0:T(8,128)(2,1)S(1)} %collective-permute-done.17.refs_5_), channel_id=1, source_target_pairs={{0,2},{2,0},{4,6},{6,4},{8,10},{10,8},{12,14},{14,12},{16,18},{18,... | collective-permute-start | bytes 442376 | tf_op jit(solution)/shard_map/ppermute | solution.py:641
  78.4 0.0 collective-permute-done.19.refs_7_
  78.4 0.0 collective-permute-done.21.refs_9_
  78.4 1.0 %collective-permute-done.20.refs_8_ = bf16[144,512]{1,0:T(8,128)(2,1)S(1)} collective-permute-done((bf16[144,512]{1,0:T(8,128)(2,1)S(1)}, bf16[144,512]{1,0:T(8,128)(2,1)S(1)}, u32[]{:S(2)}, u32[]{:S(2)}) %collective-permute-start.20) | collective-permute-done | bytes 147488 | tf_op jit(solution)/shard_map/ppermute | solution.py:641
  79.4 3.9 %last_keys.1 = bf16[128,1024]{1,0:T(8,128)(2,1)} custom-call(s32[16]{0:T(128)S(1)} %copy-done.8, bf16[128,1024]{1,0:T(8,128)(2,1)S(1)} %copy-done.4, bf16[128,512]{1,0:T(8,128)(2,1)S(1)} %collective-permute-done.query_peer_ref.refs_2_, bf16[256,512]{1,0:T(8,128)(2,1)S(1)} %collective-permute-done.2.query_far_ref.refs_3_, ...), custom_call_target="tpu_custom_call" | custom-call | flops 1073741824 | bytes 4194304 | tf_op jit(solution)/shard_map/last_keys/pallas_call | solution.py:605
  (12 shorter events, 0.0 us)
Async XLA Ops:
  4.3 4.2 %collective-permute-start.1 = (bf16[176,1024]{1,0:T(8,128)(2,1)}, bf16[176,1024]{1,0:T(8,128)(2,1)S(1)}, u32[]{:S(2)}, u32[]{:S(2)}) collective-permute-start(bf16[176,1024]{1,0:T(8,128)(2,1)} %get-tuple-element.40), channel_id=1, source_target_pairs={{0,2},{2,0},{4,6},{6,4},{8,10},{10,8},{12,14},{14,12},{16,18},{18,... | collective-permute-start | bytes 1081352 | tf_op jit(solution)/shard_map/ppermute | solution.py:641
  5.1 6.6 %copy-start.4 = (bf16[128,1024]{1,0:T(8,128)(2,1)S(1)}, bf16[128,1024]{1,0:T(8,128)(2,1)}, u32[]{:S(2)}) copy-start(bf16[128,1024]{1,0:T(8,128)(2,1)} %get-tuple-element.49.kept_ref.refs_1_) | copy-start | bytes 786436
  5.1 19.5 %copy-start.10 = (f32[1,31,1024]{2,0,1:T(1,128)S(1)}, f32[1,31,1024]{2,0,1:T(1,128)}, u32[]{:S(2)}) copy-start(f32[1,31,1024]{2,0,1:T(1,128)} %param.15) | copy-start | bytes 380932
  5.1 3.4 %collective-permute-start = (bf16[128,512]{1,0:T(8,128)(2,1)}, bf16[128,512]{1,0:T(8,128)(2,1)S(1)}, u32[]{:S(2)}, u32[]{:S(2)}) collective-permute-start(bf16[128,512]{1,0:T(8,128)(2,1)} %get-tuple-element.39.queries_ref), channel_id=1, source_target_pairs={{0,2},{2,0},{4,6},{6,4},{8,10},{10,8},{12,14},{14,12},{16,18},{18,... | collective-permute-start | bytes 393224 | tf_op jit(solution)/shard_map/ppermute | solution.py:641
  5.2 14.8 %collective-permute-start.5 = (bf16[176,1024]{1,0:T(8,128)(2,1)}, bf16[176,1024]{1,0:T(8,128)(2,1)S(1)}, u32[]{:S(2)}, u32[]{:S(2)}) collective-permute-start(bf16[176,1024]{1,0:T(8,128)(2,1)} %get-tuple-element.40), channel_id=1, source_target_pairs={{0,4},{2,6},{4,8},{6,10},{8,12},{10,14},{12,16},{14,18},{16,20},{1... | collective-permute-start | bytes 1081352 | tf_op jit(solution)/shard_map/ppermute | solution.py:641
  9.4 16.0 %copy-start.6 = (bf16[128,512]{1,0:T(8,128)(2,1)S(1)}, bf16[128,512]{1,0:T(8,128)(2,1)}, u32[]{:S(2)}) copy-start(bf16[128,512]{1,0:T(8,128)(2,1)} %get-tuple-element.39.queries_ref) | copy-start | bytes 393220
  9.4 11.6 %collective-permute-start.2 = (bf16[256,512]{1,0:T(8,128)(2,1)S(1)}, bf16[256,512]{1,0:T(8,128)(2,1)S(1)}, u32[]{:S(2)}, u32[]{:S(2)}) collective-permute-start(bf16[256,512]{1,0:T(8,128)(2,1)S(1)} %pad_maximum_fusion), channel_id=1, source_target_pairs={{4,0},{8,4},{10,2},{12,8},{14,6},{16,12},{18,10},{20,16},{22,14},{... | collective-permute-start | bytes 786440 | tf_op jit(solution)/shard_map/ppermute | solution.py:641
  11.6 11.1 %collective-permute-start.6 = (bf16[128,1024]{1,0:T(8,128)(2,1)S(1)}, bf16[128,1024]{1,0:T(8,128)(2,1)S(1)}, u32[]{:S(2)}, u32[]{:S(2)}) collective-permute-start(bf16[128,1024]{1,0:T(8,128)(2,1)S(1)} %copy-done.4), channel_id=1, source_target_pairs={{0,8},{2,10},{4,12},{6,14},{8,16},{10,18},{12,20},{14,22},{16,24},... | collective-permute-start | bytes 786440 | tf_op jit(solution)/shard_map/ppermute | solution.py:641
  14.9 10.6 %copy-start.8 = (s32[16]{0:T(128)S(1)}, s32[16]{0:T(128)}, u32[]{:S(2)}) copy-start(s32[16]{0:T(128)} %refs_0_.1) | copy-start | bytes 196
  14.9 10.6 %collective-permute-start.4 = (bf16[208,1024]{1,0:T(8,128)(2,1)}, bf16[208,1024]{1,0:T(8,128)(2,1)S(1)}, u32[]{:S(2)}, u32[]{:S(2)}) collective-permute-start(bf16[208,1024]{1,0:T(8,128)(2,1)} %get-tuple-element.42), channel_id=1, source_target_pairs={{2,0},{4,2},{6,4},{8,6},{10,8},{12,10},{14,12},{16,14},{18,16},{20... | collective-permute-start | bytes 1277960 | tf_op jit(solution)/shard_map/ppermute | solution.py:641
  19.9 5.5 %collective-permute-start.7 = (bf16[176,1024]{1,0:T(8,128)(2,1)S(1)}, bf16[176,1024]{1,0:T(8,128)(2,1)S(1)}, u32[]{:S(2)}, u32[]{:S(2)}) collective-permute-start(bf16[176,1024]{1,0:T(8,128)(2,1)S(1)} %collective-permute-done.5.back2_ref), channel_id=1, source_target_pairs={{0,2},{2,0},{4,6},{6,4},{8,10},{10,8},{12,14},{14,12},{16,18},{18,... | collective-permute-start | bytes 1081352 | tf_op jit(solution)/shard_map/ppermute | solution.py:641
  21.0 4.4 %collective-permute-start.3 = (bf16[256,512]{1,0:T(8,128)(2,1)S(1)}, bf16[256,512]{1,0:T(8,128)(2,1)S(1)}, u32[]{:S(2)}, u32[]{:S(2)}) collective-permute-start(bf16[256,512]{1,0:T(8,128)(2,1)S(1)} %collective-permute-done.2.query_far_ref.refs_3_), channel_id=1, source_target_pairs={{0,2},{2,0},{4,6},{6,4},{8,10},{10,8},{12,14},{14,12},{16,18},{18,... | collective-permute-start | bytes 786440 | tf_op jit(solution)/shard_map/ppermute | solution.py:641
  22.7 2.7 %collective-permute-start.8 = (bf16[128,1024]{1,0:T(8,128)(2,1)S(1)}, bf16[128,1024]{1,0:T(8,128)(2,1)S(1)}, u32[]{:S(2)}, u32[]{:S(2)}) collective-permute-start(bf16[128,1024]{1,0:T(8,128)(2,1)S(1)} %collective-permute-done.6.back4_ref), channel_id=1, source_target_pairs={{0,2},{2,0},{4,6},{6,4},{8,10},{10,8},{12,14},{14,12},{16,18},{18,... | collective-permute-start | bytes 786440 | tf_op jit(solution)/shard_map/ppermute | solution.py:641
  23.8 5.2 %collective-permute-start.9 = (bf16[128,1024]{1,0:T(8,128)(2,1)S(1)}, bf16[128,1024]{1,0:T(8,128)(2,1)S(1)}, u32[]{:S(2)}, u32[]{:S(2)}) collective-permute-start(bf16[128,1024]{1,0:T(8,128)(2,1)S(1)} %copy-done.4), channel_id=1, source_target_pairs={{2,12},{6,16},{10,20},{14,24},{18,28},{3,13},{7,17},{11,21},{15,25... | collective-permute-start | bytes 786440 | tf_op jit(solution)/shard_map/ppermute | solution.py:641
  24.6 4.5 %copy-start = (bf16[1,128,1024]{2,1,0:T(8,128)(2,1)S(1)}, bf16[1,128,1024]{2,1,0:T(8,128)(2,1)}, u32[]{:S(2)}) copy-start(bf16[1,128,1024]{2,1,0:T(8,128)(2,1)} %param.9) | copy-start | bytes 786436
  24.6 4.5 %copy-start.3 = (bf16[1,512,1024]{2,1,0:T(8,128)(2,1)S(1)}, bf16[1,512,1024]{2,1,0:T(8,128)(2,1)}, u32[]{:S(2)}) copy-start(bf16[1,512,1024]{2,1,0:T(8,128)(2,1)} %param.14) | copy-start | bytes 3145732
  24.6 4.5 %copy-start.5 = (bf16[128,1024]{1,0:T(8,128)(2,1)S(1)}, bf16[128,1024]{1,0:T(8,128)(2,1)}, u32[]{:S(2)}) copy-start(bf16[128,1024]{1,0:T(8,128)(2,1)} %top_ref.3) | copy-start | bytes 786436
  29.1 11.9 %copy-start.9 = (bf16[1,1024,512]{2,1,0:T(8,128)(2,1)S(1)}, bf16[1,1024,512]{2,1,0:T(8,128)(2,1)}, u32[]{:S(2)}) copy-start(bf16[1,1024,512]{2,1,0:T(8,128)(2,1)} %param.11) | copy-start | bytes 3145732
  36.3 8.6 %collective-permute-start.11 = (bf16[144,512]{1,0:T(8,128)(2,1)S(1)}, bf16[144,512]{1,0:T(8,128)(2,1)S(1)}, u32[]{:S(2)}, u32[]{:S(2)}) collective-permute-start(bf16[144,512]{1,0:T(8,128)(2,1)S(1)} %get-tuple-element.51.message_ref), channel_id=1, source_target_pairs={{9,1},{11,3},{13,5},{15,7},{17,9},{19,11},{21,13},{23,15},{25,17},... | collective-permute-start | bytes 442376 | tf_op jit(solution)/shard_map/ppermute | solution.py:641
  37.0 7.9 %collective-permute-start.10 = (bf16[144,512]{1,0:T(8,128)(2,1)S(1)}, bf16[144,512]{1,0:T(8,128)(2,1)S(1)}, u32[]{:S(2)}, u32[]{:S(2)}) collective-permute-start(bf16[144,512]{1,0:T(8,128)(2,1)S(1)} %get-tuple-element.51.message_ref), channel_id=1, source_target_pairs={{5,1},{7,3},{9,5},{11,7},{13,9},{15,11},{17,13},{19,15},{21,17},{2... | collective-permute-start | bytes 442376 | tf_op jit(solution)/shard_map/ppermute | solution.py:641
  37.6 7.9 %collective-permute-start.12 = (bf16[144,512]{1,0:T(8,128)(2,1)S(1)}, bf16[144,512]{1,0:T(8,128)(2,1)S(1)}, u32[]{:S(2)}, u32[]{:S(2)}) collective-permute-start(bf16[144,512]{1,0:T(8,128)(2,1)S(1)} %get-tuple-element.51.message_ref), channel_id=1, source_target_pairs={{0,2},{2,0},{4,6},{6,4},{8,10},{10,8},{12,14},{14,12},{16,18},{18,... | collective-permute-start | bytes 442376 | tf_op jit(solution)/shard_map/ppermute | solution.py:641
  41.0 5.5 %copy-start.1 = (bf16[1,1024,512]{2,1,0:T(8,128)(2,1)S(1)}, bf16[1,1024,512]{2,1,0:T(8,128)(2,1)}, u32[]{:S(2)}) copy-start(bf16[1,1024,512]{2,1,0:T(8,128)(2,1)} %param.12) | copy-start | bytes 3145732
  41.0 5.5 %copy-start.2 = (bf16[1,1024,512]{2,1,0:T(8,128)(2,1)S(1)}, bf16[1,1024,512]{2,1,0:T(8,128)(2,1)}, u32[]{:S(2)}) copy-start(bf16[1,1024,512]{2,1,0:T(8,128)(2,1)} %param.13) | copy-start | bytes 3145732
  44.9 1.7 %copy-start.7 = (f32[1,1024]{1,0:T(1,128)S(1)}, f32[1,1024]{1,0:T(1,128)}, u32[]{:S(2)}) copy-start(f32[1,1024]{1,0:T(1,128)} %refs_12_.1) | copy-start | bytes 12292
  44.9 1.4 %collective-permute-start.13 = (bf16[144,512]{1,0:T(8,128)(2,1)S(1)}, bf16[144,512]{1,0:T(8,128)(2,1)S(1)}, u32[]{:S(2)}, u32[]{:S(2)}) collective-permute-start(bf16[144,512]{1,0:T(8,128)(2,1)S(1)} %collective-permute-done.10.next2_ref), channel_id=1, source_target_pairs={{0,2},{2,0},{4,6},{6,4},{8,10},{10,8},{12,14},{14,12},{16,18},{18,... | collective-permute-start | bytes 442376 | tf_op jit(solution)/shard_map/ppermute | solution.py:641
  45.0 1.5 %collective-permute-start.14 = (bf16[144,512]{1,0:T(8,128)(2,1)S(1)}, bf16[144,512]{1,0:T(8,128)(2,1)S(1)}, u32[]{:S(2)}, u32[]{:S(2)}) collective-permute-start(bf16[144,512]{1,0:T(8,128)(2,1)S(1)} %collective-permute-done.11.next4_ref), channel_id=1, source_target_pairs={{0,2},{2,0},{4,6},{6,4},{8,10},{10,8},{12,14},{14,12},{16,18},{18,... | collective-permute-start | bytes 442376 | tf_op jit(solution)/shard_map/ppermute | solution.py:641
  49.9 14.5 %collective-permute-start.15 = (bf16[128,1024]{1,0:T(8,128)(2,1)S(1)}, bf16[128,1024]{1,0:T(8,128)(2,1)S(1)}, u32[]{:S(2)}, u32[]{:S(2)}) collective-permute-start(bf16[128,1024]{1,0:T(8,128)(2,1)S(1)} %get-tuple-element.59), channel_id=1, source_target_pairs={{1,0},{3,2},{5,4},{7,6},{9,8},{11,10},{13,12},{15,14},{17,16},{19,... | collective-permute-start | bytes 786440 | tf_op jit(solution)/shard_map/ppermute | solution.py:641
  56.9 7.5 %collective-permute-start.16 = (bf16[32,1024]{1,0:T(8,128)(2,1)S(1)}, bf16[32,1024]{1,0:T(8,128)(2,1)S(1)}, u32[]{:S(2)}, u32[]{:S(2)}) collective-permute-start(bf16[32,1024]{1,0:T(8,128)(2,1)S(1)} %get-tuple-element.60), channel_id=1, source_target_pairs={{3,0},{5,2},{7,4},{9,6},{11,8},{13,10},{15,12},{17,14},{19,16},{21... | collective-permute-start | bytes 196616 | tf_op jit(solution)/shard_map/ppermute | solution.py:641
  67.2 9.0 %collective-permute-start.18 = (bf16[144,512]{1,0:T(8,128)(2,1)S(1)}, bf16[144,512]{1,0:T(8,128)(2,1)S(1)}, u32[]{:S(2)}, u32[]{:S(2)}) collective-permute-start(bf16[144,512]{1,0:T(8,128)(2,1)S(1)} %get-tuple-element.62.message_ref), channel_id=1, source_target_pairs={{8,0},{10,2},{12,4},{14,6},{16,8},{18,10},{20,12},{22,14},{24,16},... | collective-permute-start | bytes 442376 | tf_op jit(solution)/shard_map/ppermute | solution.py:641
  69.1 7.2 %collective-permute-start.17 = (bf16[144,512]{1,0:T(8,128)(2,1)S(1)}, bf16[144,512]{1,0:T(8,128)(2,1)S(1)}, u32[]{:S(2)}, u32[]{:S(2)}) collective-permute-start(bf16[144,512]{1,0:T(8,128)(2,1)S(1)} %get-tuple-element.62.message_ref), channel_id=1, source_target_pairs={{4,0},{6,2},{8,4},{10,6},{12,8},{14,10},{16,12},{18,14},{20,16},{2... | collective-permute-start | bytes 442376 | tf_op jit(solution)/shard_map/ppermute | solution.py:641
  71.0 7.4 %collective-permute-start.19 = (bf16[144,512]{1,0:T(8,128)(2,1)S(1)}, bf16[144,512]{1,0:T(8,128)(2,1)S(1)}, u32[]{:S(2)}, u32[]{:S(2)}) collective-permute-start(bf16[144,512]{1,0:T(8,128)(2,1)S(1)} %get-tuple-element.62.message_ref), channel_id=1, source_target_pairs={{0,2},{2,0},{4,6},{6,4},{8,10},{10,8},{12,14},{14,12},{16,18},{18,... | collective-permute-start | bytes 442376 | tf_op jit(solution)/shard_map/ppermute | solution.py:641
  76.2 2.3 %collective-permute-start.21 = (bf16[144,512]{1,0:T(8,128)(2,1)S(1)}, bf16[144,512]{1,0:T(8,128)(2,1)S(1)}, u32[]{:S(2)}, u32[]{:S(2)}) collective-permute-start(bf16[144,512]{1,0:T(8,128)(2,1)S(1)} %collective-permute-done.18.refs_6_), channel_id=1, source_target_pairs={{0,2},{2,0},{4,6},{6,4},{8,10},{10,8},{12,14},{14,12},{16,18},{18,... | collective-permute-start | bytes 442376 | tf_op jit(solution)/shard_map/ppermute | solution.py:641
  76.3 3.2 %collective-permute-start.20 = (bf16[144,512]{1,0:T(8,128)(2,1)S(1)}, bf16[144,512]{1,0:T(8,128)(2,1)S(1)}, u32[]{:S(2)}, u32[]{:S(2)}) collective-permute-start(bf16[144,512]{1,0:T(8,128)(2,1)S(1)} %collective-permute-done.17.refs_5_), channel_id=1, source_target_pairs={{0,2},{2,0},{4,6},{6,4},{8,10},{10,8},{12,14},{14,12},{16,18},{18,... | collective-permute-start | bytes 442376 | tf_op jit(solution)/shard_map/ppermute | solution.py:641

commit v8 on v7

--- a/solution.py
+++ b/solution.py
@@ -118,7 +118,7 @@
         normed[rows, :] = (unit * gain_ref[...]).astype(BF16)
         return carry
 
-    lax.fori_loop(0, ROWS // chunk, norm_step, 0, unroll=2)
+    lax.fori_loop(0, ROWS // chunk, norm_step, 0, unroll=True)
     wide = w_key_ref.shape[1]
     half = EDGE // 2
     loads[1].wait()

time: 83.7 us -> 83.3 us (level)
  no operation moved by 1% of the time
where the time goes in v8:
time: 83.3 us; the launch traced here: 83 us
  starting transfers between devices  36.6 us (44%)
  Pallas kernels  32.2 us (39%)
  waiting for transfers between devices  12.8 us (15%)
  other arithmetic  0.92 us (1%)
    ppermute x22, starting transfers between devices, moved(): return lax.ppermute(value, ('tm', 'section'), pairs)  36.6 us
    pallas_call x8, Pallas kernels, call(): pl.pallas_call(kernel, name=name, in_specs=[kinds[place] for _, place in...  32.2 us
    ppermute x22, waiting for transfers between devices, moved(): return lax.ppermute(value, ('tm', 'section'), pairs)  12.8 us
  transfers between devices with their start and end apart: 22, of which 7 were waited for; matrix products, arithmetic and copies ran while one was open for 1% of the time, Pallas kernels for 13%

profile of v8, /device:TPU:19, one launch (start us, length us, event | category | flops | bytes accessed | tf_op | source)
XLA Modules:
  0.0 83.0 jit_solution(4148236595518632585)
XLA Ops:
  0.0 3.9 %project.1 = (bf16[128,512]{1,0:T(8,128)(2,1)}, bf16[128,1024]{1,0:T(8,128)(2,1)}, bf16[176,1024]{1,0:T(8,128)(2,1)}, bf16[208,1024]{1,0:T(8,128)(2,1)}) custom-call(bf16[128,1024]{1,0:T(8,128)(2,1)} %bitcast.9, bf16[128,1024]{1,0:T(8,128)(2,1)} %top_ref.3, f32[1,1024]{1,0:T(1,128)} %refs_12_.1, bf16[1024,512]{1,0:T(8,128)(2,1)} %bitcast.24, ...), custom_call_target="tpu_custom_call" | custom-call | flops 1073741824 | bytes 4194304 | tf_op jit(solution)/shard_map/project/pallas_call | solution.py:605
  3.9 0.7 collective-permute-start.1
  4.6 0.1 collective-permute-start
  4.7 3.3 %collective-permute-start.5 = (bf16[176,1024]{1,0:T(8,128)(2,1)}, bf16[176,1024]{1,0:T(8,128)(2,1)S(1)}, u32[]{:S(2)}, u32[]{:S(2)}) collective-permute-start(bf16[176,1024]{1,0:T(8,128)(2,1)} %get-tuple-element.40), channel_id=1, source_target_pairs={{0,4},{2,6},{4,8},{6,10},{8,12},{10,14},{12,16},{14,18},{16,20},{1... | collective-permute-start | bytes 1081352 | tf_op jit(solution)/shard_map/ppermute | solution.py:641
  8.0 0.0 collective-permute-done.query_peer_ref.refs_2_
  8.1 0.0 collective-permute-done.1.peer_ref
  8.1 0.9 %pad_maximum_fusion = bf16[256,512]{1,0:T(8,128)(2,1)S(1)} fusion(bf16[128,512]{1,0:T(8,128)(2,1)S(1)} %collective-permute-done.query_peer_ref.refs_2_, bf16[128,512]{1,0:T(8,128)(2,1)} %get-tuple-element.39.queries_ref), kind=kLoop, calls=%fused_computation | loop fusion | flops 524288 | bytes 524288 | tf_op jit(solution)/shard_map/concatenate | solution.py:684
  9.0 0.0 copy-start.6
  9.0 2.2 %collective-permute-start.2 = (bf16[256,512]{1,0:T(8,128)(2,1)S(1)}, bf16[256,512]{1,0:T(8,128)(2,1)S(1)}, u32[]{:S(2)}, u32[]{:S(2)}) collective-permute-start(bf16[256,512]{1,0:T(8,128)(2,1)S(1)} %pad_maximum_fusion), channel_id=1, source_target_pairs={{4,0},{8,4},{10,2},{12,8},{14,6},{16,12},{18,10},{20,16},{22,14},{... | collective-permute-start | bytes 786440 | tf_op jit(solution)/shard_map/ppermute | solution.py:641
  11.2 0.0 copy-done.4
  11.2 3.2 %collective-permute-start.6 = (bf16[128,1024]{1,0:T(8,128)(2,1)S(1)}, bf16[128,1024]{1,0:T(8,128)(2,1)S(1)}, u32[]{:S(2)}, u32[]{:S(2)}) collective-permute-start(bf16[128,1024]{1,0:T(8,128)(2,1)S(1)} %copy-done.4), channel_id=1, source_target_pairs={{0,8},{2,10},{4,12},{6,14},{8,16},{10,18},{12,20},{14,22},{16,24},... | collective-permute-start | bytes 786440 | tf_op jit(solution)/shard_map/ppermute | solution.py:641
  14.5 0.0 copy-start.8
  14.5 3.0 %collective-permute-start.4 = (bf16[208,1024]{1,0:T(8,128)(2,1)}, bf16[208,1024]{1,0:T(8,128)(2,1)S(1)}, u32[]{:S(2)}, u32[]{:S(2)}) collective-permute-start(bf16[208,1024]{1,0:T(8,128)(2,1)} %get-tuple-element.42), channel_id=1, source_target_pairs={{2,0},{4,2},{6,4},{8,6},{10,8},{12,10},{14,12},{16,14},{18,16},{20... | collective-permute-start | bytes 1277960 | tf_op jit(solution)/shard_map/ppermute | solution.py:641
  17.5 2.0 %collective-permute-done.5.back2_ref = bf16[176,1024]{1,0:T(8,128)(2,1)S(1)} collective-permute-done((bf16[176,1024]{1,0:T(8,128)(2,1)}, bf16[176,1024]{1,0:T(8,128)(2,1)S(1)}, u32[]{:S(2)}, u32[]{:S(2)}) %collective-permute-start.5) | collective-permute-done | bytes 360480 | tf_op jit(solution)/shard_map/ppermute | solution.py:641
  19.5 1.1 %collective-permute-start.7 = (bf16[176,1024]{1,0:T(8,128)(2,1)S(1)}, bf16[176,1024]{1,0:T(8,128)(2,1)S(1)}, u32[]{:S(2)}, u32[]{:S(2)}) collective-permute-start(bf16[176,1024]{1,0:T(8,128)(2,1)S(1)} %collective-permute-done.5.back2_ref), channel_id=1, source_target_pairs={{0,2},{2,0},{4,6},{6,4},{8,10},{10,8},{12,14},{14,12},{16,18},{18,... | collective-permute-start | bytes 1081352 | tf_op jit(solution)/shard_map/ppermute | solution.py:641
  20.6 0.0 collective-permute-done.2.query_far_ref.refs_3_
  20.6 0.0 collective-permute-start.3
  20.6 1.7 %collective-permute-done.6.back4_ref = bf16[128,1024]{1,0:T(8,128)(2,1)S(1)} collective-permute-done((bf16[128,1024]{1,0:T(8,128)(2,1)S(1)}, bf16[128,1024]{1,0:T(8,128)(2,1)S(1)}, u32[]{:S(2)}, u32[]{:S(2)}) %collective-permute-start.6) | collective-permute-done | bytes 262176 | tf_op jit(solution)/shard_map/ppermute | solution.py:641
  22.3 1.1 %collective-permute-start.8 = (bf16[128,1024]{1,0:T(8,128)(2,1)S(1)}, bf16[128,1024]{1,0:T(8,128)(2,1)S(1)}, u32[]{:S(2)}, u32[]{:S(2)}) collective-permute-start(bf16[128,1024]{1,0:T(8,128)(2,1)S(1)} %collective-permute-done.6.back4_ref), channel_id=1, source_target_pairs={{0,2},{2,0},{4,6},{6,4},{8,10},{10,8},{12,14},{14,12},{16,18},{18,... | collective-permute-start | bytes 786440 | tf_op jit(solution)/shard_map/ppermute | solution.py:641
  23.4 0.7 collective-permute-start.9
  24.1 0.0 copy-done.10
  24.1 0.0 copy-start
  24.1 0.0 copy-start.3
  24.2 0.0 copy-start.5
  24.2 0.8 %collective-permute-done.4.after_ref = bf16[208,1024]{1,0:T(8,128)(2,1)S(1)} collective-permute-done((bf16[208,1024]{1,0:T(8,128)(2,1)}, bf16[208,1024]{1,0:T(8,128)(2,1)S(1)}, u32[]{:S(2)}, u32[]{:S(2)}) %collective-permute-start.4) | collective-permute-done | bytes 426016 | tf_op jit(solution)/shard_map/ppermute | solution.py:641
  25.0 0.0 collective-permute-done.3.query_peer_far_ref.refs_4_
  25.0 0.0 collective-permute-done.8.peer_back4_ref
  25.0 0.0 collective-permute-done.7.peer_back2_ref
  25.0 0.0 copy-done.6
  25.0 0.0 copy-done.8
  25.1 3.6 %attend.1 = (bf16[160,512]{1,0:T(8,128)(2,1)S(1)}, f32[128,128]{1,0:T(8,128)S(1)}) custom-call(s32[16]{0:T(128)S(1)} %copy-done.8, bf16[128,512]{1,0:T(8,128)(2,1)S(1)} %copy-done.6, bf16[128,1024]{1,0:T(8,128)(2,1)S(1)} %copy-done.4, bf16[176,1024]{1,0:T(8,128)(2,1)S(1)} %collective-permute-done.5.back2_ref, ...), custom_call_target="tpu_custom_call" | custom-call | flops 1073741824 | bytes 4194304 | tf_op jit(solution)/shard_map/attend/pallas_call | solution.py:605
  28.6 0.0 collective-permute-done.9.back5_ref
  28.7 0.0 copy-start.9
  28.7 7.2 %mix.1 = (f32[160,1024]{1,0:T(8,128)S(1)}, f32[128,1024]{1,0:T(8,128)S(1)}, bf16[144,512]{1,0:T(8,128)(2,1)S(1)}, f32[128,128]{1,0:T(8,128)S(1)}) custom-call(s32[16]{0:T(128)S(1)} %copy-done.8, bf16[128,1024]{1,0:T(8,128)(2,1)S(1)} %bitcast.10, bf16[128,1024]{1,0:T(8,128)(2,1)S(1)} %copy-done.5, bf16[160,512]{1,0:T(8,128)(2,1)S(1)} %get-tuple-element.47.attended_ref, ...), custom_call_target="tpu_custom_call" | custom-call | flops 1073741824 | bytes 4194304 | tf_op jit(solution)/shard_map/mix/pallas_call | solution.py:605
  35.9 0.7 collective-permute-start.11
  36.5 0.7 collective-permute-start.10
  37.2 3.4 %collective-permute-start.12 = (bf16[144,512]{1,0:T(8,128)(2,1)S(1)}, bf16[144,512]{1,0:T(8,128)(2,1)S(1)}, u32[]{:S(2)}, u32[]{:S(2)}) collective-permute-start(bf16[144,512]{1,0:T(8,128)(2,1)S(1)} %get-tuple-element.51.message_ref), channel_id=1, source_target_pairs={{0,2},{2,0},{4,6},{6,4},{8,10},{10,8},{12,14},{14,12},{16,18},{18,... | collective-permute-start | bytes 442376 | tf_op jit(solution)/shard_map/ppermute | solution.py:641
  40.6 3.8 %own_queries.2 = (f32[128,1024]{1,0:T(8,128)S(1)}, f32[128,512]{1,0:T(8,128)S(1)}, f32[128,512]{1,0:T(8,128)S(1)}) custom-call(s32[16]{0:T(128)S(1)} %copy-done.8, bf16[128,512]{1,0:T(8,128)(2,1)S(1)} %copy-done.6, bf16[128,1024]{1,0:T(8,128)(2,1)S(1)} %copy-done.4, bf16[176,1024]{1,0:T(8,128)(2,1)S(1)} %collective-permute-done.5.back2_ref, ...), custom_call_target="tpu_custom_call" | custom-call | flops 1073741824 | bytes 4194304 | tf_op jit(solution)/shard_map/own_queries/pallas_call | solution.py:605
  44.5 0.0 copy-start.7
  44.5 0.0 collective-permute-done.11.next4_ref
  44.5 0.0 collective-permute-done.10.next2_ref
  44.5 0.1 collective-permute-start.13
  44.6 0.5 collective-permute-start.14
  45.1 0.0 collective-permute-done.12.peer_ref
  45.1 0.9 %collective-permute-done.13.peer_next2_ref = bf16[144,512]{1,0:T(8,128)(2,1)S(1)} collective-permute-done((bf16[144,512]{1,0:T(8,128)(2,1)S(1)}, bf16[144,512]{1,0:T(8,128)(2,1)S(1)}, u32[]{:S(2)}, u32[]{:S(2)}) %collective-permute-start.13) | collective-permute-done | bytes 147488 | tf_op jit(solution)/shard_map/ppermute | solution.py:641
  45.9 0.2 collective-permute-done.14.peer_next4_ref
  46.2 3.3 %own_keys.1 = (bf16[128,1024]{1,0:T(8,128)(2,1)S(1)}, bf16[32,1024]{1,0:T(8,128)(2,1)S(1)}, bf16[128,1024]{1,0:T(8,128)(2,1)S(1)}) custom-call(s32[16]{0:T(128)S(1)} %copy-done.8, bf16[128,1024]{1,0:T(8,128)(2,1)S(1)} %copy-done.4, bf16[128,512]{1,0:T(8,128)(2,1)S(1)} %collective-permute-done.query_peer_ref.refs_2_, ...), custom_call_target="tpu_custom_call" | custom-call | flops 1073741824 | bytes 4194304 | tf_op jit(solution)/shard_map/own_keys/pallas_call | solution.py:605
  49.4 7.0 %collective-permute-start.15 = (bf16[128,1024]{1,0:T(8,128)(2,1)S(1)}, bf16[128,1024]{1,0:T(8,128)(2,1)S(1)}, u32[]{:S(2)}, u32[]{:S(2)}) collective-permute-start(bf16[128,1024]{1,0:T(8,128)(2,1)S(1)} %get-tuple-element.59), channel_id=1, source_target_pairs={{1,0},{3,2},{5,4},{7,6},{9,8},{11,10},{13,12},{15,14},{17,16},{19,... | collective-permute-start | bytes 786440 | tf_op jit(solution)/shard_map/ppermute | solution.py:641
  56.4 1.3 %collective-permute-start.16 = (bf16[32,1024]{1,0:T(8,128)(2,1)S(1)}, bf16[32,1024]{1,0:T(8,128)(2,1)S(1)}, u32[]{:S(2)}, u32[]{:S(2)}) collective-permute-start(bf16[32,1024]{1,0:T(8,128)(2,1)S(1)} %get-tuple-element.60), channel_id=1, source_target_pairs={{3,0},{5,2},{7,4},{9,6},{11,8},{13,10},{15,12},{17,14},{19,16},{21... | collective-permute-start | bytes 196616 | tf_op jit(solution)/shard_map/ppermute | solution.py:641
  57.7 6.2 %collective-permute-done.16.next_ref = bf16[32,1024]{1,0:T(8,128)(2,1)S(1)} collective-permute-done((bf16[32,1024]{1,0:T(8,128)(2,1)S(1)}, bf16[32,1024]{1,0:T(8,128)(2,1)S(1)}, u32[]{:S(2)}, u32[]{:S(2)}) %collective-permute-start.16) | collective-permute-done | bytes 65568 | tf_op jit(solution)/shard_map/ppermute | solution.py:641
  63.9 0.0 collective-permute-done.15.upstream_ref
  63.9 2.8 %mixer.1 = (f32[128,1024]{1,0:T(8,128)S(1)}, bf16[144,512]{1,0:T(8,128)(2,1)S(1)}, f32[128,128]{1,0:T(8,128)S(1)}) custom-call(s32[16]{0:T(128)S(1)} %copy-done.8, bf16[128,1024]{1,0:T(8,128)(2,1)S(1)} %collective-permute-done.15.upstream_ref, bf16[32,1024]{1,0:T(8,128)(2,1)S(1)} %collective-permute-done.16.next_ref, ...), custom_call_target="tpu_custom_call" | custom-call | flops 1073741824 | bytes 4194304 | tf_op jit(solution)/shard_map/mixer/pallas_call | solution.py:605
  66.7 1.9 %collective-permute-start.18 = (bf16[144,512]{1,0:T(8,128)(2,1)S(1)}, bf16[144,512]{1,0:T(8,128)(2,1)S(1)}, u32[]{:S(2)}, u32[]{:S(2)}) collective-permute-start(bf16[144,512]{1,0:T(8,128)(2,1)S(1)} %get-tuple-element.62.message_ref), channel_id=1, source_target_pairs={{8,0},{10,2},{12,4},{14,6},{16,8},{18,10},{20,12},{22,14},{24,16},... | collective-permute-start | bytes 442376 | tf_op jit(solution)/shard_map/ppermute | solution.py:641
  68.7 1.9 %collective-permute-start.17 = (bf16[144,512]{1,0:T(8,128)(2,1)S(1)}, bf16[144,512]{1,0:T(8,128)(2,1)S(1)}, u32[]{:S(2)}, u32[]{:S(2)}) collective-permute-start(bf16[144,512]{1,0:T(8,128)(2,1)S(1)} %get-tuple-element.62.message_ref), channel_id=1, source_target_pairs={{4,0},{6,2},{8,4},{10,6},{12,8},{14,10},{16,12},{18,14},{20,16},{2... | collective-permute-start | bytes 442376 | tf_op jit(solution)/shard_map/ppermute | solution.py:641
  70.6 1.5 %collective-permute-start.19 = (bf16[144,512]{1,0:T(8,128)(2,1)S(1)}, bf16[144,512]{1,0:T(8,128)(2,1)S(1)}, u32[]{:S(2)}, u32[]{:S(2)}) collective-permute-start(bf16[144,512]{1,0:T(8,128)(2,1)S(1)} %get-tuple-element.62.message_ref), channel_id=1, source_target_pairs={{0,2},{2,0},{4,6},{6,4},{8,10},{10,8},{12,14},{14,12},{16,18},{18,... | collective-permute-start | bytes 442376 | tf_op jit(solution)/shard_map/ppermute | solution.py:641
  72.1 3.7 %own_queries.3 = (f32[128,1024]{1,0:T(8,128)S(1)}, f32[128,512]{1,0:T(8,128)S(1)}, f32[128,512]{1,0:T(8,128)S(1)}) custom-call(s32[16]{0:T(128)S(1)} %copy-done.8, bf16[128,512]{1,0:T(8,128)(2,1)S(1)} %copy-done.6, bf16[128,1024]{1,0:T(8,128)(2,1)S(1)} %copy-done.4, bf16[176,1024]{1,0:T(8,128)(2,1)S(1)} %collective-permute-done.5.back2_ref, ...), custom_call_target="tpu_custom_call" | custom-call | flops 1073741824 | bytes 4194304 | tf_op jit(solution)/shard_map/own_queries/pallas_call | solution.py:605
  75.7 0.0 collective-permute-done.18.refs_6_
  75.7 0.1 collective-permute-start.21
  75.8 0.0 collective-permute-done.17.refs_5_
  75.8 2.2 %collective-permute-start.20 = (bf16[144,512]{1,0:T(8,128)(2,1)S(1)}, bf16[144,512]{1,0:T(8,128)(2,1)S(1)}, u32[]{:S(2)}, u32[]{:S(2)}) collective-permute-start(bf16[144,512]{1,0:T(8,128)(2,1)S(1)} %collective-permute-done.17.refs_5_), channel_id=1, source_target_pairs={{0,2},{2,0},{4,6},{6,4},{8,10},{10,8},{12,14},{14,12},{16,18},{18,... | collective-permute-start | bytes 442376 | tf_op jit(solution)/shard_map/ppermute | solution.py:641
  78.0 0.0 collective-permute-done.19.refs_7_
  78.0 0.0 collective-permute-done.21.refs_9_
  78.0 1.0 %collective-permute-done.20.refs_8_ = bf16[144,512]{1,0:T(8,128)(2,1)S(1)} collective-permute-done((bf16[144,512]{1,0:T(8,128)(2,1)S(1)}, bf16[144,512]{1,0:T(8,128)(2,1)S(1)}, u32[]{:S(2)}, u32[]{:S(2)}) %collective-permute-start.20) | collective-permute-done | bytes 147488 | tf_op jit(solution)/shard_map/ppermute | solution.py:641
  79.0 3.9 %last_keys.1 = bf16[128,1024]{1,0:T(8,128)(2,1)} custom-call(s32[16]{0:T(128)S(1)} %copy-done.8, bf16[128,1024]{1,0:T(8,128)(2,1)S(1)} %copy-done.4, bf16[128,512]{1,0:T(8,128)(2,1)S(1)} %collective-permute-done.query_peer_ref.refs_2_, bf16[256,512]{1,0:T(8,128)(2,1)S(1)} %collective-permute-done.2.query_far_ref.refs_3_, ...), custom_call_target="tpu_custom_call" | custom-call | flops 1073741824 | bytes 4194304 | tf_op jit(solution)/shard_map/last_keys/pallas_call | solution.py:605
  (12 shorter events, 0.0 us)
Async XLA Ops:
  3.9 4.2 %collective-permute-start.1 = (bf16[176,1024]{1,0:T(8,128)(2,1)}, bf16[176,1024]{1,0:T(8,128)(2,1)S(1)}, u32[]{:S(2)}, u32[]{:S(2)}) collective-permute-start(bf16[176,1024]{1,0:T(8,128)(2,1)} %get-tuple-element.40), channel_id=1, source_target_pairs={{0,2},{2,0},{4,6},{6,4},{8,10},{10,8},{12,14},{14,12},{16,18},{18,... | collective-permute-start | bytes 1081352 | tf_op jit(solution)/shard_map/ppermute | solution.py:641
  4.6 6.6 %copy-start.4 = (bf16[128,1024]{1,0:T(8,128)(2,1)S(1)}, bf16[128,1024]{1,0:T(8,128)(2,1)}, u32[]{:S(2)}) copy-start(bf16[128,1024]{1,0:T(8,128)(2,1)} %get-tuple-element.49.kept_ref.refs_1_) | copy-start | bytes 786436
  4.6 19.5 %copy-start.10 = (f32[1,31,1024]{2,0,1:T(1,128)S(1)}, f32[1,31,1024]{2,0,1:T(1,128)}, u32[]{:S(2)}) copy-start(f32[1,31,1024]{2,0,1:T(1,128)} %param.15) | copy-start | bytes 380932
  4.6 3.4 %collective-permute-start = (bf16[128,512]{1,0:T(8,128)(2,1)}, bf16[128,512]{1,0:T(8,128)(2,1)S(1)}, u32[]{:S(2)}, u32[]{:S(2)}) collective-permute-start(bf16[128,512]{1,0:T(8,128)(2,1)} %get-tuple-element.39.queries_ref), channel_id=1, source_target_pairs={{0,2},{2,0},{4,6},{6,4},{8,10},{10,8},{12,14},{14,12},{16,18},{18,... | collective-permute-start | bytes 393224 | tf_op jit(solution)/shard_map/ppermute | solution.py:641
  4.7 14.8 %collective-permute-start.5 = (bf16[176,1024]{1,0:T(8,128)(2,1)}, bf16[176,1024]{1,0:T(8,128)(2,1)S(1)}, u32[]{:S(2)}, u32[]{:S(2)}) collective-permute-start(bf16[176,1024]{1,0:T(8,128)(2,1)} %get-tuple-element.40), channel_id=1, source_target_pairs={{0,4},{2,6},{4,8},{6,10},{8,12},{10,14},{12,16},{14,18},{16,20},{1... | collective-permute-start | bytes 1081352 | tf_op jit(solution)/shard_map/ppermute | solution.py:641
  9.0 16.0 %copy-start.6 = (bf16[128,512]{1,0:T(8,128)(2,1)S(1)}, bf16[128,512]{1,0:T(8,128)(2,1)}, u32[]{:S(2)}) copy-start(bf16[128,512]{1,0:T(8,128)(2,1)} %get-tuple-element.39.queries_ref) | copy-start | bytes 393220
  9.0 11.6 %collective-permute-start.2 = (bf16[256,512]{1,0:T(8,128)(2,1)S(1)}, bf16[256,512]{1,0:T(8,128)(2,1)S(1)}, u32[]{:S(2)}, u32[]{:S(2)}) collective-permute-start(bf16[256,512]{1,0:T(8,128)(2,1)S(1)} %pad_maximum_fusion), channel_id=1, source_target_pairs={{4,0},{8,4},{10,2},{12,8},{14,6},{16,12},{18,10},{20,16},{22,14},{... | collective-permute-start | bytes 786440 | tf_op jit(solution)/shard_map/ppermute | solution.py:641
  11.2 11.1 %collective-permute-start.6 = (bf16[128,1024]{1,0:T(8,128)(2,1)S(1)}, bf16[128,1024]{1,0:T(8,128)(2,1)S(1)}, u32[]{:S(2)}, u32[]{:S(2)}) collective-permute-start(bf16[128,1024]{1,0:T(8,128)(2,1)S(1)} %copy-done.4), channel_id=1, source_target_pairs={{0,8},{2,10},{4,12},{6,14},{8,16},{10,18},{12,20},{14,22},{16,24},... | collective-permute-start | bytes 786440 | tf_op jit(solution)/shard_map/ppermute | solution.py:641
  14.5 10.6 %copy-start.8 = (s32[16]{0:T(128)S(1)}, s32[16]{0:T(128)}, u32[]{:S(2)}) copy-start(s32[16]{0:T(128)} %refs_0_.1) | copy-start | bytes 196
  14.5 10.6 %collective-permute-start.4 = (bf16[208,1024]{1,0:T(8,128)(2,1)}, bf16[208,1024]{1,0:T(8,128)(2,1)S(1)}, u32[]{:S(2)}, u32[]{:S(2)}) collective-permute-start(bf16[208,1024]{1,0:T(8,128)(2,1)} %get-tuple-element.42), channel_id=1, source_target_pairs={{2,0},{4,2},{6,4},{8,6},{10,8},{12,10},{14,12},{16,14},{18,16},{20... | collective-permute-start | bytes 1277960 | tf_op jit(solution)/shard_map/ppermute | solution.py:641
  19.5 5.5 %collective-permute-start.7 = (bf16[176,1024]{1,0:T(8,128)(2,1)S(1)}, bf16[176,1024]{1,0:T(8,128)(2,1)S(1)}, u32[]{:S(2)}, u32[]{:S(2)}) collective-permute-start(bf16[176,1024]{1,0:T(8,128)(2,1)S(1)} %collective-permute-done.5.back2_ref), channel_id=1, source_target_pairs={{0,2},{2,0},{4,6},{6,4},{8,10},{10,8},{12,14},{14,12},{16,18},{18,... | collective-permute-start | bytes 1081352 | tf_op jit(solution)/shard_map/ppermute | solution.py:641
  20.6 4.4 %collective-permute-start.3 = (bf16[256,512]{1,0:T(8,128)(2,1)S(1)}, bf16[256,512]{1,0:T(8,128)(2,1)S(1)}, u32[]{:S(2)}, u32[]{:S(2)}) collective-permute-start(bf16[256,512]{1,0:T(8,128)(2,1)S(1)} %collective-permute-done.2.query_far_ref.refs_3_), channel_id=1, source_target_pairs={{0,2},{2,0},{4,6},{6,4},{8,10},{10,8},{12,14},{14,12},{16,18},{18,... | collective-permute-start | bytes 786440 | tf_op jit(solution)/shard_map/ppermute | solution.py:641
  22.3 2.7 %collective-permute-start.8 = (bf16[128,1024]{1,0:T(8,128)(2,1)S(1)}, bf16[128,1024]{1,0:T(8,128)(2,1)S(1)}, u32[]{:S(2)}, u32[]{:S(2)}) collective-permute-start(bf16[128,1024]{1,0:T(8,128)(2,1)S(1)} %collective-permute-done.6.back4_ref), channel_id=1, source_target_pairs={{0,2},{2,0},{4,6},{6,4},{8,10},{10,8},{12,14},{14,12},{16,18},{18,... | collective-permute-start | bytes 786440 | tf_op jit(solution)/shard_map/ppermute | solution.py:641
  23.4 5.2 %collective-permute-start.9 = (bf16[128,1024]{1,0:T(8,128)(2,1)S(1)}, bf16[128,1024]{1,0:T(8,128)(2,1)S(1)}, u32[]{:S(2)}, u32[]{:S(2)}) collective-permute-start(bf16[128,1024]{1,0:T(8,128)(2,1)S(1)} %copy-done.4), channel_id=1, source_target_pairs={{2,12},{6,16},{10,20},{14,24},{18,28},{3,13},{7,17},{11,21},{15,25... | collective-permute-start | bytes 786440 | tf_op jit(solution)/shard_map/ppermute | solution.py:641
  24.1 4.5 %copy-start = (bf16[1,128,1024]{2,1,0:T(8,128)(2,1)S(1)}, bf16[1,128,1024]{2,1,0:T(8,128)(2,1)}, u32[]{:S(2)}) copy-start(bf16[1,128,1024]{2,1,0:T(8,128)(2,1)} %param.9) | copy-start | bytes 786436
  24.1 4.5 %copy-start.3 = (bf16[1,512,1024]{2,1,0:T(8,128)(2,1)S(1)}, bf16[1,512,1024]{2,1,0:T(8,128)(2,1)}, u32[]{:S(2)}) copy-start(bf16[1,512,1024]{2,1,0:T(8,128)(2,1)} %param.14) | copy-start | bytes 3145732
  24.2 4.5 %copy-start.5 = (bf16[128,1024]{1,0:T(8,128)(2,1)S(1)}, bf16[128,1024]{1,0:T(8,128)(2,1)}, u32[]{:S(2)}) copy-start(bf16[128,1024]{1,0:T(8,128)(2,1)} %top_ref.3) | copy-start | bytes 786436
  28.7 11.9 %copy-start.9 = (bf16[1,1024,512]{2,1,0:T(8,128)(2,1)S(1)}, bf16[1,1024,512]{2,1,0:T(8,128)(2,1)}, u32[]{:S(2)}) copy-start(bf16[1,1024,512]{2,1,0:T(8,128)(2,1)} %param.11) | copy-start | bytes 3145732
  35.9 8.6 %collective-permute-start.11 = (bf16[144,512]{1,0:T(8,128)(2,1)S(1)}, bf16[144,512]{1,0:T(8,128)(2,1)S(1)}, u32[]{:S(2)}, u32[]{:S(2)}) collective-permute-start(bf16[144,512]{1,0:T(8,128)(2,1)S(1)} %get-tuple-element.51.message_ref), channel_id=1, source_target_pairs={{9,1},{11,3},{13,5},{15,7},{17,9},{19,11},{21,13},{23,15},{25,17},... | collective-permute-start | bytes 442376 | tf_op jit(solution)/shard_map/ppermute | solution.py:641
  36.5 7.9 %collective-permute-start.10 = (bf16[144,512]{1,0:T(8,128)(2,1)S(1)}, bf16[144,512]{1,0:T(8,128)(2,1)S(1)}, u32[]{:S(2)}, u32[]{:S(2)}) collective-permute-start(bf16[144,512]{1,0:T(8,128)(2,1)S(1)} %get-tuple-element.51.message_ref), channel_id=1, source_target_pairs={{5,1},{7,3},{9,5},{11,7},{13,9},{15,11},{17,13},{19,15},{21,17},{2... | collective-permute-start | bytes 442376 | tf_op jit(solution)/shard_map/ppermute | solution.py:641
  37.2 7.8 %collective-permute-start.12 = (bf16[144,512]{1,0:T(8,128)(2,1)S(1)}, bf16[144,512]{1,0:T(8,128)(2,1)S(1)}, u32[]{:S(2)}, u32[]{:S(2)}) collective-permute-start(bf16[144,512]{1,0:T(8,128)(2,1)S(1)} %get-tuple-element.51.message_ref), channel_id=1, source_target_pairs={{0,2},{2,0},{4,6},{6,4},{8,10},{10,8},{12,14},{14,12},{16,18},{18,... | collective-permute-start | bytes 442376 | tf_op jit(solution)/shard_map/ppermute | solution.py:641
  40.6 5.5 %copy-start.1 = (bf16[1,1024,512]{2,1,0:T(8,128)(2,1)S(1)}, bf16[1,1024,512]{2,1,0:T(8,128)(2,1)}, u32[]{:S(2)}) copy-start(bf16[1,1024,512]{2,1,0:T(8,128)(2,1)} %param.12) | copy-start | bytes 3145732
  40.6 5.5 %copy-start.2 = (bf16[1,1024,512]{2,1,0:T(8,128)(2,1)S(1)}, bf16[1,1024,512]{2,1,0:T(8,128)(2,1)}, u32[]{:S(2)}) copy-start(bf16[1,1024,512]{2,1,0:T(8,128)(2,1)} %param.13) | copy-start | bytes 3145732
  44.5 1.7 %copy-start.7 = (f32[1,1024]{1,0:T(1,128)S(1)}, f32[1,1024]{1,0:T(1,128)}, u32[]{:S(2)}) copy-start(f32[1,1024]{1,0:T(1,128)} %refs_12_.1) | copy-start | bytes 12292
  44.5 1.4 %collective-permute-start.13 = (bf16[144,512]{1,0:T(8,128)(2,1)S(1)}, bf16[144,512]{1,0:T(8,128)(2,1)S(1)}, u32[]{:S(2)}, u32[]{:S(2)}) collective-permute-start(bf16[144,512]{1,0:T(8,128)(2,1)S(1)} %collective-permute-done.10.next2_ref), channel_id=1, source_target_pairs={{0,2},{2,0},{4,6},{6,4},{8,10},{10,8},{12,14},{14,12},{16,18},{18,... | collective-permute-start | bytes 442376 | tf_op jit(solution)/shard_map/ppermute | solution.py:641
  44.6 1.5 %collective-permute-start.14 = (bf16[144,512]{1,0:T(8,128)(2,1)S(1)}, bf16[144,512]{1,0:T(8,128)(2,1)S(1)}, u32[]{:S(2)}, u32[]{:S(2)}) collective-permute-start(bf16[144,512]{1,0:T(8,128)(2,1)S(1)} %collective-permute-done.11.next4_ref), channel_id=1, source_target_pairs={{0,2},{2,0},{4,6},{6,4},{8,10},{10,8},{12,14},{14,12},{16,18},{18,... | collective-permute-start | bytes 442376 | tf_op jit(solution)/shard_map/ppermute | solution.py:641
  49.4 14.5 %collective-permute-start.15 = (bf16[128,1024]{1,0:T(8,128)(2,1)S(1)}, bf16[128,1024]{1,0:T(8,128)(2,1)S(1)}, u32[]{:S(2)}, u32[]{:S(2)}) collective-permute-start(bf16[128,1024]{1,0:T(8,128)(2,1)S(1)} %get-tuple-element.59), channel_id=1, source_target_pairs={{1,0},{3,2},{5,4},{7,6},{9,8},{11,10},{13,12},{15,14},{17,16},{19,... | collective-permute-start | bytes 786440 | tf_op jit(solution)/shard_map/ppermute | solution.py:641
  56.4 7.5 %collective-permute-start.16 = (bf16[32,1024]{1,0:T(8,128)(2,1)S(1)}, bf16[32,1024]{1,0:T(8,128)(2,1)S(1)}, u32[]{:S(2)}, u32[]{:S(2)}) collective-permute-start(bf16[32,1024]{1,0:T(8,128)(2,1)S(1)} %get-tuple-element.60), channel_id=1, source_target_pairs={{3,0},{5,2},{7,4},{9,6},{11,8},{13,10},{15,12},{17,14},{19,16},{21... | collective-permute-start | bytes 196616 | tf_op jit(solution)/shard_map/ppermute | solution.py:641
  66.7 9.0 %collective-permute-start.18 = (bf16[144,512]{1,0:T(8,128)(2,1)S(1)}, bf16[144,512]{1,0:T(8,128)(2,1)S(1)}, u32[]{:S(2)}, u32[]{:S(2)}) collective-permute-start(bf16[144,512]{1,0:T(8,128)(2,1)S(1)} %get-tuple-element.62.message_ref), channel_id=1, source_target_pairs={{8,0},{10,2},{12,4},{14,6},{16,8},{18,10},{20,12},{22,14},{24,16},... | collective-permute-start | bytes 442376 | tf_op jit(solution)/shard_map/ppermute | solution.py:641
  68.7 7.2 %collective-permute-start.17 = (bf16[144,512]{1,0:T(8,128)(2,1)S(1)}, bf16[144,512]{1,0:T(8,128)(2,1)S(1)}, u32[]{:S(2)}, u32[]{:S(2)}) collective-permute-start(bf16[144,512]{1,0:T(8,128)(2,1)S(1)} %get-tuple-element.62.message_ref), channel_id=1, source_target_pairs={{4,0},{6,2},{8,4},{10,6},{12,8},{14,10},{16,12},{18,14},{20,16},{2... | collective-permute-start | bytes 442376 | tf_op jit(solution)/shard_map/ppermute | solution.py:641
  70.6 7.4 %collective-permute-start.19 = (bf16[144,512]{1,0:T(8,128)(2,1)S(1)}, bf16[144,512]{1,0:T(8,128)(2,1)S(1)}, u32[]{:S(2)}, u32[]{:S(2)}) collective-permute-start(bf16[144,512]{1,0:T(8,128)(2,1)S(1)} %get-tuple-element.62.message_ref), channel_id=1, source_target_pairs={{0,2},{2,0},{4,6},{6,4},{8,10},{10,8},{12,14},{14,12},{16,18},{18,... | collective-permute-start | bytes 442376 | tf_op jit(solution)/shard_map/ppermute | solution.py:641
  75.7 2.3 %collective-permute-start.21 = (bf16[144,512]{1,0:T(8,128)(2,1)S(1)}, bf16[144,512]{1,0:T(8,128)(2,1)S(1)}, u32[]{:S(2)}, u32[]{:S(2)}) collective-permute-start(bf16[144,512]{1,0:T(8,128)(2,1)S(1)} %collective-permute-done.18.refs_6_), channel_id=1, source_target_pairs={{0,2},{2,0},{4,6},{6,4},{8,10},{10,8},{12,14},{14,12},{16,18},{18,... | collective-permute-start | bytes 442376 | tf_op jit(solution)/shard_map/ppermute | solution.py:641
  75.8 3.2 %collective-permute-start.20 = (bf16[144,512]{1,0:T(8,128)(2,1)S(1)}, bf16[144,512]{1,0:T(8,128)(2,1)S(1)}, u32[]{:S(2)}, u32[]{:S(2)}) collective-permute-start(bf16[144,512]{1,0:T(8,128)(2,1)S(1)} %collective-permute-done.17.refs_5_), channel_id=1, source_target_pairs={{0,2},{2,0},{4,6},{6,4},{8,10},{10,8},{12,14},{14,12},{16,18},{18,... | collective-permute-start | bytes 442376 | tf_op jit(solution)/shard_map/ppermute | solution.py:641

commit v9 on v8

--- a/solution.py
+++ b/solution.py
@@ -271,9 +271,37 @@
         message_ref[ROWS : ROWS + 16, index * PAIR : (index + 1) * PAIR] = part
 
 
+def slope_of(output):
+    gate = 1.0 / (1.0 + jnp.exp(-output))
+    return gate * (1.0 + output * (1.0 - gate))
+
+
+def body_kernel(valid_ref, own_ref, attended_ref, after_ref, w_out_ref, kernel_ref, mixed_ref, slope_ref):
+    place = lax.axis_index("tm")
+    projected = dot_nn(attended_ref[...], w_out_ref[...])
+    row_ids = lax.broadcasted_iota(jnp.int32, (ROWS, 1), 0)
+    edge_ids = lax.broadcasted_iota(jnp.int32, (EDGE, 1), 0)
+    here = projected[0:ROWS] + own_ref[...].astype(F32)
+    after = projected[ROWS:] + after_ref[ROWS : ROWS + EDGE, :].astype(F32)
+    here = jnp.where(row_ids < valid_count(valid_ref, place), here, 0.0)
+    after = jnp.where(edge_ids < valid_count(valid_ref, place + 1), after, 0.0)
+    mixed_ref[0:ROWS, :] = here.astype(BF16).astype(F32)
+    mixed_ref[ROWS:, :] = after.astype(BF16).astype(F32)
+    taps = kernel_ref.shape[0]
+
+    def conv_step(step, carry):
+        lanes = pl.ds(pl.multiple_of(step * PAIR, PAIR), PAIR)
+        output = tap_sum(mixed_ref[:, lanes], kernel_ref, lanes, EDGE - (taps - 1), 1, ROWS)
+        slope_ref[:, lanes] = slope_of(output)
+        return carry
+
+    lax.fori_loop(0, own_ref.shape[1] // PAIR, conv_step, 0, unroll=True)
+
+
 def mix_kernel(
     valid_ref,
-    own_ref,
+    mixed_ref,
+    late_slope_ref,
     top_ref,
     attended_ref,
     log_ref,
@@ -314,7 +342,6 @@
             (peer_ref, peer_back2_ref),
         ),
     )
-    attended_all[EDGE:, :] = attended_ref[...]
     query_tail[0:half_edge, :] = before_rows[EDGE : EDGE + half_edge, 0:wide]
     query_tail[half_edge:EDGE, :] = before_rows[EDGE : EDGE + half_edge, wide : 2 * wide]
     key_lane = lax.broadcasted_iota(jnp.int32, (1, ROWS), 1)
@@ -328,29 +355,23 @@
             shares_low, _, _ = pair_shares(scores, allowed)
             product = dot_nn(shares_low, masked_half(window[:, value_lanes], half))
             total = product if total is None else total + product
-        attended_all[0:EDGE, lanes] = total.astype(BF16)
+        attended_all[:, lanes] = total.astype(BF16)
     projected = dot_nn(attended_all[...], w_out_ref[...])
-    row_ids = lax.broadcasted_iota(jnp.int32, (ROWS, 1), 0)
     edge_ids = lax.broadcasted_iota(jnp.int32, (EDGE, 1), 0)
-    before = projected[0:EDGE] + before_rows[0:EDGE, :].astype(F32)
-    here = projected[EDGE : EDGE + ROWS] + own_ref[...].astype(F32)
-    after = projected[EDGE + ROWS :] + after_ref[ROWS : ROWS + EDGE, :].astype(F32)
+    before = projected + before_rows[0:EDGE, :].astype(F32)
     before = jnp.where(edge_ids + (ROWS - EDGE) < counts[LEFT], before, 0.0)
-    here = jnp.where(row_ids < counts[LEFT + 1], here, 0.0)
-    after = jnp.where(edge_ids < counts[LEFT + 2], after, 0.0)
     mixed[0:EDGE, :] = before.astype(BF16).astype(F32)
-    mixed[EDGE : EDGE + ROWS, :] = here.astype(BF16).astype(F32)
-    mixed[EDGE + ROWS :, :] = after.astype(BF16).astype(F32)
+    mixed[EDGE:, :] = mixed_ref[0:EDGE, :]
+    slope_ref[EDGE:, :] = late_slope_ref[...]
     taps = kernel_ref.shape[0]
 
     def conv_step(step, carry):
         lanes = pl.ds(pl.multiple_of(step * PAIR, PAIR), PAIR)
-        output = tap_sum(mixed[:, lanes], kernel_ref, lanes, EDGE - (taps - 1), 1, ROWS + EDGE)
-        gate = 1.0 / (1.0 + jnp.exp(-output))
-        slope_ref[:, lanes] = gate * (1.0 + output * (1.0 - gate))
+        output = tap_sum(mixed[:, lanes], kernel_ref, lanes, EDGE - (taps - 1), 1, EDGE)
+        slope_ref[0:EDGE, lanes] = slope_of(output)
         return carry
 
-    lax.fori_loop(0, own_ref.shape[1] // PAIR, conv_step, 0, unroll=True)
+    lax.fori_loop(0, mixed.shape[1] // PAIR, conv_step, 0, unroll=True)
     first = ROWS + EDGE + half_edge
     mixer_body(
         counts[LEFT + 1],
@@ -359,7 +380,7 @@
         slope_ref,
         kernel_ref,
         w_out_ref,
-        attended_all[EDGE : EDGE + ROWS, :],
+        attended_ref[0:ROWS, :],
         log_ref,
         total_ref,
         message_ref,
@@ -701,15 +722,23 @@
         [((ROWS + EDGE, wide), BF16), ((ROWS, PAIR), F32)],
         [(((LEFT + 2) * ROWS, 2 * wide), BF16), ((ROWS + EDGE, wide), BF16)],
     )
-    back5 = after(back5, attended)
     step_outs = [((ROWS, width), F32), ((ROWS + 16, wide), BF16), ((ROWS, PAIR), F32)]
+    mixed, late_slope = call(
+        body_kernel,
+        "body",
+        placed("svvvvv", group_valid, own, attended, after1, out_weight, kernel),
+        [((ROWS + EDGE, width), F32), ((ROWS, width), F32)],
+        [],
+    )
+    back5 = after(back5, mixed)
     slope, total, message, dots = call(
         mix_kernel,
         "mix",
         placed(
-            "svvvvvvvvvvvvv",
+            "svvvvvvvvvvvvvv",
             group_valid,
-            own,
+            mixed,
+            late_slope,
             top_grad,
             attended,
             logs,
@@ -727,8 +756,8 @@
         [
             ((span, 2 * wide), BF16),
             ((EDGE, wide), BF16),
-            ((ROWS + 2 * EDGE, wide), BF16),
-            ((ROWS + 2 * EDGE, width), F32),
+            ((EDGE, wide), BF16),
+            ((2 * EDGE, width), F32),
             ((ROWS, width), BF16),
             ((EDGE + half_edge, width), BF16),
         ],

time: 83.3 us -> 82.6 us (level)
  starting transfers between devices: 36.6 us -> 35 us
  Pallas kernels: 32.2 us -> 33.1 us
    ppermute x22, starting transfers between devices: 36.6 us -> 35 us  [moved(): return lax.ppermute(value, ('tm', 'section'), pairs)]
    pallas_call x8 -> x9, Pallas kernels: 32.2 us -> 33.1 us  [call(): pl.pallas_call(kernel, name=name, in_specs=[kinds[place] for _, place in...]
  transfers between devices with their start and end apart: 22 -> 22, of which waited for: 7 -> 7; matrix products, arithmetic and copies ran while one was open for 1% -> 1% of each run, Pallas kernels for 13% -> 17%
where the time goes in v9:
time: 82.6 us; the launch traced here: 82.2 us
  starting transfers between devices  35 us (42%)
  Pallas kernels  33.1 us (40%)
  waiting for transfers between devices  12.8 us (15%)
  other arithmetic  0.92 us (1%)
    ppermute x22, starting transfers between devices, moved(): return lax.ppermute(value, ('tm', 'section'), pairs)  35 us
    pallas_call x9, Pallas kernels, call(): pl.pallas_call(kernel, name=name, in_specs=[kinds[place] for _, place in...  33.1 us
    ppermute x22, waiting for transfers between devices, moved(): return lax.ppermute(value, ('tm', 'section'), pairs)  12.8 us
  transfers between devices with their start and end apart: 22, of which 7 were waited for; matrix products, arithmetic and copies ran while one was open for 1% of the time, Pallas kernels for 17%

profile of v9, /device:TPU:19, one launch (start us, length us, event | category | flops | bytes accessed | tf_op | source)
XLA Modules:
  0.0 82.2 jit_solution(1346332569388086067)
XLA Ops:
  0.0 3.9 %project.1 = (bf16[128,512]{1,0:T(8,128)(2,1)}, bf16[128,1024]{1,0:T(8,128)(2,1)}, bf16[176,1024]{1,0:T(8,128)(2,1)}, bf16[208,1024]{1,0:T(8,128)(2,1)}) custom-call(bf16[128,1024]{1,0:T(8,128)(2,1)} %bitcast.15, bf16[128,1024]{1,0:T(8,128)(2,1)} %top_ref.3, f32[1,1024]{1,0:T(1,128)} %refs_12_.1, bf16[1024,512]{1,0:T(8,128)(2,1)} %bitcast.26, ...), custom_call_target="tpu_custom_call" | custom-call | flops 1073741824 | bytes 4194304 | tf_op jit(solution)/shard_map/project/pallas_call | solution.py:626
  3.9 0.7 collective-permute-start.1
  4.6 0.1 collective-permute-start
  4.7 3.3 %collective-permute-start.5 = (bf16[176,1024]{1,0:T(8,128)(2,1)}, bf16[176,1024]{1,0:T(8,128)(2,1)S(1)}, u32[]{:S(2)}, u32[]{:S(2)}) collective-permute-start(bf16[176,1024]{1,0:T(8,128)(2,1)} %get-tuple-element.42), channel_id=1, source_target_pairs={{0,4},{2,6},{4,8},{6,10},{8,12},{10,14},{12,16},{14,18},{16,20},{1... | collective-permute-start | bytes 1081352 | tf_op jit(solution)/shard_map/ppermute | solution.py:662
  8.1 0.0 collective-permute-done.query_peer_ref.refs_2_
  8.1 0.0 collective-permute-done.1.peer_ref
  8.1 0.9 %pad_maximum_fusion = bf16[256,512]{1,0:T(8,128)(2,1)S(1)} fusion(bf16[128,512]{1,0:T(8,128)(2,1)S(1)} %collective-permute-done.query_peer_ref.refs_2_, bf16[128,512]{1,0:T(8,128)(2,1)} %get-tuple-element.41.queries_ref), kind=kLoop, calls=%fused_computation | loop fusion | flops 524288 | bytes 524288 | tf_op jit(solution)/shard_map/concatenate | solution.py:705
  9.0 2.2 %collective-permute-start.2 = (bf16[256,512]{1,0:T(8,128)(2,1)S(1)}, bf16[256,512]{1,0:T(8,128)(2,1)S(1)}, u32[]{:S(2)}, u32[]{:S(2)}) collective-permute-start(bf16[256,512]{1,0:T(8,128)(2,1)S(1)} %pad_maximum_fusion), channel_id=1, source_target_pairs={{4,0},{8,4},{10,2},{12,8},{14,6},{16,12},{18,10},{20,16},{22,14},{... | collective-permute-start | bytes 786440 | tf_op jit(solution)/shard_map/ppermute | solution.py:662
  11.2 0.0 copy-done.3
  11.2 3.2 %collective-permute-start.6 = (bf16[128,1024]{1,0:T(8,128)(2,1)S(1)}, bf16[128,1024]{1,0:T(8,128)(2,1)S(1)}, u32[]{:S(2)}, u32[]{:S(2)}) collective-permute-start(bf16[128,1024]{1,0:T(8,128)(2,1)S(1)} %copy-done.3), channel_id=1, source_target_pairs={{0,8},{2,10},{4,12},{6,14},{8,16},{10,18},{12,20},{14,22},{16,24},... | collective-permute-start | bytes 786440 | tf_op jit(solution)/shard_map/ppermute | solution.py:662
  14.5 0.0 copy-start.8
  14.5 3.0 %collective-permute-start.4 = (bf16[208,1024]{1,0:T(8,128)(2,1)}, bf16[208,1024]{1,0:T(8,128)(2,1)S(1)}, u32[]{:S(2)}, u32[]{:S(2)}) collective-permute-start(bf16[208,1024]{1,0:T(8,128)(2,1)} %get-tuple-element.44), channel_id=1, source_target_pairs={{2,0},{4,2},{6,4},{8,6},{10,8},{12,10},{14,12},{16,14},{18,16},{20... | collective-permute-start | bytes 1277960 | tf_op jit(solution)/shard_map/ppermute | solution.py:662
  17.5 2.0 %collective-permute-done.5.back2_ref = bf16[176,1024]{1,0:T(8,128)(2,1)S(1)} collective-permute-done((bf16[176,1024]{1,0:T(8,128)(2,1)}, bf16[176,1024]{1,0:T(8,128)(2,1)S(1)}, u32[]{:S(2)}, u32[]{:S(2)}) %collective-permute-start.5) | collective-permute-done | bytes 360480 | tf_op jit(solution)/shard_map/ppermute | solution.py:662
  19.5 1.1 %collective-permute-start.7 = (bf16[176,1024]{1,0:T(8,128)(2,1)S(1)}, bf16[176,1024]{1,0:T(8,128)(2,1)S(1)}, u32[]{:S(2)}, u32[]{:S(2)}) collective-permute-start(bf16[176,1024]{1,0:T(8,128)(2,1)S(1)} %collective-permute-done.5.back2_ref), channel_id=1, source_target_pairs={{0,2},{2,0},{4,6},{6,4},{8,10},{10,8},{12,14},{14,12},{16,18},{18,... | collective-permute-start | bytes 1081352 | tf_op jit(solution)/shard_map/ppermute | solution.py:662
  20.6 0.0 collective-permute-done.2.query_far_ref.refs_3_
  20.6 0.0 collective-permute-start.3
  20.6 1.7 %collective-permute-done.6.back4_ref = bf16[128,1024]{1,0:T(8,128)(2,1)S(1)} collective-permute-done((bf16[128,1024]{1,0:T(8,128)(2,1)S(1)}, bf16[128,1024]{1,0:T(8,128)(2,1)S(1)}, u32[]{:S(2)}, u32[]{:S(2)}) %collective-permute-start.6) | collective-permute-done | bytes 262176 | tf_op jit(solution)/shard_map/ppermute | solution.py:662
  22.3 1.1 %collective-permute-start.8 = (bf16[128,1024]{1,0:T(8,128)(2,1)S(1)}, bf16[128,1024]{1,0:T(8,128)(2,1)S(1)}, u32[]{:S(2)}, u32[]{:S(2)}) collective-permute-start(bf16[128,1024]{1,0:T(8,128)(2,1)S(1)} %collective-permute-done.6.back4_ref), channel_id=1, source_target_pairs={{0,2},{2,0},{4,6},{6,4},{8,10},{10,8},{12,14},{14,12},{16,18},{18,... | collective-permute-start | bytes 786440 | tf_op jit(solution)/shard_map/ppermute | solution.py:662
  23.4 0.7 collective-permute-start.9
  24.1 0.0 copy-start.2
  24.2 0.0 copy-start.4
  24.2 0.9 %collective-permute-done.4.after_ref = bf16[208,1024]{1,0:T(8,128)(2,1)S(1)} collective-permute-done((bf16[208,1024]{1,0:T(8,128)(2,1)}, bf16[208,1024]{1,0:T(8,128)(2,1)S(1)}, u32[]{:S(2)}, u32[]{:S(2)}) %collective-permute-start.4) | collective-permute-done | bytes 426016 | tf_op jit(solution)/shard_map/ppermute | solution.py:662
  25.0 0.0 collective-permute-done.3.query_peer_far_ref.refs_4_
  25.0 0.0 collective-permute-done.8.peer_back4_ref
  25.0 0.0 collective-permute-done.7.peer_back2_ref
  25.0 0.0 copy-done.6
  25.1 0.0 copy-done.8
  25.1 3.6 %attend.1 = (bf16[160,512]{1,0:T(8,128)(2,1)S(1)}, f32[128,128]{1,0:T(8,128)S(1)}) custom-call(s32[16]{0:T(128)S(1)} %copy-done.8, bf16[128,512]{1,0:T(8,128)(2,1)S(1)} %copy-done.6, bf16[128,1024]{1,0:T(8,128)(2,1)S(1)} %copy-done.3, bf16[176,1024]{1,0:T(8,128)(2,1)S(1)} %collective-permute-done.5.back2_ref, ...), custom_call_target="tpu_custom_call" | custom-call | flops 1073741824 | bytes 4194304 | tf_op jit(solution)/shard_map/attend/pallas_call | solution.py:626
  28.6 0.0 copy-done.2
  28.7 0.0 copy-start.5
  28.7 2.6 %body.1 = (f32[160,1024]{1,0:T(8,128)S(1)}, f32[128,1024]{1,0:T(8,128)S(1)}) custom-call(s32[16]{0:T(128)S(1)} %copy-done.8, bf16[128,1024]{1,0:T(8,128)(2,1)S(1)} %bitcast.16, bf16[160,512]{1,0:T(8,128)(2,1)S(1)} %get-tuple-element.49.attended_ref, bf16[208,1024]{1,0:T(8,128)(2,1)S(1)} %collective-permute-done.4.after_ref, bf16[512,1024]{1,0:T(8,128)(2,1)S(1)} %bitcast.20, ...), custom_call_target="tpu_custom_call" | custom-call | flops 1073741824 | bytes 4194304 | tf_op jit(solution)/shard_map/body/pallas_call | solution.py:626
  31.3 0.0 collective-permute-done.9.back5_ref
  31.4 0.0 copy-start.9
  31.4 5.4 %mix.1 = (f32[160,1024]{1,0:T(8,128)S(1)}, f32[128,1024]{1,0:T(8,128)S(1)}, bf16[144,512]{1,0:T(8,128)(2,1)S(1)}, f32[128,128]{1,0:T(8,128)S(1)}) custom-call(s32[16]{0:T(128)S(1)} %copy-done.8, f32[160,1024]{1,0:T(8,128)S(1)} %get-tuple-element.50.mixed_ref, f32[128,1024]{1,0:T(8,128)S(1)} %get-tuple-element.51.late_slope_ref, ...), custom_call_target="tpu_custom_call" | custom-call | flops 1073741824 | bytes 4194304 | tf_op jit(solution)/shard_map/mix/pallas_call | solution.py:626
  36.8 0.7 collective-permute-start.11
  37.5 0.7 collective-permute-start.10
  38.2 0.7 collective-permute-start.12
  38.9 3.8 %own_queries.2 = (f32[128,1024]{1,0:T(8,128)S(1)}, f32[128,512]{1,0:T(8,128)S(1)}, f32[128,512]{1,0:T(8,128)S(1)}) custom-call(s32[16]{0:T(128)S(1)} %copy-done.8, bf16[128,512]{1,0:T(8,128)(2,1)S(1)} %copy-done.6, bf16[128,1024]{1,0:T(8,128)(2,1)S(1)} %copy-done.3, bf16[176,1024]{1,0:T(8,128)(2,1)S(1)} %collective-permute-done.5.back2_ref, ...), custom_call_target="tpu_custom_call" | custom-call | flops 1073741824 | bytes 4194304 | tf_op jit(solution)/shard_map/own_queries/pallas_call | solution.py:626
  42.7 0.0 copy-start.7
  42.7 0.0 collective-permute-done.11.next4_ref
  42.7 0.0 collective-permute-done.10.next2_ref
  42.7 0.1 collective-permute-start.13
  42.8 0.5 collective-permute-start.14
  43.3 0.0 collective-permute-done.12.peer_ref
  43.3 0.9 %collective-permute-done.13.peer_next2_ref = bf16[144,512]{1,0:T(8,128)(2,1)S(1)} collective-permute-done((bf16[144,512]{1,0:T(8,128)(2,1)S(1)}, bf16[144,512]{1,0:T(8,128)(2,1)S(1)}, u32[]{:S(2)}, u32[]{:S(2)}) %collective-permute-start.13) | collective-permute-done | bytes 147488 | tf_op jit(solution)/shard_map/ppermute | solution.py:662
  44.2 0.2 collective-permute-done.14.peer_next4_ref
  44.4 3.3 %own_keys.1 = (bf16[128,1024]{1,0:T(8,128)(2,1)S(1)}, bf16[32,1024]{1,0:T(8,128)(2,1)S(1)}, bf16[128,1024]{1,0:T(8,128)(2,1)S(1)}) custom-call(s32[16]{0:T(128)S(1)} %copy-done.8, bf16[128,1024]{1,0:T(8,128)(2,1)S(1)} %copy-done.3, bf16[128,512]{1,0:T(8,128)(2,1)S(1)} %collective-permute-done.query_peer_ref.refs_2_, ...), custom_call_target="tpu_custom_call" | custom-call | flops 1073741824 | bytes 4194304 | tf_op jit(solution)/shard_map/own_keys/pallas_call | solution.py:626
  47.7 8.3 %collective-permute-start.15 = (bf16[128,1024]{1,0:T(8,128)(2,1)S(1)}, bf16[128,1024]{1,0:T(8,128)(2,1)S(1)}, u32[]{:S(2)}, u32[]{:S(2)}) collective-permute-start(bf16[128,1024]{1,0:T(8,128)(2,1)S(1)} %get-tuple-element.63), channel_id=1, source_target_pairs={{1,0},{3,2},{5,4},{7,6},{9,8},{11,10},{13,12},{15,14},{17,16},{19,... | collective-permute-start | bytes 786440 | tf_op jit(solution)/shard_map/ppermute | solution.py:662
  55.9 1.3 %collective-permute-start.16 = (bf16[32,1024]{1,0:T(8,128)(2,1)S(1)}, bf16[32,1024]{1,0:T(8,128)(2,1)S(1)}, u32[]{:S(2)}, u32[]{:S(2)}) collective-permute-start(bf16[32,1024]{1,0:T(8,128)(2,1)S(1)} %get-tuple-element.64), channel_id=1, source_target_pairs={{3,0},{5,2},{7,4},{9,6},{11,8},{13,10},{15,12},{17,14},{19,16},{21... | collective-permute-start | bytes 196616 | tf_op jit(solution)/shard_map/ppermute | solution.py:662
  57.2 6.2 %collective-permute-done.16.next_ref = bf16[32,1024]{1,0:T(8,128)(2,1)S(1)} collective-permute-done((bf16[32,1024]{1,0:T(8,128)(2,1)S(1)}, bf16[32,1024]{1,0:T(8,128)(2,1)S(1)}, u32[]{:S(2)}, u32[]{:S(2)}) %collective-permute-start.16) | collective-permute-done | bytes 65568 | tf_op jit(solution)/shard_map/ppermute | solution.py:662
  63.4 0.0 collective-permute-done.15.upstream_ref
  63.4 2.8 %mixer.1 = (f32[128,1024]{1,0:T(8,128)S(1)}, bf16[144,512]{1,0:T(8,128)(2,1)S(1)}, f32[128,128]{1,0:T(8,128)S(1)}) custom-call(s32[16]{0:T(128)S(1)} %copy-done.8, bf16[128,1024]{1,0:T(8,128)(2,1)S(1)} %collective-permute-done.15.upstream_ref, bf16[32,1024]{1,0:T(8,128)(2,1)S(1)} %collective-permute-done.16.next_ref, ...), custom_call_target="tpu_custom_call" | custom-call | flops 1073741824 | bytes 4194304 | tf_op jit(solution)/shard_map/mixer/pallas_call | solution.py:626
  66.2 1.9 %collective-permute-start.18 = (bf16[144,512]{1,0:T(8,128)(2,1)S(1)}, bf16[144,512]{1,0:T(8,128)(2,1)S(1)}, u32[]{:S(2)}, u32[]{:S(2)}) collective-permute-start(bf16[144,512]{1,0:T(8,128)(2,1)S(1)} %get-tuple-element.66.message_ref), channel_id=1, source_target_pairs={{8,0},{10,2},{12,4},{14,6},{16,8},{18,10},{20,12},{22,14},{24,16},... | collective-permute-start | bytes 442376 | tf_op jit(solution)/shard_map/ppermute | solution.py:662
  68.2 1.9 %collective-permute-start.17 = (bf16[144,512]{1,0:T(8,128)(2,1)S(1)}, bf16[144,512]{1,0:T(8,128)(2,1)S(1)}, u32[]{:S(2)}, u32[]{:S(2)}) collective-permute-start(bf16[144,512]{1,0:T(8,128)(2,1)S(1)} %get-tuple-element.66.message_ref), channel_id=1, source_target_pairs={{4,0},{6,2},{8,4},{10,6},{12,8},{14,10},{16,12},{18,14},{20,16},{2... | collective-permute-start | bytes 442376 | tf_op jit(solution)/shard_map/ppermute | solution.py:662
  70.1 1.3 %collective-permute-start.19 = (bf16[144,512]{1,0:T(8,128)(2,1)S(1)}, bf16[144,512]{1,0:T(8,128)(2,1)S(1)}, u32[]{:S(2)}, u32[]{:S(2)}) collective-permute-start(bf16[144,512]{1,0:T(8,128)(2,1)S(1)} %get-tuple-element.66.message_ref), channel_id=1, source_target_pairs={{0,2},{2,0},{4,6},{6,4},{8,10},{10,8},{12,14},{14,12},{16,18},{18,... | collective-permute-start | bytes 442376 | tf_op jit(solution)/shard_map/ppermute | solution.py:662
  71.3 3.7 %own_queries.3 = (f32[128,1024]{1,0:T(8,128)S(1)}, f32[128,512]{1,0:T(8,128)S(1)}, f32[128,512]{1,0:T(8,128)S(1)}) custom-call(s32[16]{0:T(128)S(1)} %copy-done.8, bf16[128,512]{1,0:T(8,128)(2,1)S(1)} %copy-done.6, bf16[128,1024]{1,0:T(8,128)(2,1)S(1)} %copy-done.3, bf16[176,1024]{1,0:T(8,128)(2,1)S(1)} %collective-permute-done.5.back2_ref, ...), custom_call_target="tpu_custom_call" | custom-call | flops 1073741824 | bytes 4194304 | tf_op jit(solution)/shard_map/own_queries/pallas_call | solution.py:626
  75.0 0.0 collective-permute-done.18.refs_6_
  75.0 0.1 collective-permute-start.21
  75.1 0.0 collective-permute-done.17.refs_5_
  75.1 2.2 %collective-permute-start.20 = (bf16[144,512]{1,0:T(8,128)(2,1)S(1)}, bf16[144,512]{1,0:T(8,128)(2,1)S(1)}, u32[]{:S(2)}, u32[]{:S(2)}) collective-permute-start(bf16[144,512]{1,0:T(8,128)(2,1)S(1)} %collective-permute-done.17.refs_5_), channel_id=1, source_target_pairs={{0,2},{2,0},{4,6},{6,4},{8,10},{10,8},{12,14},{14,12},{16,18},{18,... | collective-permute-start | bytes 442376 | tf_op jit(solution)/shard_map/ppermute | solution.py:662
  77.3 0.0 collective-permute-done.19.refs_7_
  77.3 0.0 collective-permute-done.21.refs_9_
  77.3 1.0 %collective-permute-done.20.refs_8_ = bf16[144,512]{1,0:T(8,128)(2,1)S(1)} collective-permute-done((bf16[144,512]{1,0:T(8,128)(2,1)S(1)}, bf16[144,512]{1,0:T(8,128)(2,1)S(1)}, u32[]{:S(2)}, u32[]{:S(2)}) %collective-permute-start.20) | collective-permute-done | bytes 147488 | tf_op jit(solution)/shard_map/ppermute | solution.py:662
  78.3 3.9 %last_keys.1 = bf16[128,1024]{1,0:T(8,128)(2,1)} custom-call(s32[16]{0:T(128)S(1)} %copy-done.8, bf16[128,1024]{1,0:T(8,128)(2,1)S(1)} %copy-done.3, bf16[128,512]{1,0:T(8,128)(2,1)S(1)} %collective-permute-done.query_peer_ref.refs_2_, bf16[256,512]{1,0:T(8,128)(2,1)S(1)} %collective-permute-done.2.query_far_ref.refs_3_, ...), custom_call_target="tpu_custom_call" | custom-call | flops 1073741824 | bytes 4194304 | tf_op jit(solution)/shard_map/last_keys/pallas_call | solution.py:626
  (13 shorter events, 0.0 us)
Async XLA Ops:
  3.9 4.2 %collective-permute-start.1 = (bf16[176,1024]{1,0:T(8,128)(2,1)}, bf16[176,1024]{1,0:T(8,128)(2,1)S(1)}, u32[]{:S(2)}, u32[]{:S(2)}) collective-permute-start(bf16[176,1024]{1,0:T(8,128)(2,1)} %get-tuple-element.42), channel_id=1, source_target_pairs={{0,2},{2,0},{4,6},{6,4},{8,10},{10,8},{12,14},{14,12},{16,18},{18,... | collective-permute-start | bytes 1081352 | tf_op jit(solution)/shard_map/ppermute | solution.py:662
  4.6 6.6 %copy-start.3 = (bf16[128,1024]{1,0:T(8,128)(2,1)S(1)}, bf16[128,1024]{1,0:T(8,128)(2,1)}, u32[]{:S(2)}) copy-start(bf16[128,1024]{1,0:T(8,128)(2,1)} %get-tuple-element.53.kept_ref.refs_1_) | copy-start | bytes 786436
  4.6 19.5 %copy-start.10 = (f32[1,31,1024]{2,0,1:T(1,128)S(1)}, f32[1,31,1024]{2,0,1:T(1,128)}, u32[]{:S(2)}) copy-start(f32[1,31,1024]{2,0,1:T(1,128)} %param.15) | copy-start | bytes 380932
  4.6 3.4 %collective-permute-start = (bf16[128,512]{1,0:T(8,128)(2,1)}, bf16[128,512]{1,0:T(8,128)(2,1)S(1)}, u32[]{:S(2)}, u32[]{:S(2)}) collective-permute-start(bf16[128,512]{1,0:T(8,128)(2,1)} %get-tuple-element.41.queries_ref), channel_id=1, source_target_pairs={{0,2},{2,0},{4,6},{6,4},{8,10},{10,8},{12,14},{14,12},{16,18},{18,... | collective-permute-start | bytes 393224 | tf_op jit(solution)/shard_map/ppermute | solution.py:662
  4.7 14.8 %collective-permute-start.5 = (bf16[176,1024]{1,0:T(8,128)(2,1)}, bf16[176,1024]{1,0:T(8,128)(2,1)S(1)}, u32[]{:S(2)}, u32[]{:S(2)}) collective-permute-start(bf16[176,1024]{1,0:T(8,128)(2,1)} %get-tuple-element.42), channel_id=1, source_target_pairs={{0,4},{2,6},{4,8},{6,10},{8,12},{10,14},{12,16},{14,18},{16,20},{1... | collective-permute-start | bytes 1081352 | tf_op jit(solution)/shard_map/ppermute | solution.py:662
  9.0 16.0 %copy-start.6 = (bf16[128,512]{1,0:T(8,128)(2,1)S(1)}, bf16[128,512]{1,0:T(8,128)(2,1)}, u32[]{:S(2)}) copy-start(bf16[128,512]{1,0:T(8,128)(2,1)} %get-tuple-element.41.queries_ref) | copy-start | bytes 393220
  9.0 11.6 %collective-permute-start.2 = (bf16[256,512]{1,0:T(8,128)(2,1)S(1)}, bf16[256,512]{1,0:T(8,128)(2,1)S(1)}, u32[]{:S(2)}, u32[]{:S(2)}) collective-permute-start(bf16[256,512]{1,0:T(8,128)(2,1)S(1)} %pad_maximum_fusion), channel_id=1, source_target_pairs={{4,0},{8,4},{10,2},{12,8},{14,6},{16,12},{18,10},{20,16},{22,14},{... | collective-permute-start | bytes 786440 | tf_op jit(solution)/shard_map/ppermute | solution.py:662
  11.2 11.1 %collective-permute-start.6 = (bf16[128,1024]{1,0:T(8,128)(2,1)S(1)}, bf16[128,1024]{1,0:T(8,128)(2,1)S(1)}, u32[]{:S(2)}, u32[]{:S(2)}) collective-permute-start(bf16[128,1024]{1,0:T(8,128)(2,1)S(1)} %copy-done.3), channel_id=1, source_target_pairs={{0,8},{2,10},{4,12},{6,14},{8,16},{10,18},{12,20},{14,22},{16,24},... | collective-permute-start | bytes 786440 | tf_op jit(solution)/shard_map/ppermute | solution.py:662
  14.5 10.6 %copy-start.8 = (s32[16]{0:T(128)S(1)}, s32[16]{0:T(128)}, u32[]{:S(2)}) copy-start(s32[16]{0:T(128)} %refs_0_.1) | copy-start | bytes 196
  14.5 10.6 %collective-permute-start.4 = (bf16[208,1024]{1,0:T(8,128)(2,1)}, bf16[208,1024]{1,0:T(8,128)(2,1)S(1)}, u32[]{:S(2)}, u32[]{:S(2)}) collective-permute-start(bf16[208,1024]{1,0:T(8,128)(2,1)} %get-tuple-element.44), channel_id=1, source_target_pairs={{2,0},{4,2},{6,4},{8,6},{10,8},{12,10},{14,12},{16,14},{18,16},{20... | collective-permute-start | bytes 1277960 | tf_op jit(solution)/shard_map/ppermute | solution.py:662
  19.5 5.5 %collective-permute-start.7 = (bf16[176,1024]{1,0:T(8,128)(2,1)S(1)}, bf16[176,1024]{1,0:T(8,128)(2,1)S(1)}, u32[]{:S(2)}, u32[]{:S(2)}) collective-permute-start(bf16[176,1024]{1,0:T(8,128)(2,1)S(1)} %collective-permute-done.5.back2_ref), channel_id=1, source_target_pairs={{0,2},{2,0},{4,6},{6,4},{8,10},{10,8},{12,14},{14,12},{16,18},{18,... | collective-permute-start | bytes 1081352 | tf_op jit(solution)/shard_map/ppermute | solution.py:662
  20.6 4.4 %collective-permute-start.3 = (bf16[256,512]{1,0:T(8,128)(2,1)S(1)}, bf16[256,512]{1,0:T(8,128)(2,1)S(1)}, u32[]{:S(2)}, u32[]{:S(2)}) collective-permute-start(bf16[256,512]{1,0:T(8,128)(2,1)S(1)} %collective-permute-done.2.query_far_ref.refs_3_), channel_id=1, source_target_pairs={{0,2},{2,0},{4,6},{6,4},{8,10},{10,8},{12,14},{14,12},{16,18},{18,... | collective-permute-start | bytes 786440 | tf_op jit(solution)/shard_map/ppermute | solution.py:662
  22.3 2.7 %collective-permute-start.8 = (bf16[128,1024]{1,0:T(8,128)(2,1)S(1)}, bf16[128,1024]{1,0:T(8,128)(2,1)S(1)}, u32[]{:S(2)}, u32[]{:S(2)}) collective-permute-start(bf16[128,1024]{1,0:T(8,128)(2,1)S(1)} %collective-permute-done.6.back4_ref), channel_id=1, source_target_pairs={{0,2},{2,0},{4,6},{6,4},{8,10},{10,8},{12,14},{14,12},{16,18},{18,... | collective-permute-start | bytes 786440 | tf_op jit(solution)/shard_map/ppermute | solution.py:662
  23.4 7.9 %collective-permute-start.9 = (bf16[128,1024]{1,0:T(8,128)(2,1)S(1)}, bf16[128,1024]{1,0:T(8,128)(2,1)S(1)}, u32[]{:S(2)}, u32[]{:S(2)}) collective-permute-start(bf16[128,1024]{1,0:T(8,128)(2,1)S(1)} %copy-done.3), channel_id=1, source_target_pairs={{2,12},{6,16},{10,20},{14,24},{18,28},{3,13},{7,17},{11,21},{15,25... | collective-permute-start | bytes 786440 | tf_op jit(solution)/shard_map/ppermute | solution.py:662
  24.1 4.5 %copy-start.2 = (bf16[1,128,1024]{2,1,0:T(8,128)(2,1)S(1)}, bf16[1,128,1024]{2,1,0:T(8,128)(2,1)}, u32[]{:S(2)}) copy-start(bf16[1,128,1024]{2,1,0:T(8,128)(2,1)} %param.9) | copy-start | bytes 786436
  24.2 4.5 %copy-start.4 = (bf16[1,512,1024]{2,1,0:T(8,128)(2,1)S(1)}, bf16[1,512,1024]{2,1,0:T(8,128)(2,1)}, u32[]{:S(2)}) copy-start(bf16[1,512,1024]{2,1,0:T(8,128)(2,1)} %param.14) | copy-start | bytes 3145732
  28.7 2.7 %copy-start.5 = (bf16[128,1024]{1,0:T(8,128)(2,1)S(1)}, bf16[128,1024]{1,0:T(8,128)(2,1)}, u32[]{:S(2)}) copy-start(bf16[128,1024]{1,0:T(8,128)(2,1)} %top_ref.3) | copy-start | bytes 786436
  31.4 7.5 %copy-start.9 = (bf16[1,1024,512]{2,1,0:T(8,128)(2,1)S(1)}, bf16[1,1024,512]{2,1,0:T(8,128)(2,1)}, u32[]{:S(2)}) copy-start(bf16[1,1024,512]{2,1,0:T(8,128)(2,1)} %param.11) | copy-start | bytes 3145732
  36.8 5.9 %collective-permute-start.11 = (bf16[144,512]{1,0:T(8,128)(2,1)S(1)}, bf16[144,512]{1,0:T(8,128)(2,1)S(1)}, u32[]{:S(2)}, u32[]{:S(2)}) collective-permute-start(bf16[144,512]{1,0:T(8,128)(2,1)S(1)} %get-tuple-element.55.message_ref), channel_id=1, source_target_pairs={{9,1},{11,3},{13,5},{15,7},{17,9},{19,11},{21,13},{23,15},{25,17},... | collective-permute-start | bytes 442376 | tf_op jit(solution)/shard_map/ppermute | solution.py:662
  37.5 5.2 %collective-permute-start.10 = (bf16[144,512]{1,0:T(8,128)(2,1)S(1)}, bf16[144,512]{1,0:T(8,128)(2,1)S(1)}, u32[]{:S(2)}, u32[]{:S(2)}) collective-permute-start(bf16[144,512]{1,0:T(8,128)(2,1)S(1)} %get-tuple-element.55.message_ref), channel_id=1, source_target_pairs={{5,1},{7,3},{9,5},{11,7},{13,9},{15,11},{17,13},{19,15},{21,17},{2... | collective-permute-start | bytes 442376 | tf_op jit(solution)/shard_map/ppermute | solution.py:662
  38.2 5.2 %collective-permute-start.12 = (bf16[144,512]{1,0:T(8,128)(2,1)S(1)}, bf16[144,512]{1,0:T(8,128)(2,1)S(1)}, u32[]{:S(2)}, u32[]{:S(2)}) collective-permute-start(bf16[144,512]{1,0:T(8,128)(2,1)S(1)} %get-tuple-element.55.message_ref), channel_id=1, source_target_pairs={{0,2},{2,0},{4,6},{6,4},{8,10},{10,8},{12,14},{14,12},{16,18},{18,... | collective-permute-start | bytes 442376 | tf_op jit(solution)/shard_map/ppermute | solution.py:662
  38.9 5.5 %copy-start = (bf16[1,1024,512]{2,1,0:T(8,128)(2,1)S(1)}, bf16[1,1024,512]{2,1,0:T(8,128)(2,1)}, u32[]{:S(2)}) copy-start(bf16[1,1024,512]{2,1,0:T(8,128)(2,1)} %param.12) | copy-start | bytes 3145732
  38.9 5.5 %copy-start.1 = (bf16[1,1024,512]{2,1,0:T(8,128)(2,1)S(1)}, bf16[1,1024,512]{2,1,0:T(8,128)(2,1)}, u32[]{:S(2)}) copy-start(bf16[1,1024,512]{2,1,0:T(8,128)(2,1)} %param.13) | copy-start | bytes 3145732
  42.7 1.7 %copy-start.7 = (f32[1,1024]{1,0:T(1,128)S(1)}, f32[1,1024]{1,0:T(1,128)}, u32[]{:S(2)}) copy-start(f32[1,1024]{1,0:T(1,128)} %refs_12_.1) | copy-start | bytes 12292
  42.7 1.4 %collective-permute-start.13 = (bf16[144,512]{1,0:T(8,128)(2,1)S(1)}, bf16[144,512]{1,0:T(8,128)(2,1)S(1)}, u32[]{:S(2)}, u32[]{:S(2)}) collective-permute-start(bf16[144,512]{1,0:T(8,128)(2,1)S(1)} %collective-permute-done.10.next2_ref), channel_id=1, source_target_pairs={{0,2},{2,0},{4,6},{6,4},{8,10},{10,8},{12,14},{14,12},{16,18},{18,... | collective-permute-start | bytes 442376 | tf_op jit(solution)/shard_map/ppermute | solution.py:662
  42.8 1.5 %collective-permute-start.14 = (bf16[144,512]{1,0:T(8,128)(2,1)S(1)}, bf16[144,512]{1,0:T(8,128)(2,1)S(1)}, u32[]{:S(2)}, u32[]{:S(2)}) collective-permute-start(bf16[144,512]{1,0:T(8,128)(2,1)S(1)} %collective-permute-done.11.next4_ref), channel_id=1, source_target_pairs={{0,2},{2,0},{4,6},{6,4},{8,10},{10,8},{12,14},{14,12},{16,18},{18,... | collective-permute-start | bytes 442376 | tf_op jit(solution)/shard_map/ppermute | solution.py:662
  47.7 15.8 %collective-permute-start.15 = (bf16[128,1024]{1,0:T(8,128)(2,1)S(1)}, bf16[128,1024]{1,0:T(8,128)(2,1)S(1)}, u32[]{:S(2)}, u32[]{:S(2)}) collective-permute-start(bf16[128,1024]{1,0:T(8,128)(2,1)S(1)} %get-tuple-element.63), channel_id=1, source_target_pairs={{1,0},{3,2},{5,4},{7,6},{9,8},{11,10},{13,12},{15,14},{17,16},{19,... | collective-permute-start | bytes 786440 | tf_op jit(solution)/shard_map/ppermute | solution.py:662
  55.9 7.5 %collective-permute-start.16 = (bf16[32,1024]{1,0:T(8,128)(2,1)S(1)}, bf16[32,1024]{1,0:T(8,128)(2,1)S(1)}, u32[]{:S(2)}, u32[]{:S(2)}) collective-permute-start(bf16[32,1024]{1,0:T(8,128)(2,1)S(1)} %get-tuple-element.64), channel_id=1, source_target_pairs={{3,0},{5,2},{7,4},{9,6},{11,8},{13,10},{15,12},{17,14},{19,16},{21... | collective-permute-start | bytes 196616 | tf_op jit(solution)/shard_map/ppermute | solution.py:662
  66.2 8.8 %collective-permute-start.18 = (bf16[144,512]{1,0:T(8,128)(2,1)S(1)}, bf16[144,512]{1,0:T(8,128)(2,1)S(1)}, u32[]{:S(2)}, u32[]{:S(2)}) collective-permute-start(bf16[144,512]{1,0:T(8,128)(2,1)S(1)} %get-tuple-element.66.message_ref), channel_id=1, source_target_pairs={{8,0},{10,2},{12,4},{14,6},{16,8},{18,10},{20,12},{22,14},{24,16},... | collective-permute-start | bytes 442376 | tf_op jit(solution)/shard_map/ppermute | solution.py:662
  68.2 6.9 %collective-permute-start.17 = (bf16[144,512]{1,0:T(8,128)(2,1)S(1)}, bf16[144,512]{1,0:T(8,128)(2,1)S(1)}, u32[]{:S(2)}, u32[]{:S(2)}) collective-permute-start(bf16[144,512]{1,0:T(8,128)(2,1)S(1)} %get-tuple-element.66.message_ref), channel_id=1, source_target_pairs={{4,0},{6,2},{8,4},{10,6},{12,8},{14,10},{16,12},{18,14},{20,16},{2... | collective-permute-start | bytes 442376 | tf_op jit(solution)/shard_map/ppermute | solution.py:662
  70.1 7.2 %collective-permute-start.19 = (bf16[144,512]{1,0:T(8,128)(2,1)S(1)}, bf16[144,512]{1,0:T(8,128)(2,1)S(1)}, u32[]{:S(2)}, u32[]{:S(2)}) collective-permute-start(bf16[144,512]{1,0:T(8,128)(2,1)S(1)} %get-tuple-element.66.message_ref), channel_id=1, source_target_pairs={{0,2},{2,0},{4,6},{6,4},{8,10},{10,8},{12,14},{14,12},{16,18},{18,... | collective-permute-start | bytes 442376 | tf_op jit(solution)/shard_map/ppermute | solution.py:662
  75.0 2.3 %collective-permute-start.21 = (bf16[144,512]{1,0:T(8,128)(2,1)S(1)}, bf16[144,512]{1,0:T(8,128)(2,1)S(1)}, u32[]{:S(2)}, u32[]{:S(2)}) collective-permute-start(bf16[144,512]{1,0:T(8,128)(2,1)S(1)} %collective-permute-done.18.refs_6_), channel_id=1, source_target_pairs={{0,2},{2,0},{4,6},{6,4},{8,10},{10,8},{12,14},{14,12},{16,18},{18,... | collective-permute-start | bytes 442376 | tf_op jit(solution)/shard_map/ppermute | solution.py:662
  75.1 3.2 %collective-permute-start.20 = (bf16[144,512]{1,0:T(8,128)(2,1)S(1)}, bf16[144,512]{1,0:T(8,128)(2,1)S(1)}, u32[]{:S(2)}, u32[]{:S(2)}) collective-permute-start(bf16[144,512]{1,0:T(8,128)(2,1)S(1)} %collective-permute-done.17.refs_5_), channel_id=1, source_target_pairs={{0,2},{2,0},{4,6},{6,4},{8,10},{10,8},{12,14},{14,12},{16,18},{18,... | collective-permute-start | bytes 442376 | tf_op jit(solution)/shard_map/ppermute | solution.py:662

commit v10 on v9

--- a/solution.py
+++ b/solution.py
@@ -467,9 +467,12 @@
     log_ref,
     dot_ref,
     w_query_ref,
+    own_ref,
     out_ref,
     key_sum_ref,
     value_sum_ref,
+    unit_ref,
+    inverse_ref,
     window,
     query_grad,
 ):
@@ -522,6 +525,9 @@
             key_valid,
         )
     out_ref[...] = dot_nt(query_grad[...], w_query_ref[...])
+    unit, inverse = unit_rows(own_ref[...].astype(F32))
+    unit_ref[...] = unit
+    inverse_ref[...] = jnp.broadcast_to(inverse, inverse_ref.shape)
 
 
 def key_kernel(
@@ -538,7 +544,8 @@
     w_key_ref,
     w_value_ref,
     gain_ref,
-    own_ref,
+    unit_ref,
+    inverse_ref,
     total_ref,
     partial_ref,
     key_sum_ref,
@@ -599,7 +606,7 @@
     normed_grad = partial_ref[...] + dot_nt(key_grad[...], w_key_ref[...])
     normed_grad = normed_grad + dot_nt(value_grad[...], w_value_ref[...])
     scaled = normed_grad * gain_ref[...]
-    unit, inverse = unit_rows(own_ref[...].astype(F32))
+    unit, inverse = unit_ref[...], inverse_ref[:, 0:1]
     back = inverse * (
         scaled
         - jnp.mean(scaled, axis=-1, keepdims=True)
@@ -782,11 +789,11 @@
         grad2 = moved(message, across(-2, here))
         grad4 = moved(message, across(-4, here))
         peer_grad = moved(message, swap)
-        partial, key_sum, value_sum = call(
+        partial, key_sum, value_sum, unit, inverse = call(
             query_kernel,
             "own_queries",
             placed(
-                "svvvvvvvvvvv",
+                "svvvvvvvvvvvv",
                 group_valid,
                 queries,
                 kept,
@@ -799,8 +806,15 @@
                 logs,
                 dots,
                 query_weight,
+                own,
             ),
-            [((ROWS, width), F32), ((ROWS, wide), F32), ((ROWS, wide), F32)],
+            [
+                ((ROWS, width), F32),
+                ((ROWS, wide), F32),
+                ((ROWS, wide), F32),
+                ((ROWS, width), F32),
+                ((ROWS, PAIR), F32),
+            ],
             [
                 ((span, 2 * wide), BF16),
                 ((ROWS, wide), BF16),
@@ -811,7 +825,7 @@
         peer_grad2 = moved(grad2, swap)
         peer_grad4 = moved(grad4, swap)
         key_operands = placed(
-            "svvvvvvvvvvvvvvvvvvs",
+            "svvvvvvvvvvvvvvvvvvvs",
             group_valid,
             kept,
             query_peer,
@@ -825,7 +839,8 @@
             key_weight,
             value_weight,
             norm_gain,
-            own,
+            unit,
+            inverse,
             total,
             partial,
             key_sum,

time: 82.6 us -> 83.2 us (level)
  no operation moved by 1% of the time
where the time goes in v10:
time: 83.2 us; the launch traced here: 82.8 us
  starting transfers between devices  35 us (42%)
  Pallas kernels  33 us (40%)
  waiting for transfers between devices  12.8 us (15%)
  other arithmetic  0.92 us (1%)
    ppermute x22, starting transfers between devices, moved(): return lax.ppermute(value, ('tm', 'section'), pairs)  35 us
    pallas_call x9, Pallas kernels, call(): pl.pallas_call(kernel, name=name, in_specs=[kinds[place] for _, place in...  33 us
    ppermute x22, waiting for transfers between devices, moved(): return lax.ppermute(value, ('tm', 'section'), pairs)  12.8 us
  transfers between devices with their start and end apart: 22, of which 7 were waited for; matrix products, arithmetic and copies ran while one was open for 1% of the time, Pallas kernels for 17%

profile of v10, /device:TPU:19, one launch (start us, length us, event | category | flops | bytes accessed | tf_op | source)
XLA Modules:
  0.0 82.8 jit_solution(7413463168890527490)
XLA Ops:
  0.0 3.9 %project.1 = (bf16[128,512]{1,0:T(8,128)(2,1)}, bf16[128,1024]{1,0:T(8,128)(2,1)}, bf16[176,1024]{1,0:T(8,128)(2,1)}, bf16[208,1024]{1,0:T(8,128)(2,1)}) custom-call(bf16[128,1024]{1,0:T(8,128)(2,1)} %bitcast.21, bf16[128,1024]{1,0:T(8,128)(2,1)} %top_ref.3, f32[1,1024]{1,0:T(1,128)} %refs_12_.1, bf16[1024,512]{1,0:T(8,128)(2,1)} %bitcast.26, ...), custom_call_target="tpu_custom_call" | custom-call | flops 1073741824 | bytes 4194304 | tf_op jit(solution)/shard_map/project/pallas_call | solution.py:633
  3.9 0.7 collective-permute-start.1
  4.6 0.1 collective-permute-start
  4.7 3.3 %collective-permute-start.5 = (bf16[176,1024]{1,0:T(8,128)(2,1)}, bf16[176,1024]{1,0:T(8,128)(2,1)S(1)}, u32[]{:S(2)}, u32[]{:S(2)}) collective-permute-start(bf16[176,1024]{1,0:T(8,128)(2,1)} %get-tuple-element.46), channel_id=1, source_target_pairs={{0,4},{2,6},{4,8},{6,10},{8,12},{10,14},{12,16},{14,18},{16,20},{1... | collective-permute-start | bytes 1081352 | tf_op jit(solution)/shard_map/ppermute | solution.py:669
  8.1 0.0 collective-permute-done.query_peer_ref.refs_2_
  8.1 0.0 collective-permute-done.1.peer_ref
  8.1 0.9 %pad_maximum_fusion = bf16[256,512]{1,0:T(8,128)(2,1)S(1)} fusion(bf16[128,512]{1,0:T(8,128)(2,1)S(1)} %collective-permute-done.query_peer_ref.refs_2_, bf16[128,512]{1,0:T(8,128)(2,1)} %get-tuple-element.45.queries_ref), kind=kLoop, calls=%fused_computation | loop fusion | flops 524288 | bytes 524288 | tf_op jit(solution)/shard_map/concatenate | solution.py:712
  9.0 2.2 %collective-permute-start.2 = (bf16[256,512]{1,0:T(8,128)(2,1)S(1)}, bf16[256,512]{1,0:T(8,128)(2,1)S(1)}, u32[]{:S(2)}, u32[]{:S(2)}) collective-permute-start(bf16[256,512]{1,0:T(8,128)(2,1)S(1)} %pad_maximum_fusion), channel_id=1, source_target_pairs={{4,0},{8,4},{10,2},{12,8},{14,6},{16,12},{18,10},{20,16},{22,14},{... | collective-permute-start | bytes 786440 | tf_op jit(solution)/shard_map/ppermute | solution.py:669
  11.2 0.0 copy-done.2
  11.2 3.2 %collective-permute-start.6 = (bf16[128,1024]{1,0:T(8,128)(2,1)S(1)}, bf16[128,1024]{1,0:T(8,128)(2,1)S(1)}, u32[]{:S(2)}, u32[]{:S(2)}) collective-permute-start(bf16[128,1024]{1,0:T(8,128)(2,1)S(1)} %copy-done.2), channel_id=1, source_target_pairs={{0,8},{2,10},{4,12},{6,14},{8,16},{10,18},{12,20},{14,22},{16,24},... | collective-permute-start | bytes 786440 | tf_op jit(solution)/shard_map/ppermute | solution.py:669
  14.5 0.0 copy-start.8
  14.5 3.0 %collective-permute-start.4 = (bf16[208,1024]{1,0:T(8,128)(2,1)}, bf16[208,1024]{1,0:T(8,128)(2,1)S(1)}, u32[]{:S(2)}, u32[]{:S(2)}) collective-permute-start(bf16[208,1024]{1,0:T(8,128)(2,1)} %get-tuple-element.48), channel_id=1, source_target_pairs={{2,0},{4,2},{6,4},{8,6},{10,8},{12,10},{14,12},{16,14},{18,16},{20... | collective-permute-start | bytes 1277960 | tf_op jit(solution)/shard_map/ppermute | solution.py:669
  17.5 2.0 %collective-permute-done.5.back2_ref = bf16[176,1024]{1,0:T(8,128)(2,1)S(1)} collective-permute-done((bf16[176,1024]{1,0:T(8,128)(2,1)}, bf16[176,1024]{1,0:T(8,128)(2,1)S(1)}, u32[]{:S(2)}, u32[]{:S(2)}) %collective-permute-start.5) | collective-permute-done | bytes 360480 | tf_op jit(solution)/shard_map/ppermute | solution.py:669
  19.5 1.1 %collective-permute-start.7 = (bf16[176,1024]{1,0:T(8,128)(2,1)S(1)}, bf16[176,1024]{1,0:T(8,128)(2,1)S(1)}, u32[]{:S(2)}, u32[]{:S(2)}) collective-permute-start(bf16[176,1024]{1,0:T(8,128)(2,1)S(1)} %collective-permute-done.5.back2_ref), channel_id=1, source_target_pairs={{0,2},{2,0},{4,6},{6,4},{8,10},{10,8},{12,14},{14,12},{16,18},{18,... | collective-permute-start | bytes 1081352 | tf_op jit(solution)/shard_map/ppermute | solution.py:669
  20.6 0.0 collective-permute-done.2.query_far_ref.refs_3_
  20.6 0.0 collective-permute-start.3
  20.6 1.7 %collective-permute-done.6.back4_ref = bf16[128,1024]{1,0:T(8,128)(2,1)S(1)} collective-permute-done((bf16[128,1024]{1,0:T(8,128)(2,1)S(1)}, bf16[128,1024]{1,0:T(8,128)(2,1)S(1)}, u32[]{:S(2)}, u32[]{:S(2)}) %collective-permute-start.6) | collective-permute-done | bytes 262176 | tf_op jit(solution)/shard_map/ppermute | solution.py:669
  22.3 1.1 %collective-permute-start.8 = (bf16[128,1024]{1,0:T(8,128)(2,1)S(1)}, bf16[128,1024]{1,0:T(8,128)(2,1)S(1)}, u32[]{:S(2)}, u32[]{:S(2)}) collective-permute-start(bf16[128,1024]{1,0:T(8,128)(2,1)S(1)} %collective-permute-done.6.back4_ref), channel_id=1, source_target_pairs={{0,2},{2,0},{4,6},{6,4},{8,10},{10,8},{12,14},{14,12},{16,18},{18,... | collective-permute-start | bytes 786440 | tf_op jit(solution)/shard_map/ppermute | solution.py:669
  23.4 0.7 collective-permute-start.9
  24.1 0.0 copy-start.3
  24.2 0.0 copy-start.4
  24.2 0.9 %collective-permute-done.4.after_ref = bf16[208,1024]{1,0:T(8,128)(2,1)S(1)} collective-permute-done((bf16[208,1024]{1,0:T(8,128)(2,1)}, bf16[208,1024]{1,0:T(8,128)(2,1)S(1)}, u32[]{:S(2)}, u32[]{:S(2)}) %collective-permute-start.4) | collective-permute-done | bytes 426016 | tf_op jit(solution)/shard_map/ppermute | solution.py:669
  25.0 0.0 collective-permute-done.3.query_peer_far_ref.refs_4_
  25.0 0.0 collective-permute-done.8.peer_back4_ref
  25.0 0.0 collective-permute-done.7.peer_back2_ref
  25.0 0.0 copy-done.6
  25.1 0.0 copy-done.8
  25.1 3.6 %attend.1 = (bf16[160,512]{1,0:T(8,128)(2,1)S(1)}, f32[128,128]{1,0:T(8,128)S(1)}) custom-call(s32[16]{0:T(128)S(1)} %copy-done.8, bf16[128,512]{1,0:T(8,128)(2,1)S(1)} %copy-done.6, bf16[128,1024]{1,0:T(8,128)(2,1)S(1)} %copy-done.2, bf16[176,1024]{1,0:T(8,128)(2,1)S(1)} %collective-permute-done.5.back2_ref, ...), custom_call_target="tpu_custom_call" | custom-call | flops 1073741824 | bytes 4194304 | tf_op jit(solution)/shard_map/attend/pallas_call | solution.py:633
  28.6 0.0 copy-done.3
  28.7 0.0 copy-start.5
  28.7 2.6 %body.1 = (f32[160,1024]{1,0:T(8,128)S(1)}, f32[128,1024]{1,0:T(8,128)S(1)}) custom-call(s32[16]{0:T(128)S(1)} %copy-done.8, bf16[128,1024]{1,0:T(8,128)(2,1)S(1)} %bitcast.22, bf16[160,512]{1,0:T(8,128)(2,1)S(1)} %get-tuple-element.53.attended_ref, bf16[208,1024]{1,0:T(8,128)(2,1)S(1)} %collective-permute-done.4.after_ref, bf16[512,1024]{1,0:T(8,128)(2,1)S(1)} %bitcast.15, ...), custom_call_target="tpu_custom_call" | custom-call | flops 1073741824 | bytes 4194304 | tf_op jit(solution)/shard_map/body/pallas_call | solution.py:633
  31.3 0.0 collective-permute-done.9.back5_ref
  31.4 0.0 copy-start.9
  31.4 5.4 %mix.1 = (f32[160,1024]{1,0:T(8,128)S(1)}, f32[128,1024]{1,0:T(8,128)S(1)}, bf16[144,512]{1,0:T(8,128)(2,1)S(1)}, f32[128,128]{1,0:T(8,128)S(1)}) custom-call(s32[16]{0:T(128)S(1)} %copy-done.8, f32[160,1024]{1,0:T(8,128)S(1)} %get-tuple-element.54.mixed_ref, f32[128,1024]{1,0:T(8,128)S(1)} %get-tuple-element.55.late_slope_ref, ...), custom_call_target="tpu_custom_call" | custom-call | flops 1073741824 | bytes 4194304 | tf_op jit(solution)/shard_map/mix/pallas_call | solution.py:633
  36.8 0.7 collective-permute-start.11
  37.5 0.7 collective-permute-start.10
  38.2 0.7 collective-permute-start.12
  38.9 3.9 %own_queries.2 = (f32[128,1024]{1,0:T(8,128)S(1)}, f32[128,512]{1,0:T(8,128)S(1)}, f32[128,512]{1,0:T(8,128)S(1)}, f32[128,1024]{1,0:T(8,128)S(1)}, f32[128,128]{1,0:T(8,128)S(1)}) custom-call(s32[16]{0:T(128)S(1)} %copy-done.8, bf16[128,512]{1,0:T(8,128)(2,1)S(1)} %copy-done.6, bf16[128,1024]{1,0:T(8,128)(2,1)S(1)} %copy-done.2, ...), custom_call_target="tpu_custom_call" | custom-call | flops 1073741824 | bytes 4194304 | tf_op jit(solution)/shard_map/own_queries/pallas_call | solution.py:633
  42.7 0.0 collective-permute-done.11.next4_ref
  42.7 0.0 collective-permute-done.10.next2_ref
  42.8 0.1 collective-permute-start.13
  42.9 0.5 collective-permute-start.14
  43.3 0.0 collective-permute-done.12.peer_ref
  43.3 0.9 %collective-permute-done.13.peer_next2_ref = bf16[144,512]{1,0:T(8,128)(2,1)S(1)} collective-permute-done((bf16[144,512]{1,0:T(8,128)(2,1)S(1)}, bf16[144,512]{1,0:T(8,128)(2,1)S(1)}, u32[]{:S(2)}, u32[]{:S(2)}) %collective-permute-start.13) | collective-permute-done | bytes 147488 | tf_op jit(solution)/shard_map/ppermute | solution.py:669
  44.2 0.2 collective-permute-done.14.peer_next4_ref
  44.4 0.7 copy-done.7
  45.1 3.2 %own_keys.1 = (bf16[128,1024]{1,0:T(8,128)(2,1)S(1)}, bf16[32,1024]{1,0:T(8,128)(2,1)S(1)}, bf16[128,1024]{1,0:T(8,128)(2,1)S(1)}) custom-call(s32[16]{0:T(128)S(1)} %copy-done.8, bf16[128,1024]{1,0:T(8,128)(2,1)S(1)} %copy-done.2, bf16[128,512]{1,0:T(8,128)(2,1)S(1)} %collective-permute-done.query_peer_ref.refs_2_, ...), custom_call_target="tpu_custom_call" | custom-call | flops 1073741824 | bytes 4194304 | tf_op jit(solution)/shard_map/own_keys/pallas_call | solution.py:633
  48.3 8.3 %collective-permute-start.15 = (bf16[128,1024]{1,0:T(8,128)(2,1)S(1)}, bf16[128,1024]{1,0:T(8,128)(2,1)S(1)}, u32[]{:S(2)}, u32[]{:S(2)}) collective-permute-start(bf16[128,1024]{1,0:T(8,128)(2,1)S(1)} %get-tuple-element.69), channel_id=1, source_target_pairs={{1,0},{3,2},{5,4},{7,6},{9,8},{11,10},{13,12},{15,14},{17,16},{19,... | collective-permute-start | bytes 786440 | tf_op jit(solution)/shard_map/ppermute | solution.py:669
  56.5 1.3 %collective-permute-start.16 = (bf16[32,1024]{1,0:T(8,128)(2,1)S(1)}, bf16[32,1024]{1,0:T(8,128)(2,1)S(1)}, u32[]{:S(2)}, u32[]{:S(2)}) collective-permute-start(bf16[32,1024]{1,0:T(8,128)(2,1)S(1)} %get-tuple-element.70), channel_id=1, source_target_pairs={{3,0},{5,2},{7,4},{9,6},{11,8},{13,10},{15,12},{17,14},{19,16},{21... | collective-permute-start | bytes 196616 | tf_op jit(solution)/shard_map/ppermute | solution.py:669
  57.8 6.2 %collective-permute-done.16.next_ref = bf16[32,1024]{1,0:T(8,128)(2,1)S(1)} collective-permute-done((bf16[32,1024]{1,0:T(8,128)(2,1)S(1)}, bf16[32,1024]{1,0:T(8,128)(2,1)S(1)}, u32[]{:S(2)}, u32[]{:S(2)}) %collective-permute-start.16) | collective-permute-done | bytes 65568 | tf_op jit(solution)/shard_map/ppermute | solution.py:669
  64.0 0.0 collective-permute-done.15.upstream_ref
  64.0 2.8 %mixer.1 = (f32[128,1024]{1,0:T(8,128)S(1)}, bf16[144,512]{1,0:T(8,128)(2,1)S(1)}, f32[128,128]{1,0:T(8,128)S(1)}) custom-call(s32[16]{0:T(128)S(1)} %copy-done.8, bf16[128,1024]{1,0:T(8,128)(2,1)S(1)} %collective-permute-done.15.upstream_ref, bf16[32,1024]{1,0:T(8,128)(2,1)S(1)} %collective-permute-done.16.next_ref, ...), custom_call_target="tpu_custom_call" | custom-call | flops 1073741824 | bytes 4194304 | tf_op jit(solution)/shard_map/mixer/pallas_call | solution.py:633
  66.8 1.9 %collective-permute-start.18 = (bf16[144,512]{1,0:T(8,128)(2,1)S(1)}, bf16[144,512]{1,0:T(8,128)(2,1)S(1)}, u32[]{:S(2)}, u32[]{:S(2)}) collective-permute-start(bf16[144,512]{1,0:T(8,128)(2,1)S(1)} %get-tuple-element.72.message_ref), channel_id=1, source_target_pairs={{8,0},{10,2},{12,4},{14,6},{16,8},{18,10},{20,12},{22,14},{24,16},... | collective-permute-start | bytes 442376 | tf_op jit(solution)/shard_map/ppermute | solution.py:669
  68.8 1.9 %collective-permute-start.17 = (bf16[144,512]{1,0:T(8,128)(2,1)S(1)}, bf16[144,512]{1,0:T(8,128)(2,1)S(1)}, u32[]{:S(2)}, u32[]{:S(2)}) collective-permute-start(bf16[144,512]{1,0:T(8,128)(2,1)S(1)} %get-tuple-element.72.message_ref), channel_id=1, source_target_pairs={{4,0},{6,2},{8,4},{10,6},{12,8},{14,10},{16,12},{18,14},{20,16},{2... | collective-permute-start | bytes 442376 | tf_op jit(solution)/shard_map/ppermute | solution.py:669
  70.7 1.3 %collective-permute-start.19 = (bf16[144,512]{1,0:T(8,128)(2,1)S(1)}, bf16[144,512]{1,0:T(8,128)(2,1)S(1)}, u32[]{:S(2)}, u32[]{:S(2)}) collective-permute-start(bf16[144,512]{1,0:T(8,128)(2,1)S(1)} %get-tuple-element.72.message_ref), channel_id=1, source_target_pairs={{0,2},{2,0},{4,6},{6,4},{8,10},{10,8},{12,14},{14,12},{16,18},{18,... | collective-permute-start | bytes 442376 | tf_op jit(solution)/shard_map/ppermute | solution.py:669
  71.9 3.7 %own_queries.3 = (f32[128,1024]{1,0:T(8,128)S(1)}, f32[128,512]{1,0:T(8,128)S(1)}, f32[128,512]{1,0:T(8,128)S(1)}, f32[128,1024]{1,0:T(8,128)S(1)}, f32[128,128]{1,0:T(8,128)S(1)}) custom-call(s32[16]{0:T(128)S(1)} %copy-done.8, bf16[128,512]{1,0:T(8,128)(2,1)S(1)} %copy-done.6, bf16[128,1024]{1,0:T(8,128)(2,1)S(1)} %copy-done.2, ...), custom_call_target="tpu_custom_call" | custom-call | flops 1073741824 | bytes 4194304 | tf_op jit(solution)/shard_map/own_queries/pallas_call | solution.py:633
  75.6 0.0 collective-permute-done.18.refs_6_
  75.6 0.1 collective-permute-start.21
  75.7 0.0 collective-permute-done.17.refs_5_
  75.7 2.2 %collective-permute-start.20 = (bf16[144,512]{1,0:T(8,128)(2,1)S(1)}, bf16[144,512]{1,0:T(8,128)(2,1)S(1)}, u32[]{:S(2)}, u32[]{:S(2)}) collective-permute-start(bf16[144,512]{1,0:T(8,128)(2,1)S(1)} %collective-permute-done.17.refs_5_), channel_id=1, source_target_pairs={{0,2},{2,0},{4,6},{6,4},{8,10},{10,8},{12,14},{14,12},{16,18},{18,... | collective-permute-start | bytes 442376 | tf_op jit(solution)/shard_map/ppermute | solution.py:669
  77.9 0.0 collective-permute-done.19.refs_7_
  77.9 0.0 collective-permute-done.21.refs_9_
  77.9 1.0 %collective-permute-done.20.refs_8_ = bf16[144,512]{1,0:T(8,128)(2,1)S(1)} collective-permute-done((bf16[144,512]{1,0:T(8,128)(2,1)S(1)}, bf16[144,512]{1,0:T(8,128)(2,1)S(1)}, u32[]{:S(2)}, u32[]{:S(2)}) %collective-permute-start.20) | collective-permute-done | bytes 147488 | tf_op jit(solution)/shard_map/ppermute | solution.py:669
  78.9 3.9 %last_keys.1 = bf16[128,1024]{1,0:T(8,128)(2,1)} custom-call(s32[16]{0:T(128)S(1)} %copy-done.8, bf16[128,1024]{1,0:T(8,128)(2,1)S(1)} %copy-done.2, bf16[128,512]{1,0:T(8,128)(2,1)S(1)} %collective-permute-done.query_peer_ref.refs_2_, bf16[256,512]{1,0:T(8,128)(2,1)S(1)} %collective-permute-done.2.query_far_ref.refs_3_, ...), custom_call_target="tpu_custom_call" | custom-call | flops 1073741824 | bytes 4194304 | tf_op jit(solution)/shard_map/last_keys/pallas_call | solution.py:633
  (13 shorter events, 0.0 us)
Async XLA Ops:
  3.9 4.2 %collective-permute-start.1 = (bf16[176,1024]{1,0:T(8,128)(2,1)}, bf16[176,1024]{1,0:T(8,128)(2,1)S(1)}, u32[]{:S(2)}, u32[]{:S(2)}) collective-permute-start(bf16[176,1024]{1,0:T(8,128)(2,1)} %get-tuple-element.46), channel_id=1, source_target_pairs={{0,2},{2,0},{4,6},{6,4},{8,10},{10,8},{12,14},{14,12},{16,18},{18,... | collective-permute-start | bytes 1081352 | tf_op jit(solution)/shard_map/ppermute | solution.py:669
  4.6 6.6 %copy-start.2 = (bf16[128,1024]{1,0:T(8,128)(2,1)S(1)}, bf16[128,1024]{1,0:T(8,128)(2,1)}, u32[]{:S(2)}) copy-start(bf16[128,1024]{1,0:T(8,128)(2,1)} %get-tuple-element.57.kept_ref.refs_1_) | copy-start | bytes 786436
  4.6 19.5 %copy-start.10 = (f32[1,31,1024]{2,0,1:T(1,128)S(1)}, f32[1,31,1024]{2,0,1:T(1,128)}, u32[]{:S(2)}) copy-start(f32[1,31,1024]{2,0,1:T(1,128)} %param.15) | copy-start | bytes 380932
  4.6 3.4 %collective-permute-start = (bf16[128,512]{1,0:T(8,128)(2,1)}, bf16[128,512]{1,0:T(8,128)(2,1)S(1)}, u32[]{:S(2)}, u32[]{:S(2)}) collective-permute-start(bf16[128,512]{1,0:T(8,128)(2,1)} %get-tuple-element.45.queries_ref), channel_id=1, source_target_pairs={{0,2},{2,0},{4,6},{6,4},{8,10},{10,8},{12,14},{14,12},{16,18},{18,... | collective-permute-start | bytes 393224 | tf_op jit(solution)/shard_map/ppermute | solution.py:669
  4.7 14.8 %collective-permute-start.5 = (bf16[176,1024]{1,0:T(8,128)(2,1)}, bf16[176,1024]{1,0:T(8,128)(2,1)S(1)}, u32[]{:S(2)}, u32[]{:S(2)}) collective-permute-start(bf16[176,1024]{1,0:T(8,128)(2,1)} %get-tuple-element.46), channel_id=1, source_target_pairs={{0,4},{2,6},{4,8},{6,10},{8,12},{10,14},{12,16},{14,18},{16,20},{1... | collective-permute-start | bytes 1081352 | tf_op jit(solution)/shard_map/ppermute | solution.py:669
  9.0 16.0 %copy-start.6 = (bf16[128,512]{1,0:T(8,128)(2,1)S(1)}, bf16[128,512]{1,0:T(8,128)(2,1)}, u32[]{:S(2)}) copy-start(bf16[128,512]{1,0:T(8,128)(2,1)} %get-tuple-element.45.queries_ref) | copy-start | bytes 393220
  9.0 11.6 %collective-permute-start.2 = (bf16[256,512]{1,0:T(8,128)(2,1)S(1)}, bf16[256,512]{1,0:T(8,128)(2,1)S(1)}, u32[]{:S(2)}, u32[]{:S(2)}) collective-permute-start(bf16[256,512]{1,0:T(8,128)(2,1)S(1)} %pad_maximum_fusion), channel_id=1, source_target_pairs={{4,0},{8,4},{10,2},{12,8},{14,6},{16,12},{18,10},{20,16},{22,14},{... | collective-permute-start | bytes 786440 | tf_op jit(solution)/shard_map/ppermute | solution.py:669
  11.2 11.1 %collective-permute-start.6 = (bf16[128,1024]{1,0:T(8,128)(2,1)S(1)}, bf16[128,1024]{1,0:T(8,128)(2,1)S(1)}, u32[]{:S(2)}, u32[]{:S(2)}) collective-permute-start(bf16[128,1024]{1,0:T(8,128)(2,1)S(1)} %copy-done.2), channel_id=1, source_target_pairs={{0,8},{2,10},{4,12},{6,14},{8,16},{10,18},{12,20},{14,22},{16,24},... | collective-permute-start | bytes 786440 | tf_op jit(solution)/shard_map/ppermute | solution.py:669
  14.5 10.6 %copy-start.8 = (s32[16]{0:T(128)S(1)}, s32[16]{0:T(128)}, u32[]{:S(2)}) copy-start(s32[16]{0:T(128)} %refs_0_.1) | copy-start | bytes 196
  14.5 10.6 %collective-permute-start.4 = (bf16[208,1024]{1,0:T(8,128)(2,1)}, bf16[208,1024]{1,0:T(8,128)(2,1)S(1)}, u32[]{:S(2)}, u32[]{:S(2)}) collective-permute-start(bf16[208,1024]{1,0:T(8,128)(2,1)} %get-tuple-element.48), channel_id=1, source_target_pairs={{2,0},{4,2},{6,4},{8,6},{10,8},{12,10},{14,12},{16,14},{18,16},{20... | collective-permute-start | bytes 1277960 | tf_op jit(solution)/shard_map/ppermute | solution.py:669
  19.5 5.5 %collective-permute-start.7 = (bf16[176,1024]{1,0:T(8,128)(2,1)S(1)}, bf16[176,1024]{1,0:T(8,128)(2,1)S(1)}, u32[]{:S(2)}, u32[]{:S(2)}) collective-permute-start(bf16[176,1024]{1,0:T(8,128)(2,1)S(1)} %collective-permute-done.5.back2_ref), channel_id=1, source_target_pairs={{0,2},{2,0},{4,6},{6,4},{8,10},{10,8},{12,14},{14,12},{16,18},{18,... | collective-permute-start | bytes 1081352 | tf_op jit(solution)/shard_map/ppermute | solution.py:669
  20.6 4.4 %collective-permute-start.3 = (bf16[256,512]{1,0:T(8,128)(2,1)S(1)}, bf16[256,512]{1,0:T(8,128)(2,1)S(1)}, u32[]{:S(2)}, u32[]{:S(2)}) collective-permute-start(bf16[256,512]{1,0:T(8,128)(2,1)S(1)} %collective-permute-done.2.query_far_ref.refs_3_), channel_id=1, source_target_pairs={{0,2},{2,0},{4,6},{6,4},{8,10},{10,8},{12,14},{14,12},{16,18},{18,... | collective-permute-start | bytes 786440 | tf_op jit(solution)/shard_map/ppermute | solution.py:669
  22.3 2.7 %collective-permute-start.8 = (bf16[128,1024]{1,0:T(8,128)(2,1)S(1)}, bf16[128,1024]{1,0:T(8,128)(2,1)S(1)}, u32[]{:S(2)}, u32[]{:S(2)}) collective-permute-start(bf16[128,1024]{1,0:T(8,128)(2,1)S(1)} %collective-permute-done.6.back4_ref), channel_id=1, source_target_pairs={{0,2},{2,0},{4,6},{6,4},{8,10},{10,8},{12,14},{14,12},{16,18},{18,... | collective-permute-start | bytes 786440 | tf_op jit(solution)/shard_map/ppermute | solution.py:669
  23.4 7.9 %collective-permute-start.9 = (bf16[128,1024]{1,0:T(8,128)(2,1)S(1)}, bf16[128,1024]{1,0:T(8,128)(2,1)S(1)}, u32[]{:S(2)}, u32[]{:S(2)}) collective-permute-start(bf16[128,1024]{1,0:T(8,128)(2,1)S(1)} %copy-done.2), channel_id=1, source_target_pairs={{2,12},{6,16},{10,20},{14,24},{18,28},{3,13},{7,17},{11,21},{15,25... | collective-permute-start | bytes 786440 | tf_op jit(solution)/shard_map/ppermute | solution.py:669
  24.1 4.5 %copy-start.3 = (bf16[1,512,1024]{2,1,0:T(8,128)(2,1)S(1)}, bf16[1,512,1024]{2,1,0:T(8,128)(2,1)}, u32[]{:S(2)}) copy-start(bf16[1,512,1024]{2,1,0:T(8,128)(2,1)} %param.14) | copy-start | bytes 3145732
  24.2 4.5 %copy-start.4 = (bf16[1,128,1024]{2,1,0:T(8,128)(2,1)S(1)}, bf16[1,128,1024]{2,1,0:T(8,128)(2,1)}, u32[]{:S(2)}) copy-start(bf16[1,128,1024]{2,1,0:T(8,128)(2,1)} %param.9) | copy-start | bytes 786436
  28.7 2.7 %copy-start.5 = (bf16[128,1024]{1,0:T(8,128)(2,1)S(1)}, bf16[128,1024]{1,0:T(8,128)(2,1)}, u32[]{:S(2)}) copy-start(bf16[128,1024]{1,0:T(8,128)(2,1)} %top_ref.3) | copy-start | bytes 786436
  31.4 7.5 %copy-start.9 = (bf16[1,1024,512]{2,1,0:T(8,128)(2,1)S(1)}, bf16[1,1024,512]{2,1,0:T(8,128)(2,1)}, u32[]{:S(2)}) copy-start(bf16[1,1024,512]{2,1,0:T(8,128)(2,1)} %param.11) | copy-start | bytes 3145732
  36.8 5.9 %collective-permute-start.11 = (bf16[144,512]{1,0:T(8,128)(2,1)S(1)}, bf16[144,512]{1,0:T(8,128)(2,1)S(1)}, u32[]{:S(2)}, u32[]{:S(2)}) collective-permute-start(bf16[144,512]{1,0:T(8,128)(2,1)S(1)} %get-tuple-element.59.message_ref), channel_id=1, source_target_pairs={{9,1},{11,3},{13,5},{15,7},{17,9},{19,11},{21,13},{23,15},{25,17},... | collective-permute-start | bytes 442376 | tf_op jit(solution)/shard_map/ppermute | solution.py:669
  37.5 5.3 %collective-permute-start.10 = (bf16[144,512]{1,0:T(8,128)(2,1)S(1)}, bf16[144,512]{1,0:T(8,128)(2,1)S(1)}, u32[]{:S(2)}, u32[]{:S(2)}) collective-permute-start(bf16[144,512]{1,0:T(8,128)(2,1)S(1)} %get-tuple-element.59.message_ref), channel_id=1, source_target_pairs={{5,1},{7,3},{9,5},{11,7},{13,9},{15,11},{17,13},{19,15},{21,17},{2... | collective-permute-start | bytes 442376 | tf_op jit(solution)/shard_map/ppermute | solution.py:669
  38.2 5.2 %collective-permute-start.12 = (bf16[144,512]{1,0:T(8,128)(2,1)S(1)}, bf16[144,512]{1,0:T(8,128)(2,1)S(1)}, u32[]{:S(2)}, u32[]{:S(2)}) collective-permute-start(bf16[144,512]{1,0:T(8,128)(2,1)S(1)} %get-tuple-element.59.message_ref), channel_id=1, source_target_pairs={{0,2},{2,0},{4,6},{6,4},{8,10},{10,8},{12,14},{14,12},{16,18},{18,... | collective-permute-start | bytes 442376 | tf_op jit(solution)/shard_map/ppermute | solution.py:669
  38.9 5.5 %copy-start = (bf16[1,1024,512]{2,1,0:T(8,128)(2,1)S(1)}, bf16[1,1024,512]{2,1,0:T(8,128)(2,1)}, u32[]{:S(2)}) copy-start(bf16[1,1024,512]{2,1,0:T(8,128)(2,1)} %param.12) | copy-start | bytes 3145732
  38.9 5.5 %copy-start.1 = (bf16[1,1024,512]{2,1,0:T(8,128)(2,1)S(1)}, bf16[1,1024,512]{2,1,0:T(8,128)(2,1)}, u32[]{:S(2)}) copy-start(bf16[1,1024,512]{2,1,0:T(8,128)(2,1)} %param.13) | copy-start | bytes 3145732
  42.8 1.4 %collective-permute-start.13 = (bf16[144,512]{1,0:T(8,128)(2,1)S(1)}, bf16[144,512]{1,0:T(8,128)(2,1)S(1)}, u32[]{:S(2)}, u32[]{:S(2)}) collective-permute-start(bf16[144,512]{1,0:T(8,128)(2,1)S(1)} %collective-permute-done.10.next2_ref), channel_id=1, source_target_pairs={{0,2},{2,0},{4,6},{6,4},{8,10},{10,8},{12,14},{14,12},{16,18},{18,... | collective-permute-start | bytes 442376 | tf_op jit(solution)/shard_map/ppermute | solution.py:669
  42.9 1.5 %collective-permute-start.14 = (bf16[144,512]{1,0:T(8,128)(2,1)S(1)}, bf16[144,512]{1,0:T(8,128)(2,1)S(1)}, u32[]{:S(2)}, u32[]{:S(2)}) collective-permute-start(bf16[144,512]{1,0:T(8,128)(2,1)S(1)} %collective-permute-done.11.next4_ref), channel_id=1, source_target_pairs={{0,2},{2,0},{4,6},{6,4},{8,10},{10,8},{12,14},{14,12},{16,18},{18,... | collective-permute-start | bytes 442376 | tf_op jit(solution)/shard_map/ppermute | solution.py:669
  44.4 0.7 copy-start.7
  48.3 15.7 %collective-permute-start.15 = (bf16[128,1024]{1,0:T(8,128)(2,1)S(1)}, bf16[128,1024]{1,0:T(8,128)(2,1)S(1)}, u32[]{:S(2)}, u32[]{:S(2)}) collective-permute-start(bf16[128,1024]{1,0:T(8,128)(2,1)S(1)} %get-tuple-element.69), channel_id=1, source_target_pairs={{1,0},{3,2},{5,4},{7,6},{9,8},{11,10},{13,12},{15,14},{17,16},{19,... | collective-permute-start | bytes 786440 | tf_op jit(solution)/shard_map/ppermute | solution.py:669
  56.5 7.5 %collective-permute-start.16 = (bf16[32,1024]{1,0:T(8,128)(2,1)S(1)}, bf16[32,1024]{1,0:T(8,128)(2,1)S(1)}, u32[]{:S(2)}, u32[]{:S(2)}) collective-permute-start(bf16[32,1024]{1,0:T(8,128)(2,1)S(1)} %get-tuple-element.70), channel_id=1, source_target_pairs={{3,0},{5,2},{7,4},{9,6},{11,8},{13,10},{15,12},{17,14},{19,16},{21... | collective-permute-start | bytes 196616 | tf_op jit(solution)/shard_map/ppermute | solution.py:669
  66.8 8.8 %collective-permute-start.18 = (bf16[144,512]{1,0:T(8,128)(2,1)S(1)}, bf16[144,512]{1,0:T(8,128)(2,1)S(1)}, u32[]{:S(2)}, u32[]{:S(2)}) collective-permute-start(bf16[144,512]{1,0:T(8,128)(2,1)S(1)} %get-tuple-element.72.message_ref), channel_id=1, source_target_pairs={{8,0},{10,2},{12,4},{14,6},{16,8},{18,10},{20,12},{22,14},{24,16},... | collective-permute-start | bytes 442376 | tf_op jit(solution)/shard_map/ppermute | solution.py:669
  68.8 7.0 %collective-permute-start.17 = (bf16[144,512]{1,0:T(8,128)(2,1)S(1)}, bf16[144,512]{1,0:T(8,128)(2,1)S(1)}, u32[]{:S(2)}, u32[]{:S(2)}) collective-permute-start(bf16[144,512]{1,0:T(8,128)(2,1)S(1)} %get-tuple-element.72.message_ref), channel_id=1, source_target_pairs={{4,0},{6,2},{8,4},{10,6},{12,8},{14,10},{16,12},{18,14},{20,16},{2... | collective-permute-start | bytes 442376 | tf_op jit(solution)/shard_map/ppermute | solution.py:669
  70.7 7.2 %collective-permute-start.19 = (bf16[144,512]{1,0:T(8,128)(2,1)S(1)}, bf16[144,512]{1,0:T(8,128)(2,1)S(1)}, u32[]{:S(2)}, u32[]{:S(2)}) collective-permute-start(bf16[144,512]{1,0:T(8,128)(2,1)S(1)} %get-tuple-element.72.message_ref), channel_id=1, source_target_pairs={{0,2},{2,0},{4,6},{6,4},{8,10},{10,8},{12,14},{14,12},{16,18},{18,... | collective-permute-start | bytes 442376 | tf_op jit(solution)/shard_map/ppermute | solution.py:669
  75.6 2.3 %collective-permute-start.21 = (bf16[144,512]{1,0:T(8,128)(2,1)S(1)}, bf16[144,512]{1,0:T(8,128)(2,1)S(1)}, u32[]{:S(2)}, u32[]{:S(2)}) collective-permute-start(bf16[144,512]{1,0:T(8,128)(2,1)S(1)} %collective-permute-done.18.refs_6_), channel_id=1, source_target_pairs={{0,2},{2,0},{4,6},{6,4},{8,10},{10,8},{12,14},{14,12},{16,18},{18,... | collective-permute-start | bytes 442376 | tf_op jit(solution)/shard_map/ppermute | solution.py:669
  75.7 3.2 %collective-permute-start.20 = (bf16[144,512]{1,0:T(8,128)(2,1)S(1)}, bf16[144,512]{1,0:T(8,128)(2,1)S(1)}, u32[]{:S(2)}, u32[]{:S(2)}) collective-permute-start(bf16[144,512]{1,0:T(8,128)(2,1)S(1)} %collective-permute-done.17.refs_5_), channel_id=1, source_target_pairs={{0,2},{2,0},{4,6},{6,4},{8,10},{10,8},{12,14},{14,12},{16,18},{18,... | collective-permute-start | bytes 442376 | tf_op jit(solution)/shard_map/ppermute | solution.py:669
